TPU v7x, 32 devices: a whole 2x2x4 slice. The times are simulated.
32 devices in a mesh: groups: 1, dp: 32 (over z, y, x, core).
Axes of the slice: x: 2, y: 2, z: 4, core: 2. Of those that a mesh axis runs over, the one named last changes fastest.
Arguments:
- residual: bfloat16 [512, 4096], P(('groups', 'dp')), may hold values from -11 to 11
- queries: bfloat16 [512, 8192], P(('groups', 'dp')), may hold values from -160 to 160
- new_kv: bfloat16 [2, 512, 512], P(None, ('groups', 'dp')), may hold values from -6 to 6
- cache_kv: bfloat16 [2, 512, 128, 512], P(None, ('groups', 'dp')), may hold values from -7 to 7
- lengths: int32 [512], P(('groups', 'dp')), may hold values from 2 to 128, as said below
- out_weight: bfloat16 [8192, 4096], P('dp'), may hold values from -0.0625 to 0.0625
- norm_gain: float32 [4096], replicated, may hold values from 0.1 to 1.9
- w_gate: bfloat16 [32, 4096, 768], P('dp'), may hold values from -0.09375 to 0.09375
- w_up: bfloat16 [32, 4096, 768], P('dp'), may hold values from -0.09375 to 0.09375
- w_down: bfloat16 [32, 768, 4096], P('dp'), may hold values from -0.15625 to 0.15625
- expert_ids: int32 [512, 8], P(('groups', 'dp')), may hold values from 0 to 15, all different within a row; in each aligned block of 16 rows (0 to 15, 16 to 31, ...) at most 16 rows name the same one
- combine_weights: float32 [512, 8], P(('groups', 'dp')), may hold values from 0.05 to 0.3
Outputs:
- layer_out: bfloat16 [512, 4096], P(('groups', 'dp'))
Inputs may be any that keep to these rules, and one draw needn't show every extreme that they name: `expert_ids`: in the 16 rows of each device no expert is named more than 16 times, a bound that some block reaches. Sequence t attends to cached positions 0 to lengths[t] - 1; some sequence uses all 128.
All inputs are finite; a program needn't handle non-finite values.
Results may differ from a plain program's by a relative error of at most 0.028.
Values may be sent and summed in bfloat16 or wider, within the bound.
No kernel may reach another device: no remote copies, remote signals or barrier semaphores. Data moves between devices by JAX's collectives and lax.ppermute only.
A program may use at most 128 MiB of HBM per device.

v0:
```python
import math

import jax
import jax.numpy as jnp
from jax import lax
from jax.sharding import PartitionSpec as P

H = 64
KVH = 4
DH = 128
TOP = 8


def attend(queries, new_kv, cache_kv, lengths):
    count_rows = queries.shape[0]
    span = cache_kv.shape[2]
    per_group = H // KVH
    score_scale = 1.0 / math.sqrt(DH)
    query_heads = queries.reshape(count_rows, KVH, per_group, DH)
    cached_keys = cache_kv[0].reshape(count_rows, span, KVH, DH)
    cached_values = cache_kv[1].reshape(count_rows, span, KVH, DH)
    new_key = new_kv[0].reshape(count_rows, KVH, DH)
    new_value = new_kv[1].reshape(count_rows, KVH, DH)
    cached_scores = (
        jnp.einsum("tkgd,tckd->tkgc", query_heads, cached_keys, preferred_element_type=jnp.float32)
        * score_scale
    )
    own_score = (
        jnp.einsum("tkgd,tkd->tkg", query_heads, new_key, preferred_element_type=jnp.float32)
        * score_scale
    )
    live_mask = (jnp.arange(span, dtype=jnp.int32)[None, :] < lengths[:, None])[:, None, None, :]
    cached_scores = jnp.where(live_mask, cached_scores, -1e30)
    row_peak = jnp.maximum(jnp.max(cached_scores, axis=-1), own_score)
    cached_exp = jnp.exp(cached_scores - row_peak[..., None])
    own_exp = jnp.exp(own_score - row_peak)
    denominator = jnp.sum(cached_exp, axis=-1) + own_exp
    cached_probs = (cached_exp / denominator[..., None]).astype(jnp.bfloat16)
    own_probs = (own_exp / denominator).astype(jnp.bfloat16)
    attended = jnp.einsum(
        "tkgc,tckd->tkgd", cached_probs, cached_values, preferred_element_type=jnp.float32
    )
    attended = (
        attended
        + own_probs.astype(jnp.float32)[..., None] * new_value.astype(jnp.float32)[:, :, None, :]
    )
    return attended.reshape(count_rows, H * DH).astype(jnp.bfloat16)


def normalize(hidden_state, norm_gain):
    values = hidden_state.astype(jnp.float32)
    mean_square = jnp.mean(values * values, axis=-1, keepdims=True)
    return (values * lax.rsqrt(mean_square + 1e-06) * norm_gain).astype(jnp.bfloat16)


def per_device(
    residual,
    queries,
    new_kv,
    cache_kv,
    lengths,
    out_weight,
    norm_gain,
    w_gate,
    w_up,
    w_down,
    expert_ids,
    combine_weights,
):
    local_rows = residual.shape[0]
    model_width = residual.shape[1]
    devices = lax.axis_size("dp")
    experts = devices // 2
    capacity = min(local_rows, 4 * local_rows * TOP // devices)
    attn_out = attend(queries, new_kv, cache_kv, lengths)
    blocks = lax.all_to_all(attn_out, "dp", split_axis=1, concat_axis=0, tiled=True)
    projected = lax.psum_scatter(
        jnp.dot(blocks, out_weight, preferred_element_type=jnp.float32).astype(jnp.bfloat16),
        "dp",
        scatter_dimension=0,
        tiled=True,
    ).astype(jnp.float32)
    hidden_state = (residual.astype(jnp.float32) + projected).astype(jnp.bfloat16)
    normed = normalize(hidden_state, norm_gain)
    flat_ids = expert_ids.reshape(-1)
    expert_hot = (flat_ids[:, None] == jnp.arange(experts, dtype=jnp.int32)[None, :]).astype(
        jnp.int32
    )
    position = jnp.cumsum(expert_hot, axis=0) - expert_hot
    slot_index = jnp.sum(position * expert_hot, axis=1)
    destination = flat_ids * capacity + slot_index
    dest_match = destination[:, None] == jnp.arange(experts * capacity, dtype=jnp.int32)[None, :]
    dest_match = dest_match.reshape(local_rows, TOP, experts * capacity)
    gather_matrix = jnp.any(dest_match, axis=1).astype(jnp.bfloat16)
    outgoing = jnp.dot(gather_matrix.T, normed, preferred_element_type=jnp.float32).astype(
        jnp.bfloat16
    )
    outgoing = outgoing.reshape(experts, capacity, model_width)
    weight_matrix = jnp.sum(jnp.where(dest_match, combine_weights[:, :, None], 0.0), axis=1)
    doubled = jnp.repeat(outgoing, 2, axis=0)
    arrived = lax.all_to_all(doubled, "dp", split_axis=0, concat_axis=0, tiled=True)
    shape_in = arrived.shape
    flat_rows = arrived.reshape(-1, model_width)
    gate_part = jnp.dot(flat_rows, w_gate[0], preferred_element_type=jnp.float32)
    up_part = jnp.dot(flat_rows, w_up[0], preferred_element_type=jnp.float32)
    activated = (jax.nn.silu(gate_part) * up_part).astype(jnp.bfloat16)
    half_out = jnp.dot(activated, w_down[0], preferred_element_type=jnp.float32).astype(
        jnp.bfloat16
    )
    partial_out = half_out.reshape(shape_in)
    returned = lax.all_to_all(partial_out, "dp", split_axis=0, concat_axis=0, tiled=True)
    returned = returned.reshape(experts, 2, capacity, model_width).astype(jnp.float32)
    expert_sum = jnp.sum(returned, axis=1).reshape(experts * capacity, model_width)
    mixture = jnp.dot(
        weight_matrix,
        expert_sum,
        precision=lax.Precision.HIGHEST,
        preferred_element_type=jnp.float32,
    )
    return (hidden_state.astype(jnp.float32) + mixture).astype(jnp.bfloat16)


def solution(mesh):
    placed = (
        P(("groups", "dp"), None),
        P(("groups", "dp"), None),
        P(None, ("groups", "dp"), None),
        P(None, ("groups", "dp"), None, None),
        P(("groups", "dp")),
        P("dp", None),
        P(),
        P("dp", None, None),
        P("dp", None, None),
        P("dp", None, None),
        P(("groups", "dp"), None),
        P(("groups", "dp"), None),
    )
    return jax.shard_map(
        per_device, mesh=mesh, in_specs=placed, out_specs=P(("groups", "dp"), None), check_vma=False
    )
```

profile of v0, /device:TPU:0, one launch (start us, length us, event | category | flops | bytes accessed | tf_op | source)
XLA Modules:
  0.0 419.0 jit_solution(617986943651883065)
XLA Ops:
  6.5 4.8 %fusion.30 = (bf16[1,16,128,512]{3,2,1,0:T(8,128)(2,1)}, bf16[1,16,128,512]{3,2,1,0:T(8,128)(2,1)}) fusion(bf16[2,16,128,512]{3,2,1,0:T(8,128)(2,1)} %param.15), kind=kLoop, calls=%fused_computation.46 | loop fusion | bytes 8388608 | tf_op jit(solution)/shard_map/slice | solution.py:20
  11.3 4.0 copy.36
  15.4 0.1 iota_compare_fusion.2
  15.5 0.2 fusion.33
  15.7 2.3 fusion.32
  18.1 0.4 fusion.16
  18.6 3.9 copy.37
  22.5 2.8 fusion.13
  25.3 0.1 convert_element_type.74
  25.5 0.2 copy.28
  25.6 17.7 %all_to_all.26 = bf16[16,32,256]{2,0,1:T(8,128)(2,1)S(1)} all-to-all(bf16[16,32,256]{2,0,1:T(8,128)(2,1)S(1)} %copy.28), channel_id=1, replica_groups=mesh['groups'=1,'dp'=32] {'dp'}, dimensions={1} | all-to-all | bytes 524288 | tf_op jit(solution)/shard_map/all_to_all | solution.py:76
  43.3 3.2 convolution_convert_fusion
  46.6 0.1 copy.29
  46.6 0.1 eq.29
  46.7 0.1 fusion.26
  46.8 0.2 reduce_window_sum.11
  47.0 0.2 select_reduce_fusion.1
  47.2 0.1 reduce_sum.49
  47.3 0.1 fusion.25
  47.4 137.9 %reduce-scatter.2.cloned.1.call-done = bf16[16,4096]{1,0:T(8,128)(2,1)} async-done(((bf16[512,4096]{1,0:T(8,128)(2,1)}), bf16[16,4096]{1,0:T(8,128)(2,1)}) %reduce-scatter.2.cloned.1.call-update) | async-done | bytes 131088 | tf_op jit(solution)/shard_map/reduce_scatter | solution.py:77
  185.3 1.1 fusion.17
  186.4 1.7 convolution_convert_fusion.1
  188.0 0.5 broadcast_in_dim.44
  188.6 95.7 %all_to_all.27 = bf16[32,16,4096]{2,1,0:T(8,128)(2,1)S(1)} all-to-all(bf16[32,16,4096]{2,1,0:T(8,128)(2,1)S(1)} %bitcast.48), channel_id=1, replica_groups=mesh['groups'=1,'dp'=32] {'dp'}, dimensions={0} | all-to-all | bytes 8388608 | tf_op jit(solution)/shard_map/all_to_all | solution.py:101
  284.2 2.0 copy-done.1
  286.2 4.7 %fusion.4 = f32[512,768]{1,0:T(8,128)} fusion(bf16[512,4096]{1,0:T(8,128)(2,1)S(1)} %bitcast.52, bf16[1,4096,768]{2,1,0:T(8,128)(2,1)S(1)} %bitcast.62), kind=kOutput, calls=%fused_computation.5 | convolution fusion | flops 3221225472 | bytes 12058624 | tf_op jit(solution)/shard_map/dot_general | solution.py:104
  290.9 17.0 %fusion.6 = bf16[512,4096]{1,0:T(8,128)(2,1)} fusion(bf16[1,768,4096]{2,1,0:T(8,128)(2,1)} %param.21, f32[512,768]{1,0:T(8,128)} %fusion.4, bf16[512,4096]{1,0:T(8,128)(2,1)} %bitcast.53, bf16[1,4096,768]{2,1,0:T(8,128)(2,1)} %param.20), kind=kOutput, calls=%fused_computation.7 | convolution fusion | flops 6446907392 | bytes 22544384 | tf_op jit(solution)/shard_map/dot_general | solution.py:107
  307.9 4.0 all-to-all-start.2
  312.0 0.1 select_reduce_fusion
  312.1 93.6 %all-to-all-done.2 = bf16[32,16,4096]{2,1,0:T(8,128)(2,1)} async-done(((bf16[32,16,4096]{2,1,0:T(8,128)(2,1)}), bf16[32,16,4096]{2,1,0:T(8,128)(2,1)}, u32[]{:S(2)}, u32[]{:S(2)}) %all-to-all-start.2) | async-done | bytes 4194336 | tf_op jit(solution)/shard_map/all_to_all | solution.py:111
  405.7 3.7 convert_reduce_fusion
  409.4 2.7 fusion.9
  (35 shorter events, 0.3 us)
Async XLA Ops:
  6.5 36.8 %copy-start = (bf16[256,4096]{1,0:T(8,128)(2,1)S(1)}, bf16[256,4096]{1,0:T(8,128)(2,1)}, u32[]{:S(2)}) copy-start(bf16[256,4096]{1,0:T(8,128)(2,1)} %param.17) | copy-start | bytes 6291460
  6.5 178.8 %reduce-scatter.2.cloned.1.call-start = ((), (), s32[]{:S(2)}) async-start(), calls=%async_computation.4 | async-start | bytes 4325376 | tf_op jit(solution)/shard_map/reduce_scatter | solution.py:77
  11.3 4.0 copy-start.4
  11.3 4.0 copy-start.9
  11.3 4.1 copy-start.5
  43.3 3.2 copy-start.7
  43.3 142.0 %copy-start.2 = (bf16[16,4096]{1,0:T(8,128)(2,1)S(1)}, bf16[16,4096]{1,0:T(8,128)(2,1)}, u32[]{:S(2)}) copy-start(bf16[16,4096]{1,0:T(8,128)(2,1)} %param.12) | copy-start | bytes 393220
  43.3 143.0 %copy-start.6 = (f32[4096]{0:T(1024)S(1)}, f32[4096]{0:T(1024)}, u32[]{:S(2)}) copy-start(f32[4096]{0:T(1024)} %param.18) | copy-start | bytes 49156
  188.0 98.2 %slice-start = ((s8[6291456]{0:T(1024)(128)(4,1)}), s8[2097152]{0:T(1024)(128)(4,1)S(1)}, s32[]{:S(2)}) async-start(s8[6291456]{0:T(1024)(128)(4,1)} %bitcast.61), calls=%async_computation.5 | async-start | bytes 4194304
  188.6 97.6 %slice-start.1 = ((s8[6291456]{0:T(1024)(128)(4,1)}), s8[4194304]{0:T(1024)(128)(4,1)S(1)}, s32[]{:S(2)}) async-start(s8[6291456]{0:T(1024)(128)(4,1)} %bitcast.61), calls=%async_computation.6 | async-start | bytes 8388608
  284.2 2.0 copy-start.1
  307.9 4.0 copy-start.8
  307.9 97.8 %all-to-all-start.2 = ((bf16[32,16,4096]{2,1,0:T(8,128)(2,1)}), bf16[32,16,4096]{2,1,0:T(8,128)(2,1)}, u32[]{:S(2)}, u32[]{:S(2)}) async-start(bf16[32,16,4096]{2,1,0:T(8,128)(2,1)} %bitcast.51), calls=%async_computation.3 | async-start | bytes 8388608 | tf_op jit(solution)/shard_map/all_to_all | solution.py:111
  312.1 97.3 %copy-start.3 = (bf16[16,4096]{1,0:T(8,128)(2,1)S(1)}, bf16[16,4096]{1,0:T(8,128)(2,1)}, u32[]{:S(2)}) copy-start(bf16[16,4096]{1,0:T(8,128)(2,1)} %reduce-scatter.2.cloned.1.call-done) | copy-start | bytes 393220
Sparse Core Ops, SparseCore 0:
  46.7 138.5 reduce-scatter.1
where the time goes:
time: 419 us
  waiting for transfers between devices  232 us (55%)
  blocking collectives  113 us (27%)
  matrix products  34.7 us (8%)
  local copies, waits for them, and re-layouts  15.8 us (4%)
  between operations  13.6 us (3%)
  other arithmetic  6.03 us (1%)
    reduce_scatter x1, waiting for transfers between devices, per_device(): lax.psum_scatter(jnp.dot(blocks, out_weight, preferred_element_type=jnp.f...  138 us
    all_to_all x1, blocking collectives, per_device(): lax.all_to_all(doubled, 'dp', split_axis=0, concat_axis=0, tiled=True)  95.7 us
    all_to_all x1, waiting for transfers between devices, per_device(): lax.all_to_all(partial_out, 'dp', split_axis=0, concat_axis=0, tiled=True)  93.6 us
    all_to_all x1, blocking collectives, per_device(): lax.all_to_all(attn_out, 'dp', split_axis=1, concat_axis=0, tiled=True)  17.7 us
    dot_general x1, matrix products, per_device(): jnp.dot(activated, w_down[0], preferred_element_type=jnp.float32)  17 us
    unnamed x29, local copies, waits for them, and re-layouts  10.1 us
  transfers between devices with their start and end apart: 2, of which 2 were waited for; matrix products, arithmetic and copies ran while one was open for 0% of the time, Pallas kernels for 0%

commit v1 on v0

v1 whole, which is shorter than its diff:
```python
import math

import jax
import jax.numpy as jnp
from jax import lax
from jax.sharding import PartitionSpec as P

H = 64
KVH = 4
DH = 128
TOP = 8
F32 = jnp.float32
BF16 = jnp.bfloat16


def attend(queries, new_kv, cache_kv, lengths):
    count_rows = queries.shape[0]
    span = cache_kv.shape[2]
    per_group = H // KVH
    score_scale = 1.0 / math.sqrt(DH)
    query_heads = queries.reshape(count_rows, KVH, per_group, DH)
    cached_keys = cache_kv[0].reshape(count_rows, span, KVH, DH)
    cached_values = cache_kv[1].reshape(count_rows, span, KVH, DH)
    new_key = new_kv[0].reshape(count_rows, KVH, DH)
    new_value = new_kv[1].reshape(count_rows, KVH, DH)
    cached_scores = (
        jnp.einsum("tkgd,tckd->tkgc", query_heads, cached_keys, preferred_element_type=jnp.float32)
        * score_scale
    )
    own_score = (
        jnp.einsum("tkgd,tkd->tkg", query_heads, new_key, preferred_element_type=jnp.float32)
        * score_scale
    )
    live_mask = (jnp.arange(span, dtype=jnp.int32)[None, :] < lengths[:, None])[:, None, None, :]
    cached_scores = jnp.where(live_mask, cached_scores, -1e30)
    row_peak = jnp.maximum(jnp.max(cached_scores, axis=-1), own_score)
    cached_exp = jnp.exp(cached_scores - row_peak[..., None])
    own_exp = jnp.exp(own_score - row_peak)
    denominator = jnp.sum(cached_exp, axis=-1) + own_exp
    cached_probs = (cached_exp / denominator[..., None]).astype(jnp.bfloat16)
    own_probs = (own_exp / denominator).astype(jnp.bfloat16)
    attended = jnp.einsum(
        "tkgc,tckd->tkgd", cached_probs, cached_values, preferred_element_type=jnp.float32
    )
    attended = (
        attended
        + own_probs.astype(jnp.float32)[..., None] * new_value.astype(jnp.float32)[:, :, None, :]
    )
    return attended.reshape(count_rows, H * DH).astype(jnp.bfloat16)


def normalize(hidden_state, norm_gain):
    values = hidden_state.astype(jnp.float32)
    mean_square = jnp.mean(values * values, axis=-1, keepdims=True)
    return (values * lax.rsqrt(mean_square + 1e-06) * norm_gain).astype(jnp.bfloat16)


def step_bits(devices):
    bits = [1 << i for i in range(1, devices.bit_length() - 1)]
    other = bits[1::-1] + bits[2:] if len(bits) > 1 else bits
    return bits, other


def swap_step(step, devices):
    orders = step_bits(devices)
    return [(i, i ^ orders[i & 1][step]) for i in range(devices)]


def reduce_slots(parts, rows, devices):
    steps = devices.bit_length() - 2
    kept = parts
    for step in range(steps):
        half = kept.shape[0] // 2
        came = lax.ppermute(kept[half:].astype(BF16), "dp", swap_step(step, devices))
        kept = kept[:half].astype(F32) + came.astype(F32)
    return kept


def gather_slots(own, devices):
    steps = devices.bit_length() - 2
    for step in reversed(range(steps)):
        own = jnp.concatenate([own, lax.ppermute(own, "dp", swap_step(step, devices))], axis=0)
    return own


def per_device(
    residual,
    queries,
    new_kv,
    cache_kv,
    lengths,
    out_weight,
    norm_gain,
    w_gate,
    w_up,
    w_down,
    expert_ids,
    combine_weights,
):
    rows = residual.shape[0]
    width = residual.shape[1]
    devices = lax.axis_size("dp")
    chips = devices // 2
    block = out_weight.shape[0]
    me = lax.axis_index("dp")
    core = me % 2
    chip = me // 2
    steps = devices.bit_length() - 2
    core_swap = [(i, i ^ 1) for i in range(devices)]
    core_groups = [[2 * i + c for i in range(chips)] for c in range(2)]

    out_other = lax.ppermute(out_weight, "dp", core_swap)
    gate_other = lax.ppermute(w_gate[0], "dp", core_swap)
    up_other = lax.ppermute(w_up[0], "dp", core_swap)
    down_other = lax.ppermute(w_down[0], "dp", core_swap)

    attn_out = attend(queries, new_kv, cache_kv, lengths).reshape(rows, chips, 2, block)
    attn_out = jnp.where(core == 0, attn_out, attn_out[:, :, ::-1]).reshape(rows, chips * 2 * block)
    blocks = lax.all_to_all(
        attn_out, "dp", split_axis=1, concat_axis=0, axis_index_groups=core_groups, tiled=True
    ).reshape(chips, rows, 2 * block)

    orders = step_bits(devices)
    slot = jnp.arange(chips, dtype=jnp.int32)
    offset = jnp.zeros_like(slot)
    for step in range(steps):
        here = jnp.where(core == 0, orders[0][step], orders[1][step]) // 2
        offset = offset + here * ((slot >> (steps - 1 - step)) & 1)
    blocks = jnp.take(blocks, chip ^ offset, axis=0).reshape(chips * rows, 2 * block)

    partial = jnp.dot(blocks[:, :block], out_weight, preferred_element_type=F32) + jnp.dot(
        blocks[:, block:], out_other, preferred_element_type=F32
    )
    projected = reduce_slots(partial.astype(BF16), rows, devices)
    hidden_state = (residual.astype(F32) + projected).astype(BF16)
    normed = normalize(hidden_state, norm_gain)

    picks = expert_ids[:, :, None] == jnp.arange(chips, dtype=jnp.int32)
    mix = jnp.sum(jnp.where(picks, combine_weights[:, :, None], 0.0), axis=1)
    mix_hi = mix.astype(BF16)
    mix_mid = (mix - mix_hi.astype(F32)).astype(BF16)
    mix_low = (mix - mix_hi.astype(F32) - mix_mid.astype(F32)).astype(BF16)
    extra = jnp.concatenate([mix_hi, mix_mid, mix_low], axis=1)
    extra = jnp.pad(extra, ((0, 0), (0, -extra.shape[1] % 128)))
    gathered = gather_slots(jnp.concatenate([normed, extra], axis=1), devices)
    tokens = gathered[:, :width]
    extra = gathered[:, width : width + 3 * chips].reshape(chips * rows, 3, chips).astype(F32)
    mine = jnp.where(jnp.arange(chips) == chip, extra, 0.0)
    weight = jnp.sum(mine, axis=(1, 2))[:, None]

    total = 0.0
    for gate, up, down in ((w_gate[0], w_up[0], w_down[0]), (gate_other, up_other, down_other)):
        gate_part = jnp.dot(tokens, gate, preferred_element_type=F32)
        up_part = jnp.dot(tokens, up, preferred_element_type=F32)
        activated = (jax.nn.silu(gate_part) * up_part).astype(BF16)
        total = total + jnp.dot(activated, down, preferred_element_type=F32)
    mixture = reduce_slots((total * weight).astype(BF16), rows, devices)
    return (hidden_state.astype(F32) + mixture).astype(BF16)


def solution(mesh):
    placed = (
        P(("groups", "dp"), None),
        P(("groups", "dp"), None),
        P(None, ("groups", "dp"), None),
        P(None, ("groups", "dp"), None, None),
        P(("groups", "dp")),
        P("dp", None),
        P(),
        P("dp", None, None),
        P("dp", None, None),
        P("dp", None, None),
        P(("groups", "dp"), None),
        P(("groups", "dp"), None),
    )
    return jax.shard_map(
        per_device, mesh=mesh, in_specs=placed, out_specs=P(("groups", "dp"), None), check_vma=False
    )
```

time: 419 us -> 200 us (0.48)
  blocking collectives: 113 us -> 0 us
  waiting for transfers between devices: 232 us -> 123 us
  starting transfers between devices: 3.99 us -> 18.5 us
  between operations: 13.6 us -> 0.47 us
    reduce_scatter x1 -> x0, waiting for transfers between devices: 138 us -> none  [per_device(): lax.psum_scatter(jnp.dot(blocks, out_weight, preferred_element_type=jnp.f...]
    all_to_all x2 -> x0, blocking collectives: 113 us -> none  [the longest x1 95.7 us: per_device(): lax.all_to_all(doubled, 'dp', split_axis=0, concat_axis=0, tiled=True)]
    ppermute x0 -> x16, waiting for transfers between devices: none -> 113 us  [the longest x8 75.7 us: reduce_slots(): lax.ppermute(kept[half:].astype(BF16), 'dp', swap_step(step, devices))]
    all_to_all x1, waiting for transfers between devices: 93.6 us -> 10.1 us  [per_device(): lax.all_to_all(attn_out, 'dp', split_axis=1, concat_axis=0, axis_index_gr...]
    ppermute x0 -> x16, starting transfers between devices: none -> 10.5 us  [the longest x8 7.07 us: reduce_slots(): lax.ppermute(kept[half:].astype(BF16), 'dp', swap_step(step, devices))]
    dot_general x5 -> x6, matrix products: 29.3 us -> 35.2 us  [the longest x2 22.2 us: per_device(): total = total + jnp.dot(activated, down, preferred_element_type=F32)]
    unnamed x29 -> x20, local copies, waits for them, and re-layouts: 10.1 us -> 7.33 us
  transfers between devices with their start and end apart: 2 -> 17, of which waited for: 2 -> 13; matrix products, arithmetic and copies ran while one was open for 0% -> 21% of each run, Pallas kernels for 0% -> 0%
where the time goes in v1:
time: 200 us
  waiting for transfers between devices  123 us (62%)
  matrix products  37.5 us (19%)
  starting transfers between devices  18.5 us (9%)
  local copies, waits for them, and re-layouts  16 us (8%)
  other arithmetic  4.39 us (2%)
    ppermute x8, waiting for transfers between devices, reduce_slots(): lax.ppermute(kept[half:].astype(BF16), 'dp', swap_step(step, devices))  75.7 us
    ppermute x4, waiting for transfers between devices, gather_slots(): lax.ppermute(own, 'dp', swap_step(step, devices))  37.2 us
    dot_general x2, matrix products, per_device(): total = total + jnp.dot(activated, down, preferred_element_type=F32)  22.2 us
    all_to_all x1, waiting for transfers between devices, per_device(): lax.all_to_all(attn_out, 'dp', split_axis=1, concat_axis=0, axis_index_gr...  10.1 us
    dot_general x2, matrix products, per_device(): up_part = jnp.dot(tokens, up, preferred_element_type=F32)  9.89 us
    all_to_all x1, starting transfers between devices, per_device(): lax.all_to_all(attn_out, 'dp', split_axis=1, concat_axis=0, axis_index_gr...  8.04 us
    unnamed x20, local copies, waits for them, and re-layouts  7.33 us
    ppermute x8, starting transfers between devices, reduce_slots(): lax.ppermute(kept[half:].astype(BF16), 'dp', swap_step(step, devices))  7.07 us
  transfers between devices with their start and end apart: 17, of which 13 were waited for; matrix products, arithmetic and copies ran while one was open for 21% of the time, Pallas kernels for 0%

profile of v1, /device:TPU:0, one launch (start us, length us, event | category | flops | bytes accessed | tf_op | source)
XLA Modules:
  0.0 199.9 jit_solution(5048814531735817079)
XLA Ops:
  1.9 1.0 copy.36
  2.9 4.7 %fusion.52 = (bf16[1,16,128,512]{3,2,1,0:T(8,128)(2,1)}, bf16[1,16,128,512]{3,2,1,0:T(8,128)(2,1)}) fusion(bf16[2,16,128,512]{3,2,1,0:T(8,128)(2,1)} %param.15), kind=kLoop, calls=%fused_computation.96 | loop fusion | bytes 8388608 | tf_op jit(solution)/shard_map/slice | solution.py:22
  7.6 3.0 %copy.34 = bf16[1,16,128,512]{2,3,1,0:T(8,128)(2,1)S(1)} copy(bf16[1,16,128,512]{3,2,1,0:T(8,128)(2,1)} %get-tuple-element.7) | data formatting | bytes 4194304
  10.9 0.8 fusion.55
  11.7 3.0 %copy.35 = bf16[1,16,128,512]{2,3,1,0:T(8,128)(2,1)S(1)} copy(bf16[1,16,128,512]{3,2,1,0:T(8,128)(2,1)} %get-tuple-element.8) | data formatting | bytes 4194304
  15.3 1.2 fusion.12
  16.7 1.4 rev.3
  18.3 0.9 copy.33
  19.2 8.0 %all-to-all-start = ((bf16[16,16,512]{2,0,1:T(8,128)(2,1)}), bf16[16,16,512]{2,0,1:T(8,128)(2,1)S(1)}, u32[]{:S(2)}, u32[]{:S(2)}) async-start(bf16[16,16,512]{2,0,1:T(8,128)(2,1)} %copy.33), calls=%async_computation | async-start | bytes 524288 | tf_op jit(solution)/shard_map/all_to_all | solution.py:119
  27.5 10.1 %all-to-all-done = bf16[16,16,512]{2,0,1:T(8,128)(2,1)S(1)} async-done(((bf16[16,16,512]{2,0,1:T(8,128)(2,1)}), bf16[16,16,512]{2,0,1:T(8,128)(2,1)S(1)}, u32[]{:S(2)}, u32[]{:S(2)}) %all-to-all-start) | async-done | bytes 262176 | tf_op jit(solution)/shard_map/all_to_all | solution.py:119
  39.0 2.4 %fusion.1 = bf16[256,4096]{1,0:T(8,128)(2,1)S(1)} fusion(f32[256,4096]{1,0:T(8,128)S(1)} %fusion.34, bf16[256,4096]{1,0:T(8,128)(2,1)} %collective-permute-done, bf16[256,512]{1,0:T(8,128)(2,1)S(1)} %bitcast_select_fusion), kind=kOutput, calls=%fused_computation.4 | convolution fusion | flops 538968064 | bytes 8519680 | tf_op jit(solution)/shard_map/dot_general | solution.py:131
  41.5 0.8 collective-permute-start.1
  42.3 14.0 %collective-permute-done.1 = bf16[128,4096]{1,0:T(8,128)(2,1)S(1)} collective-permute-done((bf16[128,4096]{1,0:T(8,128)(2,1)S(1)}, bf16[128,4096]{1,0:T(8,128)(2,1)S(1)}, u32[]{:S(2)}, u32[]{:S(2)}) %collective-permute-start.1) | collective-permute-done | bytes 1048608 | tf_op jit(solution)/shard_map/ppermute | solution.py:74
  56.7 1.0 collective-permute-start.2
  57.7 8.3 %collective-permute-done.2 = bf16[64,4096]{1,0:T(8,128)(2,1)S(1)} collective-permute-done((bf16[64,4096]{1,0:T(8,128)(2,1)S(1)}, bf16[64,4096]{1,0:T(8,128)(2,1)S(1)}, u32[]{:S(2)}, u32[]{:S(2)}) %collective-permute-start.2) | collective-permute-done | bytes 524320 | tf_op jit(solution)/shard_map/ppermute | solution.py:74
  66.1 1.2 collective-permute-start.3
  67.6 5.6 %collective-permute-done.3 = bf16[32,4096]{1,0:T(8,128)(2,1)S(1)} collective-permute-done((bf16[32,4096]{1,0:T(8,128)(2,1)S(1)}, bf16[32,4096]{1,0:T(8,128)(2,1)S(1)}, u32[]{:S(2)}, u32[]{:S(2)}) %collective-permute-start.3) | collective-permute-done | bytes 262176 | tf_op jit(solution)/shard_map/ppermute | solution.py:74
  73.6 9.3 %collective-permute-done.4 = bf16[16,4096]{1,0:T(8,128)(2,1)S(1)} collective-permute-done((bf16[16,4096]{1,0:T(8,128)(2,1)S(1)}, bf16[16,4096]{1,0:T(8,128)(2,1)S(1)}, u32[]{:S(2)}, u32[]{:S(2)}) %collective-permute-start.4) | collective-permute-done | bytes 131104 | tf_op jit(solution)/shard_map/ppermute | solution.py:74
  83.9 5.4 %collective-permute-done.5 = bf16[16,4224]{1,0:T(8,128)(2,1)S(1)} collective-permute-done((bf16[16,4224]{1,0:T(8,128)(2,1)S(1)}, bf16[16,4224]{1,0:T(8,128)(2,1)S(1)}, u32[]{:S(2)}, u32[]{:S(2)}) %collective-permute-start.5) | collective-permute-done | bytes 135200 | tf_op jit(solution)/shard_map/ppermute | solution.py:82
  89.5 6.3 %collective-permute-done.6 = bf16[32,4224]{1,0:T(8,128)(2,1)S(1)} collective-permute-done((bf16[32,4224]{1,0:T(8,128)(2,1)S(1)}, bf16[32,4224]{1,0:T(8,128)(2,1)S(1)}, u32[]{:S(2)}, u32[]{:S(2)}) %collective-permute-start.6) | collective-permute-done | bytes 270368 | tf_op jit(solution)/shard_map/ppermute | solution.py:82
  95.9 2.1 %collective-permute-start.7 = (bf16[64,4224]{1,0:T(8,128)(2,1)S(1)}, bf16[64,4224]{1,0:T(8,128)(2,1)S(1)}, u32[]{:S(2)}, u32[]{:S(2)}) collective-permute-start(bf16[64,4224]{1,0:T(8,128)(2,1)S(1)} %pad_maximum_fusion.1), channel_id=1, source_target_pairs={{0,4},{1,3},{2,6},{3,1},{4,0},{5,7},{6,2},{7,5},{8,12},{9,11},{10,... | collective-permute-start | bytes 1622024 | tf_op jit(solution)/shard_map/ppermute | solution.py:82
  98.0 10.5 %collective-permute-done.7 = bf16[64,4224]{1,0:T(8,128)(2,1)S(1)} collective-permute-done((bf16[64,4224]{1,0:T(8,128)(2,1)S(1)}, bf16[64,4224]{1,0:T(8,128)(2,1)S(1)}, u32[]{:S(2)}, u32[]{:S(2)}) %collective-permute-start.7) | collective-permute-done | bytes 540704 | tf_op jit(solution)/shard_map/ppermute | solution.py:82
  108.8 15.0 %collective-permute-done.8 = bf16[128,4224]{1,0:T(8,128)(2,1)S(1)} collective-permute-done((bf16[128,4224]{1,0:T(8,128)(2,1)S(1)}, bf16[128,4224]{1,0:T(8,128)(2,1)S(1)}, u32[]{:S(2)}, u32[]{:S(2)}) %collective-permute-start.8) | collective-permute-done | bytes 1081376 | tf_op jit(solution)/shard_map/ppermute | solution.py:82
  124.0 5.3 %fusion.7 = f32[256,768]{1,0:T(8,128)S(1)} fusion(bf16[256,4224]{1,0:T(8,128)(2,1)S(1)} %constant_dynamic-update-slice_fusion, bf16[1,4096,768]{2,1,0:T(8,128)(2,1)} %param.20), kind=kOutput, calls=%fused_computation.12 | convolution fusion | flops 1610612736 | bytes 9175040 | tf_op jit(solution)/shard_map/dot_general | solution.py:154
  129.3 11.3 %fusion.14 = f32[256,4096]{1,0:T(8,128)} fusion(f32[256,768]{1,0:T(8,128)S(1)} %fusion.7, bf16[256,4224]{1,0:T(8,128)(2,1)S(1)} %constant_dynamic-update-slice_fusion, bf16[1,768,4096]{2,1,0:T(8,128)(2,1)} %param.21, bf16[1,4096,768]{2,1,0:T(8,128)(2,1)} %param.19), kind=kOutput, calls=%fused_computation.36 | convolution fusion | flops 3222405120 | bytes 19660800 | tf_op jit(solution)/shard_map/dot_general | solution.py:156
  140.6 4.6 %fusion.3 = f32[256,768]{1,0:T(8,128)S(1)} fusion(bf16[4096,768]{1,0:T(8,128)(2,1)} %collective-permute-done.10, bf16[256,4224]{1,0:T(8,128)(2,1)S(1)} %constant_dynamic-update-slice_fusion), kind=kOutput, calls=%fused_computation.8 | convolution fusion | flops 1610612736 | bytes 9175040 | tf_op jit(solution)/shard_map/dot_general | solution.py:154
  145.2 11.0 %fusion.2 = bf16[256,4096]{1,0:T(8,128)(2,1)S(1)} fusion(f32[256,4096]{1,0:T(8,128)} %fusion.14, bf16[768,4096]{1,0:T(8,128)(2,1)} %collective-permute-done.11, f32[256]{0:T(256)S(1)} %select_reduce_fusion, f32[256,768]{1,0:T(8,128)S(1)} %fusion.3, bf16[4096,768]{1,0:T(8,128)(2,1)} %collective-permute-done.9, bf16[256,4224]{1,0:T(8,128)(2,1)} %copy-done.2), kind=kOutput, calls=%fused_computation.5 | convolution fusion | flops 3225550848 | bytes 21758976 | tf_op jit(solution)/shard_map/dot_general | solution.py:156
  156.4 19.0 %collective-permute-done.12 = bf16[128,4096]{1,0:T(8,128)(2,1)S(1)} collective-permute-done((bf16[128,4096]{1,0:T(8,128)(2,1)S(1)}, bf16[128,4096]{1,0:T(8,128)(2,1)S(1)}, u32[]{:S(2)}, u32[]{:S(2)}) %collective-permute-start.12) | collective-permute-done | bytes 1048608 | tf_op jit(solution)/shard_map/ppermute | solution.py:74
  175.7 2.8 %collective-permute-start.13 = (bf16[64,4096]{1,0:T(8,128)(2,1)S(1)}, bf16[64,4096]{1,0:T(8,128)(2,1)S(1)}, u32[]{:S(2)}, u32[]{:S(2)}) collective-permute-start(bf16[64,4096]{1,0:T(8,128)(2,1)S(1)} %slice.166), channel_id=1, source_target_pairs={{0,4},{1,3},{2,6},{3,1},{4,0},{5,7},{6,2},{7,5},{8,12},{9,11},{10,... | collective-permute-start | bytes 1572872 | tf_op jit(solution)/shard_map/ppermute | solution.py:74
  178.6 7.2 %collective-permute-done.13 = bf16[64,4096]{1,0:T(8,128)(2,1)S(1)} collective-permute-done((bf16[64,4096]{1,0:T(8,128)(2,1)S(1)}, bf16[64,4096]{1,0:T(8,128)(2,1)S(1)}, u32[]{:S(2)}, u32[]{:S(2)}) %collective-permute-start.13) | collective-permute-done | bytes 524320 | tf_op jit(solution)/shard_map/ppermute | solution.py:74
  186.0 6.4 %collective-permute-done.14 = bf16[32,4096]{1,0:T(8,128)(2,1)S(1)} collective-permute-done((bf16[32,4096]{1,0:T(8,128)(2,1)S(1)}, bf16[32,4096]{1,0:T(8,128)(2,1)S(1)}, u32[]{:S(2)}, u32[]{:S(2)}) %collective-permute-start.14) | collective-permute-done | bytes 262176 | tf_op jit(solution)/shard_map/ppermute | solution.py:74
  193.2 6.0 %collective-permute-done.15 = bf16[16,4096]{1,0:T(8,128)(2,1)S(1)} collective-permute-done((bf16[16,4096]{1,0:T(8,128)(2,1)S(1)}, bf16[16,4096]{1,0:T(8,128)(2,1)S(1)}, u32[]{:S(2)}, u32[]{:S(2)}) %collective-permute-start.15) | collective-permute-done | bytes 131104 | tf_op jit(solution)/shard_map/ppermute | solution.py:74
  (80 shorter events, 9.9 us)
Async XLA Ops:
  0.0 39.0 %collective-permute-start = (bf16[256,4096]{1,0:T(8,128)(2,1)}, bf16[256,4096]{1,0:T(8,128)(2,1)}, u32[]{:S(2)}, u32[]{:S(2)}) collective-permute-start(bf16[256,4096]{1,0:T(8,128)(2,1)} %param.17), channel_id=1, source_target_pairs={{0,1},{1,0},{2,3},{3,2},{4,5},{5,4},{6,7},{7,6},{8,9},{9,8},{10,11... | collective-permute-start | bytes 6291464 | tf_op jit(solution)/shard_map/ppermute | solution.py:112
  16.5 21.8 %copy-start = (bf16[256,4096]{1,0:T(8,128)(2,1)S(1)}, bf16[256,4096]{1,0:T(8,128)(2,1)}, u32[]{:S(2)}) copy-start(bf16[256,4096]{1,0:T(8,128)(2,1)} %param.17) | copy-start | bytes 6291460
  19.2 18.4 %all-to-all-start = ((bf16[16,16,512]{2,0,1:T(8,128)(2,1)}), bf16[16,16,512]{2,0,1:T(8,128)(2,1)S(1)}, u32[]{:S(2)}, u32[]{:S(2)}) async-start(bf16[16,16,512]{2,0,1:T(8,128)(2,1)} %copy.33), calls=%async_computation | async-start | bytes 524288 | tf_op jit(solution)/shard_map/all_to_all | solution.py:119
  41.5 14.9 %collective-permute-start.1 = (bf16[128,4096]{1,0:T(8,128)(2,1)S(1)}, bf16[128,4096]{1,0:T(8,128)(2,1)S(1)}, u32[]{:S(2)}, u32[]{:S(2)}) collective-permute-start(bf16[128,4096]{1,0:T(8,128)(2,1)S(1)} %slice.107), channel_id=1, source_target_pairs={{0,2},{1,5},{2,0},{3,7},{4,6},{5,1},{6,4},{7,3},{8,10},{9,13},{10,... | collective-permute-start | bytes 3145736 | tf_op jit(solution)/shard_map/ppermute | solution.py:74
  56.6 10.7 %copy-start.4 = (s32[16,8]{0,1:T(8,128)S(1)}, s32[16,8]{0,1:T(8,128)}, u32[]{:S(2)}) copy-start(s32[16,8]{0,1:T(8,128)} %param.22) | copy-start | bytes 1540
  56.6 10.7 %copy-start.5 = (f32[16,8]{0,1:T(8,128)S(1)}, f32[16,8]{0,1:T(8,128)}, u32[]{:S(2)}) copy-start(f32[16,8]{0,1:T(8,128)} %param.23) | copy-start | bytes 1540
  56.7 26.2 %copy-start.1 = (bf16[16,4096]{1,0:T(8,128)(2,1)S(1)}, bf16[16,4096]{1,0:T(8,128)(2,1)}, u32[]{:S(2)}) copy-start(bf16[16,4096]{1,0:T(8,128)(2,1)} %param.12) | copy-start | bytes 393220
  56.7 26.4 %copy-start.3 = (f32[4096]{0:T(1024)S(1)}, f32[4096]{0:T(1024)}, u32[]{:S(2)}) copy-start(f32[4096]{0:T(1024)} %param.18) | copy-start | bytes 49156
  56.7 9.2 %collective-permute-start.2 = (bf16[64,4096]{1,0:T(8,128)(2,1)S(1)}, bf16[64,4096]{1,0:T(8,128)(2,1)S(1)}, u32[]{:S(2)}, u32[]{:S(2)}) collective-permute-start(bf16[64,4096]{1,0:T(8,128)(2,1)S(1)} %slice.167), channel_id=1, source_target_pairs={{0,4},{1,3},{2,6},{3,1},{4,0},{5,7},{6,2},{7,5},{8,12},{9,11},{10,... | collective-permute-start | bytes 1572872 | tf_op jit(solution)/shard_map/ppermute | solution.py:74
  66.1 7.0 %collective-permute-start.3 = (bf16[32,4096]{1,0:T(8,128)(2,1)S(1)}, bf16[32,4096]{1,0:T(8,128)(2,1)S(1)}, u32[]{:S(2)}, u32[]{:S(2)}) collective-permute-start(bf16[32,4096]{1,0:T(8,128)(2,1)S(1)} %slice.169), channel_id=1, source_target_pairs={{0,8},{1,9},{2,10},{3,11},{4,12},{5,13},{6,14},{7,15},{8,0},{9,1},... | collective-permute-start | bytes 786440 | tf_op jit(solution)/shard_map/ppermute | solution.py:74
  67.3 73.3 %collective-permute-start.10 = (bf16[4096,768]{1,0:T(8,128)(2,1)}, bf16[4096,768]{1,0:T(8,128)(2,1)}, u32[]{:S(2)}, u32[]{:S(2)}) collective-permute-start(bf16[4096,768]{1,0:T(8,128)(2,1)} %bitcast.8), channel_id=1, source_target_pairs={{0,1},{1,0},{2,3},{3,2},{4,5},{5,4},{6,7},{7,6},{8,9},{9,8},{10,11... | collective-permute-start | bytes 18874376 | tf_op jit(solution)/shard_map/ppermute | solution.py:114
  73.2 9.7 %collective-permute-start.4 = (bf16[16,4096]{1,0:T(8,128)(2,1)S(1)}, bf16[16,4096]{1,0:T(8,128)(2,1)S(1)}, u32[]{:S(2)}, u32[]{:S(2)}) collective-permute-start(bf16[16,4096]{1,0:T(8,128)(2,1)S(1)} %slice.171), channel_id=1, source_target_pairs={{0,16},{1,17},{2,18},{3,19},{4,20},{5,21},{6,22},{7,23},{8,24},{9,... | collective-permute-start | bytes 393224 | tf_op jit(solution)/shard_map/ppermute | solution.py:74
  83.2 6.1 %collective-permute-start.5 = (bf16[16,4224]{1,0:T(8,128)(2,1)S(1)}, bf16[16,4224]{1,0:T(8,128)(2,1)S(1)}, u32[]{:S(2)}, u32[]{:S(2)}) collective-permute-start(bf16[16,4224]{1,0:T(8,128)(2,1)S(1)} %get-tuple-element.9), channel_id=1, source_target_pairs={{0,16},{1,17},{2,18},{3,19},{4,20},{5,21},{6,22},{7,23},{8,24},{9,... | collective-permute-start | bytes 405512 | tf_op jit(solution)/shard_map/ppermute | solution.py:82
  83.3 61.9 %collective-permute-start.11 = (bf16[768,4096]{1,0:T(8,128)(2,1)}, bf16[768,4096]{1,0:T(8,128)(2,1)}, u32[]{:S(2)}, u32[]{:S(2)}) collective-permute-start(bf16[768,4096]{1,0:T(8,128)(2,1)} %bitcast.48), channel_id=1, source_target_pairs={{0,1},{1,0},{2,3},{3,2},{4,5},{5,4},{6,7},{7,6},{8,9},{9,8},{10,11... | collective-permute-start | bytes 18874376 | tf_op jit(solution)/shard_map/ppermute | solution.py:115
  83.4 61.8 %collective-permute-start.9 = (bf16[4096,768]{1,0:T(8,128)(2,1)}, bf16[4096,768]{1,0:T(8,128)(2,1)}, u32[]{:S(2)}, u32[]{:S(2)}) collective-permute-start(bf16[4096,768]{1,0:T(8,128)(2,1)} %bitcast.49), channel_id=1, source_target_pairs={{0,1},{1,0},{2,3},{3,2},{4,5},{5,4},{6,7},{7,6},{8,9},{9,8},{10,11... | collective-permute-start | bytes 18874376 | tf_op jit(solution)/shard_map/ppermute | solution.py:113
  89.3 6.5 %collective-permute-start.6 = (bf16[32,4224]{1,0:T(8,128)(2,1)S(1)}, bf16[32,4224]{1,0:T(8,128)(2,1)S(1)}, u32[]{:S(2)}, u32[]{:S(2)}) collective-permute-start(bf16[32,4224]{1,0:T(8,128)(2,1)S(1)} %pad_maximum_fusion.2), channel_id=1, source_target_pairs={{0,8},{1,9},{2,10},{3,11},{4,12},{5,13},{6,14},{7,15},{8,0},{9,1},... | collective-permute-start | bytes 811016 | tf_op jit(solution)/shard_map/ppermute | solution.py:82
  95.9 12.5 %collective-permute-start.7 = (bf16[64,4224]{1,0:T(8,128)(2,1)S(1)}, bf16[64,4224]{1,0:T(8,128)(2,1)S(1)}, u32[]{:S(2)}, u32[]{:S(2)}) collective-permute-start(bf16[64,4224]{1,0:T(8,128)(2,1)S(1)} %pad_maximum_fusion.1), channel_id=1, source_target_pairs={{0,4},{1,3},{2,6},{3,1},{4,0},{5,7},{6,2},{7,5},{8,12},{9,11},{10,... | collective-permute-start | bytes 1622024 | tf_op jit(solution)/shard_map/ppermute | solution.py:82
  108.5 15.2 %collective-permute-start.8 = (bf16[128,4224]{1,0:T(8,128)(2,1)S(1)}, bf16[128,4224]{1,0:T(8,128)(2,1)S(1)}, u32[]{:S(2)}, u32[]{:S(2)}) collective-permute-start(bf16[128,4224]{1,0:T(8,128)(2,1)S(1)} %pad_maximum_fusion), channel_id=1, source_target_pairs={{0,2},{1,5},{2,0},{3,7},{4,6},{5,1},{6,4},{7,3},{8,10},{9,13},{10,... | collective-permute-start | bytes 3244040 | tf_op jit(solution)/shard_map/ppermute | solution.py:82
  123.9 16.7 %copy-start.2 = (bf16[256,4224]{1,0:T(8,128)(2,1)}, bf16[256,4224]{1,0:T(8,128)(2,1)S(1)}, u32[]{:S(2)}) copy-start(bf16[256,4224]{1,0:T(8,128)(2,1)S(1)} %constant_dynamic-update-slice_fusion) | copy-start | bytes 6488068
  156.3 19.1 %collective-permute-start.12 = (bf16[128,4096]{1,0:T(8,128)(2,1)S(1)}, bf16[128,4096]{1,0:T(8,128)(2,1)S(1)}, u32[]{:S(2)}, u32[]{:S(2)}) collective-permute-start(bf16[128,4096]{1,0:T(8,128)(2,1)S(1)} %slice.117), channel_id=1, source_target_pairs={{0,2},{1,5},{2,0},{3,7},{4,6},{5,1},{6,4},{7,3},{8,10},{9,13},{10,... | collective-permute-start | bytes 3145736 | tf_op jit(solution)/shard_map/ppermute | solution.py:74
  175.7 10.0 %collective-permute-start.13 = (bf16[64,4096]{1,0:T(8,128)(2,1)S(1)}, bf16[64,4096]{1,0:T(8,128)(2,1)S(1)}, u32[]{:S(2)}, u32[]{:S(2)}) collective-permute-start(bf16[64,4096]{1,0:T(8,128)(2,1)S(1)} %slice.166), channel_id=1, source_target_pairs={{0,4},{1,3},{2,6},{3,1},{4,0},{5,7},{6,2},{7,5},{8,12},{9,11},{10,... | collective-permute-start | bytes 1572872 | tf_op jit(solution)/shard_map/ppermute | solution.py:74
  185.9 6.4 %collective-permute-start.14 = (bf16[32,4096]{1,0:T(8,128)(2,1)S(1)}, bf16[32,4096]{1,0:T(8,128)(2,1)S(1)}, u32[]{:S(2)}, u32[]{:S(2)}) collective-permute-start(bf16[32,4096]{1,0:T(8,128)(2,1)S(1)} %slice.168), channel_id=1, source_target_pairs={{0,8},{1,9},{2,10},{3,11},{4,12},{5,13},{6,14},{7,15},{8,0},{9,1},... | collective-permute-start | bytes 786440 | tf_op jit(solution)/shard_map/ppermute | solution.py:74
  192.4 6.8 %collective-permute-start.15 = (bf16[16,4096]{1,0:T(8,128)(2,1)S(1)}, bf16[16,4096]{1,0:T(8,128)(2,1)S(1)}, u32[]{:S(2)}, u32[]{:S(2)}) collective-permute-start(bf16[16,4096]{1,0:T(8,128)(2,1)S(1)} %slice.170), channel_id=1, source_target_pairs={{0,16},{1,17},{2,18},{3,19},{4,20},{5,21},{6,22},{7,23},{8,24},{9,... | collective-permute-start | bytes 393224 | tf_op jit(solution)/shard_map/ppermute | solution.py:74

commit v2 on v1

v2 whole, which is shorter than its diff:
```python
import math

import jax
import jax.numpy as jnp
from jax import lax
from jax.experimental import pallas as pl
from jax.experimental.pallas import tpu as pltpu
from jax.sharding import PartitionSpec as P

H = 64
KVH = 4
DH = 128
TOP = 8
F32 = jnp.float32
BF16 = jnp.bfloat16


def attend_kernel(core_ref, lengths_ref, q_ref, new_ref, cache_ref, out_ref, q_rows, out_rows):
    rows = q_ref.shape[0]
    heads = q_ref.shape[1] // DH
    per_group = heads // KVH
    count = cache_ref.shape[1]
    span = cache_ref.shape[2]
    step = pl.program_id(0)
    scale = 1.0 / math.sqrt(DH)

    @pl.when(step == 0)
    def _():
        for h in range(heads):
            q_rows[h * rows : (h + 1) * rows, :] = q_ref[:, h * DH : (h + 1) * DH].astype(F32)

    position = lax.broadcasted_iota(jnp.int32, (heads, span), 1)
    for i in range(count):
        t = step * count + i
        query = q_rows[pl.ds(t, heads, stride=rows), :]
        query16 = query.astype(BF16)
        new_key = new_ref[0, pl.ds(t, 1), :]
        new_value = new_ref[1, pl.ds(t, 1), :]
        scores, own = [], []
        for g in range(KVH):
            part = slice(g * per_group, (g + 1) * per_group)
            lanes = slice(g * DH, (g + 1) * DH)
            scores.append(
                lax.dot_general(
                    query16[part],
                    cache_ref[0, i, :, lanes],
                    (((1,), (1,)), ((), ())),
                    preferred_element_type=F32,
                )
            )
            own.append(jnp.sum(query[part] * new_key[:, lanes], axis=1, keepdims=True))
        scores = jnp.concatenate(scores, axis=0) * scale
        own = jnp.concatenate(own, axis=0) * scale
        scores = jnp.where(position < lengths_ref[t], scores, -1e30)
        peak = jnp.maximum(jnp.max(scores, axis=1, keepdims=True), own)
        cached_exp = jnp.exp(scores - peak)
        own_exp = jnp.exp(own - peak)
        denominator = jnp.sum(cached_exp, axis=1, keepdims=True) + own_exp
        probs = (cached_exp / denominator).astype(BF16)
        own_probs = (own_exp / denominator).astype(BF16).astype(F32)
        for g in range(KVH):
            part = slice(g * per_group, (g + 1) * per_group)
            lanes = slice(g * DH, (g + 1) * DH)
            value = jnp.dot(probs[part], cache_ref[1, i, :, lanes], preferred_element_type=F32)
            value = value + own_probs[part] * new_value[:, lanes]
            out_rows[pl.ds(g * per_group * rows + t, per_group, stride=rows), :] = value

    chips = out_ref.shape[0]
    per_chip = heads // chips
    for side in range(2):

        @pl.when((step == pl.num_programs(0) - 1) & (core_ref[0] == side))
        def _():
            for e in range(chips):
                for i in range(per_chip):
                    h = e * per_chip + (i + side * (per_chip // 2)) % per_chip
                    out_ref[e, :, i * DH : (i + 1) * DH] = out_rows[h * rows : (h + 1) * rows, :].astype(BF16)


def attend(core, queries, new_kv, cache_kv, lengths, chips):
    rows, features = queries.shape
    span, width = cache_kv.shape[2:]
    count = 4 if rows % 4 == 0 else 1
    whole = lambda shape: pl.BlockSpec(shape, lambda s, *_: (0,) * len(shape))
    return pl.pallas_call(
        attend_kernel,
        out_shape=jax.ShapeDtypeStruct((chips, rows, features // chips), BF16),
        grid_spec=pltpu.PrefetchScalarGridSpec(
            num_scalar_prefetch=2,
            grid=(rows // count,),
            in_specs=[
                whole((rows, features)),
                whole((2, rows, width)),
                pl.BlockSpec((2, count, span, width), lambda s, *_: (0, s, 0, 0)),
            ],
            out_specs=whole((chips, rows, features // chips)),
            scratch_shapes=[
                pltpu.VMEM((features // DH * rows, DH), F32),
                pltpu.VMEM((features // DH * rows, DH), F32),
            ],
        ),
        compiler_params=pltpu.CompilerParams(vmem_limit_bytes=24 << 20),
        cost_estimate=pl.CostEstimate(flops=4 * rows * features * span, bytes_accessed=2 * cache_kv.size, transcendentals=rows * features),
    )(core, lengths, queries, new_kv.astype(F32), cache_kv)


def project_kernel(index_ref, blocks_ref, own_ref, other_ref, keep_ref, send_ref, ordered):
    chips, rows, features = blocks_ref.shape
    half = features // 2

    @pl.when(pl.program_id(0) == 0)
    def _():
        for k in range(chips):
            ordered[k * rows : (k + 1) * rows, :] = blocks_ref[index_ref[k]]

    total = jnp.dot(ordered[:, :half], own_ref[...], preferred_element_type=F32)
    total = total + jnp.dot(ordered[:, half:], other_ref[...], preferred_element_type=F32)
    cut = keep_ref.shape[0]
    keep_ref[...] = total[:cut].astype(BF16)
    send_ref[...] = total[cut:].astype(BF16)


def project(index, blocks, own, other):
    chips, rows, features = blocks.shape
    depth, width = own.shape
    tile = 512
    weights = pl.BlockSpec((depth, tile), lambda s, *_: (0, s))
    result = pl.BlockSpec((chips * rows // 2, tile), lambda s, *_: (0, s))
    return pl.pallas_call(
        project_kernel,
        out_shape=[jax.ShapeDtypeStruct((chips * rows // 2, width), BF16)] * 2,
        grid_spec=pltpu.PrefetchScalarGridSpec(
            num_scalar_prefetch=1,
            grid=(width // tile,),
            in_specs=[pl.BlockSpec(blocks.shape, lambda s, *_: (0, 0, 0)), weights, weights],
            out_specs=[result, result],
            scratch_shapes=[pltpu.VMEM((chips * rows, features), BF16)],
        ),
        compiler_params=pltpu.CompilerParams(vmem_limit_bytes=24 << 20),
        cost_estimate=pl.CostEstimate(flops=2 * blocks.size * width, bytes_accessed=4 * own.size, transcendentals=0),
    )(index, blocks, own, other)


F_TILE = 256
N_TILE = 512


def expert_kernel(
    chip_ref, low_ref, high_ref, gate0, gate1, up0, up1, down0, down1, keep_ref, send_ref,
    tokens, gates, ups, downs, active, gate_sem, up_sem, down_sem,
):
    half, width = keep_ref.shape
    hidden = gate0.shape[1]
    per_half = hidden // F_TILE
    copies = []
    for j, (gate, up) in enumerate(((gate0, up0), (gate1, up1))):
        for i in range(per_half):
            t = j * per_half + i
            lanes = pl.ds(i * F_TILE, F_TILE)
            copies.append(pltpu.make_async_copy(gate.at[:, lanes], gates.at[t], gate_sem.at[t]))
            copies.append(pltpu.make_async_copy(up.at[:, lanes], ups.at[t], up_sem.at[t]))
    n_tiles = width // N_TILE
    for n in range(n_tiles):
        for j, down in enumerate((down0, down1)):
            copies.append(
                pltpu.make_async_copy(
                    down.at[:, pl.ds(n * N_TILE, N_TILE)],
                    downs.at[n, pl.ds(j * hidden, hidden), :],
                    down_sem.at[n, j],
                )
            )
    for copy in copies:
        copy.start()
    tokens[:half, :] = low_ref[:, :width]
    tokens[half:, :] = high_ref[:, :width]

    for t in range(2 * per_half):
        copies[2 * t].wait()
        gate_part = jnp.dot(tokens[...], gates[t], preferred_element_type=F32)
        copies[2 * t + 1].wait()
        up_part = jnp.dot(tokens[...], ups[t], preferred_element_type=F32)
        lanes = slice(t * F_TILE, (t + 1) * F_TILE)
        active[:, lanes] = (gate_part / (1.0 + jnp.exp(-gate_part)) * up_part).astype(BF16)

    chips = chip_ref[1]
    lane = lax.broadcasted_iota(jnp.int32, (half, low_ref.shape[1] - width), 1)
    first = chip_ref[0]
    mine = (lane == first) | (lane == first + chips) | (lane == first + 2 * chips)
    weights = [
        jnp.sum(jnp.where(mine, ref[:, width:].astype(F32), 0.0), axis=1, keepdims=True)
        for ref in (low_ref, high_ref)
    ]
    for n in range(n_tiles):
        copies[4 * per_half + 2 * n].wait()
        copies[4 * per_half + 2 * n + 1].wait()
        total = jnp.dot(active[...], downs[n], preferred_element_type=F32)
        lanes = slice(n * N_TILE, (n + 1) * N_TILE)
        keep_ref[:, lanes] = (total[:half] * weights[0]).astype(BF16)
        send_ref[:, lanes] = (total[half:] * weights[1]).astype(BF16)


def experts(chip, low, high, gates, ups, downs):
    half = low.shape[0]
    width, hidden = gates[0].shape
    tiles = 2 * hidden // F_TILE
    blocks = width // N_TILE
    any_space = pl.BlockSpec(memory_space=pl.ANY)
    vmem = pl.BlockSpec(memory_space=pltpu.VMEM)
    return pl.pallas_call(
        expert_kernel,
        out_shape=[jax.ShapeDtypeStruct((half, width), BF16)] * 2,
        in_specs=[pl.BlockSpec(memory_space=pltpu.SMEM), vmem, vmem] + [any_space] * 6,
        out_specs=[vmem, vmem],
        scratch_shapes=[
            pltpu.VMEM((2 * half, width), BF16),
            pltpu.VMEM((tiles, width, F_TILE), BF16),
            pltpu.VMEM((tiles, width, F_TILE), BF16),
            pltpu.VMEM((blocks, 2 * hidden, N_TILE), BF16),
            pltpu.VMEM((2 * half, 2 * hidden), BF16),
            pltpu.SemaphoreType.DMA((tiles,)),
            pltpu.SemaphoreType.DMA((tiles,)),
            pltpu.SemaphoreType.DMA((blocks, 2)),
        ],
        compiler_params=pltpu.CompilerParams(vmem_limit_bytes=56 << 20),
        cost_estimate=pl.CostEstimate(flops=24 * half * width * hidden, bytes_accessed=12 * width * hidden, transcendentals=4 * half * hidden),
    )(chip, low, high, *gates, *ups, *downs)


def normalize(hidden_state, norm_gain):
    values = hidden_state.astype(jnp.float32)
    mean_square = jnp.mean(values * values, axis=-1, keepdims=True)
    return (values * lax.rsqrt(mean_square + 1e-06) * norm_gain).astype(jnp.bfloat16)


def step_bits(devices):
    bits = [1 << i for i in range(1, devices.bit_length() - 1)]
    other = bits[1::-1] + bits[2:] if len(bits) > 1 else bits
    return bits, other


def swap_step(step, devices):
    orders = step_bits(devices)
    return [(i, i ^ orders[i & 1][step]) for i in range(devices)]


def reduce_slots(kept, sent, devices):
    steps = devices.bit_length() - 2
    for step in range(steps):
        came = lax.ppermute(sent, "dp", swap_step(step, devices))
        kept = kept.astype(F32) + came.astype(F32)
        half = kept.shape[0] // 2
        if step < steps - 1:
            sent = kept[half:].astype(BF16)
            kept = kept[:half]
    return kept


def gather_slots(own, devices):
    steps = devices.bit_length() - 2
    for step in reversed(range(steps)):
        came = lax.ppermute(own, "dp", swap_step(step, devices))
        if step == 0:
            return own, came
        own = jnp.concatenate([own, came], axis=0)


def per_device(
    residual,
    queries,
    new_kv,
    cache_kv,
    lengths,
    out_weight,
    norm_gain,
    w_gate,
    w_up,
    w_down,
    expert_ids,
    combine_weights,
):
    rows = residual.shape[0]
    width = residual.shape[1]
    devices = lax.axis_size("dp")
    chips = devices // 2
    me = lax.axis_index("dp")
    core = me % 2
    chip = me // 2
    steps = devices.bit_length() - 2
    core_swap = [(i, i ^ 1) for i in range(devices)]
    core_groups = [[2 * i + c for i in range(chips)] for c in range(2)]

    out_other = lax.ppermute(out_weight, "dp", core_swap)
    gate_other = lax.ppermute(w_gate[0], "dp", core_swap)
    up_other = lax.ppermute(w_up[0], "dp", core_swap)
    down_other = lax.ppermute(w_down[0], "dp", core_swap)

    attn_out = attend(core[None], queries, new_kv, cache_kv, lengths, chips)
    blocks = lax.all_to_all(
        attn_out, "dp", split_axis=0, concat_axis=0, axis_index_groups=core_groups, tiled=True
    )

    orders = step_bits(devices)
    slot = jnp.arange(chips, dtype=jnp.int32)
    offset = jnp.zeros_like(slot)
    for step in range(steps):
        here = jnp.where(core == 0, orders[0][step], orders[1][step]) // 2
        offset = offset + here * ((slot >> (steps - 1 - step)) & 1)
    kept, sent = project(chip ^ offset, blocks, out_weight, out_other)
    projected = reduce_slots(kept, sent, devices)
    hidden_state = (residual.astype(F32) + projected).astype(BF16)
    normed = normalize(hidden_state, norm_gain)

    picks = expert_ids[:, :, None] == jnp.arange(chips, dtype=jnp.int32)
    mix = jnp.sum(jnp.where(picks, combine_weights[:, :, None], 0.0), axis=1)
    mix_hi = mix.astype(BF16)
    mix_mid = (mix - mix_hi.astype(F32)).astype(BF16)
    mix_low = (mix - mix_hi.astype(F32) - mix_mid.astype(F32)).astype(BF16)
    extra = jnp.concatenate([mix_hi, mix_mid, mix_low], axis=1)
    extra = jnp.pad(extra, ((0, 0), (0, -extra.shape[1] % 128)))
    low, high = gather_slots(jnp.concatenate([normed, extra], axis=1), devices)
    place = jnp.stack([chip, jnp.int32(chips)])
    kept, sent = experts(
        place, low, high, (w_gate[0], gate_other), (w_up[0], up_other), (w_down[0], down_other)
    )
    mixture = reduce_slots(kept, sent, devices)
    return (hidden_state.astype(F32) + mixture).astype(BF16)


def solution(mesh):
    placed = (
        P(("groups", "dp"), None),
        P(("groups", "dp"), None),
        P(None, ("groups", "dp"), None),
        P(None, ("groups", "dp"), None, None),
        P(("groups", "dp")),
        P("dp", None),
        P(),
        P("dp", None, None),
        P("dp", None, None),
        P("dp", None, None),
        P(("groups", "dp"), None),
        P(("groups", "dp"), None),
    )
    return jax.shard_map(
        per_device, mesh=mesh, in_specs=placed, out_specs=P(("groups", "dp"), None), check_vma=False
    )
```

time: 200 us -> 197 us (0.985)
  Pallas kernels: 0 us -> 42.6 us
  matrix products: 37.5 us -> 0 us
  local copies, waits for them, and re-layouts: 16 us -> 5.11 us
  waiting for transfers between devices: 123 us -> 125 us
    pallas_call x0 -> x3, Pallas kernels: none -> 42.6 us  [the longest x1 26.5 us: experts(): pl.pallas_call(expert_kernel, out_shape=[jax.ShapeDtypeStruct((half, widt...]
    dot_general x9 -> x0, matrix products: 37.5 us -> none  [the longest x2 22.2 us: per_device(): total = total + jnp.dot(activated, down, preferred_element_type=F32)]
    slice x9 -> x6, local copies, waits for them, and re-layouts: 5.05 us -> 0.2 us  [reduce_slots(): sent = kept[half:].astype(BF16)]
    unnamed x20 -> x22, local copies, waits for them, and re-layouts: 7.33 us -> 4.91 us
  transfers between devices with their start and end apart: 17 -> 17, of which waited for: 13 -> 13; matrix products, arithmetic and copies ran while one was open for 21% -> 1% of each run, Pallas kernels for 0% -> 5%
where the time goes in v2:
time: 197 us
  waiting for transfers between devices  125 us (63%)
  Pallas kernels  42.6 us (22%)
  starting transfers between devices  18.5 us (9%)
  local copies, waits for them, and re-layouts  5.11 us (3%)
  other arithmetic  4.82 us (2%)
    ppermute x8, waiting for transfers between devices, reduce_slots(): came = lax.ppermute(sent, 'dp', swap_step(step, devices))  75 us
    ppermute x4, waiting for transfers between devices, gather_slots(): came = lax.ppermute(own, 'dp', swap_step(step, devices))  39.9 us
    pallas_call x1, Pallas kernels, experts(): pl.pallas_call(expert_kernel, out_shape=[jax.ShapeDtypeStruct((half, widt...  26.5 us
    all_to_all x1, waiting for transfers between devices, per_device(): lax.all_to_all(attn_out, 'dp', split_axis=0, concat_axis=0, axis_index_gr...  10.5 us
    pallas_call x1, Pallas kernels, attend(): pl.pallas_call(attend_kernel, out_shape=jax.ShapeDtypeStruct((chips, rows...  9.9 us
    all_to_all x1, starting transfers between devices, per_device(): lax.all_to_all(attn_out, 'dp', split_axis=0, concat_axis=0, axis_index_gr...  7.86 us
    ppermute x8, starting transfers between devices, reduce_slots(): came = lax.ppermute(sent, 'dp', swap_step(step, devices))  7.58 us
    pallas_call x1, Pallas kernels, project(): pl.pallas_call(project_kernel, out_shape=[jax.ShapeDtypeStruct((chips * r...  6.17 us
  transfers between devices with their start and end apart: 17, of which 13 were waited for; matrix products, arithmetic and copies ran while one was open for 1% of the time, Pallas kernels for 5%

profile of v2, /device:TPU:0, one launch (start us, length us, event | category | flops | bytes accessed | tf_op | source)
XLA Modules:
  0.0 196.6 jit_solution(6988635757569329265)
XLA Ops:
  0.5 0.8 convert_element_type.74.new_ref
  1.2 2.2 %copy-done = bf16[2,16,128,512]{3,2,1,0:T(8,128)(2,1)S(1)} copy-done((bf16[2,16,128,512]{3,2,1,0:T(8,128)(2,1)S(1)}, bf16[2,16,128,512]{3,2,1,0:T(8,128)(2,1)}, u32[]{:S(2)}) %copy-start) | copy-done | bytes 4194328
  3.4 0.9 copy-done.2
  4.4 0.7 copy-done.3
  5.0 9.9 %shard_map.118 = bf16[16,16,512]{2,1,0:T(8,128)(2,1)} custom-call(s32[1]{0:T(128)} %bitcast.core_ref, s32[16]{0:T(128)S(1)} %copy-done.3, bf16[16,8192]{1,0:T(8,128)(2,1)S(1)} %copy-done.2, f32[2,16,512]{2,1,0:T(8,128)S(1)} %convert_element_type.74.new_ref, bf16[2,16,128,512]{3,2,1,0:T(8,128)(2,1)S(1)} %copy-done), custom_call_target="tpu_custom_call" | custom-call | flops 67108864 | bytes 4194304 | tf_op jit(solution)/shard_map/pallas_call | solution.py:85
  14.9 7.9 %all-to-all-start = ((bf16[16,16,512]{2,1,0:T(8,128)(2,1)}), bf16[16,16,512]{2,1,0:T(8,128)(2,1)S(1)}, u32[]{:S(2)}, u32[]{:S(2)}) async-start(bf16[16,16,512]{2,1,0:T(8,128)(2,1)} %shard_map.118), calls=%async_computation | async-start | bytes 524288 | tf_op jit(solution)/shard_map/all_to_all | solution.py:298
  22.8 10.5 %all-to-all-done.blocks_ref = bf16[16,16,512]{2,1,0:T(8,128)(2,1)S(1)} async-done(((bf16[16,16,512]{2,1,0:T(8,128)(2,1)}), bf16[16,16,512]{2,1,0:T(8,128)(2,1)S(1)}, u32[]{:S(2)}, u32[]{:S(2)}) %all-to-all-start) | async-done | bytes 262176 | tf_op jit(solution)/shard_map/all_to_all | solution.py:298
  33.3 6.2 %shard_map.119 = (bf16[128,4096]{1,0:T(8,128)(2,1)S(1)}, bf16[128,4096]{1,0:T(8,128)(2,1)S(1)}) custom-call(s32[16]{0:T(128)S(1)} %add_xor_fusion.index_ref, bf16[16,16,512]{2,1,0:T(8,128)(2,1)S(1)} %all-to-all-done.blocks_ref, bf16[256,4096]{1,0:T(8,128)(2,1)S(1)} %copy-done.1, bf16[256,4096]{1,0:T(8,128)(2,1)} %collective-permute-done.other_ref), custom_call_target="tpu_custom_call" | custom-call | flops 1073741824 | bytes 4194304 | tf_op jit(solution)/shard_map/pallas_call | solution.py:129
  39.5 0.8 collective-permute-start.1
  40.3 14.0 %collective-permute-done.1 = bf16[128,4096]{1,0:T(8,128)(2,1)S(1)} collective-permute-done((bf16[128,4096]{1,0:T(8,128)(2,1)S(1)}, bf16[128,4096]{1,0:T(8,128)(2,1)S(1)}, u32[]{:S(2)}, u32[]{:S(2)}) %collective-permute-start.1) | collective-permute-done | bytes 1048608 | tf_op jit(solution)/shard_map/ppermute | solution.py:249
  54.7 1.0 collective-permute-start.2
  55.7 8.3 %collective-permute-done.2 = bf16[64,4096]{1,0:T(8,128)(2,1)S(1)} collective-permute-done((bf16[64,4096]{1,0:T(8,128)(2,1)S(1)}, bf16[64,4096]{1,0:T(8,128)(2,1)S(1)}, u32[]{:S(2)}, u32[]{:S(2)}) %collective-permute-start.2) | collective-permute-done | bytes 524320 | tf_op jit(solution)/shard_map/ppermute | solution.py:249
  64.1 1.2 collective-permute-start.3
  65.3 0.5 collective-permute-start.10
  66.1 5.0 %collective-permute-done.3 = bf16[32,4096]{1,0:T(8,128)(2,1)S(1)} collective-permute-done((bf16[32,4096]{1,0:T(8,128)(2,1)S(1)}, bf16[32,4096]{1,0:T(8,128)(2,1)S(1)}, u32[]{:S(2)}, u32[]{:S(2)}) %collective-permute-start.3) | collective-permute-done | bytes 262176 | tf_op jit(solution)/shard_map/ppermute | solution.py:249
  71.3 9.3 %collective-permute-done.4 = bf16[16,4096]{1,0:T(8,128)(2,1)S(1)} collective-permute-done((bf16[16,4096]{1,0:T(8,128)(2,1)S(1)}, bf16[16,4096]{1,0:T(8,128)(2,1)S(1)}, u32[]{:S(2)}, u32[]{:S(2)}) %collective-permute-start.4) | collective-permute-done | bytes 131104 | tf_op jit(solution)/shard_map/ppermute | solution.py:249
  81.0 6.7 %collective-permute-done.5 = bf16[16,4224]{1,0:T(8,128)(2,1)S(1)} collective-permute-done((bf16[16,4224]{1,0:T(8,128)(2,1)S(1)}, bf16[16,4224]{1,0:T(8,128)(2,1)S(1)}, u32[]{:S(2)}, u32[]{:S(2)}) %collective-permute-start.5) | collective-permute-done | bytes 135200 | tf_op jit(solution)/shard_map/ppermute | solution.py:261
  87.9 6.4 %collective-permute-done.6 = bf16[32,4224]{1,0:T(8,128)(2,1)S(1)} collective-permute-done((bf16[32,4224]{1,0:T(8,128)(2,1)S(1)}, bf16[32,4224]{1,0:T(8,128)(2,1)S(1)}, u32[]{:S(2)}, u32[]{:S(2)}) %collective-permute-start.6) | collective-permute-done | bytes 270368 | tf_op jit(solution)/shard_map/ppermute | solution.py:261
  94.3 1.6 collective-permute-start.7
  96.0 12.4 %collective-permute-done.7 = bf16[64,4224]{1,0:T(8,128)(2,1)S(1)} collective-permute-done((bf16[64,4224]{1,0:T(8,128)(2,1)S(1)}, bf16[64,4224]{1,0:T(8,128)(2,1)S(1)}, u32[]{:S(2)}, u32[]{:S(2)}) %collective-permute-start.7) | collective-permute-done | bytes 540704 | tf_op jit(solution)/shard_map/ppermute | solution.py:261
  108.8 0.6 pad_add_fusion.chip_ref
  109.4 14.3 %collective-permute-done.8.high_ref = bf16[128,4224]{1,0:T(8,128)(2,1)S(1)} collective-permute-done((bf16[128,4224]{1,0:T(8,128)(2,1)S(1)}, bf16[128,4224]{1,0:T(8,128)(2,1)S(1)}, u32[]{:S(2)}, u32[]{:S(2)}) %collective-permute-start.8) | collective-permute-done | bytes 1081376 | tf_op jit(solution)/shard_map/ppermute | solution.py:261
  123.8 0.9 copy-done.5
  124.7 26.5 %shard_map.120 = (bf16[128,4096]{1,0:T(8,128)(2,1)}, bf16[128,4096]{1,0:T(8,128)(2,1)}) custom-call(s32[2]{0:T(128)} %pad_add_fusion.chip_ref, bf16[128,4224]{1,0:T(8,128)(2,1)} %copy-done.4, bf16[128,4224]{1,0:T(8,128)(2,1)} %copy-done.5, bf16[4096,768]{1,0:T(8,128)(2,1)} %bitcast.2.gate0, bf16[4096,768]{1,0:T(8,128)(2,1)} %collective-permute-done.9.gate1, ...), custom_call_target="tpu_custom_call" | custom-call | flops 9663676416 | bytes 37748736 | tf_op jit(solution)/shard_map/pallas_call | solution.py:209
  151.5 19.6 %collective-permute-done.12 = bf16[128,4096]{1,0:T(8,128)(2,1)S(1)} collective-permute-done((bf16[128,4096]{1,0:T(8,128)(2,1)}, bf16[128,4096]{1,0:T(8,128)(2,1)S(1)}, u32[]{:S(2)}, u32[]{:S(2)}) %collective-permute-start.12) | collective-permute-done | bytes 1048608 | tf_op jit(solution)/shard_map/ppermute | solution.py:249
  171.1 1.5 convert_add_fusion
  172.7 1.9 collective-permute-start.13
  174.5 7.4 %collective-permute-done.13 = bf16[64,4096]{1,0:T(8,128)(2,1)S(1)} collective-permute-done((bf16[64,4096]{1,0:T(8,128)(2,1)S(1)}, bf16[64,4096]{1,0:T(8,128)(2,1)S(1)}, u32[]{:S(2)}, u32[]{:S(2)}) %collective-permute-start.13) | collective-permute-done | bytes 524320 | tf_op jit(solution)/shard_map/ppermute | solution.py:249
  182.2 6.4 %collective-permute-done.14 = bf16[32,4096]{1,0:T(8,128)(2,1)S(1)} collective-permute-done((bf16[32,4096]{1,0:T(8,128)(2,1)S(1)}, bf16[32,4096]{1,0:T(8,128)(2,1)S(1)}, u32[]{:S(2)}, u32[]{:S(2)}) %collective-permute-start.14) | collective-permute-done | bytes 262176 | tf_op jit(solution)/shard_map/ppermute | solution.py:249
  188.6 2.2 %collective-permute-start.15 = (bf16[16,4096]{1,0:T(8,128)(2,1)S(1)}, bf16[16,4096]{1,0:T(8,128)(2,1)S(1)}, u32[]{:S(2)}, u32[]{:S(2)}) collective-permute-start(bf16[16,4096]{1,0:T(8,128)(2,1)S(1)} %slice.88), channel_id=1, source_target_pairs={{0,16},{1,17},{2,18},{3,19},{4,20},{5,21},{6,22},{7,23},{8,24},{9,... | collective-permute-start | bytes 393224 | tf_op jit(solution)/shard_map/ppermute | solution.py:249
  190.8 5.1 %collective-permute-done.15 = bf16[16,4096]{1,0:T(8,128)(2,1)S(1)} collective-permute-done((bf16[16,4096]{1,0:T(8,128)(2,1)S(1)}, bf16[16,4096]{1,0:T(8,128)(2,1)S(1)}, u32[]{:S(2)}, u32[]{:S(2)}) %collective-permute-start.15) | collective-permute-done | bytes 131104 | tf_op jit(solution)/shard_map/ppermute | solution.py:249
  195.9 0.7 fusion.3
  (53 shorter events, 3.0 us)
Async XLA Ops:
  0.0 33.3 %collective-permute-start = (bf16[256,4096]{1,0:T(8,128)(2,1)}, bf16[256,4096]{1,0:T(8,128)(2,1)}, u32[]{:S(2)}, u32[]{:S(2)}) collective-permute-start(bf16[256,4096]{1,0:T(8,128)(2,1)} %own_ref.1), channel_id=1, source_target_pairs={{0,1},{1,0},{2,3},{3,2},{4,5},{5,4},{6,7},{7,6},{8,9},{9,8},{10,11... | collective-permute-start | bytes 6291464 | tf_op jit(solution)/shard_map/ppermute | solution.py:292
  1.2 2.2 %copy-start = (bf16[2,16,128,512]{3,2,1,0:T(8,128)(2,1)S(1)}, bf16[2,16,128,512]{3,2,1,0:T(8,128)(2,1)}, u32[]{:S(2)}) copy-start(bf16[2,16,128,512]{3,2,1,0:T(8,128)(2,1)} %cache_ref.1) | copy-start | bytes 12582916
  3.4 0.9 copy-start.2
  4.4 0.7 copy-start.3
  5.0 28.3 %copy-start.1 = (bf16[256,4096]{1,0:T(8,128)(2,1)S(1)}, bf16[256,4096]{1,0:T(8,128)(2,1)}, u32[]{:S(2)}) copy-start(bf16[256,4096]{1,0:T(8,128)(2,1)} %own_ref.1) | copy-start | bytes 6291460
  14.9 18.4 %all-to-all-start = ((bf16[16,16,512]{2,1,0:T(8,128)(2,1)}), bf16[16,16,512]{2,1,0:T(8,128)(2,1)S(1)}, u32[]{:S(2)}, u32[]{:S(2)}) async-start(bf16[16,16,512]{2,1,0:T(8,128)(2,1)} %shard_map.118), calls=%async_computation | async-start | bytes 524288 | tf_op jit(solution)/shard_map/all_to_all | solution.py:298
  39.5 14.9 %collective-permute-start.1 = (bf16[128,4096]{1,0:T(8,128)(2,1)S(1)}, bf16[128,4096]{1,0:T(8,128)(2,1)S(1)}, u32[]{:S(2)}, u32[]{:S(2)}) collective-permute-start(bf16[128,4096]{1,0:T(8,128)(2,1)S(1)} %get-tuple-element.10), channel_id=1, source_target_pairs={{0,2},{1,5},{2,0},{3,7},{4,6},{5,1},{6,4},{7,3},{8,10},{9,13},{10,... | collective-permute-start | bytes 3145736 | tf_op jit(solution)/shard_map/ppermute | solution.py:249
  54.6 11.2 %copy-start.8 = (s32[16,8]{0,1:T(8,128)S(1)}, s32[16,8]{0,1:T(8,128)}, u32[]{:S(2)}) copy-start(s32[16,8]{0,1:T(8,128)} %param.22) | copy-start | bytes 1540
  54.6 11.3 %copy-start.9 = (f32[16,8]{0,1:T(8,128)S(1)}, f32[16,8]{0,1:T(8,128)}, u32[]{:S(2)}) copy-start(f32[16,8]{0,1:T(8,128)} %param.23) | copy-start | bytes 1540
  54.7 25.9 %copy-start.6 = (bf16[16,4096]{1,0:T(8,128)(2,1)S(1)}, bf16[16,4096]{1,0:T(8,128)(2,1)}, u32[]{:S(2)}) copy-start(bf16[16,4096]{1,0:T(8,128)(2,1)} %param.12) | copy-start | bytes 393220
  54.7 26.1 %copy-start.7 = (f32[4096]{0:T(1024)S(1)}, f32[4096]{0:T(1024)}, u32[]{:S(2)}) copy-start(f32[4096]{0:T(1024)} %param.18) | copy-start | bytes 49156
  54.7 9.2 %collective-permute-start.2 = (bf16[64,4096]{1,0:T(8,128)(2,1)S(1)}, bf16[64,4096]{1,0:T(8,128)(2,1)S(1)}, u32[]{:S(2)}, u32[]{:S(2)}) collective-permute-start(bf16[64,4096]{1,0:T(8,128)(2,1)S(1)} %slice.85), channel_id=1, source_target_pairs={{0,4},{1,3},{2,6},{3,1},{4,0},{5,7},{6,2},{7,5},{8,12},{9,11},{10,... | collective-permute-start | bytes 1572872 | tf_op jit(solution)/shard_map/ppermute | solution.py:249
  64.1 6.9 %collective-permute-start.3 = (bf16[32,4096]{1,0:T(8,128)(2,1)S(1)}, bf16[32,4096]{1,0:T(8,128)(2,1)S(1)}, u32[]{:S(2)}, u32[]{:S(2)}) collective-permute-start(bf16[32,4096]{1,0:T(8,128)(2,1)S(1)} %slice.87), channel_id=1, source_target_pairs={{0,8},{1,9},{2,10},{3,11},{4,12},{5,13},{6,14},{7,15},{8,0},{9,1},... | collective-permute-start | bytes 786440 | tf_op jit(solution)/shard_map/ppermute | solution.py:249
  65.3 58.4 %collective-permute-start.9 = (bf16[4096,768]{1,0:T(8,128)(2,1)}, bf16[4096,768]{1,0:T(8,128)(2,1)}, u32[]{:S(2)}, u32[]{:S(2)}) collective-permute-start(bf16[4096,768]{1,0:T(8,128)(2,1)} %bitcast.2.gate0), channel_id=1, source_target_pairs={{0,1},{1,0},{2,3},{3,2},{4,5},{5,4},{6,7},{7,6},{8,9},{9,8},{10,11... | collective-permute-start | bytes 18874376 | tf_op jit(solution)/shard_map/ppermute | solution.py:293
  65.3 58.4 %collective-permute-start.10 = (bf16[4096,768]{1,0:T(8,128)(2,1)}, bf16[4096,768]{1,0:T(8,128)(2,1)}, u32[]{:S(2)}, u32[]{:S(2)}) collective-permute-start(bf16[4096,768]{1,0:T(8,128)(2,1)} %bitcast.3.up0), channel_id=1, source_target_pairs={{0,1},{1,0},{2,3},{3,2},{4,5},{5,4},{6,7},{7,6},{8,9},{9,8},{10,11... | collective-permute-start | bytes 18874376 | tf_op jit(solution)/shard_map/ppermute | solution.py:294
  65.8 57.9 %collective-permute-start.11 = (bf16[768,4096]{1,0:T(8,128)(2,1)}, bf16[768,4096]{1,0:T(8,128)(2,1)}, u32[]{:S(2)}, u32[]{:S(2)}) collective-permute-start(bf16[768,4096]{1,0:T(8,128)(2,1)} %bitcast.4.down0), channel_id=1, source_target_pairs={{0,1},{1,0},{2,3},{3,2},{4,5},{5,4},{6,7},{7,6},{8,9},{9,8},{10,11... | collective-permute-start | bytes 18874376 | tf_op jit(solution)/shard_map/ppermute | solution.py:295
  71.1 9.5 %collective-permute-start.4 = (bf16[16,4096]{1,0:T(8,128)(2,1)S(1)}, bf16[16,4096]{1,0:T(8,128)(2,1)S(1)}, u32[]{:S(2)}, u32[]{:S(2)}) collective-permute-start(bf16[16,4096]{1,0:T(8,128)(2,1)S(1)} %slice.89), channel_id=1, source_target_pairs={{0,16},{1,17},{2,18},{3,19},{4,20},{5,21},{6,22},{7,23},{8,24},{9,... | collective-permute-start | bytes 393224 | tf_op jit(solution)/shard_map/ppermute | solution.py:249
  81.0 6.8 %collective-permute-start.5 = (bf16[16,4224]{1,0:T(8,128)(2,1)S(1)}, bf16[16,4224]{1,0:T(8,128)(2,1)S(1)}, u32[]{:S(2)}, u32[]{:S(2)}) collective-permute-start(bf16[16,4224]{1,0:T(8,128)(2,1)S(1)} %pad_maximum_fusion.3), channel_id=1, source_target_pairs={{0,16},{1,17},{2,18},{3,19},{4,20},{5,21},{6,22},{7,23},{8,24},{9,... | collective-permute-start | bytes 405512 | tf_op jit(solution)/shard_map/ppermute | solution.py:261
  87.8 6.5 %collective-permute-start.6 = (bf16[32,4224]{1,0:T(8,128)(2,1)S(1)}, bf16[32,4224]{1,0:T(8,128)(2,1)S(1)}, u32[]{:S(2)}, u32[]{:S(2)}) collective-permute-start(bf16[32,4224]{1,0:T(8,128)(2,1)S(1)} %pad_maximum_fusion.2), channel_id=1, source_target_pairs={{0,8},{1,9},{2,10},{3,11},{4,12},{5,13},{6,14},{7,15},{8,0},{9,1},... | collective-permute-start | bytes 811016 | tf_op jit(solution)/shard_map/ppermute | solution.py:261
  94.3 14.1 %collective-permute-start.7 = (bf16[64,4224]{1,0:T(8,128)(2,1)S(1)}, bf16[64,4224]{1,0:T(8,128)(2,1)S(1)}, u32[]{:S(2)}, u32[]{:S(2)}) collective-permute-start(bf16[64,4224]{1,0:T(8,128)(2,1)S(1)} %pad_maximum_fusion.1), channel_id=1, source_target_pairs={{0,4},{1,3},{2,6},{3,1},{4,0},{5,7},{6,2},{7,5},{8,12},{9,11},{10,... | collective-permute-start | bytes 1622024 | tf_op jit(solution)/shard_map/ppermute | solution.py:261
  108.5 15.2 %copy-start.4 = (bf16[128,4224]{1,0:T(8,128)(2,1)}, bf16[128,4224]{1,0:T(8,128)(2,1)S(1)}, u32[]{:S(2)}) copy-start(bf16[128,4224]{1,0:T(8,128)(2,1)S(1)} %pad_maximum_fusion.low_ref) | copy-start | bytes 3244036
  108.5 15.2 %collective-permute-start.8 = (bf16[128,4224]{1,0:T(8,128)(2,1)S(1)}, bf16[128,4224]{1,0:T(8,128)(2,1)S(1)}, u32[]{:S(2)}, u32[]{:S(2)}) collective-permute-start(bf16[128,4224]{1,0:T(8,128)(2,1)S(1)} %pad_maximum_fusion.low_ref), channel_id=1, source_target_pairs={{0,2},{1,5},{2,0},{3,7},{4,6},{5,1},{6,4},{7,3},{8,10},{9,13},{10,... | collective-permute-start | bytes 3244040 | tf_op jit(solution)/shard_map/ppermute | solution.py:261
  123.7 1.0 copy-start.5
  151.2 19.9 %collective-permute-start.12 = (bf16[128,4096]{1,0:T(8,128)(2,1)}, bf16[128,4096]{1,0:T(8,128)(2,1)S(1)}, u32[]{:S(2)}, u32[]{:S(2)}) collective-permute-start(bf16[128,4096]{1,0:T(8,128)(2,1)} %get-tuple-element.12), channel_id=1, source_target_pairs={{0,2},{1,5},{2,0},{3,7},{4,6},{5,1},{6,4},{7,3},{8,10},{9,13},{10,... | collective-permute-start | bytes 3145736 | tf_op jit(solution)/shard_map/ppermute | solution.py:249
  172.7 9.2 %collective-permute-start.13 = (bf16[64,4096]{1,0:T(8,128)(2,1)S(1)}, bf16[64,4096]{1,0:T(8,128)(2,1)S(1)}, u32[]{:S(2)}, u32[]{:S(2)}) collective-permute-start(bf16[64,4096]{1,0:T(8,128)(2,1)S(1)} %slice.84), channel_id=1, source_target_pairs={{0,4},{1,3},{2,6},{3,1},{4,0},{5,7},{6,2},{7,5},{8,12},{9,11},{10,... | collective-permute-start | bytes 1572872 | tf_op jit(solution)/shard_map/ppermute | solution.py:249
  182.1 6.4 %collective-permute-start.14 = (bf16[32,4096]{1,0:T(8,128)(2,1)S(1)}, bf16[32,4096]{1,0:T(8,128)(2,1)S(1)}, u32[]{:S(2)}, u32[]{:S(2)}) collective-permute-start(bf16[32,4096]{1,0:T(8,128)(2,1)S(1)} %slice.86), channel_id=1, source_target_pairs={{0,8},{1,9},{2,10},{3,11},{4,12},{5,13},{6,14},{7,15},{8,0},{9,1},... | collective-permute-start | bytes 786440 | tf_op jit(solution)/shard_map/ppermute | solution.py:249
  188.6 7.3 %collective-permute-start.15 = (bf16[16,4096]{1,0:T(8,128)(2,1)S(1)}, bf16[16,4096]{1,0:T(8,128)(2,1)S(1)}, u32[]{:S(2)}, u32[]{:S(2)}) collective-permute-start(bf16[16,4096]{1,0:T(8,128)(2,1)S(1)} %slice.88), channel_id=1, source_target_pairs={{0,16},{1,17},{2,18},{3,19},{4,20},{5,21},{6,22},{7,23},{8,24},{9,... | collective-permute-start | bytes 393224 | tf_op jit(solution)/shard_map/ppermute | solution.py:249

commit v3 on v2

v3 whole, which is shorter than its diff:
```python
import math

import jax
import jax.numpy as jnp
from jax import lax
from jax.experimental import pallas as pl
from jax.experimental.pallas import tpu as pltpu
from jax.sharding import PartitionSpec as P

H = 64
KVH = 4
DH = 128
TOP = 8
F32 = jnp.float32
BF16 = jnp.bfloat16


CHUNKS = 2


def attend_kernel(core_ref, lengths_ref, q_ref, new_ref, cache_ref, out_ref, q_rows, out_rows, new_rows):
    rows = q_ref.shape[0]
    heads = q_ref.shape[1] // DH
    per_group = heads // KVH
    count = cache_ref.shape[1]
    span, width = cache_ref.shape[2:]
    step = pl.program_id(0)
    scale = 1.0 / math.sqrt(DH)

    @pl.when(step == 0)
    def _():
        new_rows[...] = new_ref[...].astype(F32)
        for h in range(heads):
            q_rows[h * rows : (h + 1) * rows, :] = q_ref[:, h * DH : (h + 1) * DH].astype(F32)

    position = lax.broadcasted_iota(jnp.int32, (heads, span), 1)
    row_group = lax.broadcasted_iota(jnp.int32, (heads, width), 0) // per_group
    lane_group = lax.broadcasted_iota(jnp.int32, (heads, width), 1) // DH
    own_lanes = row_group == lane_group
    for i in range(count):
        t = step * count + i
        query = q_rows[pl.ds(t, heads, stride=rows), :]
        new_key = new_rows[0, pl.ds(t, 1), :]
        new_value = new_rows[1, pl.ds(t, 1), :]
        spread = jnp.where(own_lanes, jnp.concatenate([query] * KVH, axis=1), 0.0)
        scores = lax.dot_general(
            spread.astype(BF16), cache_ref[0, i], (((1,), (1,)), ((), ())), preferred_element_type=F32
        )
        own = jnp.sum(spread * new_key, axis=1, keepdims=True) * scale
        scores = jnp.where(position < lengths_ref[t], scores * scale, -1e30)
        peak = jnp.maximum(jnp.max(scores, axis=1, keepdims=True), own)
        cached_exp = jnp.exp(scores - peak)
        own_exp = jnp.exp(own - peak)
        denominator = jnp.sum(cached_exp, axis=1, keepdims=True) + own_exp
        probs = (cached_exp / denominator).astype(BF16)
        own_probs = (own_exp / denominator).astype(BF16).astype(F32)
        values = jnp.dot(probs, cache_ref[1, i], preferred_element_type=F32)
        for g in range(KVH):
            part = slice(g * per_group, (g + 1) * per_group)
            lanes = slice(g * DH, (g + 1) * DH)
            value = values[part, lanes] + own_probs[part] * new_value[:, lanes]
            out_rows[pl.ds(g * per_group * rows + t, per_group, stride=rows), :] = value

    chips = out_ref.shape[0]
    per_chip = heads // chips
    for side in range(2):

        @pl.when((step == pl.num_programs(0) - 1) & (core_ref[0] == side))
        def _():
            for e in range(chips):
                for i in range(per_chip):
                    h = e * per_chip + (i + side * (per_chip // 2)) % per_chip
                    out_ref[e, :, i * DH : (i + 1) * DH] = out_rows[h * rows : (h + 1) * rows, :].astype(BF16)


def attend(core, queries, new_kv, cache_kv, lengths, chips):
    rows, features = queries.shape
    span, width = cache_kv.shape[2:]
    count = 4 if rows % 4 == 0 else 1
    whole = lambda shape: pl.BlockSpec(shape, lambda s, *_: (0,) * len(shape))
    return pl.pallas_call(
        attend_kernel,
        out_shape=jax.ShapeDtypeStruct((chips, rows, features // chips), BF16),
        grid_spec=pltpu.PrefetchScalarGridSpec(
            num_scalar_prefetch=2,
            grid=(rows // count,),
            in_specs=[
                whole((rows, features)),
                whole((2, rows, width)),
                pl.BlockSpec((2, count, span, width), lambda s, *_: (0, s, 0, 0)),
            ],
            out_specs=whole((chips, rows, features // chips)),
            scratch_shapes=[
                pltpu.VMEM((features // DH * rows, DH), F32),
                pltpu.VMEM((features // DH * rows, DH), F32),
                pltpu.VMEM((2, rows, width), F32),
            ],
        ),
        compiler_params=pltpu.CompilerParams(vmem_limit_bytes=58 << 20),
        cost_estimate=pl.CostEstimate(flops=4 * rows * features * span, bytes_accessed=2 * cache_kv.size, transcendentals=rows * features),
    )(core, lengths, queries, new_kv, cache_kv)


P_TILE = 512


def project_kernel(index_ref, blocks_ref, own_ref, other_ref, *rest):
    results, ordered = rest[:-1], rest[-1]
    chips, rows, features = blocks_ref.shape
    half = features // 2
    cut = results[0].shape[0]
    chunk = results[0].shape[1]
    for k in range(chips):
        ordered[k * rows : (k + 1) * rows, :] = blocks_ref[index_ref[k]]
    for n in range(own_ref.shape[1] // P_TILE):
        lanes = slice(n * P_TILE, (n + 1) * P_TILE)
        total = jnp.dot(ordered[:, :half], own_ref[:, lanes], preferred_element_type=F32)
        total = total + jnp.dot(ordered[:, half:], other_ref[:, lanes], preferred_element_type=F32)
        c, at = divmod(n * P_TILE, chunk)
        lanes = slice(at, at + P_TILE)
        results[2 * c][:, lanes] = total[:cut].astype(BF16)
        results[2 * c + 1][:, lanes] = total[cut:].astype(BF16)


def project(index, blocks, own, other):
    chips, rows, features = blocks.shape
    width = own.shape[1]
    vmem = pl.BlockSpec(memory_space=pltpu.VMEM)
    return pl.pallas_call(
        project_kernel,
        out_shape=[jax.ShapeDtypeStruct((chips * rows // 2, width // CHUNKS), BF16)] * (2 * CHUNKS),
        in_specs=[pl.BlockSpec(memory_space=pltpu.SMEM), vmem, vmem, vmem],
        out_specs=[vmem] * (2 * CHUNKS),
        scratch_shapes=[pltpu.VMEM((chips * rows, features), BF16)],
        compiler_params=pltpu.CompilerParams(vmem_limit_bytes=12 << 20),
        cost_estimate=pl.CostEstimate(flops=2 * blocks.size * width, bytes_accessed=4 * own.size, transcendentals=0),
    )(index, blocks, own, other)


F_TILE = 256
N_TILE = 512


def expert_kernel(chip_ref, *refs):
    pieces, refs = refs[: 2 * CHUNKS], refs[2 * CHUNKS :]
    (gate0, gate1, up0, up1, down0, down1), refs = refs[:6], refs[6:]
    results, (tokens, active) = refs[: 2 * CHUNKS], refs[2 * CHUNKS :]
    half, chunk = results[0].shape
    hidden = gate0.shape[1]
    per_half = hidden // F_TILE
    for c in range(CHUNKS):
        for side in range(2):
            tokens[side * half : (side + 1) * half, c * chunk : (c + 1) * chunk] = pieces[2 * c + side][:, :chunk]

    for j, (gate, up) in enumerate(((gate0, up0), (gate1, up1))):
        for i in range(per_half):
            lanes = slice(i * F_TILE, (i + 1) * F_TILE)
            gate_part = jnp.dot(tokens[...], gate[:, lanes], preferred_element_type=F32)
            up_part = jnp.dot(tokens[...], up[:, lanes], preferred_element_type=F32)
            at = j * hidden + i * F_TILE
            active[:, at : at + F_TILE] = (gate_part / (1.0 + jnp.exp(-gate_part)) * up_part).astype(BF16)

    first, chips = chip_ref[0], chip_ref[1]
    lane = lax.broadcasted_iota(jnp.int32, (half, pieces[0].shape[1] - chunk), 1)
    mine = (lane == first) | (lane == first + chips) | (lane == first + 2 * chips)
    weights = [
        jnp.sum(jnp.where(mine, ref[:, chunk:].astype(F32), 0.0), axis=1, keepdims=True) for ref in pieces[:2]
    ]
    for n in range(CHUNKS * chunk // N_TILE):
        lanes = slice(n * N_TILE, (n + 1) * N_TILE)
        total = jnp.dot(active[:, :hidden], down0[:, lanes], preferred_element_type=F32)
        total = total + jnp.dot(active[:, hidden:], down1[:, lanes], preferred_element_type=F32)
        c, at = divmod(n * N_TILE, chunk)
        lanes = slice(at, at + N_TILE)
        results[2 * c][:, lanes] = (total[:half] * weights[0]).astype(BF16)
        results[2 * c + 1][:, lanes] = (total[half:] * weights[1]).astype(BF16)


def experts(chip, pieces, gates, ups, downs):
    half = pieces[0].shape[0]
    width, hidden = gates[0].shape
    vmem = pl.BlockSpec(memory_space=pltpu.VMEM)
    return pl.pallas_call(
        expert_kernel,
        out_shape=[jax.ShapeDtypeStruct((half, width // CHUNKS), BF16)] * (2 * CHUNKS),
        in_specs=[pl.BlockSpec(memory_space=pltpu.SMEM)] + [vmem] * (2 * CHUNKS + 6),
        out_specs=[vmem] * (2 * CHUNKS),
        scratch_shapes=[pltpu.VMEM((2 * half, width), BF16), pltpu.VMEM((2 * half, 2 * hidden), BF16)],
        compiler_params=pltpu.CompilerParams(vmem_limit_bytes=28 << 20),
        cost_estimate=pl.CostEstimate(flops=24 * half * width * hidden, bytes_accessed=12 * width * hidden, transcendentals=4 * half * hidden),
    )(chip, *pieces, *gates, *ups, *downs)


def normalize(hidden_state, norm_gain):
    values = [part.astype(F32) for part in hidden_state]
    square = sum(jnp.sum(part * part, axis=-1, keepdims=True) for part in values)
    scale = lax.rsqrt(square / norm_gain.size + 1e-06)
    gains = jnp.split(norm_gain, CHUNKS)
    return [(part * scale * gain).astype(BF16) for part, gain in zip(values, gains)]


def step_bits(devices):
    bits = [1 << i for i in range(1, devices.bit_length() - 1)]
    other = bits[1::-1] + bits[2:] if len(bits) > 1 else bits
    return bits, other


def swap_step(step, devices):
    orders = step_bits(devices)
    return [(i, i ^ orders[i & 1][step]) for i in range(devices)]


def reduce_slots(pieces, devices):
    steps = devices.bit_length() - 2
    kept, sent = list(pieces[::2]), list(pieces[1::2])
    for step in range(steps):
        for c in range(CHUNKS):
            came = lax.ppermute(sent[c], "dp", swap_step(step, devices))
            kept[c] = kept[c].astype(F32) + came.astype(F32)
            half = kept[c].shape[0] // 2
            if step < steps - 1:
                sent[c] = kept[c][half:].astype(BF16)
                kept[c] = kept[c][:half]
    return kept


def gather_slots(own, devices):
    own = list(own)
    steps = devices.bit_length() - 2
    pieces = []
    for step in reversed(range(steps)):
        for c in range(CHUNKS):
            came = lax.ppermute(own[c], "dp", swap_step(step, devices))
            if step == 0:
                pieces += [own[c], came]
            else:
                own[c] = jnp.concatenate([own[c], came], axis=0)
    return pieces


def per_device(
    residual,
    queries,
    new_kv,
    cache_kv,
    lengths,
    out_weight,
    norm_gain,
    w_gate,
    w_up,
    w_down,
    expert_ids,
    combine_weights,
):
    rows = residual.shape[0]
    devices = lax.axis_size("dp")
    chips = devices // 2
    me = lax.axis_index("dp")
    core = me % 2
    chip = me // 2
    steps = devices.bit_length() - 2
    core_swap = [(i, i ^ 1) for i in range(devices)]
    core_groups = [[2 * i + c for i in range(chips)] for c in range(2)]

    out_other = lax.ppermute(out_weight, "dp", core_swap)
    gate_other = lax.ppermute(w_gate[0], "dp", core_swap)
    up_other = lax.ppermute(w_up[0], "dp", core_swap)
    down_other = lax.ppermute(w_down[0], "dp", core_swap)

    attn_out = attend(core[None], queries, new_kv, cache_kv, lengths, chips)
    blocks = lax.all_to_all(
        attn_out, "dp", split_axis=0, concat_axis=0, axis_index_groups=core_groups, tiled=True
    )

    orders = step_bits(devices)
    slot = jnp.arange(chips, dtype=jnp.int32)
    offset = jnp.zeros_like(slot)
    for step in range(steps):
        here = jnp.where(core == 0, orders[0][step], orders[1][step]) // 2
        offset = offset + here * ((slot >> (steps - 1 - step)) & 1)
    projected = reduce_slots(project(chip ^ offset, blocks, out_weight, out_other), devices)
    hidden_state = [
        (part.astype(F32) + add).astype(BF16) for part, add in zip(jnp.split(residual, CHUNKS, axis=1), projected)
    ]
    normed = normalize(hidden_state, norm_gain)

    picks = expert_ids[:, :, None] == jnp.arange(chips, dtype=jnp.int32)
    mix = jnp.sum(jnp.where(picks, combine_weights[:, :, None], 0.0), axis=1)
    mix_hi = mix.astype(BF16)
    mix_mid = (mix - mix_hi.astype(F32)).astype(BF16)
    mix_low = (mix - mix_hi.astype(F32) - mix_mid.astype(F32)).astype(BF16)
    extra = jnp.concatenate([mix_hi, mix_mid, mix_low], axis=1)
    extra = jnp.pad(extra, ((0, 0), (0, -extra.shape[1] % 128)))
    normed[0] = jnp.concatenate([normed[0], extra], axis=1)
    pieces = gather_slots(normed, devices)
    place = jnp.stack([chip, jnp.int32(chips)])
    outs = experts(place, pieces, (w_gate[0], gate_other), (w_up[0], up_other), (w_down[0], down_other))
    mixture = reduce_slots(outs, devices)
    return jnp.concatenate(
        [(part.astype(F32) + add).astype(BF16) for part, add in zip(hidden_state, mixture)], axis=1
    )


def solution(mesh):
    placed = (
        P(("groups", "dp"), None),
        P(("groups", "dp"), None),
        P(None, ("groups", "dp"), None),
        P(None, ("groups", "dp"), None, None),
        P(("groups", "dp")),
        P("dp", None),
        P(),
        P("dp", None, None),
        P("dp", None, None),
        P("dp", None, None),
        P(("groups", "dp"), None),
        P(("groups", "dp"), None),
    )
    return jax.shard_map(
        per_device, mesh=mesh, in_specs=placed, out_specs=P(("groups", "dp"), None), check_vma=False
    )
```

time: 197 us -> 161 us (0.82)
  waiting for transfers between devices: 125 us -> 96.4 us
  starting transfers between devices: 18.5 us -> 31.1 us
  Pallas kernels: 42.6 us -> 30.6 us
  local copies, waits for them, and re-layouts: 5.11 us -> 0.41 us
  other arithmetic: 4.82 us -> 2.25 us
    ppermute x12 -> x24, waiting for transfers between devices: 115 us -> 86.8 us  [the longest x16 57.7 us: reduce_slots(): came = lax.ppermute(sent[c], 'dp', swap_step(step, devices))]
    ppermute x12 -> x24, starting transfers between devices: 9.62 us -> 22 us  [the longest x16 15.6 us: reduce_slots(): came = lax.ppermute(sent[c], 'dp', swap_step(step, devices))]
    pallas_call x1, Pallas kernels: 26.5 us -> 18.1 us  [experts(): pl.pallas_call(expert_kernel, out_shape=[jax.ShapeDtypeStruct((half, widt...]
    unnamed x22 -> x20, local copies, waits for them, and re-layouts: 4.91 us -> 0.19 us
    pallas_call x1, Pallas kernels: 6.17 us -> 3.01 us  [project(): pl.pallas_call(project_kernel, out_shape=[jax.ShapeDtypeStruct((chips * r...]
  transfers between devices with their start and end apart: 17 -> 29, of which waited for: 13 -> 19; matrix products, arithmetic and copies ran while one was open for 1% -> 1% of each run, Pallas kernels for 5% -> 8%
where the time goes in v3:
time: 161 us
  waiting for transfers between devices  96.4 us (60%)
  starting transfers between devices  31.1 us (19%)
  Pallas kernels  30.6 us (19%)
  other arithmetic  2.25 us (1%)
    ppermute x16, waiting for transfers between devices, reduce_slots(): came = lax.ppermute(sent[c], 'dp', swap_step(step, devices))  57.7 us
    ppermute x8, waiting for transfers between devices, gather_slots(): came = lax.ppermute(own[c], 'dp', swap_step(step, devices))  29.1 us
    pallas_call x1, Pallas kernels, experts(): pl.pallas_call(expert_kernel, out_shape=[jax.ShapeDtypeStruct((half, widt...  18.1 us
    ppermute x16, starting transfers between devices, reduce_slots(): came = lax.ppermute(sent[c], 'dp', swap_step(step, devices))  15.6 us
    all_to_all x1, waiting for transfers between devices, per_device(): lax.all_to_all(attn_out, 'dp', split_axis=0, concat_axis=0, axis_index_gr...  9.57 us
    pallas_call x1, Pallas kernels, attend(): pl.pallas_call(attend_kernel, out_shape=jax.ShapeDtypeStruct((chips, rows...  9.51 us
    all_to_all x1, starting transfers between devices, per_device(): lax.all_to_all(attn_out, 'dp', split_axis=0, concat_axis=0, axis_index_gr...  7.88 us
    ppermute x8, starting transfers between devices, gather_slots(): came = lax.ppermute(own[c], 'dp', swap_step(step, devices))  6.42 us
  transfers between devices with their start and end apart: 29, of which 19 were waited for; matrix products, arithmetic and copies ran while one was open for 1% of the time, Pallas kernels for 8%

profile of v3, /device:TPU:0, one launch (start us, length us, event | category | flops | bytes accessed | tf_op | source)
XLA Modules:
  0.0 161.2 jit_solution(532765997066344673)
XLA Ops:
  0.5 9.5 %shard_map.118 = bf16[16,16,512]{2,1,0:T(8,128)(2,1)} custom-call(s32[1]{0:T(128)} %bitcast.core_ref, s32[16]{0:T(128)} %lengths_ref.1, bf16[16,8192]{1,0:T(8,128)(2,1)} %q_ref.1, bf16[2,16,512]{2,1,0:T(8,128)(2,1)} %new_ref.1, bf16[2,16,128,512]{3,2,1,0:T(8,128)(2,1)} %cache_ref.1), custom_call_target="tpu_custom_call" | custom-call | flops 67108864 | bytes 4194304 | tf_op jit(solution)/shard_map/pallas_call | solution.py:81
  10.0 7.9 %all-to-all-start = ((bf16[16,16,512]{2,1,0:T(8,128)(2,1)}), bf16[16,16,512]{2,1,0:T(8,128)(2,1)S(1)}, u32[]{:S(2)}, u32[]{:S(2)}) async-start(bf16[16,16,512]{2,1,0:T(8,128)(2,1)} %shard_map.118), calls=%async_computation | async-start | bytes 524288 | tf_op jit(solution)/shard_map/all_to_all | solution.py:271
  18.8 9.6 %all-to-all-done.blocks_ref = bf16[16,16,512]{2,1,0:T(8,128)(2,1)S(1)} async-done(((bf16[16,16,512]{2,1,0:T(8,128)(2,1)}), bf16[16,16,512]{2,1,0:T(8,128)(2,1)S(1)}, u32[]{:S(2)}, u32[]{:S(2)}) %all-to-all-start) | async-done | bytes 262176 | tf_op jit(solution)/shard_map/all_to_all | solution.py:271
  28.4 3.0 %shard_map.119 = (bf16[128,2048]{1,0:T(8,128)(2,1)S(1)}, bf16[128,2048]{1,0:T(8,128)(2,1)S(1)}, bf16[128,2048]{1,0:T(8,128)(2,1)S(1)}, bf16[128,2048]{1,0:T(8,128)(2,1)S(1)}) custom-call(s32[16]{0:T(128)S(1)} %add_xor_fusion.index_ref, bf16[16,16,512]{2,1,0:T(8,128)(2,1)S(1)} %all-to-all-done.blocks_ref, bf16[256,4096]{1,0:T(8,128)(2,1)S(1)} %copy-done, ...), custom_call_target="tpu_custom_call" | custom-call | flops 1073741824 | bytes 4194304 | tf_op jit(solution)/shard_map/pallas_call | solution.py:129
  31.4 0.8 collective-permute-start.1
  32.4 1.3 collective-permute-start.5
  33.7 6.9 %collective-permute-done.1 = bf16[128,2048]{1,0:T(8,128)(2,1)S(1)} collective-permute-done((bf16[128,2048]{1,0:T(8,128)(2,1)S(1)}, bf16[128,2048]{1,0:T(8,128)(2,1)S(1)}, u32[]{:S(2)}, u32[]{:S(2)}) %collective-permute-start.1) | collective-permute-done | bytes 524320 | tf_op jit(solution)/shard_map/ppermute | solution.py:218
  40.8 1.0 collective-permute-start.2
  41.8 9.4 %collective-permute-done.5 = bf16[128,2048]{1,0:T(8,128)(2,1)S(1)} collective-permute-done((bf16[128,2048]{1,0:T(8,128)(2,1)S(1)}, bf16[128,2048]{1,0:T(8,128)(2,1)S(1)}, u32[]{:S(2)}, u32[]{:S(2)}) %collective-permute-start.5) | collective-permute-done | bytes 524320 | tf_op jit(solution)/shard_map/ppermute | solution.py:218
  51.4 1.6 collective-permute-start.6
  53.1 4.7 %collective-permute-done.6 = bf16[64,2048]{1,0:T(8,128)(2,1)S(1)} collective-permute-done((bf16[64,2048]{1,0:T(8,128)(2,1)S(1)}, bf16[64,2048]{1,0:T(8,128)(2,1)S(1)}, u32[]{:S(2)}, u32[]{:S(2)}) %collective-permute-start.6) | collective-permute-done | bytes 262176 | tf_op jit(solution)/shard_map/ppermute | solution.py:218
  57.9 1.6 collective-permute-start.7
  59.7 3.2 %collective-permute-done.7 = bf16[32,2048]{1,0:T(8,128)(2,1)S(1)} collective-permute-done((bf16[32,2048]{1,0:T(8,128)(2,1)S(1)}, bf16[32,2048]{1,0:T(8,128)(2,1)S(1)}, u32[]{:S(2)}, u32[]{:S(2)}) %collective-permute-start.7) | collective-permute-done | bytes 131104 | tf_op jit(solution)/shard_map/ppermute | solution.py:218
  63.7 3.2 %collective-permute-done.4 = bf16[16,2048]{1,0:T(8,128)(2,1)S(1)} collective-permute-done((bf16[16,2048]{1,0:T(8,128)(2,1)S(1)}, bf16[16,2048]{1,0:T(8,128)(2,1)S(1)}, u32[]{:S(2)}, u32[]{:S(2)}) %collective-permute-start.4) | collective-permute-done | bytes 65568 | tf_op jit(solution)/shard_map/ppermute | solution.py:218
  66.9 2.8 %collective-permute-done.8 = bf16[16,2048]{1,0:T(8,128)(2,1)S(1)} collective-permute-done((bf16[16,2048]{1,0:T(8,128)(2,1)S(1)}, bf16[16,2048]{1,0:T(8,128)(2,1)S(1)}, u32[]{:S(2)}, u32[]{:S(2)}) %collective-permute-start.8) | collective-permute-done | bytes 65568 | tf_op jit(solution)/shard_map/ppermute | solution.py:218
  70.1 2.9 %collective-permute-start.13 = (bf16[16,2048]{1,0:T(8,128)(2,1)S(1)}, bf16[16,2048]{1,0:T(8,128)(2,1)S(1)}, u32[]{:S(2)}, u32[]{:S(2)}) collective-permute-start(bf16[16,2048]{1,0:T(8,128)(2,1)S(1)} %get-tuple-element.32), channel_id=1, source_target_pairs={{0,16},{1,17},{2,18},{3,19},{4,20},{5,21},{6,22},{7,23},{8,24},{9,... | collective-permute-start | bytes 196616 | tf_op jit(solution)/shard_map/ppermute | solution.py:233
  73.0 2.7 %collective-permute-done.9 = bf16[16,2176]{1,0:T(8,128)(2,1)S(1)} collective-permute-done((bf16[16,2176]{1,0:T(8,128)(2,1)S(1)}, bf16[16,2176]{1,0:T(8,128)(2,1)S(1)}, u32[]{:S(2)}, u32[]{:S(2)}) %collective-permute-start.9) | collective-permute-done | bytes 69664 | tf_op jit(solution)/shard_map/ppermute | solution.py:233
  75.8 1.3 collective-permute-done.13
  77.9 2.9 %collective-permute-done.10 = bf16[32,2176]{1,0:T(8,128)(2,1)S(1)} collective-permute-done((bf16[32,2176]{1,0:T(8,128)(2,1)S(1)}, bf16[32,2176]{1,0:T(8,128)(2,1)S(1)}, u32[]{:S(2)}, u32[]{:S(2)}) %collective-permute-start.10) | collective-permute-done | bytes 139296 | tf_op jit(solution)/shard_map/ppermute | solution.py:233
  81.3 0.9 collective-permute-done.14
  83.0 7.5 %collective-permute-done.11 = bf16[64,2176]{1,0:T(8,128)(2,1)S(1)} collective-permute-done((bf16[64,2176]{1,0:T(8,128)(2,1)S(1)}, bf16[64,2176]{1,0:T(8,128)(2,1)S(1)}, u32[]{:S(2)}, u32[]{:S(2)}) %collective-permute-start.11) | collective-permute-done | bytes 278560 | tf_op jit(solution)/shard_map/ppermute | solution.py:233
  91.3 4.9 %collective-permute-done.15 = bf16[64,2048]{1,0:T(8,128)(2,1)S(1)} collective-permute-done((bf16[64,2048]{1,0:T(8,128)(2,1)S(1)}, bf16[64,2048]{1,0:T(8,128)(2,1)S(1)}, u32[]{:S(2)}, u32[]{:S(2)}) %collective-permute-start.15) | collective-permute-done | bytes 262176 | tf_op jit(solution)/shard_map/ppermute | solution.py:233
  96.9 8.8 %collective-permute-done.16.refs_3_ = bf16[128,2048]{1,0:T(8,128)(2,1)S(1)} collective-permute-done((bf16[128,2048]{1,0:T(8,128)(2,1)S(1)}, bf16[128,2048]{1,0:T(8,128)(2,1)S(1)}, u32[]{:S(2)}, u32[]{:S(2)}) %collective-permute-start.16) | collective-permute-done | bytes 524320 | tf_op jit(solution)/shard_map/ppermute | solution.py:233
  105.9 18.1 %shard_map.120 = (bf16[128,2048]{1,0:T(8,128)(2,1)S(1)}, bf16[128,2048]{1,0:T(8,128)(2,1)S(1)}, bf16[128,2048]{1,0:T(8,128)(2,1)S(1)}, bf16[128,2048]{1,0:T(8,128)(2,1)S(1)}) custom-call(s32[2]{0:T(128)S(1)} %pad_add_fusion.chip_ref, bf16[128,2176]{1,0:T(8,128)(2,1)S(1)} %pad_maximum_fusion.refs_0_, bf16[128,2176]{1,0:T(8,128)(2,1)S(1)} %collective-permute-done.12.refs_1_, ...), custom_call_target="tpu_custom_call" | custom-call | flops 9663676416 | bytes 37748736 | tf_op jit(solution)/shard_map/pallas_call | solution.py:183
  124.7 1.4 collective-permute-start.24
  126.1 10.9 %collective-permute-done.20 = bf16[128,2048]{1,0:T(8,128)(2,1)S(1)} collective-permute-done((bf16[128,2048]{1,0:T(8,128)(2,1)S(1)}, bf16[128,2048]{1,0:T(8,128)(2,1)S(1)}, u32[]{:S(2)}, u32[]{:S(2)}) %collective-permute-start.20) | collective-permute-done | bytes 524320 | tf_op jit(solution)/shard_map/ppermute | solution.py:218
  138.0 5.0 %collective-permute-done.24 = bf16[128,2048]{1,0:T(8,128)(2,1)S(1)} collective-permute-done((bf16[128,2048]{1,0:T(8,128)(2,1)S(1)}, bf16[128,2048]{1,0:T(8,128)(2,1)S(1)}, u32[]{:S(2)}, u32[]{:S(2)}) %collective-permute-start.24) | collective-permute-done | bytes 524320 | tf_op jit(solution)/shard_map/ppermute | solution.py:218
  144.1 5.4 %collective-permute-done.25 = bf16[64,2048]{1,0:T(8,128)(2,1)S(1)} collective-permute-done((bf16[64,2048]{1,0:T(8,128)(2,1)S(1)}, bf16[64,2048]{1,0:T(8,128)(2,1)S(1)}, u32[]{:S(2)}, u32[]{:S(2)}) %collective-permute-start.25) | collective-permute-done | bytes 262176 | tf_op jit(solution)/shard_map/ppermute | solution.py:218
  150.2 2.6 %collective-permute-start.23 = (bf16[16,2048]{1,0:T(8,128)(2,1)S(1)}, bf16[16,2048]{1,0:T(8,128)(2,1)S(1)}, u32[]{:S(2)}, u32[]{:S(2)}) collective-permute-start(bf16[16,2048]{1,0:T(8,128)(2,1)S(1)} %slice.177), channel_id=1, source_target_pairs={{0,16},{1,17},{2,18},{3,19},{4,20},{5,21},{6,22},{7,23},{8,24},{9,... | collective-permute-start | bytes 196616 | tf_op jit(solution)/shard_map/ppermute | solution.py:218
  152.7 1.9 %collective-permute-done.26 = bf16[32,2048]{1,0:T(8,128)(2,1)S(1)} collective-permute-done((bf16[32,2048]{1,0:T(8,128)(2,1)S(1)}, bf16[32,2048]{1,0:T(8,128)(2,1)S(1)}, u32[]{:S(2)}, u32[]{:S(2)}) %collective-permute-start.26) | collective-permute-done | bytes 131104 | tf_op jit(solution)/shard_map/ppermute | solution.py:218
  154.7 1.5 collective-permute-start.27
  156.3 4.2 %collective-permute-done.27 = bf16[16,2048]{1,0:T(8,128)(2,1)S(1)} collective-permute-done((bf16[16,2048]{1,0:T(8,128)(2,1)S(1)}, bf16[16,2048]{1,0:T(8,128)(2,1)S(1)}, u32[]{:S(2)}, u32[]{:S(2)}) %collective-permute-start.27) | collective-permute-done | bytes 65568 | tf_op jit(solution)/shard_map/ppermute | solution.py:218
  (94 shorter events, 11.2 us)
Async XLA Ops:
  0.0 28.4 %collective-permute-start = (bf16[256,4096]{1,0:T(8,128)(2,1)}, bf16[256,4096]{1,0:T(8,128)(2,1)}, u32[]{:S(2)}, u32[]{:S(2)}) collective-permute-start(bf16[256,4096]{1,0:T(8,128)(2,1)} %own_ref.1), channel_id=1, source_target_pairs={{0,1},{1,0},{2,3},{3,2},{4,5},{5,4},{6,7},{7,6},{8,9},{9,8},{10,11... | collective-permute-start | bytes 6291464 | tf_op jit(solution)/shard_map/ppermute | solution.py:265
  10.0 18.4 %all-to-all-start = ((bf16[16,16,512]{2,1,0:T(8,128)(2,1)}), bf16[16,16,512]{2,1,0:T(8,128)(2,1)S(1)}, u32[]{:S(2)}, u32[]{:S(2)}) async-start(bf16[16,16,512]{2,1,0:T(8,128)(2,1)} %shard_map.118), calls=%async_computation | async-start | bytes 524288 | tf_op jit(solution)/shard_map/all_to_all | solution.py:271
  17.9 87.9 %collective-permute-start.17 = (bf16[4096,768]{1,0:T(8,128)(2,1)}, bf16[4096,768]{1,0:T(8,128)(2,1)}, u32[]{:S(2)}, u32[]{:S(2)}) collective-permute-start(bf16[4096,768]{1,0:T(8,128)(2,1)} %bitcast.5), channel_id=1, source_target_pairs={{0,1},{1,0},{2,3},{3,2},{4,5},{5,4},{6,7},{7,6},{8,9},{9,8},{10,11... | collective-permute-start | bytes 18874376 | tf_op jit(solution)/shard_map/ppermute | solution.py:266
  18.1 87.7 %collective-permute-start.18 = (bf16[4096,768]{1,0:T(8,128)(2,1)}, bf16[4096,768]{1,0:T(8,128)(2,1)}, u32[]{:S(2)}, u32[]{:S(2)}) collective-permute-start(bf16[4096,768]{1,0:T(8,128)(2,1)} %bitcast.9), channel_id=1, source_target_pairs={{0,1},{1,0},{2,3},{3,2},{4,5},{5,4},{6,7},{7,6},{8,9},{9,8},{10,11... | collective-permute-start | bytes 18874376 | tf_op jit(solution)/shard_map/ppermute | solution.py:267
  18.4 87.4 %collective-permute-start.19 = (bf16[768,4096]{1,0:T(8,128)(2,1)}, bf16[768,4096]{1,0:T(8,128)(2,1)}, u32[]{:S(2)}, u32[]{:S(2)}) collective-permute-start(bf16[768,4096]{1,0:T(8,128)(2,1)} %bitcast.13), channel_id=1, source_target_pairs={{0,1},{1,0},{2,3},{3,2},{4,5},{5,4},{6,7},{7,6},{8,9},{9,8},{10,11... | collective-permute-start | bytes 18874376 | tf_op jit(solution)/shard_map/ppermute | solution.py:268
  28.4 77.4 %slice-start.2 = ((s8[6291456]{0:T(1024)(128)(4,1)}), s8[4194304]{0:T(1024)(128)(4,1)S(1)}, s32[]{:S(2)}) async-start(s8[6291456]{0:T(1024)(128)(4,1)} %bitcast.10), calls=%async_computation.3 | async-start | bytes 8388608
  31.4 9.2 %collective-permute-start.1 = (bf16[128,2048]{1,0:T(8,128)(2,1)S(1)}, bf16[128,2048]{1,0:T(8,128)(2,1)S(1)}, u32[]{:S(2)}, u32[]{:S(2)}) collective-permute-start(bf16[128,2048]{1,0:T(8,128)(2,1)S(1)} %get-tuple-element.14), channel_id=1, source_target_pairs={{0,2},{1,5},{2,0},{3,7},{4,6},{5,1},{6,4},{7,3},{8,10},{9,13},{10,... | collective-permute-start | bytes 1572872 | tf_op jit(solution)/shard_map/ppermute | solution.py:218
  32.4 18.8 %collective-permute-start.5 = (bf16[128,2048]{1,0:T(8,128)(2,1)S(1)}, bf16[128,2048]{1,0:T(8,128)(2,1)S(1)}, u32[]{:S(2)}, u32[]{:S(2)}) collective-permute-start(bf16[128,2048]{1,0:T(8,128)(2,1)S(1)} %get-tuple-element.16), channel_id=1, source_target_pairs={{0,2},{1,5},{2,0},{3,7},{4,6},{5,1},{6,4},{7,3},{8,10},{9,13},{10,... | collective-permute-start | bytes 1572872 | tf_op jit(solution)/shard_map/ppermute | solution.py:218
  40.6 65.2 %slice-start = ((s8[6291456]{0:T(1024)(128)(4,1)}), s8[4194304]{0:T(1024)(128)(4,1)S(1)}, s32[]{:S(2)}) async-start(s8[6291456]{0:T(1024)(128)(4,1)} %bitcast.6), calls=%async_computation.1 | async-start | bytes 8388608
  40.8 12.1 %collective-permute-start.2 = (bf16[64,2048]{1,0:T(8,128)(2,1)S(1)}, bf16[64,2048]{1,0:T(8,128)(2,1)S(1)}, u32[]{:S(2)}, u32[]{:S(2)}) collective-permute-start(bf16[64,2048]{1,0:T(8,128)(2,1)S(1)} %slice.171), channel_id=1, source_target_pairs={{0,4},{1,3},{2,6},{3,1},{4,0},{5,7},{6,2},{7,5},{8,12},{9,11},{10,... | collective-permute-start | bytes 786440 | tf_op jit(solution)/shard_map/ppermute | solution.py:218
  51.3 54.5 %slice-start.3 = ((s8[6291456]{0:T(1024)(128)(4,1)}), s8[2097152]{0:T(1024)(128)(4,1)S(1)}, s32[]{:S(2)}) async-start(s8[6291456]{0:T(1024)(128)(4,1)} %bitcast.10), calls=%async_computation.4 | async-start | bytes 4194304
  51.4 6.4 %collective-permute-start.6 = (bf16[64,2048]{1,0:T(8,128)(2,1)S(1)}, bf16[64,2048]{1,0:T(8,128)(2,1)S(1)}, u32[]{:S(2)}, u32[]{:S(2)}) collective-permute-start(bf16[64,2048]{1,0:T(8,128)(2,1)S(1)} %slice.170), channel_id=1, source_target_pairs={{0,4},{1,3},{2,6},{3,1},{4,0},{5,7},{6,2},{7,5},{8,12},{9,11},{10,... | collective-permute-start | bytes 786440 | tf_op jit(solution)/shard_map/ppermute | solution.py:218
  53.1 6.4 %collective-permute-start.3 = (bf16[32,2048]{1,0:T(8,128)(2,1)S(1)}, bf16[32,2048]{1,0:T(8,128)(2,1)S(1)}, u32[]{:S(2)}, u32[]{:S(2)}) collective-permute-start(bf16[32,2048]{1,0:T(8,128)(2,1)S(1)} %slice.175), channel_id=1, source_target_pairs={{0,8},{1,9},{2,10},{3,11},{4,12},{5,13},{6,14},{7,15},{8,0},{9,1},... | collective-permute-start | bytes 393224 | tf_op jit(solution)/shard_map/ppermute | solution.py:218
  57.9 5.0 %collective-permute-start.7 = (bf16[32,2048]{1,0:T(8,128)(2,1)S(1)}, bf16[32,2048]{1,0:T(8,128)(2,1)S(1)}, u32[]{:S(2)}, u32[]{:S(2)}) collective-permute-start(bf16[32,2048]{1,0:T(8,128)(2,1)S(1)} %slice.174), channel_id=1, source_target_pairs={{0,8},{1,9},{2,10},{3,11},{4,12},{5,13},{6,14},{7,15},{8,0},{9,1},... | collective-permute-start | bytes 393224 | tf_op jit(solution)/shard_map/ppermute | solution.py:218
  59.5 7.4 %collective-permute-start.4 = (bf16[16,2048]{1,0:T(8,128)(2,1)S(1)}, bf16[16,2048]{1,0:T(8,128)(2,1)S(1)}, u32[]{:S(2)}, u32[]{:S(2)}) collective-permute-start(bf16[16,2048]{1,0:T(8,128)(2,1)S(1)} %slice.179), channel_id=1, source_target_pairs={{0,16},{1,17},{2,18},{3,19},{4,20},{5,21},{6,22},{7,23},{8,24},{9,... | collective-permute-start | bytes 196616 | tf_op jit(solution)/shard_map/ppermute | solution.py:218
  63.0 6.7 %collective-permute-start.8 = (bf16[16,2048]{1,0:T(8,128)(2,1)S(1)}, bf16[16,2048]{1,0:T(8,128)(2,1)S(1)}, u32[]{:S(2)}, u32[]{:S(2)}) collective-permute-start(bf16[16,2048]{1,0:T(8,128)(2,1)S(1)} %slice.178), channel_id=1, source_target_pairs={{0,16},{1,17},{2,18},{3,19},{4,20},{5,21},{6,22},{7,23},{8,24},{9,... | collective-permute-start | bytes 196616 | tf_op jit(solution)/shard_map/ppermute | solution.py:218
  70.0 5.7 %collective-permute-start.9 = (bf16[16,2176]{1,0:T(8,128)(2,1)S(1)}, bf16[16,2176]{1,0:T(8,128)(2,1)S(1)}, u32[]{:S(2)}, u32[]{:S(2)}) collective-permute-start(bf16[16,2176]{1,0:T(8,128)(2,1)S(1)} %pad_maximum_fusion.7), channel_id=1, source_target_pairs={{0,16},{1,17},{2,18},{3,19},{4,20},{5,21},{6,22},{7,23},{8,24},{9,... | collective-permute-start | bytes 208904 | tf_op jit(solution)/shard_map/ppermute | solution.py:233
  70.1 7.0 %collective-permute-start.13 = (bf16[16,2048]{1,0:T(8,128)(2,1)S(1)}, bf16[16,2048]{1,0:T(8,128)(2,1)S(1)}, u32[]{:S(2)}, u32[]{:S(2)}) collective-permute-start(bf16[16,2048]{1,0:T(8,128)(2,1)S(1)} %get-tuple-element.32), channel_id=1, source_target_pairs={{0,16},{1,17},{2,18},{3,19},{4,20},{5,21},{6,22},{7,23},{8,24},{9,... | collective-permute-start | bytes 196616 | tf_op jit(solution)/shard_map/ppermute | solution.py:233
  75.7 5.1 %collective-permute-start.10 = (bf16[32,2176]{1,0:T(8,128)(2,1)S(1)}, bf16[32,2176]{1,0:T(8,128)(2,1)S(1)}, u32[]{:S(2)}, u32[]{:S(2)}) collective-permute-start(bf16[32,2176]{1,0:T(8,128)(2,1)S(1)} %pad_maximum_fusion.4), channel_id=1, source_target_pairs={{0,8},{1,9},{2,10},{3,11},{4,12},{5,13},{6,14},{7,15},{8,0},{9,1},... | collective-permute-start | bytes 417800 | tf_op jit(solution)/shard_map/ppermute | solution.py:233
  77.1 5.1 %collective-permute-start.14 = (bf16[32,2048]{1,0:T(8,128)(2,1)S(1)}, bf16[32,2048]{1,0:T(8,128)(2,1)S(1)}, u32[]{:S(2)}, u32[]{:S(2)}) collective-permute-start(bf16[32,2048]{1,0:T(8,128)(2,1)S(1)} %pad_maximum_fusion.5), channel_id=1, source_target_pairs={{0,8},{1,9},{2,10},{3,11},{4,12},{5,13},{6,14},{7,15},{8,0},{9,1},... | collective-permute-start | bytes 393224 | tf_op jit(solution)/shard_map/ppermute | solution.py:233
  80.9 9.7 %collective-permute-start.11 = (bf16[64,2176]{1,0:T(8,128)(2,1)S(1)}, bf16[64,2176]{1,0:T(8,128)(2,1)S(1)}, u32[]{:S(2)}, u32[]{:S(2)}) collective-permute-start(bf16[64,2176]{1,0:T(8,128)(2,1)S(1)} %pad_maximum_fusion.2), channel_id=1, source_target_pairs={{0,4},{1,3},{2,6},{3,1},{4,0},{5,7},{6,2},{7,5},{8,12},{9,11},{10,... | collective-permute-start | bytes 835592 | tf_op jit(solution)/shard_map/ppermute | solution.py:233
  82.3 13.9 %collective-permute-start.15 = (bf16[64,2048]{1,0:T(8,128)(2,1)S(1)}, bf16[64,2048]{1,0:T(8,128)(2,1)S(1)}, u32[]{:S(2)}, u32[]{:S(2)}) collective-permute-start(bf16[64,2048]{1,0:T(8,128)(2,1)S(1)} %pad_maximum_fusion.3), channel_id=1, source_target_pairs={{0,4},{1,3},{2,6},{3,1},{4,0},{5,7},{6,2},{7,5},{8,12},{9,11},{10,... | collective-permute-start | bytes 786440 | tf_op jit(solution)/shard_map/ppermute | solution.py:233
  90.6 15.2 %collective-permute-start.12 = (bf16[128,2176]{1,0:T(8,128)(2,1)S(1)}, bf16[128,2176]{1,0:T(8,128)(2,1)S(1)}, u32[]{:S(2)}, u32[]{:S(2)}) collective-permute-start(bf16[128,2176]{1,0:T(8,128)(2,1)S(1)} %pad_maximum_fusion.refs_0_), channel_id=1, source_target_pairs={{0,2},{1,5},{2,0},{3,7},{4,6},{5,1},{6,4},{7,3},{8,10},{9,13},{10,... | collective-permute-start | bytes 1671176 | tf_op jit(solution)/shard_map/ppermute | solution.py:233
  96.2 9.6 %collective-permute-start.16 = (bf16[128,2048]{1,0:T(8,128)(2,1)S(1)}, bf16[128,2048]{1,0:T(8,128)(2,1)S(1)}, u32[]{:S(2)}, u32[]{:S(2)}) collective-permute-start(bf16[128,2048]{1,0:T(8,128)(2,1)S(1)} %pad_maximum_fusion.1.refs_2_), channel_id=1, source_target_pairs={{0,2},{1,5},{2,0},{3,7},{4,6},{5,1},{6,4},{7,3},{8,10},{9,13},{10,... | collective-permute-start | bytes 1572872 | tf_op jit(solution)/shard_map/ppermute | solution.py:233
  124.0 13.0 %collective-permute-start.20 = (bf16[128,2048]{1,0:T(8,128)(2,1)S(1)}, bf16[128,2048]{1,0:T(8,128)(2,1)S(1)}, u32[]{:S(2)}, u32[]{:S(2)}) collective-permute-start(bf16[128,2048]{1,0:T(8,128)(2,1)S(1)} %get-tuple-element.18), channel_id=1, source_target_pairs={{0,2},{1,5},{2,0},{3,7},{4,6},{5,1},{6,4},{7,3},{8,10},{9,13},{10,... | collective-permute-start | bytes 1572872 | tf_op jit(solution)/shard_map/ppermute | solution.py:218
  124.7 18.3 %collective-permute-start.24 = (bf16[128,2048]{1,0:T(8,128)(2,1)S(1)}, bf16[128,2048]{1,0:T(8,128)(2,1)S(1)}, u32[]{:S(2)}, u32[]{:S(2)}) collective-permute-start(bf16[128,2048]{1,0:T(8,128)(2,1)S(1)} %get-tuple-element.20), channel_id=1, source_target_pairs={{0,2},{1,5},{2,0},{3,7},{4,6},{5,1},{6,4},{7,3},{8,10},{9,13},{10,... | collective-permute-start | bytes 1572872 | tf_op jit(solution)/shard_map/ppermute | solution.py:218
  137.2 6.8 %collective-permute-start.21 = (bf16[64,2048]{1,0:T(8,128)(2,1)S(1)}, bf16[64,2048]{1,0:T(8,128)(2,1)S(1)}, u32[]{:S(2)}, u32[]{:S(2)}) collective-permute-start(bf16[64,2048]{1,0:T(8,128)(2,1)S(1)} %slice.169), channel_id=1, source_target_pairs={{0,4},{1,3},{2,6},{3,1},{4,0},{5,7},{6,2},{7,5},{8,12},{9,11},{10,... | collective-permute-start | bytes 786440 | tf_op jit(solution)/shard_map/ppermute | solution.py:218
  143.1 6.4 %collective-permute-start.25 = (bf16[64,2048]{1,0:T(8,128)(2,1)S(1)}, bf16[64,2048]{1,0:T(8,128)(2,1)S(1)}, u32[]{:S(2)}, u32[]{:S(2)}) collective-permute-start(bf16[64,2048]{1,0:T(8,128)(2,1)S(1)} %slice.168), channel_id=1, source_target_pairs={{0,4},{1,3},{2,6},{3,1},{4,0},{5,7},{6,2},{7,5},{8,12},{9,11},{10,... | collective-permute-start | bytes 786440 | tf_op jit(solution)/shard_map/ppermute | solution.py:218
  144.0 6.1 %collective-permute-start.22 = (bf16[32,2048]{1,0:T(8,128)(2,1)S(1)}, bf16[32,2048]{1,0:T(8,128)(2,1)S(1)}, u32[]{:S(2)}, u32[]{:S(2)}) collective-permute-start(bf16[32,2048]{1,0:T(8,128)(2,1)S(1)} %slice.173), channel_id=1, source_target_pairs={{0,8},{1,9},{2,10},{3,11},{4,12},{5,13},{6,14},{7,15},{8,0},{9,1},... | collective-permute-start | bytes 393224 | tf_op jit(solution)/shard_map/ppermute | solution.py:218
  149.7 5.0 %collective-permute-start.26 = (bf16[32,2048]{1,0:T(8,128)(2,1)S(1)}, bf16[32,2048]{1,0:T(8,128)(2,1)S(1)}, u32[]{:S(2)}, u32[]{:S(2)}) collective-permute-start(bf16[32,2048]{1,0:T(8,128)(2,1)S(1)} %slice.172), channel_id=1, source_target_pairs={{0,8},{1,9},{2,10},{3,11},{4,12},{5,13},{6,14},{7,15},{8,0},{9,1},... | collective-permute-start | bytes 393224 | tf_op jit(solution)/shard_map/ppermute | solution.py:218
  150.2 6.1 %collective-permute-start.23 = (bf16[16,2048]{1,0:T(8,128)(2,1)S(1)}, bf16[16,2048]{1,0:T(8,128)(2,1)S(1)}, u32[]{:S(2)}, u32[]{:S(2)}) collective-permute-start(bf16[16,2048]{1,0:T(8,128)(2,1)S(1)} %slice.177), channel_id=1, source_target_pairs={{0,16},{1,17},{2,18},{3,19},{4,20},{5,21},{6,22},{7,23},{8,24},{9,... | collective-permute-start | bytes 196616 | tf_op jit(solution)/shard_map/ppermute | solution.py:218
  154.7 5.8 %collective-permute-start.27 = (bf16[16,2048]{1,0:T(8,128)(2,1)S(1)}, bf16[16,2048]{1,0:T(8,128)(2,1)S(1)}, u32[]{:S(2)}, u32[]{:S(2)}) collective-permute-start(bf16[16,2048]{1,0:T(8,128)(2,1)S(1)} %slice.176), channel_id=1, source_target_pairs={{0,16},{1,17},{2,18},{3,19},{4,20},{5,21},{6,22},{7,23},{8,24},{9,... | collective-permute-start | bytes 196616 | tf_op jit(solution)/shard_map/ppermute | solution.py:218
  (6 other events, 149.1 us)

commit v4 on v3

--- a/solution.py
+++ b/solution.py
@@ -104,6 +104,14 @@
 P_TILE = 512
 
 
+def quarters(chunk, half):
+    size = half // 2
+    order = (0, 2, 1, 3) if chunk % 2 else (0, 1, 2, 3)
+    for place, quarter in enumerate(order):
+        at = place % 2 * size
+        yield place // 2, slice(at, at + size), slice(quarter * size, (quarter + 1) * size)
+
+
 def project_kernel(index_ref, blocks_ref, own_ref, other_ref, *rest):
     results, ordered = rest[:-1], rest[-1]
     chips, rows, features = blocks_ref.shape
@@ -117,9 +125,8 @@
         total = jnp.dot(ordered[:, :half], own_ref[:, lanes], preferred_element_type=F32)
         total = total + jnp.dot(ordered[:, half:], other_ref[:, lanes], preferred_element_type=F32)
         c, at = divmod(n * P_TILE, chunk)
-        lanes = slice(at, at + P_TILE)
-        results[2 * c][:, lanes] = total[:cut].astype(BF16)
-        results[2 * c + 1][:, lanes] = total[cut:].astype(BF16)
+        for to, here, where in quarters(c, cut):
+            results[2 * c + to][here, at : at + P_TILE] = total[where].astype(BF16)
 
 
 def project(index, blocks, own, other):
@@ -149,8 +156,8 @@
     hidden = gate0.shape[1]
     per_half = hidden // F_TILE
     for c in range(CHUNKS):
-        for side in range(2):
-            tokens[side * half : (side + 1) * half, c * chunk : (c + 1) * chunk] = pieces[2 * c + side][:, :chunk]
+        for side, here, where in quarters(c, half):
+            tokens[where, c * chunk : (c + 1) * chunk] = pieces[2 * c + side][here, :chunk]
 
     for j, (gate, up) in enumerate(((gate0, up0), (gate1, up1))):
         for i in range(per_half):
@@ -163,17 +170,17 @@
     first, chips = chip_ref[0], chip_ref[1]
     lane = lax.broadcasted_iota(jnp.int32, (half, pieces[0].shape[1] - chunk), 1)
     mine = (lane == first) | (lane == first + chips) | (lane == first + 2 * chips)
-    weights = [
-        jnp.sum(jnp.where(mine, ref[:, chunk:].astype(F32), 0.0), axis=1, keepdims=True) for ref in pieces[:2]
-    ]
+    weights = jnp.concatenate(
+        [jnp.sum(jnp.where(mine, ref[:, chunk:].astype(F32), 0.0), axis=1, keepdims=True) for ref in pieces[:2]], axis=0
+    )
     for n in range(CHUNKS * chunk // N_TILE):
         lanes = slice(n * N_TILE, (n + 1) * N_TILE)
         total = jnp.dot(active[:, :hidden], down0[:, lanes], preferred_element_type=F32)
         total = total + jnp.dot(active[:, hidden:], down1[:, lanes], preferred_element_type=F32)
+        total = total * weights
         c, at = divmod(n * N_TILE, chunk)
-        lanes = slice(at, at + N_TILE)
-        results[2 * c][:, lanes] = (total[:half] * weights[0]).astype(BF16)
-        results[2 * c + 1][:, lanes] = (total[half:] * weights[1]).astype(BF16)
+        for to, here, where in quarters(c, half):
+            results[2 * c + to][here, at : at + N_TILE] = total[where].astype(BF16)
 
 
 def experts(chip, pieces, gates, ups, downs):
@@ -205,9 +212,9 @@
     return bits, other
 
 
-def swap_step(step, devices):
+def swap_step(step, chunk, devices):
     orders = step_bits(devices)
-    return [(i, i ^ orders[i & 1][step]) for i in range(devices)]
+    return [(i, i ^ orders[(i + chunk) & 1][step]) for i in range(devices)]
 
 
 def reduce_slots(pieces, devices):
@@ -215,7 +222,7 @@
     kept, sent = list(pieces[::2]), list(pieces[1::2])
     for step in range(steps):
         for c in range(CHUNKS):
-            came = lax.ppermute(sent[c], "dp", swap_step(step, devices))
+            came = lax.ppermute(sent[c], "dp", swap_step(step, c, devices))
             kept[c] = kept[c].astype(F32) + came.astype(F32)
             half = kept[c].shape[0] // 2
             if step < steps - 1:
@@ -230,7 +237,7 @@
     pieces = []
     for step in reversed(range(steps)):
         for c in range(CHUNKS):
-            came = lax.ppermute(own[c], "dp", swap_step(step, devices))
+            came = lax.ppermute(own[c], "dp", swap_step(step, c, devices))
             if step == 0:
                 pieces += [own[c], came]
             else:
@@ -291,7 +298,8 @@
     mix_low = (mix - mix_hi.astype(F32) - mix_mid.astype(F32)).astype(BF16)
     extra = jnp.concatenate([mix_hi, mix_mid, mix_low], axis=1)
     extra = jnp.pad(extra, ((0, 0), (0, -extra.shape[1] % 128)))
-    normed[0] = jnp.concatenate([normed[0], extra], axis=1)
+    normed, gate_other, up_other, down_other = lax.optimization_barrier((normed, gate_other, up_other, down_other))
+    normed = [jnp.concatenate([normed[0], extra], axis=1)] + list(normed[1:])
     pieces = gather_slots(normed, devices)
     place = jnp.stack([chip, jnp.int32(chips)])
     outs = experts(place, pieces, (w_gate[0], gate_other), (w_up[0], up_other), (w_down[0], down_other))

time: 161 us -> 148 us (0.919)
  waiting for transfers between devices: 96.4 us -> 72.2 us
  starting transfers between devices: 31.1 us -> 41.7 us
    ppermute x24, waiting for transfers between devices: 86.8 us -> 62.4 us  [the longest x16 42.2 us: reduce_slots(): came = lax.ppermute(sent[c], 'dp', swap_step(step, c, devices))]
    ppermute x24, starting transfers between devices: 22 us -> 32.3 us  [the longest x16 20.9 us: reduce_slots(): came = lax.ppermute(sent[c], 'dp', swap_step(step, c, devices))]
  transfers between devices with their start and end apart: 29 -> 29, of which waited for: 19 -> 18; matrix products, arithmetic and copies ran while one was open for 1% -> 1% of each run, Pallas kernels for 8% -> 8%
where the time goes in v4:
time: 148 us
  waiting for transfers between devices  72.2 us (49%)
  starting transfers between devices  41.7 us (28%)
  Pallas kernels  30.7 us (21%)
  other arithmetic  2.21 us (1%)
    ppermute x16, waiting for transfers between devices, reduce_slots(): came = lax.ppermute(sent[c], 'dp', swap_step(step, c, devices))  42.2 us
    ppermute x16, starting transfers between devices, reduce_slots(): came = lax.ppermute(sent[c], 'dp', swap_step(step, c, devices))  20.9 us
    ppermute x8, waiting for transfers between devices, gather_slots(): came = lax.ppermute(own[c], 'dp', swap_step(step, c, devices))  20.2 us
    pallas_call x1, Pallas kernels, experts(): pl.pallas_call(expert_kernel, out_shape=[jax.ShapeDtypeStruct((half, widt...  18.2 us
    ppermute x8, starting transfers between devices, gather_slots(): came = lax.ppermute(own[c], 'dp', swap_step(step, c, devices))  11.4 us
    all_to_all x1, waiting for transfers between devices, per_device(): lax.all_to_all(attn_out, 'dp', split_axis=0, concat_axis=0, axis_index_gr...  9.85 us
    pallas_call x1, Pallas kernels, attend(): pl.pallas_call(attend_kernel, out_shape=jax.ShapeDtypeStruct((chips, rows...  9.51 us
    all_to_all x1, starting transfers between devices, per_device(): lax.all_to_all(attn_out, 'dp', split_axis=0, concat_axis=0, axis_index_gr...  8.31 us
  transfers between devices with their start and end apart: 29, of which 18 were waited for; matrix products, arithmetic and copies ran while one was open for 1% of the time, Pallas kernels for 8%

profile of v4, /device:TPU:0, one launch (start us, length us, event | category | flops | bytes accessed | tf_op | source)
XLA Modules:
  0.0 147.7 jit_solution(12022673722532967282)
XLA Ops:
  1.0 9.5 %shard_map.118 = bf16[16,16,512]{2,1,0:T(8,128)(2,1)} custom-call(s32[1]{0:T(128)} %bitcast.core_ref, s32[16]{0:T(128)} %lengths_ref.1, bf16[16,8192]{1,0:T(8,128)(2,1)} %q_ref.1, bf16[2,16,512]{2,1,0:T(8,128)(2,1)} %new_ref.1, bf16[2,16,128,512]{3,2,1,0:T(8,128)(2,1)} %cache_ref.1), custom_call_target="tpu_custom_call" | custom-call | flops 67108864 | bytes 4194304 | tf_op jit(solution)/shard_map/pallas_call | solution.py:81
  10.5 8.3 %all-to-all-start = ((bf16[16,16,512]{2,1,0:T(8,128)(2,1)}), bf16[16,16,512]{2,1,0:T(8,128)(2,1)S(1)}, u32[]{:S(2)}, u32[]{:S(2)}) async-start(bf16[16,16,512]{2,1,0:T(8,128)(2,1)} %shard_map.118), calls=%async_computation | async-start | bytes 524288 | tf_op jit(solution)/shard_map/all_to_all | solution.py:278
  19.1 9.8 %all-to-all-done.blocks_ref = bf16[16,16,512]{2,1,0:T(8,128)(2,1)S(1)} async-done(((bf16[16,16,512]{2,1,0:T(8,128)(2,1)}), bf16[16,16,512]{2,1,0:T(8,128)(2,1)S(1)}, u32[]{:S(2)}, u32[]{:S(2)}) %all-to-all-start) | async-done | bytes 262176 | tf_op jit(solution)/shard_map/all_to_all | solution.py:278
  28.9 3.0 %shard_map.119 = (bf16[128,2048]{1,0:T(8,128)(2,1)S(1)}, bf16[128,2048]{1,0:T(8,128)(2,1)S(1)}, bf16[128,2048]{1,0:T(8,128)(2,1)S(1)}, bf16[128,2048]{1,0:T(8,128)(2,1)S(1)}) custom-call(s32[16]{0:T(128)S(1)} %add_xor_fusion.index_ref, bf16[16,16,512]{2,1,0:T(8,128)(2,1)S(1)} %all-to-all-done.blocks_ref, bf16[256,4096]{1,0:T(8,128)(2,1)S(1)} %copy-done, ...), custom_call_target="tpu_custom_call" | custom-call | flops 1073741824 | bytes 4194304 | tf_op jit(solution)/shard_map/pallas_call | solution.py:136
  33.7 11.1 %collective-permute-done.1 = bf16[128,2048]{1,0:T(8,128)(2,1)S(1)} collective-permute-done((bf16[128,2048]{1,0:T(8,128)(2,1)S(1)}, bf16[128,2048]{1,0:T(8,128)(2,1)S(1)}, u32[]{:S(2)}, u32[]{:S(2)}) %collective-permute-start.1) | collective-permute-done | bytes 524320 | tf_op jit(solution)/shard_map/ppermute | solution.py:225
  44.9 3.1 %collective-permute-start.2 = (bf16[64,2048]{1,0:T(8,128)(2,1)S(1)}, bf16[64,2048]{1,0:T(8,128)(2,1)S(1)}, u32[]{:S(2)}, u32[]{:S(2)}) collective-permute-start(bf16[64,2048]{1,0:T(8,128)(2,1)S(1)} %slice.171), channel_id=1, source_target_pairs={{0,4},{1,3},{2,6},{3,1},{4,0},{5,7},{6,2},{7,5},{8,12},{9,11},{10,... | collective-permute-start | bytes 786440 | tf_op jit(solution)/shard_map/ppermute | solution.py:225
  48.8 3.6 %collective-permute-done.2 = bf16[64,2048]{1,0:T(8,128)(2,1)S(1)} collective-permute-done((bf16[64,2048]{1,0:T(8,128)(2,1)S(1)}, bf16[64,2048]{1,0:T(8,128)(2,1)S(1)}, u32[]{:S(2)}, u32[]{:S(2)}) %collective-permute-start.2) | collective-permute-done | bytes 262176 | tf_op jit(solution)/shard_map/ppermute | solution.py:225
  52.4 2.3 %collective-permute-start.3 = (bf16[32,2048]{1,0:T(8,128)(2,1)S(1)}, bf16[32,2048]{1,0:T(8,128)(2,1)S(1)}, u32[]{:S(2)}, u32[]{:S(2)}) collective-permute-start(bf16[32,2048]{1,0:T(8,128)(2,1)S(1)} %slice.175), channel_id=1, source_target_pairs={{0,8},{1,9},{2,10},{3,11},{4,12},{5,13},{6,14},{7,15},{8,0},{9,1},... | collective-permute-start | bytes 393224 | tf_op jit(solution)/shard_map/ppermute | solution.py:225
  55.0 3.4 %collective-permute-done.3 = bf16[32,2048]{1,0:T(8,128)(2,1)S(1)} collective-permute-done((bf16[32,2048]{1,0:T(8,128)(2,1)S(1)}, bf16[32,2048]{1,0:T(8,128)(2,1)S(1)}, u32[]{:S(2)}, u32[]{:S(2)}) %collective-permute-start.3) | collective-permute-done | bytes 131104 | tf_op jit(solution)/shard_map/ppermute | solution.py:225
  59.9 1.6 %collective-permute-start.8 = (bf16[16,2048]{1,0:T(8,128)(2,1)S(1)}, bf16[16,2048]{1,0:T(8,128)(2,1)S(1)}, u32[]{:S(2)}, u32[]{:S(2)}) collective-permute-start(bf16[16,2048]{1,0:T(8,128)(2,1)S(1)} %slice.178), channel_id=1, source_target_pairs={{0,16},{1,17},{2,18},{3,19},{4,20},{5,21},{6,22},{7,23},{8,24},{9,... | collective-permute-start | bytes 196616 | tf_op jit(solution)/shard_map/ppermute | solution.py:225
  61.6 2.9 %collective-permute-done.4 = bf16[16,2048]{1,0:T(8,128)(2,1)S(1)} collective-permute-done((bf16[16,2048]{1,0:T(8,128)(2,1)S(1)}, bf16[16,2048]{1,0:T(8,128)(2,1)S(1)}, u32[]{:S(2)}, u32[]{:S(2)}) %collective-permute-start.4) | collective-permute-done | bytes 65568 | tf_op jit(solution)/shard_map/ppermute | solution.py:225
  64.5 3.5 %collective-permute-done.8 = bf16[16,2048]{1,0:T(8,128)(2,1)S(1)} collective-permute-done((bf16[16,2048]{1,0:T(8,128)(2,1)S(1)}, bf16[16,2048]{1,0:T(8,128)(2,1)S(1)}, u32[]{:S(2)}, u32[]{:S(2)}) %collective-permute-start.8) | collective-permute-done | bytes 65568 | tf_op jit(solution)/shard_map/ppermute | solution.py:225
  68.4 3.0 %collective-permute-start.12 = (bf16[16,2176]{1,0:T(8,128)(2,1)S(1)}, bf16[16,2176]{1,0:T(8,128)(2,1)S(1)}, u32[]{:S(2)}, u32[]{:S(2)}) collective-permute-start(bf16[16,2176]{1,0:T(8,128)(2,1)S(1)} %pad_maximum_fusion.6), channel_id=1, source_target_pairs={{0,16},{1,17},{2,18},{3,19},{4,20},{5,21},{6,22},{7,23},{8,24},{9,... | collective-permute-start | bytes 208904 | tf_op jit(solution)/shard_map/ppermute | solution.py:240
  71.4 2.7 %collective-permute-done.16 = bf16[16,2048]{1,0:T(8,128)(2,1)S(1)} collective-permute-done((bf16[16,2048]{1,0:T(8,128)(2,1)S(1)}, bf16[16,2048]{1,0:T(8,128)(2,1)S(1)}, u32[]{:S(2)}, u32[]{:S(2)}) %collective-permute-start.16) | collective-permute-done | bytes 65568 | tf_op jit(solution)/shard_map/ppermute | solution.py:240
  74.9 2.1 %collective-permute-start.13 = (bf16[32,2176]{1,0:T(8,128)(2,1)S(1)}, bf16[32,2176]{1,0:T(8,128)(2,1)S(1)}, u32[]{:S(2)}, u32[]{:S(2)}) collective-permute-start(bf16[32,2176]{1,0:T(8,128)(2,1)S(1)} %pad_maximum_fusion.3), channel_id=1, source_target_pairs={{0,8},{1,9},{2,10},{3,11},{4,12},{5,13},{6,14},{7,15},{8,0},{9,1},... | collective-permute-start | bytes 417800 | tf_op jit(solution)/shard_map/ppermute | solution.py:240
  77.0 3.6 %collective-permute-done.13 = bf16[32,2176]{1,0:T(8,128)(2,1)S(1)} collective-permute-done((bf16[32,2176]{1,0:T(8,128)(2,1)S(1)}, bf16[32,2176]{1,0:T(8,128)(2,1)S(1)}, u32[]{:S(2)}, u32[]{:S(2)}) %collective-permute-start.13) | collective-permute-done | bytes 139296 | tf_op jit(solution)/shard_map/ppermute | solution.py:240
  81.6 1.6 %collective-permute-start.18 = (bf16[64,2048]{1,0:T(8,128)(2,1)S(1)}, bf16[64,2048]{1,0:T(8,128)(2,1)S(1)}, u32[]{:S(2)}, u32[]{:S(2)}) collective-permute-start(bf16[64,2048]{1,0:T(8,128)(2,1)S(1)} %pad_maximum_fusion.2), channel_id=1, source_target_pairs={{0,2},{1,5},{2,0},{3,7},{4,6},{5,1},{6,4},{7,3},{8,10},{9,13},{10,... | collective-permute-start | bytes 786440 | tf_op jit(solution)/shard_map/ppermute | solution.py:240
  83.2 5.9 %collective-permute-done.14 = bf16[64,2176]{1,0:T(8,128)(2,1)S(1)} collective-permute-done((bf16[64,2176]{1,0:T(8,128)(2,1)S(1)}, bf16[64,2176]{1,0:T(8,128)(2,1)S(1)}, u32[]{:S(2)}, u32[]{:S(2)}) %collective-permute-start.14) | collective-permute-done | bytes 278560 | tf_op jit(solution)/shard_map/ppermute | solution.py:240
  89.2 1.7 %collective-permute-start.15 = (bf16[128,2176]{1,0:T(8,128)(2,1)S(1)}, bf16[128,2176]{1,0:T(8,128)(2,1)S(1)}, u32[]{:S(2)}, u32[]{:S(2)}) collective-permute-start(bf16[128,2176]{1,0:T(8,128)(2,1)S(1)} %pad_maximum_fusion.refs_0_), channel_id=1, source_target_pairs={{0,2},{1,5},{2,0},{3,7},{4,6},{5,1},{6,4},{7,3},{8,10},{9,13},{10,... | collective-permute-start | bytes 1671176 | tf_op jit(solution)/shard_map/ppermute | solution.py:240
  91.0 1.5 %collective-permute-start.19 = (bf16[128,2048]{1,0:T(8,128)(2,1)S(1)}, bf16[128,2048]{1,0:T(8,128)(2,1)S(1)}, u32[]{:S(2)}, u32[]{:S(2)}) collective-permute-start(bf16[128,2048]{1,0:T(8,128)(2,1)S(1)} %constant_dynamic-update-slice_fusion.refs_2_), channel_id=1, source_target_pairs={{0,4},{1,3},{2,6},{3,1},{4,0},{5,7},{6,2},{7,5},{8,12},{9,11},{10,... | collective-permute-start | bytes 1572872 | tf_op jit(solution)/shard_map/ppermute | solution.py:240
  92.5 7.7 %collective-permute-done.19.refs_3_ = bf16[128,2048]{1,0:T(8,128)(2,1)S(1)} collective-permute-done((bf16[128,2048]{1,0:T(8,128)(2,1)S(1)}, bf16[128,2048]{1,0:T(8,128)(2,1)S(1)}, u32[]{:S(2)}, u32[]{:S(2)}) %collective-permute-start.19) | collective-permute-done | bytes 524320 | tf_op jit(solution)/shard_map/ppermute | solution.py:240
  100.3 18.2 %shard_map.120 = (bf16[128,2048]{1,0:T(8,128)(2,1)S(1)}, bf16[128,2048]{1,0:T(8,128)(2,1)S(1)}, bf16[128,2048]{1,0:T(8,128)(2,1)S(1)}, bf16[128,2048]{1,0:T(8,128)(2,1)S(1)}) custom-call(s32[2]{0:T(128)S(1)} %pad_add_fusion.chip_ref, bf16[128,2176]{1,0:T(8,128)(2,1)S(1)} %pad_maximum_fusion.refs_0_, bf16[128,2176]{1,0:T(8,128)(2,1)S(1)} %collective-permute-done.15.refs_1_, ...), custom_call_target="tpu_custom_call" | custom-call | flops 9663676416 | bytes 37748736 | tf_op jit(solution)/shard_map/pallas_call | solution.py:190
  120.2 7.5 %collective-permute-done.20 = bf16[128,2048]{1,0:T(8,128)(2,1)S(1)} collective-permute-done((bf16[128,2048]{1,0:T(8,128)(2,1)S(1)}, bf16[128,2048]{1,0:T(8,128)(2,1)S(1)}, u32[]{:S(2)}, u32[]{:S(2)}) %collective-permute-start.20) | collective-permute-done | bytes 524320 | tf_op jit(solution)/shard_map/ppermute | solution.py:225
  127.8 1.5 %collective-permute-start.21 = (bf16[64,2048]{1,0:T(8,128)(2,1)S(1)}, bf16[64,2048]{1,0:T(8,128)(2,1)S(1)}, u32[]{:S(2)}, u32[]{:S(2)}) collective-permute-start(bf16[64,2048]{1,0:T(8,128)(2,1)S(1)} %slice.169), channel_id=1, source_target_pairs={{0,4},{1,3},{2,6},{3,1},{4,0},{5,7},{6,2},{7,5},{8,12},{9,11},{10,... | collective-permute-start | bytes 786440 | tf_op jit(solution)/shard_map/ppermute | solution.py:225
  130.0 4.3 %collective-permute-done.21 = bf16[64,2048]{1,0:T(8,128)(2,1)S(1)} collective-permute-done((bf16[64,2048]{1,0:T(8,128)(2,1)S(1)}, bf16[64,2048]{1,0:T(8,128)(2,1)S(1)}, u32[]{:S(2)}, u32[]{:S(2)}) %collective-permute-start.21) | collective-permute-done | bytes 262176 | tf_op jit(solution)/shard_map/ppermute | solution.py:225
  134.4 1.5 %collective-permute-start.22 = (bf16[32,2048]{1,0:T(8,128)(2,1)S(1)}, bf16[32,2048]{1,0:T(8,128)(2,1)S(1)}, u32[]{:S(2)}, u32[]{:S(2)}) collective-permute-start(bf16[32,2048]{1,0:T(8,128)(2,1)S(1)} %slice.173), channel_id=1, source_target_pairs={{0,8},{1,9},{2,10},{3,11},{4,12},{5,13},{6,14},{7,15},{8,0},{9,1},... | collective-permute-start | bytes 393224 | tf_op jit(solution)/shard_map/ppermute | solution.py:225
  136.1 1.5 %collective-permute-start.26 = (bf16[32,2048]{1,0:T(8,128)(2,1)S(1)}, bf16[32,2048]{1,0:T(8,128)(2,1)S(1)}, u32[]{:S(2)}, u32[]{:S(2)}) collective-permute-start(bf16[32,2048]{1,0:T(8,128)(2,1)S(1)} %slice.172), channel_id=1, source_target_pairs={{0,8},{1,9},{2,10},{3,11},{4,12},{5,13},{6,14},{7,15},{8,0},{9,1},... | collective-permute-start | bytes 393224 | tf_op jit(solution)/shard_map/ppermute | solution.py:225
  137.5 1.8 %collective-permute-done.22 = bf16[32,2048]{1,0:T(8,128)(2,1)S(1)} collective-permute-done((bf16[32,2048]{1,0:T(8,128)(2,1)S(1)}, bf16[32,2048]{1,0:T(8,128)(2,1)S(1)}, u32[]{:S(2)}, u32[]{:S(2)}) %collective-permute-start.22) | collective-permute-done | bytes 131104 | tf_op jit(solution)/shard_map/ppermute | solution.py:225
  139.4 2.3 %collective-permute-start.23 = (bf16[16,2048]{1,0:T(8,128)(2,1)S(1)}, bf16[16,2048]{1,0:T(8,128)(2,1)S(1)}, u32[]{:S(2)}, u32[]{:S(2)}) collective-permute-start(bf16[16,2048]{1,0:T(8,128)(2,1)S(1)} %slice.177), channel_id=1, source_target_pairs={{0,16},{1,17},{2,18},{3,19},{4,20},{5,21},{6,22},{7,23},{8,24},{9,... | collective-permute-start | bytes 196616 | tf_op jit(solution)/shard_map/ppermute | solution.py:225
  141.7 1.4 collective-permute-start.27
  143.1 1.6 %collective-permute-done.23 = bf16[16,2048]{1,0:T(8,128)(2,1)S(1)} collective-permute-done((bf16[16,2048]{1,0:T(8,128)(2,1)S(1)}, bf16[16,2048]{1,0:T(8,128)(2,1)S(1)}, u32[]{:S(2)}, u32[]{:S(2)}) %collective-permute-start.23) | collective-permute-done | bytes 65568 | tf_op jit(solution)/shard_map/ppermute | solution.py:225
  144.7 2.3 %collective-permute-done.27 = bf16[16,2048]{1,0:T(8,128)(2,1)S(1)} collective-permute-done((bf16[16,2048]{1,0:T(8,128)(2,1)S(1)}, bf16[16,2048]{1,0:T(8,128)(2,1)S(1)}, u32[]{:S(2)}, u32[]{:S(2)}) %collective-permute-start.27) | collective-permute-done | bytes 65568 | tf_op jit(solution)/shard_map/ppermute | solution.py:225
  (97 shorter events, 11.6 us)
Async XLA Ops:
  0.0 28.9 %collective-permute-start = (bf16[256,4096]{1,0:T(8,128)(2,1)}, bf16[256,4096]{1,0:T(8,128)(2,1)}, u32[]{:S(2)}, u32[]{:S(2)}) collective-permute-start(bf16[256,4096]{1,0:T(8,128)(2,1)} %own_ref.1), channel_id=1, source_target_pairs={{0,1},{1,0},{2,3},{3,2},{4,5},{5,4},{6,7},{7,6},{8,9},{9,8},{10,11... | collective-permute-start | bytes 6291464 | tf_op jit(solution)/shard_map/ppermute | solution.py:272
  0.5 67.8 %collective-permute-start.9 = (bf16[4096,768]{1,0:T(8,128)(2,1)}, bf16[4096,768]{1,0:T(8,128)(2,1)}, u32[]{:S(2)}, u32[]{:S(2)}) collective-permute-start(bf16[4096,768]{1,0:T(8,128)(2,1)} %bitcast.5), channel_id=1, source_target_pairs={{0,1},{1,0},{2,3},{3,2},{4,5},{5,4},{6,7},{7,6},{8,9},{9,8},{10,11... | collective-permute-start | bytes 18874376 | tf_op jit(solution)/shard_map/ppermute | solution.py:273
  0.5 67.8 %collective-permute-start.10 = (bf16[4096,768]{1,0:T(8,128)(2,1)}, bf16[4096,768]{1,0:T(8,128)(2,1)}, u32[]{:S(2)}, u32[]{:S(2)}) collective-permute-start(bf16[4096,768]{1,0:T(8,128)(2,1)} %bitcast.9), channel_id=1, source_target_pairs={{0,1},{1,0},{2,3},{3,2},{4,5},{5,4},{6,7},{7,6},{8,9},{9,8},{10,11... | collective-permute-start | bytes 18874376 | tf_op jit(solution)/shard_map/ppermute | solution.py:274
  1.0 67.3 %collective-permute-start.11 = (bf16[768,4096]{1,0:T(8,128)(2,1)}, bf16[768,4096]{1,0:T(8,128)(2,1)}, u32[]{:S(2)}, u32[]{:S(2)}) collective-permute-start(bf16[768,4096]{1,0:T(8,128)(2,1)} %bitcast.13), channel_id=1, source_target_pairs={{0,1},{1,0},{2,3},{3,2},{4,5},{5,4},{6,7},{7,6},{8,9},{9,8},{10,11... | collective-permute-start | bytes 18874376 | tf_op jit(solution)/shard_map/ppermute | solution.py:275
  10.5 18.4 %all-to-all-start = ((bf16[16,16,512]{2,1,0:T(8,128)(2,1)}), bf16[16,16,512]{2,1,0:T(8,128)(2,1)S(1)}, u32[]{:S(2)}, u32[]{:S(2)}) async-start(bf16[16,16,512]{2,1,0:T(8,128)(2,1)} %shard_map.118), calls=%async_computation | async-start | bytes 524288 | tf_op jit(solution)/shard_map/all_to_all | solution.py:278
  28.9 71.3 %slice-start.2 = ((s8[6291456]{0:T(1024)(128)(4,1)}), s8[4194304]{0:T(1024)(128)(4,1)S(1)}, s32[]{:S(2)}) async-start(s8[6291456]{0:T(1024)(128)(4,1)} %bitcast.10), calls=%async_computation.3 | async-start | bytes 8388608
  31.9 12.8 %collective-permute-start.1 = (bf16[128,2048]{1,0:T(8,128)(2,1)S(1)}, bf16[128,2048]{1,0:T(8,128)(2,1)S(1)}, u32[]{:S(2)}, u32[]{:S(2)}) collective-permute-start(bf16[128,2048]{1,0:T(8,128)(2,1)S(1)} %get-tuple-element.19), channel_id=1, source_target_pairs={{0,2},{1,5},{2,0},{3,7},{4,6},{5,1},{6,4},{7,3},{8,10},{9,13},{10,... | collective-permute-start | bytes 1572872 | tf_op jit(solution)/shard_map/ppermute | solution.py:225
  32.9 15.1 %collective-permute-start.5 = (bf16[128,2048]{1,0:T(8,128)(2,1)S(1)}, bf16[128,2048]{1,0:T(8,128)(2,1)S(1)}, u32[]{:S(2)}, u32[]{:S(2)}) collective-permute-start(bf16[128,2048]{1,0:T(8,128)(2,1)S(1)} %get-tuple-element.21), channel_id=1, source_target_pairs={{0,4},{1,3},{2,6},{3,1},{4,0},{5,7},{6,2},{7,5},{8,12},{9,11},{10,... | collective-permute-start | bytes 1572872 | tf_op jit(solution)/shard_map/ppermute | solution.py:225
  44.8 55.4 %slice-start = ((s8[6291456]{0:T(1024)(128)(4,1)}), s8[4194304]{0:T(1024)(128)(4,1)S(1)}, s32[]{:S(2)}) async-start(s8[6291456]{0:T(1024)(128)(4,1)} %bitcast.6), calls=%async_computation.1 | async-start | bytes 8388608
  44.9 7.4 %collective-permute-start.2 = (bf16[64,2048]{1,0:T(8,128)(2,1)S(1)}, bf16[64,2048]{1,0:T(8,128)(2,1)S(1)}, u32[]{:S(2)}, u32[]{:S(2)}) collective-permute-start(bf16[64,2048]{1,0:T(8,128)(2,1)S(1)} %slice.171), channel_id=1, source_target_pairs={{0,4},{1,3},{2,6},{3,1},{4,0},{5,7},{6,2},{7,5},{8,12},{9,11},{10,... | collective-permute-start | bytes 786440 | tf_op jit(solution)/shard_map/ppermute | solution.py:225
  48.1 52.1 %slice-start.3 = ((s8[6291456]{0:T(1024)(128)(4,1)}), s8[2097152]{0:T(1024)(128)(4,1)S(1)}, s32[]{:S(2)}) async-start(s8[6291456]{0:T(1024)(128)(4,1)} %bitcast.10), calls=%async_computation.4 | async-start | bytes 4194304
  48.2 6.5 %collective-permute-start.6 = (bf16[64,2048]{1,0:T(8,128)(2,1)S(1)}, bf16[64,2048]{1,0:T(8,128)(2,1)S(1)}, u32[]{:S(2)}, u32[]{:S(2)}) collective-permute-start(bf16[64,2048]{1,0:T(8,128)(2,1)S(1)} %slice.170), channel_id=1, source_target_pairs={{0,2},{1,5},{2,0},{3,7},{4,6},{5,1},{6,4},{7,3},{8,10},{9,13},{10,... | collective-permute-start | bytes 786440 | tf_op jit(solution)/shard_map/ppermute | solution.py:225
  52.4 5.9 %collective-permute-start.3 = (bf16[32,2048]{1,0:T(8,128)(2,1)S(1)}, bf16[32,2048]{1,0:T(8,128)(2,1)S(1)}, u32[]{:S(2)}, u32[]{:S(2)}) collective-permute-start(bf16[32,2048]{1,0:T(8,128)(2,1)S(1)} %slice.175), channel_id=1, source_target_pairs={{0,8},{1,9},{2,10},{3,11},{4,12},{5,13},{6,14},{7,15},{8,0},{9,1},... | collective-permute-start | bytes 393224 | tf_op jit(solution)/shard_map/ppermute | solution.py:225
  54.8 5.0 %collective-permute-start.7 = (bf16[32,2048]{1,0:T(8,128)(2,1)S(1)}, bf16[32,2048]{1,0:T(8,128)(2,1)S(1)}, u32[]{:S(2)}, u32[]{:S(2)}) collective-permute-start(bf16[32,2048]{1,0:T(8,128)(2,1)S(1)} %slice.174), channel_id=1, source_target_pairs={{0,8},{1,9},{2,10},{3,11},{4,12},{5,13},{6,14},{7,15},{8,0},{9,1},... | collective-permute-start | bytes 393224 | tf_op jit(solution)/shard_map/ppermute | solution.py:225
  58.4 6.0 %collective-permute-start.4 = (bf16[16,2048]{1,0:T(8,128)(2,1)S(1)}, bf16[16,2048]{1,0:T(8,128)(2,1)S(1)}, u32[]{:S(2)}, u32[]{:S(2)}) collective-permute-start(bf16[16,2048]{1,0:T(8,128)(2,1)S(1)} %slice.179), channel_id=1, source_target_pairs={{0,16},{1,17},{2,18},{3,19},{4,20},{5,21},{6,22},{7,23},{8,24},{9,... | collective-permute-start | bytes 196616 | tf_op jit(solution)/shard_map/ppermute | solution.py:225
  59.9 8.1 %collective-permute-start.8 = (bf16[16,2048]{1,0:T(8,128)(2,1)S(1)}, bf16[16,2048]{1,0:T(8,128)(2,1)S(1)}, u32[]{:S(2)}, u32[]{:S(2)}) collective-permute-start(bf16[16,2048]{1,0:T(8,128)(2,1)S(1)} %slice.178), channel_id=1, source_target_pairs={{0,16},{1,17},{2,18},{3,19},{4,20},{5,21},{6,22},{7,23},{8,24},{9,... | collective-permute-start | bytes 196616 | tf_op jit(solution)/shard_map/ppermute | solution.py:225
  68.3 5.8 %collective-permute-start.16 = (bf16[16,2048]{1,0:T(8,128)(2,1)S(1)}, bf16[16,2048]{1,0:T(8,128)(2,1)S(1)}, u32[]{:S(2)}, u32[]{:S(2)}) collective-permute-start(bf16[16,2048]{1,0:T(8,128)(2,1)S(1)} %get-tuple-element.23), channel_id=1, source_target_pairs={{0,16},{1,17},{2,18},{3,19},{4,20},{5,21},{6,22},{7,23},{8,24},{9,... | collective-permute-start | bytes 196616 | tf_op jit(solution)/shard_map/ppermute | solution.py:240
  68.4 6.5 %collective-permute-start.12 = (bf16[16,2176]{1,0:T(8,128)(2,1)S(1)}, bf16[16,2176]{1,0:T(8,128)(2,1)S(1)}, u32[]{:S(2)}, u32[]{:S(2)}) collective-permute-start(bf16[16,2176]{1,0:T(8,128)(2,1)S(1)} %pad_maximum_fusion.6), channel_id=1, source_target_pairs={{0,16},{1,17},{2,18},{3,19},{4,20},{5,21},{6,22},{7,23},{8,24},{9,... | collective-permute-start | bytes 208904 | tf_op jit(solution)/shard_map/ppermute | solution.py:240
  74.1 7.5 %collective-permute-start.17 = (bf16[32,2048]{1,0:T(8,128)(2,1)S(1)}, bf16[32,2048]{1,0:T(8,128)(2,1)S(1)}, u32[]{:S(2)}, u32[]{:S(2)}) collective-permute-start(bf16[32,2048]{1,0:T(8,128)(2,1)S(1)} %pad_maximum_fusion.4), channel_id=1, source_target_pairs={{0,8},{1,9},{2,10},{3,11},{4,12},{5,13},{6,14},{7,15},{8,0},{9,1},... | collective-permute-start | bytes 393224 | tf_op jit(solution)/shard_map/ppermute | solution.py:240
  74.9 5.8 %collective-permute-start.13 = (bf16[32,2176]{1,0:T(8,128)(2,1)S(1)}, bf16[32,2176]{1,0:T(8,128)(2,1)S(1)}, u32[]{:S(2)}, u32[]{:S(2)}) collective-permute-start(bf16[32,2176]{1,0:T(8,128)(2,1)S(1)} %pad_maximum_fusion.3), channel_id=1, source_target_pairs={{0,8},{1,9},{2,10},{3,11},{4,12},{5,13},{6,14},{7,15},{8,0},{9,1},... | collective-permute-start | bytes 417800 | tf_op jit(solution)/shard_map/ppermute | solution.py:240
  80.7 8.4 %collective-permute-start.14 = (bf16[64,2176]{1,0:T(8,128)(2,1)S(1)}, bf16[64,2176]{1,0:T(8,128)(2,1)S(1)}, u32[]{:S(2)}, u32[]{:S(2)}) collective-permute-start(bf16[64,2176]{1,0:T(8,128)(2,1)S(1)} %pad_maximum_fusion.1), channel_id=1, source_target_pairs={{0,4},{1,3},{2,6},{3,1},{4,0},{5,7},{6,2},{7,5},{8,12},{9,11},{10,... | collective-permute-start | bytes 835592 | tf_op jit(solution)/shard_map/ppermute | solution.py:240
  81.6 9.3 %collective-permute-start.18 = (bf16[64,2048]{1,0:T(8,128)(2,1)S(1)}, bf16[64,2048]{1,0:T(8,128)(2,1)S(1)}, u32[]{:S(2)}, u32[]{:S(2)}) collective-permute-start(bf16[64,2048]{1,0:T(8,128)(2,1)S(1)} %pad_maximum_fusion.2), channel_id=1, source_target_pairs={{0,2},{1,5},{2,0},{3,7},{4,6},{5,1},{6,4},{7,3},{8,10},{9,13},{10,... | collective-permute-start | bytes 786440 | tf_op jit(solution)/shard_map/ppermute | solution.py:240
  89.2 11.0 %collective-permute-start.15 = (bf16[128,2176]{1,0:T(8,128)(2,1)S(1)}, bf16[128,2176]{1,0:T(8,128)(2,1)S(1)}, u32[]{:S(2)}, u32[]{:S(2)}) collective-permute-start(bf16[128,2176]{1,0:T(8,128)(2,1)S(1)} %pad_maximum_fusion.refs_0_), channel_id=1, source_target_pairs={{0,2},{1,5},{2,0},{3,7},{4,6},{5,1},{6,4},{7,3},{8,10},{9,13},{10,... | collective-permute-start | bytes 1671176 | tf_op jit(solution)/shard_map/ppermute | solution.py:240
  91.0 9.2 %collective-permute-start.19 = (bf16[128,2048]{1,0:T(8,128)(2,1)S(1)}, bf16[128,2048]{1,0:T(8,128)(2,1)S(1)}, u32[]{:S(2)}, u32[]{:S(2)}) collective-permute-start(bf16[128,2048]{1,0:T(8,128)(2,1)S(1)} %constant_dynamic-update-slice_fusion.refs_2_), channel_id=1, source_target_pairs={{0,4},{1,3},{2,6},{3,1},{4,0},{5,7},{6,2},{7,5},{8,12},{9,11},{10,... | collective-permute-start | bytes 1572872 | tf_op jit(solution)/shard_map/ppermute | solution.py:240
  118.4 9.2 %collective-permute-start.20 = (bf16[128,2048]{1,0:T(8,128)(2,1)S(1)}, bf16[128,2048]{1,0:T(8,128)(2,1)S(1)}, u32[]{:S(2)}, u32[]{:S(2)}) collective-permute-start(bf16[128,2048]{1,0:T(8,128)(2,1)S(1)} %get-tuple-element.28), channel_id=1, source_target_pairs={{0,2},{1,5},{2,0},{3,7},{4,6},{5,1},{6,4},{7,3},{8,10},{9,13},{10,... | collective-permute-start | bytes 1572872 | tf_op jit(solution)/shard_map/ppermute | solution.py:225
  119.1 10.3 %collective-permute-start.24 = (bf16[128,2048]{1,0:T(8,128)(2,1)S(1)}, bf16[128,2048]{1,0:T(8,128)(2,1)S(1)}, u32[]{:S(2)}, u32[]{:S(2)}) collective-permute-start(bf16[128,2048]{1,0:T(8,128)(2,1)S(1)} %get-tuple-element.30), channel_id=1, source_target_pairs={{0,4},{1,3},{2,6},{3,1},{4,0},{5,7},{6,2},{7,5},{8,12},{9,11},{10,... | collective-permute-start | bytes 1572872 | tf_op jit(solution)/shard_map/ppermute | solution.py:225
  127.8 6.4 %collective-permute-start.21 = (bf16[64,2048]{1,0:T(8,128)(2,1)S(1)}, bf16[64,2048]{1,0:T(8,128)(2,1)S(1)}, u32[]{:S(2)}, u32[]{:S(2)}) collective-permute-start(bf16[64,2048]{1,0:T(8,128)(2,1)S(1)} %slice.169), channel_id=1, source_target_pairs={{0,4},{1,3},{2,6},{3,1},{4,0},{5,7},{6,2},{7,5},{8,12},{9,11},{10,... | collective-permute-start | bytes 786440 | tf_op jit(solution)/shard_map/ppermute | solution.py:225
  129.5 6.4 %collective-permute-start.25 = (bf16[64,2048]{1,0:T(8,128)(2,1)S(1)}, bf16[64,2048]{1,0:T(8,128)(2,1)S(1)}, u32[]{:S(2)}, u32[]{:S(2)}) collective-permute-start(bf16[64,2048]{1,0:T(8,128)(2,1)S(1)} %slice.168), channel_id=1, source_target_pairs={{0,2},{1,5},{2,0},{3,7},{4,6},{5,1},{6,4},{7,3},{8,10},{9,13},{10,... | collective-permute-start | bytes 786440 | tf_op jit(solution)/shard_map/ppermute | solution.py:225
  134.4 5.0 %collective-permute-start.22 = (bf16[32,2048]{1,0:T(8,128)(2,1)S(1)}, bf16[32,2048]{1,0:T(8,128)(2,1)S(1)}, u32[]{:S(2)}, u32[]{:S(2)}) collective-permute-start(bf16[32,2048]{1,0:T(8,128)(2,1)S(1)} %slice.173), channel_id=1, source_target_pairs={{0,8},{1,9},{2,10},{3,11},{4,12},{5,13},{6,14},{7,15},{8,0},{9,1},... | collective-permute-start | bytes 393224 | tf_op jit(solution)/shard_map/ppermute | solution.py:225
  136.1 5.6 %collective-permute-start.26 = (bf16[32,2048]{1,0:T(8,128)(2,1)S(1)}, bf16[32,2048]{1,0:T(8,128)(2,1)S(1)}, u32[]{:S(2)}, u32[]{:S(2)}) collective-permute-start(bf16[32,2048]{1,0:T(8,128)(2,1)S(1)} %slice.172), channel_id=1, source_target_pairs={{0,8},{1,9},{2,10},{3,11},{4,12},{5,13},{6,14},{7,15},{8,0},{9,1},... | collective-permute-start | bytes 393224 | tf_op jit(solution)/shard_map/ppermute | solution.py:225
  139.4 5.2 %collective-permute-start.23 = (bf16[16,2048]{1,0:T(8,128)(2,1)S(1)}, bf16[16,2048]{1,0:T(8,128)(2,1)S(1)}, u32[]{:S(2)}, u32[]{:S(2)}) collective-permute-start(bf16[16,2048]{1,0:T(8,128)(2,1)S(1)} %slice.177), channel_id=1, source_target_pairs={{0,16},{1,17},{2,18},{3,19},{4,20},{5,21},{6,22},{7,23},{8,24},{9,... | collective-permute-start | bytes 196616 | tf_op jit(solution)/shard_map/ppermute | solution.py:225
  141.7 5.2 %collective-permute-start.27 = (bf16[16,2048]{1,0:T(8,128)(2,1)S(1)}, bf16[16,2048]{1,0:T(8,128)(2,1)S(1)}, u32[]{:S(2)}, u32[]{:S(2)}) collective-permute-start(bf16[16,2048]{1,0:T(8,128)(2,1)S(1)} %slice.176), channel_id=1, source_target_pairs={{0,16},{1,17},{2,18},{3,19},{4,20},{5,21},{6,22},{7,23},{8,24},{9,... | collective-permute-start | bytes 196616 | tf_op jit(solution)/shard_map/ppermute | solution.py:225
  (6 other events, 145.1 us)

commit v5 on v4

v5 whole, which is shorter than its diff:
```python
import functools
import math

import jax
import jax.numpy as jnp
from jax import lax
from jax.experimental import pallas as pl
from jax.experimental.pallas import tpu as pltpu
from jax.sharding import PartitionSpec as P

H = 64
KVH = 4
DH = 128
TOP = 8
F32 = jnp.float32
BF16 = jnp.bfloat16


CHUNKS = 2


GROUP = 4


def attend_kernel(core_ref, lengths_ref, q_ref, new_ref, cache_ref, out_ref, cache, q_rows, out_rows, new_rows, sems):
    rows = q_ref.shape[0]
    heads = q_ref.shape[1] // DH
    per_group = heads // KVH
    span, width = cache_ref.shape[2:]
    scale = 1.0 / math.sqrt(DH)

    def copy(side, at):
        part = pl.ds(at * GROUP, GROUP)
        return pltpu.make_async_copy(cache_ref.at[side, part], cache.at[side, part], sems.at[side, at])

    for at in range(rows // GROUP):
        copy(0, at).start()
        copy(1, at).start()
    new_rows[...] = new_ref[...].astype(F32)
    for h in range(heads):
        q_rows[h * rows : (h + 1) * rows, :] = q_ref[:, h * DH : (h + 1) * DH].astype(F32)

    position = lax.broadcasted_iota(jnp.int32, (heads, span), 1)
    row_group = lax.broadcasted_iota(jnp.int32, (heads, width), 0) // per_group
    lane_group = lax.broadcasted_iota(jnp.int32, (heads, width), 1) // DH
    own_lanes = row_group == lane_group

    @pl.loop(0, rows // GROUP)
    def _(at):
        copy(0, at).wait()
        copy(1, at).wait()
        for i in range(GROUP):
            t = at * GROUP + i
            query = q_rows[pl.ds(t, heads, stride=rows), :]
            new_key = new_rows[0, pl.ds(t, 1), :]
            new_value = new_rows[1, pl.ds(t, 1), :]
            spread = jnp.where(own_lanes, jnp.concatenate([query] * KVH, axis=1), 0.0)
            scores = lax.dot_general(
                spread.astype(BF16), cache[0, t], (((1,), (1,)), ((), ())), preferred_element_type=F32
            )
            own = jnp.concatenate(
                [
                    jnp.sum(
                        query[g * per_group : (g + 1) * per_group] * new_key[:, g * DH : (g + 1) * DH],
                        axis=1,
                        keepdims=True,
                    )
                    for g in range(KVH)
                ],
                axis=0,
            )
            own = own * scale
            scores = jnp.where(position < lengths_ref[t], scores * scale, -1e30)
            peak = jnp.maximum(jnp.max(scores, axis=1, keepdims=True), own)
            cached_exp = jnp.exp(scores - peak)
            own_exp = jnp.exp(own - peak)
            inverse = 1.0 / (jnp.sum(cached_exp, axis=1, keepdims=True) + own_exp)
            probs = (cached_exp * inverse).astype(BF16)
            own_probs = (own_exp * inverse).astype(BF16).astype(F32)
            values = jnp.dot(probs, cache[1, t], preferred_element_type=F32)
            for g in range(KVH):
                part = slice(g * per_group, (g + 1) * per_group)
                lanes = slice(g * DH, (g + 1) * DH)
                value = values[part, lanes] + own_probs[part] * new_value[:, lanes]
                out_rows[pl.ds(g * per_group * rows + t, per_group, stride=rows), :] = value

    chips = out_ref.shape[0]
    per_chip = heads // chips
    for side in range(2):

        @pl.when(core_ref[0] == side)
        def _():
            for e in range(chips):
                for i in range(per_chip):
                    h = e * per_chip + (i + side * (per_chip // 2)) % per_chip
                    out_ref[e, :, i * DH : (i + 1) * DH] = out_rows[h * rows : (h + 1) * rows, :].astype(BF16)


def attend(core, queries, new_kv, cache_kv, lengths, chips):
    rows, features = queries.shape
    span, width = cache_kv.shape[2:]
    vmem = pl.BlockSpec(memory_space=pltpu.VMEM)
    smem = pl.BlockSpec(memory_space=pltpu.SMEM)
    return pl.pallas_call(
        attend_kernel,
        out_shape=jax.ShapeDtypeStruct((chips, rows, features // chips), BF16),
        in_specs=[smem, smem, vmem, vmem, pl.BlockSpec(memory_space=pl.ANY)],
        out_specs=vmem,
        scratch_shapes=[
            pltpu.VMEM(cache_kv.shape, BF16),
            pltpu.VMEM((features // DH * rows, DH), F32),
            pltpu.VMEM((features // DH * rows, DH), F32),
            pltpu.VMEM((2, rows, width), F32),
            pltpu.SemaphoreType.DMA((2, rows // GROUP)),
        ],
        compiler_params=pltpu.CompilerParams(vmem_limit_bytes=58 << 20),
        cost_estimate=pl.CostEstimate(flops=4 * rows * features * span, bytes_accessed=2 * cache_kv.size, transcendentals=rows * features),
    )(core, lengths, queries, new_kv, cache_kv)


P_TILE = 512


def quarters(chunk, half):
    size = half // 2
    order = (0, 2, 1, 3) if chunk % 2 else (0, 1, 2, 3)
    for place, quarter in enumerate(order):
        at = place % 2 * size
        yield place // 2, slice(at, at + size), slice(quarter * size, (quarter + 1) * size)


def project_kernel(chunk, index_ref, blocks_ref, own_ref, other_ref, keep_ref, send_ref, ordered):
    chips, rows, features = blocks_ref.shape
    half = features // 2
    for k in range(chips):
        ordered[k * rows : (k + 1) * rows, :] = blocks_ref[index_ref[k]]
    for at in range(0, keep_ref.shape[1], P_TILE):
        lanes = slice(at, at + P_TILE)
        total = jnp.dot(ordered[:, :half], own_ref[:, lanes], preferred_element_type=F32)
        total = total + jnp.dot(ordered[:, half:], other_ref[:, lanes], preferred_element_type=F32)
        for to, here, where in quarters(chunk, keep_ref.shape[0]):
            (keep_ref, send_ref)[to][here, lanes] = total[where].astype(BF16)


def whole(shape):
    return pl.BlockSpec(shape, lambda s: (0,) * len(shape))


def project(chunk, index, blocks, own, other):
    chips, rows, features = blocks.shape
    depth, width = own.shape
    size = width // CHUNKS
    weights = pl.BlockSpec((depth, size), lambda s: (0, chunk))
    half = (chips * rows // 2, size)
    return pl.pallas_call(
        functools.partial(project_kernel, chunk),
        out_shape=[jax.ShapeDtypeStruct(half, BF16)] * 2,
        grid=(1,),
        in_specs=[pl.BlockSpec(memory_space=pltpu.SMEM), whole(blocks.shape), weights, weights],
        out_specs=[whole(half)] * 2,
        scratch_shapes=[pltpu.VMEM((chips * rows, features), BF16)],
        compiler_params=pltpu.CompilerParams(vmem_limit_bytes=16 << 20),
        cost_estimate=pl.CostEstimate(flops=2 * blocks.size * size, bytes_accessed=4 * depth * size, transcendentals=0),
    )(index, blocks, own, other)


def bring_kernel(after_ref, *refs):
    count = len(refs) // 2
    sems = refs[-1]
    copies = [pltpu.make_async_copy(refs[i], refs[count + i], sems.at[i]) for i in range(count)]
    for copy in copies:
        copy.start()
    for copy in copies:
        copy.wait()


def bring(after, arrays):
    space = pl.BlockSpec(memory_space=pl.ANY)
    return pl.pallas_call(
        bring_kernel,
        out_shape=[jax.ShapeDtypeStruct(a.shape, a.dtype) for a in arrays],
        in_specs=[space] * (1 + len(arrays)),
        out_specs=[pl.BlockSpec(memory_space=pltpu.VMEM)] * len(arrays),
        scratch_shapes=[pltpu.SemaphoreType.DMA((len(arrays),))],
        compiler_params=pltpu.CompilerParams(vmem_limit_bytes=2 << 20),
        cost_estimate=pl.CostEstimate(flops=0, bytes_accessed=2 * sum(a.size for a in arrays), transcendentals=0),
    )(after, *arrays)


F_TILE = 256
N_TILE = 512


def activate(tokens_ref, gate_ref, up_ref, active_ref):
    for at in range(0, gate_ref.shape[1], F_TILE):
        lanes = slice(at, at + F_TILE)
        gate_part = jnp.dot(tokens_ref[...], gate_ref[:, lanes], preferred_element_type=F32)
        up_part = jnp.dot(tokens_ref[...], up_ref[:, lanes], preferred_element_type=F32)
        active_ref[:, lanes] = (gate_part / (1.0 + jnp.exp(-gate_part)) * up_part).astype(BF16)


def first_kernel(chip_ref, *refs):
    pieces, (gate_ref, up_ref, tokens_ref, active_ref, weights_ref) = refs[: 2 * CHUNKS], refs[2 * CHUNKS :]
    half = pieces[0].shape[0]
    chunk = tokens_ref.shape[1] // CHUNKS
    for c in range(CHUNKS):
        for side, here, where in quarters(c, half):
            tokens_ref[where, c * chunk : (c + 1) * chunk] = pieces[2 * c + side][here, :chunk]
    first, chips = chip_ref[0], chip_ref[1]
    lane = lax.broadcasted_iota(jnp.int32, (half, pieces[0].shape[1] - chunk), 1)
    mine = (lane == first) | (lane == first + chips) | (lane == first + 2 * chips)
    for side in range(2):
        weights_ref[side * half : (side + 1) * half, :] = jnp.sum(
            jnp.where(mine, pieces[side][:, chunk:].astype(F32), 0.0), axis=1, keepdims=True
        )
    activate(tokens_ref, gate_ref, up_ref, active_ref)


def down_kernel(chunk, active0, active1, weights_ref, down0, down1, keep_ref, send_ref):
    for at in range(0, keep_ref.shape[1], N_TILE):
        lanes = slice(at, at + N_TILE)
        total = jnp.dot(active0[...], down0[:, lanes], preferred_element_type=F32)
        total = total + jnp.dot(active1[...], down1[:, lanes], preferred_element_type=F32)
        total = total * weights_ref[...]
        for to, here, where in quarters(chunk, keep_ref.shape[0]):
            (keep_ref, send_ref)[to][here, lanes] = total[where].astype(BF16)


def experts(chip, pieces, gates, ups, downs):
    half = pieces[0].shape[0]
    rows = 2 * half
    width, hidden = gates[0].shape
    size = width // CHUNKS
    params = pltpu.CompilerParams(vmem_limit_bytes=20 << 20)
    cost = pl.CostEstimate(flops=4 * rows * width * hidden, bytes_accessed=4 * width * hidden, transcendentals=rows * hidden)
    vmem = pl.BlockSpec(memory_space=pltpu.VMEM)
    active = jax.ShapeDtypeStruct((rows, hidden), BF16)
    tokens, active0, weights = pl.pallas_call(
        first_kernel,
        out_shape=[jax.ShapeDtypeStruct((rows, width), BF16), active, jax.ShapeDtypeStruct((rows, 1), F32)],
        in_specs=[pl.BlockSpec(memory_space=pltpu.SMEM)] + [vmem] * (2 * CHUNKS + 2),
        out_specs=[vmem] * 3,
        compiler_params=params,
        cost_estimate=cost,
    )(chip, *pieces, gates[0], ups[0])
    active1 = pl.pallas_call(
        activate,
        out_shape=active,
        in_specs=[vmem] * 3,
        out_specs=vmem,
        compiler_params=params,
        cost_estimate=cost,
    )(tokens, gates[1], ups[1])
    results = []
    for c in range(CHUNKS):
        block = pl.BlockSpec((hidden, size), lambda s: (0, c))
        results += pl.pallas_call(
            functools.partial(down_kernel, c),
            out_shape=[jax.ShapeDtypeStruct((half, size), BF16)] * 2,
            grid=(1,),
            in_specs=[whole((rows, hidden)), whole((rows, hidden)), whole((rows, 1)), block, block],
            out_specs=[whole((half, size))] * 2,
            compiler_params=params,
            cost_estimate=pl.CostEstimate(flops=4 * rows * size * hidden, bytes_accessed=4 * size * hidden, transcendentals=0),
        )(active0, active1, weights, *downs)
    return results


def normalize(hidden_state, norm_gain):
    values = [part.astype(F32) for part in hidden_state]
    square = sum(jnp.sum(part * part, axis=-1, keepdims=True) for part in values)
    scale = lax.rsqrt(square / norm_gain.size + 1e-06)
    gains = jnp.split(norm_gain, CHUNKS)
    return [(part * scale * gain).astype(BF16) for part, gain in zip(values, gains)]


def step_bits(devices):
    bits = [1 << i for i in range(1, devices.bit_length() - 1)]
    other = bits[1::-1] + bits[2:] if len(bits) > 1 else bits
    return bits, other


def swap_step(step, chunk, devices):
    orders = step_bits(devices)
    return [(i, i ^ orders[(i + chunk) & 1][step]) for i in range(devices)]


def reduce_slots(pieces, devices):
    steps = devices.bit_length() - 2
    kept, sent = list(pieces[::2]), list(pieces[1::2])
    for step in range(steps):
        for c in range(CHUNKS):
            came = lax.ppermute(sent[c], "dp", swap_step(step, c, devices))
            kept[c] = kept[c].astype(F32) + came.astype(F32)
            half = kept[c].shape[0] // 2
            if step < steps - 1:
                sent[c] = kept[c][half:].astype(BF16)
                kept[c] = kept[c][:half]
    return kept


def gather_slots(own, devices):
    own = list(own)
    steps = devices.bit_length() - 2
    pieces = []
    for step in reversed(range(steps)):
        for c in range(CHUNKS):
            came = lax.ppermute(own[c], "dp", swap_step(step, c, devices))
            if step == 0:
                pieces += [own[c], came]
            else:
                own[c] = jnp.concatenate([own[c], came], axis=0)
    return pieces


def per_device(
    residual,
    queries,
    new_kv,
    cache_kv,
    lengths,
    out_weight,
    norm_gain,
    w_gate,
    w_up,
    w_down,
    expert_ids,
    combine_weights,
):
    rows = residual.shape[0]
    devices = lax.axis_size("dp")
    chips = devices // 2
    me = lax.axis_index("dp")
    core = me % 2
    chip = me // 2
    steps = devices.bit_length() - 2
    core_swap = [(i, i ^ 1) for i in range(devices)]
    core_groups = [[2 * i + c for i in range(chips)] for c in range(2)]

    out_other = lax.ppermute(out_weight, "dp", core_swap)
    gate_other = lax.ppermute(w_gate[0], "dp", core_swap)
    up_other = lax.ppermute(w_up[0], "dp", core_swap)
    down_other = lax.ppermute(w_down[0], "dp", core_swap)

    attn_out = attend(core[None], queries, new_kv, cache_kv, lengths, chips)
    blocks = lax.all_to_all(
        attn_out, "dp", split_axis=0, concat_axis=0, axis_index_groups=core_groups, tiled=True
    )

    orders = step_bits(devices)
    slot = jnp.arange(chips, dtype=jnp.int32)
    offset = jnp.zeros_like(slot)
    for step in range(steps):
        here = jnp.where(core == 0, orders[0][step], orders[1][step]) // 2
        offset = offset + here * ((slot >> (steps - 1 - step)) & 1)
    partial = [part for c in range(CHUNKS) for part in project(c, chip ^ offset, blocks, out_weight, out_other)]
    projected = reduce_slots(partial, devices)
    hidden_state = [
        (part.astype(F32) + add).astype(BF16) for part, add in zip(jnp.split(residual, CHUNKS, axis=1), projected)
    ]
    normed = normalize(hidden_state, norm_gain)

    picks = expert_ids[:, :, None] == jnp.arange(chips, dtype=jnp.int32)
    mix = jnp.sum(jnp.where(picks, combine_weights[:, :, None], 0.0), axis=1)
    mix_hi = mix.astype(BF16)
    mix_mid = (mix - mix_hi.astype(F32)).astype(BF16)
    mix_low = (mix - mix_hi.astype(F32) - mix_mid.astype(F32)).astype(BF16)
    extra = jnp.concatenate([mix_hi, mix_mid, mix_low], axis=1)
    extra = jnp.pad(extra, ((0, 0), (0, -extra.shape[1] % 128)))
    normed, gate_other, up_other, down_other = lax.optimization_barrier((normed, gate_other, up_other, down_other))
    normed = [jnp.concatenate([normed[0], extra], axis=1)] + list(normed[1:])
    pieces = gather_slots(normed, devices)
    gate_other, up_other, down_other = bring(pieces[2], (gate_other, up_other, down_other))
    place = jnp.stack([chip, jnp.int32(chips)])
    outs = experts(place, pieces, (w_gate[0], gate_other), (w_up[0], up_other), (w_down[0], down_other))
    mixture = reduce_slots(outs, devices)
    return jnp.concatenate(
        [(part.astype(F32) + add).astype(BF16) for part, add in zip(hidden_state, mixture)], axis=1
    )


def solution(mesh):
    placed = (
        P(("groups", "dp"), None),
        P(("groups", "dp"), None),
        P(None, ("groups", "dp"), None),
        P(None, ("groups", "dp"), None, None),
        P(("groups", "dp")),
        P("dp", None),
        P(),
        P("dp", None, None),
        P("dp", None, None),
        P("dp", None, None),
        P(("groups", "dp"), None),
        P(("groups", "dp"), None),
    )
    return jax.shard_map(
        per_device, mesh=mesh, in_specs=placed, out_specs=P(("groups", "dp"), None), check_vma=False
    )
```

time: 148 us -> 146 us (0.986)
  starting transfers between devices: 41.7 us -> 33.1 us
  waiting for transfers between devices: 72.2 us -> 75.4 us
  Pallas kernels: 30.7 us -> 33.4 us
    ppermute x16, starting transfers between devices: 20.9 us -> 15 us  [reduce_slots(): came = lax.ppermute(sent[c], 'dp', swap_step(step, c, devices))]
    ppermute x16, waiting for transfers between devices: 42.2 us -> 47.6 us  [reduce_slots(): came = lax.ppermute(sent[c], 'dp', swap_step(step, c, devices))]
    ppermute x8, starting transfers between devices: 11.4 us -> 8.69 us  [gather_slots(): came = lax.ppermute(own[c], 'dp', swap_step(step, c, devices))]
    pallas_call x1, Pallas kernels: 9.51 us -> 11.9 us  [attend(): pl.pallas_call(attend_kernel, out_shape=jax.ShapeDtypeStruct((chips, rows...]
    ppermute x8, waiting for transfers between devices: 20.2 us -> 18 us  [gather_slots(): came = lax.ppermute(own[c], 'dp', swap_step(step, c, devices))]
    pallas_call x2 -> x7, Pallas kernels: 21.2 us -> 21.5 us  [the longest x1 6.56 us: bring(): pl.pallas_call(bring_kernel, out_shape=[jax.ShapeDtypeStruct(a.shape, a.d...]
  transfers between devices with their start and end apart: 29 -> 29, of which waited for: 18 -> 20; matrix products, arithmetic and copies ran while one was open for 1% -> 1% of each run, Pallas kernels for 8% -> 17%
where the time goes in v5:
time: 146 us
  waiting for transfers between devices  75.4 us (52%)
  Pallas kernels  33.4 us (23%)
  starting transfers between devices  33.1 us (23%)
  other arithmetic  2.21 us (2%)
    ppermute x16, waiting for transfers between devices, reduce_slots(): came = lax.ppermute(sent[c], 'dp', swap_step(step, c, devices))  47.6 us
    ppermute x8, waiting for transfers between devices, gather_slots(): came = lax.ppermute(own[c], 'dp', swap_step(step, c, devices))  18 us
    ppermute x16, starting transfers between devices, reduce_slots(): came = lax.ppermute(sent[c], 'dp', swap_step(step, c, devices))  15 us
    pallas_call x1, Pallas kernels, attend(): pl.pallas_call(attend_kernel, out_shape=jax.ShapeDtypeStruct((chips, rows...  11.9 us
    all_to_all x1, waiting for transfers between devices, per_device(): lax.all_to_all(attn_out, 'dp', split_axis=0, concat_axis=0, axis_index_gr...  9.85 us
    ppermute x8, starting transfers between devices, gather_slots(): came = lax.ppermute(own[c], 'dp', swap_step(step, c, devices))  8.69 us
    all_to_all x1, starting transfers between devices, per_device(): lax.all_to_all(attn_out, 'dp', split_axis=0, concat_axis=0, axis_index_gr...  8.32 us
    pallas_call x1, Pallas kernels, bring(): pl.pallas_call(bring_kernel, out_shape=[jax.ShapeDtypeStruct(a.shape, a.d...  6.56 us
  transfers between devices with their start and end apart: 29, of which 20 were waited for; matrix products, arithmetic and copies ran while one was open for 1% of the time, Pallas kernels for 17%

profile of v5, /device:TPU:0, one launch (start us, length us, event | category | flops | bytes accessed | tf_op | source)
XLA Modules:
  0.0 145.9 jit_solution(5292820787050292416)
XLA Ops:
  1.0 11.9 %shard_map.118 = bf16[16,16,512]{2,1,0:T(8,128)(2,1)} custom-call(s32[1]{0:T(128)} %bitcast.core_ref, s32[16]{0:T(128)} %lengths_ref.1, bf16[16,8192]{1,0:T(8,128)(2,1)} %q_ref.1, bf16[2,16,512]{2,1,0:T(8,128)(2,1)} %new_ref.1, bf16[2,16,128,512]{3,2,1,0:T(8,128)(2,1)} %cache_ref.1), custom_call_target="tpu_custom_call" | custom-call | flops 67108864 | bytes 4194304 | tf_op jit(solution)/shard_map/pallas_call | solution.py:104
  12.9 8.3 %all-to-all-start = ((bf16[16,16,512]{2,1,0:T(8,128)(2,1)}), bf16[16,16,512]{2,1,0:T(8,128)(2,1)S(1)}, u32[]{:S(2)}, u32[]{:S(2)}) async-start(bf16[16,16,512]{2,1,0:T(8,128)(2,1)} %shard_map.118), calls=%async_computation | async-start | bytes 524288 | tf_op jit(solution)/shard_map/all_to_all | solution.py:346
  21.4 9.8 %all-to-all-done.blocks_ref = bf16[16,16,512]{2,1,0:T(8,128)(2,1)S(1)} async-done(((bf16[16,16,512]{2,1,0:T(8,128)(2,1)}), bf16[16,16,512]{2,1,0:T(8,128)(2,1)S(1)}, u32[]{:S(2)}, u32[]{:S(2)}) %all-to-all-start) | async-done | bytes 262176 | tf_op jit(solution)/shard_map/all_to_all | solution.py:346
  31.3 2.0 %shard_map.120 = (bf16[128,2048]{1,0:T(8,128)(2,1)S(1)}, bf16[128,2048]{1,0:T(8,128)(2,1)S(1)}) custom-call(s32[16]{0:T(128)S(1)} %add_xor_fusion.index_ref, bf16[16,16,512]{2,1,0:T(8,128)(2,1)S(1)} %all-to-all-done.blocks_ref, bf16[256,4096]{1,0:T(8,128)(2,1)S(1)} %copy-done, bf16[256,4096]{1,0:T(8,128)(2,1)} %collective-permute-done.other_ref), custom_call_target="tpu_custom_call" | custom-call | flops 536870912 | bytes 2097152 | tf_op jit(solution)/shard_map/pallas_call | solution.py:155
  34.4 2.0 %shard_map.119 = (bf16[128,2048]{1,0:T(8,128)(2,1)S(1)}, bf16[128,2048]{1,0:T(8,128)(2,1)S(1)}) custom-call(s32[16]{0:T(128)S(1)} %add_xor_fusion.index_ref, bf16[16,16,512]{2,1,0:T(8,128)(2,1)S(1)} %all-to-all-done.blocks_ref, bf16[256,4096]{1,0:T(8,128)(2,1)S(1)} %copy-done, bf16[256,4096]{1,0:T(8,128)(2,1)} %collective-permute-done.other_ref), custom_call_target="tpu_custom_call" | custom-call | flops 536870912 | bytes 2097152 | tf_op jit(solution)/shard_map/pallas_call | solution.py:155
  37.1 10.6 %collective-permute-done.5 = bf16[128,2048]{1,0:T(8,128)(2,1)S(1)} collective-permute-done((bf16[128,2048]{1,0:T(8,128)(2,1)S(1)}, bf16[128,2048]{1,0:T(8,128)(2,1)S(1)}, u32[]{:S(2)}, u32[]{:S(2)}) %collective-permute-start.5) | collective-permute-done | bytes 524320 | tf_op jit(solution)/shard_map/ppermute | solution.py:293
  50.1 6.4 %collective-permute-done.6 = bf16[64,2048]{1,0:T(8,128)(2,1)S(1)} collective-permute-done((bf16[64,2048]{1,0:T(8,128)(2,1)S(1)}, bf16[64,2048]{1,0:T(8,128)(2,1)S(1)}, u32[]{:S(2)}, u32[]{:S(2)}) %collective-permute-start.6) | collective-permute-done | bytes 262176 | tf_op jit(solution)/shard_map/ppermute | solution.py:293
  56.7 2.0 %collective-permute-start.3 = (bf16[32,2048]{1,0:T(8,128)(2,1)S(1)}, bf16[32,2048]{1,0:T(8,128)(2,1)S(1)}, u32[]{:S(2)}, u32[]{:S(2)}) collective-permute-start(bf16[32,2048]{1,0:T(8,128)(2,1)S(1)} %slice.175), channel_id=1, source_target_pairs={{0,8},{1,9},{2,10},{3,11},{4,12},{5,13},{6,14},{7,15},{8,0},{9,1},... | collective-permute-start | bytes 393224 | tf_op jit(solution)/shard_map/ppermute | solution.py:293
  58.8 3.5 %collective-permute-done.7 = bf16[32,2048]{1,0:T(8,128)(2,1)S(1)} collective-permute-done((bf16[32,2048]{1,0:T(8,128)(2,1)S(1)}, bf16[32,2048]{1,0:T(8,128)(2,1)S(1)}, u32[]{:S(2)}, u32[]{:S(2)}) %collective-permute-start.7) | collective-permute-done | bytes 131104 | tf_op jit(solution)/shard_map/ppermute | solution.py:293
  63.7 1.7 %collective-permute-start.4 = (bf16[16,2048]{1,0:T(8,128)(2,1)S(1)}, bf16[16,2048]{1,0:T(8,128)(2,1)S(1)}, u32[]{:S(2)}, u32[]{:S(2)}) collective-permute-start(bf16[16,2048]{1,0:T(8,128)(2,1)S(1)} %slice.179), channel_id=1, source_target_pairs={{0,16},{1,17},{2,18},{3,19},{4,20},{5,21},{6,22},{7,23},{8,24},{9,... | collective-permute-start | bytes 196616 | tf_op jit(solution)/shard_map/ppermute | solution.py:293
  65.5 2.5 %collective-permute-done.8 = bf16[16,2048]{1,0:T(8,128)(2,1)S(1)} collective-permute-done((bf16[16,2048]{1,0:T(8,128)(2,1)S(1)}, bf16[16,2048]{1,0:T(8,128)(2,1)S(1)}, u32[]{:S(2)}, u32[]{:S(2)}) %collective-permute-start.8) | collective-permute-done | bytes 65568 | tf_op jit(solution)/shard_map/ppermute | solution.py:293
  67.9 2.8 %collective-permute-done.4 = bf16[16,2048]{1,0:T(8,128)(2,1)S(1)} collective-permute-done((bf16[16,2048]{1,0:T(8,128)(2,1)S(1)}, bf16[16,2048]{1,0:T(8,128)(2,1)S(1)}, u32[]{:S(2)}, u32[]{:S(2)}) %collective-permute-start.4) | collective-permute-done | bytes 65568 | tf_op jit(solution)/shard_map/ppermute | solution.py:293
  71.4 2.7 %collective-permute-start.12 = (bf16[16,2176]{1,0:T(8,128)(2,1)S(1)}, bf16[16,2176]{1,0:T(8,128)(2,1)S(1)}, u32[]{:S(2)}, u32[]{:S(2)}) collective-permute-start(bf16[16,2176]{1,0:T(8,128)(2,1)S(1)} %pad_maximum_fusion.6), channel_id=1, source_target_pairs={{0,16},{1,17},{2,18},{3,19},{4,20},{5,21},{6,22},{7,23},{8,24},{9,... | collective-permute-start | bytes 208904 | tf_op jit(solution)/shard_map/ppermute | solution.py:308
  74.1 2.5 %collective-permute-done.16 = bf16[16,2048]{1,0:T(8,128)(2,1)S(1)} collective-permute-done((bf16[16,2048]{1,0:T(8,128)(2,1)S(1)}, bf16[16,2048]{1,0:T(8,128)(2,1)S(1)}, u32[]{:S(2)}, u32[]{:S(2)}) %collective-permute-start.16) | collective-permute-done | bytes 65568 | tf_op jit(solution)/shard_map/ppermute | solution.py:308
  78.8 4.4 %collective-permute-done.13 = bf16[32,2176]{1,0:T(8,128)(2,1)S(1)} collective-permute-done((bf16[32,2176]{1,0:T(8,128)(2,1)S(1)}, bf16[32,2176]{1,0:T(8,128)(2,1)S(1)}, u32[]{:S(2)}, u32[]{:S(2)}) %collective-permute-start.13) | collective-permute-done | bytes 139296 | tf_op jit(solution)/shard_map/ppermute | solution.py:308
  83.7 2.1 %collective-permute-start.18 = (bf16[64,2048]{1,0:T(8,128)(2,1)S(1)}, bf16[64,2048]{1,0:T(8,128)(2,1)S(1)}, u32[]{:S(2)}, u32[]{:S(2)}) collective-permute-start(bf16[64,2048]{1,0:T(8,128)(2,1)S(1)} %pad_maximum_fusion.2), channel_id=1, source_target_pairs={{0,2},{1,5},{2,0},{3,7},{4,6},{5,1},{6,4},{7,3},{8,10},{9,13},{10,... | collective-permute-start | bytes 786440 | tf_op jit(solution)/shard_map/ppermute | solution.py:308
  85.8 7.1 %collective-permute-done.14 = bf16[64,2176]{1,0:T(8,128)(2,1)S(1)} collective-permute-done((bf16[64,2176]{1,0:T(8,128)(2,1)S(1)}, bf16[64,2176]{1,0:T(8,128)(2,1)S(1)}, u32[]{:S(2)}, u32[]{:S(2)}) %collective-permute-start.14) | collective-permute-done | bytes 278560 | tf_op jit(solution)/shard_map/ppermute | solution.py:308
  92.9 2.4 %collective-permute-start.15 = (bf16[128,2176]{1,0:T(8,128)(2,1)S(1)}, bf16[128,2176]{1,0:T(8,128)(2,1)S(1)}, u32[]{:S(2)}, u32[]{:S(2)}) collective-permute-start(bf16[128,2176]{1,0:T(8,128)(2,1)S(1)} %pad_maximum_fusion.refs_0_), channel_id=1, source_target_pairs={{0,2},{1,5},{2,0},{3,7},{4,6},{5,1},{6,4},{7,3},{8,10},{9,13},{10,... | collective-permute-start | bytes 1671176 | tf_op jit(solution)/shard_map/ppermute | solution.py:308
  95.5 6.6 %shard_map.122 = (bf16[4096,768]{1,0:T(8,128)(2,1)S(1)}, bf16[4096,768]{1,0:T(8,128)(2,1)S(1)}, bf16[768,4096]{1,0:T(8,128)(2,1)S(1)}) custom-call(bf16[128,2048]{1,0:T(8,128)(2,1)S(1)} %constant_dynamic-update-slice_fusion.refs_2_.after_ref, bf16[4096,768]{1,0:T(8,128)(2,1)} %collective-permute-done.9.refs_0_, ...), custom_call_target="tpu_custom_call" | custom-call | bytes 18874368 | tf_op jit(solution)/shard_map/pallas_call | solution.py:179
  102.1 2.5 %collective-permute-done.19.refs_3_ = bf16[128,2048]{1,0:T(8,128)(2,1)S(1)} collective-permute-done((bf16[128,2048]{1,0:T(8,128)(2,1)S(1)}, bf16[128,2048]{1,0:T(8,128)(2,1)S(1)}, u32[]{:S(2)}, u32[]{:S(2)}) %collective-permute-start.19) | collective-permute-done | bytes 524320 | tf_op jit(solution)/shard_map/ppermute | solution.py:308
  105.5 4.0 %shard_map.121 = (bf16[256,4096]{1,0:T(8,128)(2,1)S(1)}, bf16[256,768]{1,0:T(8,128)(2,1)S(1)}, f32[256,1]{1,0:T(8,128)S(1)}) custom-call(s32[2]{0:T(128)S(1)} %pad_add_fusion.chip_ref, bf16[128,2176]{1,0:T(8,128)(2,1)S(1)} %pad_maximum_fusion.refs_0_, bf16[128,2176]{1,0:T(8,128)(2,1)S(1)} %collective-permute-done.15.refs_1_, ...), custom_call_target="tpu_custom_call" | custom-call | flops 3221225472 | bytes 12582912 | tf_op jit(solution)/shard_map/pallas_call | solution.py:238
  109.5 3.4 %shard_map.123.active1 = bf16[256,768]{1,0:T(8,128)(2,1)S(1)} custom-call(bf16[256,4096]{1,0:T(8,128)(2,1)S(1)} %get-tuple-element.31.tokens_ref, bf16[4096,768]{1,0:T(8,128)(2,1)S(1)} %get-tuple-element.35.gate_ref, bf16[4096,768]{1,0:T(8,128)(2,1)S(1)} %get-tuple-element.36.up_ref), custom_call_target="tpu_custom_call" | custom-call | flops 3221225472 | bytes 12582912 | tf_op jit(solution)/shard_map/pallas_call | solution.py:246
  112.9 1.8 %shard_map.124 = (bf16[128,2048]{1,0:T(8,128)(2,1)S(1)}, bf16[128,2048]{1,0:T(8,128)(2,1)S(1)}) custom-call(bf16[256,768]{1,0:T(8,128)(2,1)S(1)} %get-tuple-element.30.active0, bf16[256,768]{1,0:T(8,128)(2,1)S(1)} %shard_map.123.active1, f32[256,1]{1,0:T(8,128)S(1)} %get-tuple-element.37.weights_ref, bf16[768,4096]{1,0:T(8,128)(2,1)S(1)} %bitcast.8, ...), custom_call_target="tpu_custom_call" | custom-call | flops 1610612736 | bytes 6291456 | tf_op jit(solution)/shard_map/pallas_call | solution.py:257
  114.7 1.7 %collective-permute-start.20 = (bf16[128,2048]{1,0:T(8,128)(2,1)S(1)}, bf16[128,2048]{1,0:T(8,128)(2,1)S(1)}, u32[]{:S(2)}, u32[]{:S(2)}) collective-permute-start(bf16[128,2048]{1,0:T(8,128)(2,1)S(1)} %get-tuple-element.40), channel_id=1, source_target_pairs={{0,2},{1,5},{2,0},{3,7},{4,6},{5,1},{6,4},{7,3},{8,10},{9,13},{10,... | collective-permute-start | bytes 1572872 | tf_op jit(solution)/shard_map/ppermute | solution.py:293
  116.5 1.8 %shard_map.125 = (bf16[128,2048]{1,0:T(8,128)(2,1)S(1)}, bf16[128,2048]{1,0:T(8,128)(2,1)S(1)}) custom-call(bf16[256,768]{1,0:T(8,128)(2,1)S(1)} %get-tuple-element.30.active0, bf16[256,768]{1,0:T(8,128)(2,1)S(1)} %shard_map.123.active1, f32[256,1]{1,0:T(8,128)S(1)} %get-tuple-element.37.weights_ref, bf16[768,4096]{1,0:T(8,128)(2,1)S(1)} %bitcast.9, ...), custom_call_target="tpu_custom_call" | custom-call | flops 1610612736 | bytes 6291456 | tf_op jit(solution)/shard_map/pallas_call | solution.py:257
  118.7 6.2 %collective-permute-done.20 = bf16[128,2048]{1,0:T(8,128)(2,1)S(1)} collective-permute-done((bf16[128,2048]{1,0:T(8,128)(2,1)S(1)}, bf16[128,2048]{1,0:T(8,128)(2,1)S(1)}, u32[]{:S(2)}, u32[]{:S(2)}) %collective-permute-start.20) | collective-permute-done | bytes 524320 | tf_op jit(solution)/shard_map/ppermute | solution.py:293
  128.9 2.6 %collective-permute-done.21 = bf16[64,2048]{1,0:T(8,128)(2,1)S(1)} collective-permute-done((bf16[64,2048]{1,0:T(8,128)(2,1)S(1)}, bf16[64,2048]{1,0:T(8,128)(2,1)S(1)}, u32[]{:S(2)}, u32[]{:S(2)}) %collective-permute-start.21) | collective-permute-done | bytes 262176 | tf_op jit(solution)/shard_map/ppermute | solution.py:293
  131.6 2.5 %collective-permute-done.25 = bf16[64,2048]{1,0:T(8,128)(2,1)S(1)} collective-permute-done((bf16[64,2048]{1,0:T(8,128)(2,1)S(1)}, bf16[64,2048]{1,0:T(8,128)(2,1)S(1)}, u32[]{:S(2)}, u32[]{:S(2)}) %collective-permute-start.25) | collective-permute-done | bytes 262176 | tf_op jit(solution)/shard_map/ppermute | solution.py:293
  135.0 1.6 %collective-permute-done.22 = bf16[32,2048]{1,0:T(8,128)(2,1)S(1)} collective-permute-done((bf16[32,2048]{1,0:T(8,128)(2,1)S(1)}, bf16[32,2048]{1,0:T(8,128)(2,1)S(1)}, u32[]{:S(2)}, u32[]{:S(2)}) %collective-permute-start.22) | collective-permute-done | bytes 131104 | tf_op jit(solution)/shard_map/ppermute | solution.py:293
  137.0 2.3 %collective-permute-done.26 = bf16[32,2048]{1,0:T(8,128)(2,1)S(1)} collective-permute-done((bf16[32,2048]{1,0:T(8,128)(2,1)S(1)}, bf16[32,2048]{1,0:T(8,128)(2,1)S(1)}, u32[]{:S(2)}, u32[]{:S(2)}) %collective-permute-start.26) | collective-permute-done | bytes 131104 | tf_op jit(solution)/shard_map/ppermute | solution.py:293
  140.4 1.6 %collective-permute-done.23 = bf16[16,2048]{1,0:T(8,128)(2,1)S(1)} collective-permute-done((bf16[16,2048]{1,0:T(8,128)(2,1)S(1)}, bf16[16,2048]{1,0:T(8,128)(2,1)S(1)}, u32[]{:S(2)}, u32[]{:S(2)}) %collective-permute-start.23) | collective-permute-done | bytes 65568 | tf_op jit(solution)/shard_map/ppermute | solution.py:293
  142.0 3.2 %collective-permute-done.27 = bf16[16,2048]{1,0:T(8,128)(2,1)S(1)} collective-permute-done((bf16[16,2048]{1,0:T(8,128)(2,1)S(1)}, bf16[16,2048]{1,0:T(8,128)(2,1)S(1)}, u32[]{:S(2)}, u32[]{:S(2)}) %collective-permute-start.27) | collective-permute-done | bytes 65568 | tf_op jit(solution)/shard_map/ppermute | solution.py:293
  (107 shorter events, 19.1 us)
Async XLA Ops:
  0.0 31.3 %collective-permute-start = (bf16[256,4096]{1,0:T(8,128)(2,1)}, bf16[256,4096]{1,0:T(8,128)(2,1)}, u32[]{:S(2)}, u32[]{:S(2)}) collective-permute-start(bf16[256,4096]{1,0:T(8,128)(2,1)} %own_ref.3), channel_id=1, source_target_pairs={{0,1},{1,0},{2,3},{3,2},{4,5},{5,4},{6,7},{7,6},{8,9},{9,8},{10,11... | collective-permute-start | bytes 6291464 | tf_op jit(solution)/shard_map/ppermute | solution.py:340
  0.5 70.6 %collective-permute-start.11 = (bf16[768,4096]{1,0:T(8,128)(2,1)}, bf16[768,4096]{1,0:T(8,128)(2,1)}, u32[]{:S(2)}, u32[]{:S(2)}) collective-permute-start(bf16[768,4096]{1,0:T(8,128)(2,1)} %bitcast.5), channel_id=1, source_target_pairs={{0,1},{1,0},{2,3},{3,2},{4,5},{5,4},{6,7},{7,6},{8,9},{9,8},{10,11... | collective-permute-start | bytes 18874376 | tf_op jit(solution)/shard_map/ppermute | solution.py:343
  0.5 70.5 %collective-permute-start.10 = (bf16[4096,768]{1,0:T(8,128)(2,1)}, bf16[4096,768]{1,0:T(8,128)(2,1)}, u32[]{:S(2)}, u32[]{:S(2)}) collective-permute-start(bf16[4096,768]{1,0:T(8,128)(2,1)} %bitcast.14), channel_id=1, source_target_pairs={{0,1},{1,0},{2,3},{3,2},{4,5},{5,4},{6,7},{7,6},{8,9},{9,8},{10,11... | collective-permute-start | bytes 18874376 | tf_op jit(solution)/shard_map/ppermute | solution.py:342
  1.0 70.1 %collective-permute-start.9 = (bf16[4096,768]{1,0:T(8,128)(2,1)}, bf16[4096,768]{1,0:T(8,128)(2,1)}, u32[]{:S(2)}, u32[]{:S(2)}) collective-permute-start(bf16[4096,768]{1,0:T(8,128)(2,1)} %bitcast.10), channel_id=1, source_target_pairs={{0,1},{1,0},{2,3},{3,2},{4,5},{5,4},{6,7},{7,6},{8,9},{9,8},{10,11... | collective-permute-start | bytes 18874376 | tf_op jit(solution)/shard_map/ppermute | solution.py:341
  1.0 20.3 %copy-start.4 = (f32[16,8]{0,1:T(8,128)S(1)}, f32[16,8]{0,1:T(8,128)}, u32[]{:S(2)}) copy-start(f32[16,8]{0,1:T(8,128)} %param.23) | copy-start | bytes 1540
  1.0 30.3 %copy-start = (bf16[256,4096]{1,0:T(8,128)(2,1)S(1)}, bf16[256,4096]{1,0:T(8,128)(2,1)}, u32[]{:S(2)}) copy-start(bf16[256,4096]{1,0:T(8,128)(2,1)} %own_ref.3) | copy-start | bytes 6291460
  12.9 18.4 %all-to-all-start = ((bf16[16,16,512]{2,1,0:T(8,128)(2,1)}), bf16[16,16,512]{2,1,0:T(8,128)(2,1)S(1)}, u32[]{:S(2)}, u32[]{:S(2)}) async-start(bf16[16,16,512]{2,1,0:T(8,128)(2,1)} %shard_map.118), calls=%async_computation | async-start | bytes 524288 | tf_op jit(solution)/shard_map/all_to_all | solution.py:346
  33.3 14.4 %collective-permute-start.5 = (bf16[128,2048]{1,0:T(8,128)(2,1)S(1)}, bf16[128,2048]{1,0:T(8,128)(2,1)S(1)}, u32[]{:S(2)}, u32[]{:S(2)}) collective-permute-start(bf16[128,2048]{1,0:T(8,128)(2,1)S(1)} %get-tuple-element.27), channel_id=1, source_target_pairs={{0,4},{1,3},{2,6},{3,1},{4,0},{5,7},{6,2},{7,5},{8,12},{9,11},{10,... | collective-permute-start | bytes 1572872 | tf_op jit(solution)/shard_map/ppermute | solution.py:293
  36.4 12.7 %collective-permute-start.1 = (bf16[128,2048]{1,0:T(8,128)(2,1)S(1)}, bf16[128,2048]{1,0:T(8,128)(2,1)S(1)}, u32[]{:S(2)}, u32[]{:S(2)}) collective-permute-start(bf16[128,2048]{1,0:T(8,128)(2,1)S(1)} %get-tuple-element.25), channel_id=1, source_target_pairs={{0,2},{1,5},{2,0},{3,7},{4,6},{5,1},{6,4},{7,3},{8,10},{9,13},{10,... | collective-permute-start | bytes 1572872 | tf_op jit(solution)/shard_map/ppermute | solution.py:293
  47.8 8.6 %collective-permute-start.6 = (bf16[64,2048]{1,0:T(8,128)(2,1)S(1)}, bf16[64,2048]{1,0:T(8,128)(2,1)S(1)}, u32[]{:S(2)}, u32[]{:S(2)}) collective-permute-start(bf16[64,2048]{1,0:T(8,128)(2,1)S(1)} %slice.170), channel_id=1, source_target_pairs={{0,2},{1,5},{2,0},{3,7},{4,6},{5,1},{6,4},{7,3},{8,10},{9,13},{10,... | collective-permute-start | bytes 786440 | tf_op jit(solution)/shard_map/ppermute | solution.py:293
  49.2 21.5 %copy-start.1 = (bf16[16,4096]{1,0:T(8,128)(2,1)S(1)}, bf16[16,4096]{1,0:T(8,128)(2,1)}, u32[]{:S(2)}) copy-start(bf16[16,4096]{1,0:T(8,128)(2,1)} %param.12) | copy-start | bytes 393220
  49.3 7.4 %collective-permute-start.2 = (bf16[64,2048]{1,0:T(8,128)(2,1)S(1)}, bf16[64,2048]{1,0:T(8,128)(2,1)S(1)}, u32[]{:S(2)}, u32[]{:S(2)}) collective-permute-start(bf16[64,2048]{1,0:T(8,128)(2,1)S(1)} %slice.171), channel_id=1, source_target_pairs={{0,4},{1,3},{2,6},{3,1},{4,0},{5,7},{6,2},{7,5},{8,12},{9,11},{10,... | collective-permute-start | bytes 786440 | tf_op jit(solution)/shard_map/ppermute | solution.py:293
  56.5 5.7 %collective-permute-start.7 = (bf16[32,2048]{1,0:T(8,128)(2,1)S(1)}, bf16[32,2048]{1,0:T(8,128)(2,1)S(1)}, u32[]{:S(2)}, u32[]{:S(2)}) collective-permute-start(bf16[32,2048]{1,0:T(8,128)(2,1)S(1)} %slice.174), channel_id=1, source_target_pairs={{0,8},{1,9},{2,10},{3,11},{4,12},{5,13},{6,14},{7,15},{8,0},{9,1},... | collective-permute-start | bytes 393224 | tf_op jit(solution)/shard_map/ppermute | solution.py:293
  56.7 6.9 %collective-permute-start.3 = (bf16[32,2048]{1,0:T(8,128)(2,1)S(1)}, bf16[32,2048]{1,0:T(8,128)(2,1)S(1)}, u32[]{:S(2)}, u32[]{:S(2)}) collective-permute-start(bf16[32,2048]{1,0:T(8,128)(2,1)S(1)} %slice.175), channel_id=1, source_target_pairs={{0,8},{1,9},{2,10},{3,11},{4,12},{5,13},{6,14},{7,15},{8,0},{9,1},... | collective-permute-start | bytes 393224 | tf_op jit(solution)/shard_map/ppermute | solution.py:293
  62.3 5.7 %collective-permute-start.8 = (bf16[16,2048]{1,0:T(8,128)(2,1)S(1)}, bf16[16,2048]{1,0:T(8,128)(2,1)S(1)}, u32[]{:S(2)}, u32[]{:S(2)}) collective-permute-start(bf16[16,2048]{1,0:T(8,128)(2,1)S(1)} %slice.178), channel_id=1, source_target_pairs={{0,16},{1,17},{2,18},{3,19},{4,20},{5,21},{6,22},{7,23},{8,24},{9,... | collective-permute-start | bytes 196616 | tf_op jit(solution)/shard_map/ppermute | solution.py:293
  63.7 7.0 %collective-permute-start.4 = (bf16[16,2048]{1,0:T(8,128)(2,1)S(1)}, bf16[16,2048]{1,0:T(8,128)(2,1)S(1)}, u32[]{:S(2)}, u32[]{:S(2)}) collective-permute-start(bf16[16,2048]{1,0:T(8,128)(2,1)S(1)} %slice.179), channel_id=1, source_target_pairs={{0,16},{1,17},{2,18},{3,19},{4,20},{5,21},{6,22},{7,23},{8,24},{9,... | collective-permute-start | bytes 196616 | tf_op jit(solution)/shard_map/ppermute | solution.py:293
  71.0 5.6 %collective-permute-start.16 = (bf16[16,2048]{1,0:T(8,128)(2,1)S(1)}, bf16[16,2048]{1,0:T(8,128)(2,1)S(1)}, u32[]{:S(2)}, u32[]{:S(2)}) collective-permute-start(bf16[16,2048]{1,0:T(8,128)(2,1)S(1)} %get-tuple-element.29), channel_id=1, source_target_pairs={{0,16},{1,17},{2,18},{3,19},{4,20},{5,21},{6,22},{7,23},{8,24},{9,... | collective-permute-start | bytes 196616 | tf_op jit(solution)/shard_map/ppermute | solution.py:308
  71.4 6.7 %collective-permute-start.12 = (bf16[16,2176]{1,0:T(8,128)(2,1)S(1)}, bf16[16,2176]{1,0:T(8,128)(2,1)S(1)}, u32[]{:S(2)}, u32[]{:S(2)}) collective-permute-start(bf16[16,2176]{1,0:T(8,128)(2,1)S(1)} %pad_maximum_fusion.6), channel_id=1, source_target_pairs={{0,16},{1,17},{2,18},{3,19},{4,20},{5,21},{6,22},{7,23},{8,24},{9,... | collective-permute-start | bytes 208904 | tf_op jit(solution)/shard_map/ppermute | solution.py:308
  76.6 7.0 %collective-permute-start.17 = (bf16[32,2048]{1,0:T(8,128)(2,1)S(1)}, bf16[32,2048]{1,0:T(8,128)(2,1)S(1)}, u32[]{:S(2)}, u32[]{:S(2)}) collective-permute-start(bf16[32,2048]{1,0:T(8,128)(2,1)S(1)} %pad_maximum_fusion.4), channel_id=1, source_target_pairs={{0,8},{1,9},{2,10},{3,11},{4,12},{5,13},{6,14},{7,15},{8,0},{9,1},... | collective-permute-start | bytes 393224 | tf_op jit(solution)/shard_map/ppermute | solution.py:308
  78.1 5.1 %collective-permute-start.13 = (bf16[32,2176]{1,0:T(8,128)(2,1)S(1)}, bf16[32,2176]{1,0:T(8,128)(2,1)S(1)}, u32[]{:S(2)}, u32[]{:S(2)}) collective-permute-start(bf16[32,2176]{1,0:T(8,128)(2,1)S(1)} %pad_maximum_fusion.3), channel_id=1, source_target_pairs={{0,8},{1,9},{2,10},{3,11},{4,12},{5,13},{6,14},{7,15},{8,0},{9,1},... | collective-permute-start | bytes 417800 | tf_op jit(solution)/shard_map/ppermute | solution.py:308
  83.3 9.6 %collective-permute-start.14 = (bf16[64,2176]{1,0:T(8,128)(2,1)S(1)}, bf16[64,2176]{1,0:T(8,128)(2,1)S(1)}, u32[]{:S(2)}, u32[]{:S(2)}) collective-permute-start(bf16[64,2176]{1,0:T(8,128)(2,1)S(1)} %pad_maximum_fusion.1), channel_id=1, source_target_pairs={{0,4},{1,3},{2,6},{3,1},{4,0},{5,7},{6,2},{7,5},{8,12},{9,11},{10,... | collective-permute-start | bytes 835592 | tf_op jit(solution)/shard_map/ppermute | solution.py:308
  83.7 11.6 %collective-permute-start.18 = (bf16[64,2048]{1,0:T(8,128)(2,1)S(1)}, bf16[64,2048]{1,0:T(8,128)(2,1)S(1)}, u32[]{:S(2)}, u32[]{:S(2)}) collective-permute-start(bf16[64,2048]{1,0:T(8,128)(2,1)S(1)} %pad_maximum_fusion.2), channel_id=1, source_target_pairs={{0,2},{1,5},{2,0},{3,7},{4,6},{5,1},{6,4},{7,3},{8,10},{9,13},{10,... | collective-permute-start | bytes 786440 | tf_op jit(solution)/shard_map/ppermute | solution.py:308
  92.9 11.6 %collective-permute-start.15 = (bf16[128,2176]{1,0:T(8,128)(2,1)S(1)}, bf16[128,2176]{1,0:T(8,128)(2,1)S(1)}, u32[]{:S(2)}, u32[]{:S(2)}) collective-permute-start(bf16[128,2176]{1,0:T(8,128)(2,1)S(1)} %pad_maximum_fusion.refs_0_), channel_id=1, source_target_pairs={{0,2},{1,5},{2,0},{3,7},{4,6},{5,1},{6,4},{7,3},{8,10},{9,13},{10,... | collective-permute-start | bytes 1671176 | tf_op jit(solution)/shard_map/ppermute | solution.py:308
  95.3 9.2 %collective-permute-start.19 = (bf16[128,2048]{1,0:T(8,128)(2,1)S(1)}, bf16[128,2048]{1,0:T(8,128)(2,1)S(1)}, u32[]{:S(2)}, u32[]{:S(2)}) collective-permute-start(bf16[128,2048]{1,0:T(8,128)(2,1)S(1)} %constant_dynamic-update-slice_fusion.refs_2_.after_ref), channel_id=1, source_target_pairs={{0,4},{1,3},{2,6},{3,1},{4,0},{5,7},{6,2},{7,5},{8,12},{9,11},{10,... | collective-permute-start | bytes 1572872 | tf_op jit(solution)/shard_map/ppermute | solution.py:308
  114.7 10.1 %collective-permute-start.20 = (bf16[128,2048]{1,0:T(8,128)(2,1)S(1)}, bf16[128,2048]{1,0:T(8,128)(2,1)S(1)}, u32[]{:S(2)}, u32[]{:S(2)}) collective-permute-start(bf16[128,2048]{1,0:T(8,128)(2,1)S(1)} %get-tuple-element.40), channel_id=1, source_target_pairs={{0,2},{1,5},{2,0},{3,7},{4,6},{5,1},{6,4},{7,3},{8,10},{9,13},{10,... | collective-permute-start | bytes 1572872 | tf_op jit(solution)/shard_map/ppermute | solution.py:293
  118.3 9.2 %collective-permute-start.24 = (bf16[128,2048]{1,0:T(8,128)(2,1)S(1)}, bf16[128,2048]{1,0:T(8,128)(2,1)S(1)}, u32[]{:S(2)}, u32[]{:S(2)}) collective-permute-start(bf16[128,2048]{1,0:T(8,128)(2,1)S(1)} %get-tuple-element.42), channel_id=1, source_target_pairs={{0,4},{1,3},{2,6},{3,1},{4,0},{5,7},{6,2},{7,5},{8,12},{9,11},{10,... | collective-permute-start | bytes 1572872 | tf_op jit(solution)/shard_map/ppermute | solution.py:293
  125.0 6.4 %collective-permute-start.21 = (bf16[64,2048]{1,0:T(8,128)(2,1)S(1)}, bf16[64,2048]{1,0:T(8,128)(2,1)S(1)}, u32[]{:S(2)}, u32[]{:S(2)}) collective-permute-start(bf16[64,2048]{1,0:T(8,128)(2,1)S(1)} %slice.169), channel_id=1, source_target_pairs={{0,4},{1,3},{2,6},{3,1},{4,0},{5,7},{6,2},{7,5},{8,12},{9,11},{10,... | collective-permute-start | bytes 786440 | tf_op jit(solution)/shard_map/ppermute | solution.py:293
  127.7 6.4 %collective-permute-start.25 = (bf16[64,2048]{1,0:T(8,128)(2,1)S(1)}, bf16[64,2048]{1,0:T(8,128)(2,1)S(1)}, u32[]{:S(2)}, u32[]{:S(2)}) collective-permute-start(bf16[64,2048]{1,0:T(8,128)(2,1)S(1)} %slice.168), channel_id=1, source_target_pairs={{0,2},{1,5},{2,0},{3,7},{4,6},{5,1},{6,4},{7,3},{8,10},{9,13},{10,... | collective-permute-start | bytes 786440 | tf_op jit(solution)/shard_map/ppermute | solution.py:293
  131.6 5.0 %collective-permute-start.22 = (bf16[32,2048]{1,0:T(8,128)(2,1)S(1)}, bf16[32,2048]{1,0:T(8,128)(2,1)S(1)}, u32[]{:S(2)}, u32[]{:S(2)}) collective-permute-start(bf16[32,2048]{1,0:T(8,128)(2,1)S(1)} %slice.173), channel_id=1, source_target_pairs={{0,8},{1,9},{2,10},{3,11},{4,12},{5,13},{6,14},{7,15},{8,0},{9,1},... | collective-permute-start | bytes 393224 | tf_op jit(solution)/shard_map/ppermute | solution.py:293
  134.2 5.0 %collective-permute-start.26 = (bf16[32,2048]{1,0:T(8,128)(2,1)S(1)}, bf16[32,2048]{1,0:T(8,128)(2,1)S(1)}, u32[]{:S(2)}, u32[]{:S(2)}) collective-permute-start(bf16[32,2048]{1,0:T(8,128)(2,1)S(1)} %slice.172), channel_id=1, source_target_pairs={{0,8},{1,9},{2,10},{3,11},{4,12},{5,13},{6,14},{7,15},{8,0},{9,1},... | collective-permute-start | bytes 393224 | tf_op jit(solution)/shard_map/ppermute | solution.py:293
  136.6 5.4 %collective-permute-start.23 = (bf16[16,2048]{1,0:T(8,128)(2,1)S(1)}, bf16[16,2048]{1,0:T(8,128)(2,1)S(1)}, u32[]{:S(2)}, u32[]{:S(2)}) collective-permute-start(bf16[16,2048]{1,0:T(8,128)(2,1)S(1)} %slice.177), channel_id=1, source_target_pairs={{0,16},{1,17},{2,18},{3,19},{4,20},{5,21},{6,22},{7,23},{8,24},{9,... | collective-permute-start | bytes 196616 | tf_op jit(solution)/shard_map/ppermute | solution.py:293
  139.3 5.9 %collective-permute-start.27 = (bf16[16,2048]{1,0:T(8,128)(2,1)S(1)}, bf16[16,2048]{1,0:T(8,128)(2,1)S(1)}, u32[]{:S(2)}, u32[]{:S(2)}) collective-permute-start(bf16[16,2048]{1,0:T(8,128)(2,1)S(1)} %slice.176), channel_id=1, source_target_pairs={{0,16},{1,17},{2,18},{3,19},{4,20},{5,21},{6,22},{7,23},{8,24},{9,... | collective-permute-start | bytes 196616 | tf_op jit(solution)/shard_map/ppermute | solution.py:293
  (8 other events, 77.8 us)

commit v6 on v5

--- a/solution.py
+++ b/solution.py
@@ -19,7 +19,8 @@
 CHUNKS = 2
 
 
-GROUP = 4
+GROUP = 8
+PAD = 16
 
 
 def attend_kernel(core_ref, lengths_ref, q_ref, new_ref, cache_ref, out_ref, cache, q_rows, out_rows, new_rows, sems):
@@ -31,7 +32,7 @@
 
     def copy(side, at):
         part = pl.ds(at * GROUP, GROUP)
-        return pltpu.make_async_copy(cache_ref.at[side, part], cache.at[side, part], sems.at[side, at])
+        return pltpu.make_async_copy(cache_ref.at[side, part], cache.at[side, part, pl.ds(0, span)], sems.at[side, at])
 
     for at in range(rows // GROUP):
         copy(0, at).start()
@@ -40,7 +41,7 @@
     for h in range(heads):
         q_rows[h * rows : (h + 1) * rows, :] = q_ref[:, h * DH : (h + 1) * DH].astype(F32)
 
-    position = lax.broadcasted_iota(jnp.int32, (heads, span), 1)
+    position = lax.broadcasted_iota(jnp.int32, (span + PAD, heads), 0)
     row_group = lax.broadcasted_iota(jnp.int32, (heads, width), 0) // per_group
     lane_group = lax.broadcasted_iota(jnp.int32, (heads, width), 1) // DH
     own_lanes = row_group == lane_group
@@ -49,40 +50,28 @@
     def _(at):
         copy(0, at).wait()
         copy(1, at).wait()
+        scores, probs = [], []
         for i in range(GROUP):
             t = at * GROUP + i
+            for side in range(2):
+                cache[side, t, span:, :] = jnp.broadcast_to(new_rows[side, pl.ds(t, 1), :], (PAD, width)).astype(BF16)
             query = q_rows[pl.ds(t, heads, stride=rows), :]
-            new_key = new_rows[0, pl.ds(t, 1), :]
-            new_value = new_rows[1, pl.ds(t, 1), :]
-            spread = jnp.where(own_lanes, jnp.concatenate([query] * KVH, axis=1), 0.0)
-            scores = lax.dot_general(
-                spread.astype(BF16), cache[0, t], (((1,), (1,)), ((), ())), preferred_element_type=F32
+            spread = jnp.where(own_lanes, jnp.concatenate([query] * KVH, axis=1), 0.0).astype(BF16)
+            scores.append(
+                lax.dot_general(cache[0, t], spread, (((1,), (1,)), ((), ())), preferred_element_type=F32)
             )
-            own = jnp.concatenate(
-                [
-                    jnp.sum(
-                        query[g * per_group : (g + 1) * per_group] * new_key[:, g * DH : (g + 1) * DH],
-                        axis=1,
-                        keepdims=True,
-                    )
-                    for g in range(KVH)
-                ],
-                axis=0,
-            )
-            own = own * scale
-            scores = jnp.where(position < lengths_ref[t], scores * scale, -1e30)
-            peak = jnp.maximum(jnp.max(scores, axis=1, keepdims=True), own)
-            cached_exp = jnp.exp(scores - peak)
-            own_exp = jnp.exp(own - peak)
-            inverse = 1.0 / (jnp.sum(cached_exp, axis=1, keepdims=True) + own_exp)
-            probs = (cached_exp * inverse).astype(BF16)
-            own_probs = (own_exp * inverse).astype(BF16).astype(F32)
-            values = jnp.dot(probs, cache[1, t], preferred_element_type=F32)
+        for i in range(GROUP):
+            live = (position < lengths_ref[at * GROUP + i]) | (position == span)
+            score = jnp.where(live, scores[i] * scale, -1e30)
+            weights = jnp.exp(score - jnp.max(score, axis=0, keepdims=True))
+            probs.append((weights * (1.0 / jnp.sum(weights, axis=0, keepdims=True))).astype(BF16))
+        for i in range(GROUP):
+            t = at * GROUP + i
+            values = lax.dot_general(probs[i], cache[1, t], (((0,), (0,)), ((), ())), preferred_element_type=F32)
             for g in range(KVH):
-                part = slice(g * per_group, (g + 1) * per_group)
-                lanes = slice(g * DH, (g + 1) * DH)
-                value = values[part, lanes] + own_probs[part] * new_value[:, lanes]
-                out_rows[pl.ds(g * per_group * rows + t, per_group, stride=rows), :] = value
+                out_rows[pl.ds(g * per_group * rows + t, per_group, stride=rows), :] = values[
+                    g * per_group : (g + 1) * per_group, g * DH : (g + 1) * DH
+                ]
 
     chips = out_ref.shape[0]
     per_chip = heads // chips
@@ -98,7 +87,7 @@
 
 def attend(core, queries, new_kv, cache_kv, lengths, chips):
     rows, features = queries.shape
-    span, width = cache_kv.shape[2:]
+    sides, _, span, width = cache_kv.shape
     vmem = pl.BlockSpec(memory_space=pltpu.VMEM)
     smem = pl.BlockSpec(memory_space=pltpu.SMEM)
     return pl.pallas_call(
@@ -107,7 +96,7 @@
         in_specs=[smem, smem, vmem, vmem, pl.BlockSpec(memory_space=pl.ANY)],
         out_specs=vmem,
         scratch_shapes=[
-            pltpu.VMEM(cache_kv.shape, BF16),
+            pltpu.VMEM((sides, rows, span + PAD, width), BF16),
             pltpu.VMEM((features // DH * rows, DH), F32),
             pltpu.VMEM((features // DH * rows, DH), F32),
             pltpu.VMEM((2, rows, width), F32),
@@ -343,6 +332,7 @@
     down_other = lax.ppermute(w_down[0], "dp", core_swap)
 
     attn_out = attend(core[None], queries, new_kv, cache_kv, lengths, chips)
+    (out_other,) = bring(attn_out, (out_other,))
     blocks = lax.all_to_all(
         attn_out, "dp", split_axis=0, concat_axis=0, axis_index_groups=core_groups, tiled=True
     )

time: 146 us -> 139 us (0.952)
  Pallas kernels: 33.4 us -> 25.1 us
  waiting for transfers between devices: 75.4 us -> 67.2 us
  local copies, waits for them, and re-layouts: 1.36 us -> 7.92 us
  starting transfers between devices: 33.1 us -> 36.1 us
    pallas_call x1, Pallas kernels: 11.9 us -> 4.94 us  [attend(): pl.pallas_call(attend_kernel, out_shape=jax.ShapeDtypeStruct((chips, rows...]
    unnamed x27 -> x33, local copies, waits for them, and re-layouts: 1.12 us -> 7.67 us
    all_to_all x1, waiting for transfers between devices: 9.85 us -> 5.8 us  [per_device(): lax.all_to_all(attn_out, 'dp', split_axis=0, concat_axis=0, axis_index_gr...]
    ppermute x16, starting transfers between devices: 15 us -> 18.3 us  [reduce_slots(): came = lax.ppermute(sent[c], 'dp', swap_step(step, c, devices))]
    ppermute x16, waiting for transfers between devices: 47.6 us -> 44.7 us  [reduce_slots(): came = lax.ppermute(sent[c], 'dp', swap_step(step, c, devices))]
    pallas_call x2, Pallas kernels: 4 us -> 2.49 us  [project(): pl.pallas_call(functools.partial(project_kernel, chunk), out_shape=[jax.S...]
    pallas_call x1 -> x2, Pallas kernels: 6.56 us -> 6.71 us  [bring(): pl.pallas_call(bring_kernel, out_shape=[jax.ShapeDtypeStruct(a.shape, a.d...]
  transfers between devices with their start and end apart: 29 -> 29, of which waited for: 20 -> 19; matrix products, arithmetic and copies ran while one was open for 1% -> 1% of each run, Pallas kernels for 17% -> 11%
where the time goes in v6:
time: 139 us
  waiting for transfers between devices  67.2 us (48%)
  starting transfers between devices  36.1 us (26%)
  Pallas kernels  25.1 us (18%)
  local copies, waits for them, and re-layouts  7.92 us (6%)
  other arithmetic  2.2 us (2%)
    ppermute x16, waiting for transfers between devices, reduce_slots(): came = lax.ppermute(sent[c], 'dp', swap_step(step, c, devices))  44.7 us
    ppermute x16, starting transfers between devices, reduce_slots(): came = lax.ppermute(sent[c], 'dp', swap_step(step, c, devices))  18.3 us
    ppermute x8, waiting for transfers between devices, gather_slots(): came = lax.ppermute(own[c], 'dp', swap_step(step, c, devices))  16.7 us
    ppermute x8, starting transfers between devices, gather_slots(): came = lax.ppermute(own[c], 'dp', swap_step(step, c, devices))  8.45 us
    all_to_all x1, starting transfers between devices, per_device(): lax.all_to_all(attn_out, 'dp', split_axis=0, concat_axis=0, axis_index_gr...  8.33 us
    unnamed x33, local copies, waits for them, and re-layouts  7.67 us
    pallas_call x2, Pallas kernels, bring(): pl.pallas_call(bring_kernel, out_shape=[jax.ShapeDtypeStruct(a.shape, a.d...  6.71 us
    all_to_all x1, waiting for transfers between devices, per_device(): lax.all_to_all(attn_out, 'dp', split_axis=0, concat_axis=0, axis_index_gr...  5.8 us
  transfers between devices with their start and end apart: 29, of which 19 were waited for; matrix products, arithmetic and copies ran while one was open for 1% of the time, Pallas kernels for 11%

profile of v6, /device:TPU:0, one launch (start us, length us, event | category | flops | bytes accessed | tf_op | source)
XLA Modules:
  0.0 139.1 jit_solution(9442248253415344453)
XLA Ops:
  1.0 4.9 %shard_map.118.after_ref = bf16[16,16,512]{2,1,0:T(8,128)(2,1)} custom-call(s32[1]{0:T(128)} %bitcast.core_ref, s32[16]{0:T(128)} %lengths_ref.1, bf16[16,8192]{1,0:T(8,128)(2,1)} %q_ref.1, bf16[2,16,512]{2,1,0:T(8,128)(2,1)} %new_ref.1, bf16[2,16,128,512]{3,2,1,0:T(8,128)(2,1)} %cache_ref.1), custom_call_target="tpu_custom_call" | custom-call | flops 67108864 | bytes 4194304 | tf_op jit(solution)/shard_map/pallas_call | solution.py:93
  6.0 8.3 %all-to-all-start = ((bf16[16,16,512]{2,1,0:T(8,128)(2,1)}), bf16[16,16,512]{2,1,0:T(8,128)(2,1)S(1)}, u32[]{:S(2)}, u32[]{:S(2)}) async-start(bf16[16,16,512]{2,1,0:T(8,128)(2,1)} %shard_map.118.after_ref), calls=%async_computation | async-start | bytes 524288 | tf_op jit(solution)/shard_map/all_to_all | solution.py:336
  16.8 1.6 %copy-done.3 = bf16[256,4096]{1,0:T(8,128)(2,1)S(1)} copy-done((bf16[256,4096]{1,0:T(8,128)(2,1)S(1)}, bf16[256,4096]{1,0:T(8,128)(2,1)}, u32[]{:S(2)}) %copy-start.3) | copy-done | bytes 2097176
  18.5 5.8 %all-to-all-done.blocks_ref = bf16[16,16,512]{2,1,0:T(8,128)(2,1)S(1)} async-done(((bf16[16,16,512]{2,1,0:T(8,128)(2,1)}), bf16[16,16,512]{2,1,0:T(8,128)(2,1)S(1)}, u32[]{:S(2)}, u32[]{:S(2)}) %all-to-all-start) | async-done | bytes 262176 | tf_op jit(solution)/shard_map/all_to_all | solution.py:336
  24.3 1.6 %copy-done = bf16[256,4096]{1,0:T(8,128)(2,1)S(1)} copy-done((bf16[256,4096]{1,0:T(8,128)(2,1)S(1)}, bf16[256,4096]{1,0:T(8,128)(2,1)}, u32[]{:S(2)}) %copy-start) | copy-done | bytes 2097176
  30.2 11.9 %collective-permute-done.5 = bf16[128,2048]{1,0:T(8,128)(2,1)S(1)} collective-permute-done((bf16[128,2048]{1,0:T(8,128)(2,1)S(1)}, bf16[128,2048]{1,0:T(8,128)(2,1)S(1)}, u32[]{:S(2)}, u32[]{:S(2)}) %collective-permute-start.5) | collective-permute-done | bytes 524320 | tf_op jit(solution)/shard_map/ppermute | solution.py:282
  44.0 6.2 %collective-permute-done.6 = bf16[64,2048]{1,0:T(8,128)(2,1)S(1)} collective-permute-done((bf16[64,2048]{1,0:T(8,128)(2,1)S(1)}, bf16[64,2048]{1,0:T(8,128)(2,1)S(1)}, u32[]{:S(2)}, u32[]{:S(2)}) %collective-permute-start.6) | collective-permute-done | bytes 262176 | tf_op jit(solution)/shard_map/ppermute | solution.py:282
  50.5 2.1 %collective-permute-start.3 = (bf16[32,2048]{1,0:T(8,128)(2,1)S(1)}, bf16[32,2048]{1,0:T(8,128)(2,1)S(1)}, u32[]{:S(2)}, u32[]{:S(2)}) collective-permute-start(bf16[32,2048]{1,0:T(8,128)(2,1)S(1)} %slice.175), channel_id=1, source_target_pairs={{0,8},{1,9},{2,10},{3,11},{4,12},{5,13},{6,14},{7,15},{8,0},{9,1},... | collective-permute-start | bytes 393224 | tf_op jit(solution)/shard_map/ppermute | solution.py:282
  52.5 2.8 %collective-permute-done.7 = bf16[32,2048]{1,0:T(8,128)(2,1)S(1)} collective-permute-done((bf16[32,2048]{1,0:T(8,128)(2,1)S(1)}, bf16[32,2048]{1,0:T(8,128)(2,1)S(1)}, u32[]{:S(2)}, u32[]{:S(2)}) %collective-permute-start.7) | collective-permute-done | bytes 131104 | tf_op jit(solution)/shard_map/ppermute | solution.py:282
  55.4 1.6 %collective-permute-start.8 = (bf16[16,2048]{1,0:T(8,128)(2,1)S(1)}, bf16[16,2048]{1,0:T(8,128)(2,1)S(1)}, u32[]{:S(2)}, u32[]{:S(2)}) collective-permute-start(bf16[16,2048]{1,0:T(8,128)(2,1)S(1)} %slice.178), channel_id=1, source_target_pairs={{0,16},{1,17},{2,18},{3,19},{4,20},{5,21},{6,22},{7,23},{8,24},{9,... | collective-permute-start | bytes 196616 | tf_op jit(solution)/shard_map/ppermute | solution.py:282
  57.1 2.1 %collective-permute-start.4 = (bf16[16,2048]{1,0:T(8,128)(2,1)S(1)}, bf16[16,2048]{1,0:T(8,128)(2,1)S(1)}, u32[]{:S(2)}, u32[]{:S(2)}) collective-permute-start(bf16[16,2048]{1,0:T(8,128)(2,1)S(1)} %slice.179), channel_id=1, source_target_pairs={{0,16},{1,17},{2,18},{3,19},{4,20},{5,21},{6,22},{7,23},{8,24},{9,... | collective-permute-start | bytes 196616 | tf_op jit(solution)/shard_map/ppermute | solution.py:282
  59.2 1.9 %collective-permute-done.8 = bf16[16,2048]{1,0:T(8,128)(2,1)S(1)} collective-permute-done((bf16[16,2048]{1,0:T(8,128)(2,1)S(1)}, bf16[16,2048]{1,0:T(8,128)(2,1)S(1)}, u32[]{:S(2)}, u32[]{:S(2)}) %collective-permute-start.8) | collective-permute-done | bytes 65568 | tf_op jit(solution)/shard_map/ppermute | solution.py:282
  61.0 3.8 %collective-permute-done.4 = bf16[16,2048]{1,0:T(8,128)(2,1)S(1)} collective-permute-done((bf16[16,2048]{1,0:T(8,128)(2,1)S(1)}, bf16[16,2048]{1,0:T(8,128)(2,1)S(1)}, u32[]{:S(2)}, u32[]{:S(2)}) %collective-permute-start.4) | collective-permute-done | bytes 65568 | tf_op jit(solution)/shard_map/ppermute | solution.py:282
  65.3 3.0 %collective-permute-start.12 = (bf16[16,2176]{1,0:T(8,128)(2,1)S(1)}, bf16[16,2176]{1,0:T(8,128)(2,1)S(1)}, u32[]{:S(2)}, u32[]{:S(2)}) collective-permute-start(bf16[16,2176]{1,0:T(8,128)(2,1)S(1)} %pad_maximum_fusion.6), channel_id=1, source_target_pairs={{0,16},{1,17},{2,18},{3,19},{4,20},{5,21},{6,22},{7,23},{8,24},{9,... | collective-permute-start | bytes 208904 | tf_op jit(solution)/shard_map/ppermute | solution.py:297
  68.2 2.9 %collective-permute-done.16 = bf16[16,2048]{1,0:T(8,128)(2,1)S(1)} collective-permute-done((bf16[16,2048]{1,0:T(8,128)(2,1)S(1)}, bf16[16,2048]{1,0:T(8,128)(2,1)S(1)}, u32[]{:S(2)}, u32[]{:S(2)}) %collective-permute-start.16) | collective-permute-done | bytes 65568 | tf_op jit(solution)/shard_map/ppermute | solution.py:297
  71.9 2.0 %collective-permute-start.13 = (bf16[32,2176]{1,0:T(8,128)(2,1)S(1)}, bf16[32,2176]{1,0:T(8,128)(2,1)S(1)}, u32[]{:S(2)}, u32[]{:S(2)}) collective-permute-start(bf16[32,2176]{1,0:T(8,128)(2,1)S(1)} %pad_maximum_fusion.3), channel_id=1, source_target_pairs={{0,8},{1,9},{2,10},{3,11},{4,12},{5,13},{6,14},{7,15},{8,0},{9,1},... | collective-permute-start | bytes 417800 | tf_op jit(solution)/shard_map/ppermute | solution.py:297
  73.9 3.7 %collective-permute-done.13 = bf16[32,2176]{1,0:T(8,128)(2,1)S(1)} collective-permute-done((bf16[32,2176]{1,0:T(8,128)(2,1)S(1)}, bf16[32,2176]{1,0:T(8,128)(2,1)S(1)}, u32[]{:S(2)}, u32[]{:S(2)}) %collective-permute-start.13) | collective-permute-done | bytes 139296 | tf_op jit(solution)/shard_map/ppermute | solution.py:297
  78.9 8.4 %collective-permute-done.14 = bf16[64,2176]{1,0:T(8,128)(2,1)S(1)} collective-permute-done((bf16[64,2176]{1,0:T(8,128)(2,1)S(1)}, bf16[64,2176]{1,0:T(8,128)(2,1)S(1)}, u32[]{:S(2)}, u32[]{:S(2)}) %collective-permute-start.14) | collective-permute-done | bytes 278560 | tf_op jit(solution)/shard_map/ppermute | solution.py:297
  89.2 6.6 %shard_map.123 = (bf16[4096,768]{1,0:T(8,128)(2,1)S(1)}, bf16[4096,768]{1,0:T(8,128)(2,1)S(1)}, bf16[768,4096]{1,0:T(8,128)(2,1)S(1)}) custom-call(bf16[128,2048]{1,0:T(8,128)(2,1)S(1)} %constant_dynamic-update-slice_fusion.refs_2_.after_ref, bf16[4096,768]{1,0:T(8,128)(2,1)} %collective-permute-done.9.refs_0_, ...), custom_call_target="tpu_custom_call" | custom-call | bytes 18874368 | tf_op jit(solution)/shard_map/pallas_call | solution.py:168
  95.8 1.4 %collective-permute-done.19.refs_3_ = bf16[128,2048]{1,0:T(8,128)(2,1)S(1)} collective-permute-done((bf16[128,2048]{1,0:T(8,128)(2,1)S(1)}, bf16[128,2048]{1,0:T(8,128)(2,1)S(1)}, u32[]{:S(2)}, u32[]{:S(2)}) %collective-permute-start.19) | collective-permute-done | bytes 524320 | tf_op jit(solution)/shard_map/ppermute | solution.py:297
  99.2 4.0 %shard_map.122 = (bf16[256,4096]{1,0:T(8,128)(2,1)S(1)}, bf16[256,768]{1,0:T(8,128)(2,1)S(1)}, f32[256,1]{1,0:T(8,128)S(1)}) custom-call(s32[2]{0:T(128)S(1)} %pad_add_fusion.chip_ref, bf16[128,2176]{1,0:T(8,128)(2,1)S(1)} %pad_maximum_fusion.refs_0_, bf16[128,2176]{1,0:T(8,128)(2,1)S(1)} %collective-permute-done.15.refs_1_, ...), custom_call_target="tpu_custom_call" | custom-call | flops 3221225472 | bytes 12582912 | tf_op jit(solution)/shard_map/pallas_call | solution.py:227
  103.2 3.4 %shard_map.124.active1 = bf16[256,768]{1,0:T(8,128)(2,1)S(1)} custom-call(bf16[256,4096]{1,0:T(8,128)(2,1)S(1)} %get-tuple-element.31.tokens_ref, bf16[4096,768]{1,0:T(8,128)(2,1)S(1)} %get-tuple-element.35.gate_ref, bf16[4096,768]{1,0:T(8,128)(2,1)S(1)} %get-tuple-element.36.up_ref), custom_call_target="tpu_custom_call" | custom-call | flops 3221225472 | bytes 12582912 | tf_op jit(solution)/shard_map/pallas_call | solution.py:235
  106.7 1.8 %shard_map.125 = (bf16[128,2048]{1,0:T(8,128)(2,1)S(1)}, bf16[128,2048]{1,0:T(8,128)(2,1)S(1)}) custom-call(bf16[256,768]{1,0:T(8,128)(2,1)S(1)} %get-tuple-element.30.active0, bf16[256,768]{1,0:T(8,128)(2,1)S(1)} %shard_map.124.active1, f32[256,1]{1,0:T(8,128)S(1)} %get-tuple-element.37.weights_ref, bf16[768,4096]{1,0:T(8,128)(2,1)S(1)} %bitcast.8, ...), custom_call_target="tpu_custom_call" | custom-call | flops 1610612736 | bytes 6291456 | tf_op jit(solution)/shard_map/pallas_call | solution.py:246
  109.1 1.8 %shard_map.126 = (bf16[128,2048]{1,0:T(8,128)(2,1)S(1)}, bf16[128,2048]{1,0:T(8,128)(2,1)S(1)}) custom-call(bf16[256,768]{1,0:T(8,128)(2,1)S(1)} %get-tuple-element.30.active0, bf16[256,768]{1,0:T(8,128)(2,1)S(1)} %shard_map.124.active1, f32[256,1]{1,0:T(8,128)S(1)} %get-tuple-element.37.weights_ref, bf16[768,4096]{1,0:T(8,128)(2,1)S(1)} %bitcast.9, ...), custom_call_target="tpu_custom_call" | custom-call | flops 1610612736 | bytes 6291456 | tf_op jit(solution)/shard_map/pallas_call | solution.py:246
  110.9 1.9 %collective-permute-start.24 = (bf16[128,2048]{1,0:T(8,128)(2,1)S(1)}, bf16[128,2048]{1,0:T(8,128)(2,1)S(1)}, u32[]{:S(2)}, u32[]{:S(2)}) collective-permute-start(bf16[128,2048]{1,0:T(8,128)(2,1)S(1)} %get-tuple-element.42), channel_id=1, source_target_pairs={{0,4},{1,3},{2,6},{3,1},{4,0},{5,7},{6,2},{7,5},{8,12},{9,11},{10,... | collective-permute-start | bytes 1572872 | tf_op jit(solution)/shard_map/ppermute | solution.py:282
  112.8 5.3 %collective-permute-done.20 = bf16[128,2048]{1,0:T(8,128)(2,1)S(1)} collective-permute-done((bf16[128,2048]{1,0:T(8,128)(2,1)S(1)}, bf16[128,2048]{1,0:T(8,128)(2,1)S(1)}, u32[]{:S(2)}, u32[]{:S(2)}) %collective-permute-start.20) | collective-permute-done | bytes 524320 | tf_op jit(solution)/shard_map/ppermute | solution.py:282
  121.9 2.8 %collective-permute-done.21 = bf16[64,2048]{1,0:T(8,128)(2,1)S(1)} collective-permute-done((bf16[64,2048]{1,0:T(8,128)(2,1)S(1)}, bf16[64,2048]{1,0:T(8,128)(2,1)S(1)}, u32[]{:S(2)}, u32[]{:S(2)}) %collective-permute-start.21) | collective-permute-done | bytes 262176 | tf_op jit(solution)/shard_map/ppermute | solution.py:282
  125.5 1.8 %collective-permute-done.25 = bf16[64,2048]{1,0:T(8,128)(2,1)S(1)} collective-permute-done((bf16[64,2048]{1,0:T(8,128)(2,1)S(1)}, bf16[64,2048]{1,0:T(8,128)(2,1)S(1)}, u32[]{:S(2)}, u32[]{:S(2)}) %collective-permute-start.25) | collective-permute-done | bytes 262176 | tf_op jit(solution)/shard_map/ppermute | solution.py:282
  130.9 1.5 %collective-permute-done.26 = bf16[32,2048]{1,0:T(8,128)(2,1)S(1)} collective-permute-done((bf16[32,2048]{1,0:T(8,128)(2,1)S(1)}, bf16[32,2048]{1,0:T(8,128)(2,1)S(1)}, u32[]{:S(2)}, u32[]{:S(2)}) %collective-permute-start.26) | collective-permute-done | bytes 131104 | tf_op jit(solution)/shard_map/ppermute | solution.py:282
  132.5 1.7 %collective-permute-start.27 = (bf16[16,2048]{1,0:T(8,128)(2,1)S(1)}, bf16[16,2048]{1,0:T(8,128)(2,1)S(1)}, u32[]{:S(2)}, u32[]{:S(2)}) collective-permute-start(bf16[16,2048]{1,0:T(8,128)(2,1)S(1)} %slice.176), channel_id=1, source_target_pairs={{0,16},{1,17},{2,18},{3,19},{4,20},{5,21},{6,22},{7,23},{8,24},{9,... | collective-permute-start | bytes 196616 | tf_op jit(solution)/shard_map/ppermute | solution.py:282
  134.2 1.6 %collective-permute-done.23 = bf16[16,2048]{1,0:T(8,128)(2,1)S(1)} collective-permute-done((bf16[16,2048]{1,0:T(8,128)(2,1)S(1)}, bf16[16,2048]{1,0:T(8,128)(2,1)S(1)}, u32[]{:S(2)}, u32[]{:S(2)}) %collective-permute-start.23) | collective-permute-done | bytes 65568 | tf_op jit(solution)/shard_map/ppermute | solution.py:282
  135.8 2.6 %collective-permute-done.27 = bf16[16,2048]{1,0:T(8,128)(2,1)S(1)} collective-permute-done((bf16[16,2048]{1,0:T(8,128)(2,1)S(1)}, bf16[16,2048]{1,0:T(8,128)(2,1)S(1)}, u32[]{:S(2)}, u32[]{:S(2)}) %collective-permute-start.27) | collective-permute-done | bytes 65568 | tf_op jit(solution)/shard_map/ppermute | solution.py:282
  (114 shorter events, 26.0 us)
Async XLA Ops:
  0.0 14.5 %collective-permute-start = (bf16[256,4096]{1,0:T(8,128)(2,1)}, bf16[256,4096]{1,0:T(8,128)(2,1)S(1)}, u32[]{:S(2)}, u32[]{:S(2)}) collective-permute-start(bf16[256,4096]{1,0:T(8,128)(2,1)} %own_ref.3), channel_id=1, source_target_pairs={{0,1},{1,0},{2,3},{3,2},{4,5},{5,4},{6,7},{7,6},{8,9},{9,8},{10,11... | collective-permute-start | bytes 6291464 | tf_op jit(solution)/shard_map/ppermute | solution.py:329
  0.5 64.7 %collective-permute-start.11 = (bf16[768,4096]{1,0:T(8,128)(2,1)}, bf16[768,4096]{1,0:T(8,128)(2,1)}, u32[]{:S(2)}, u32[]{:S(2)}) collective-permute-start(bf16[768,4096]{1,0:T(8,128)(2,1)} %bitcast.5), channel_id=1, source_target_pairs={{0,1},{1,0},{2,3},{3,2},{4,5},{5,4},{6,7},{7,6},{8,9},{9,8},{10,11... | collective-permute-start | bytes 18874376 | tf_op jit(solution)/shard_map/ppermute | solution.py:332
  0.5 64.6 %collective-permute-start.10 = (bf16[4096,768]{1,0:T(8,128)(2,1)}, bf16[4096,768]{1,0:T(8,128)(2,1)}, u32[]{:S(2)}, u32[]{:S(2)}) collective-permute-start(bf16[4096,768]{1,0:T(8,128)(2,1)} %bitcast.14), channel_id=1, source_target_pairs={{0,1},{1,0},{2,3},{3,2},{4,5},{5,4},{6,7},{7,6},{8,9},{9,8},{10,11... | collective-permute-start | bytes 18874376 | tf_op jit(solution)/shard_map/ppermute | solution.py:331
  1.0 64.2 %collective-permute-start.9 = (bf16[4096,768]{1,0:T(8,128)(2,1)}, bf16[4096,768]{1,0:T(8,128)(2,1)}, u32[]{:S(2)}, u32[]{:S(2)}) collective-permute-start(bf16[4096,768]{1,0:T(8,128)(2,1)} %bitcast.10), channel_id=1, source_target_pairs={{0,1},{1,0},{2,3},{3,2},{4,5},{5,4},{6,7},{7,6},{8,9},{9,8},{10,11... | collective-permute-start | bytes 18874376 | tf_op jit(solution)/shard_map/ppermute | solution.py:330
  1.0 13.3 %copy-start.6 = (s32[16,8]{0,1:T(8,128)S(1)}, s32[16,8]{0,1:T(8,128)}, u32[]{:S(2)}) copy-start(s32[16,8]{0,1:T(8,128)} %param.22) | copy-start | bytes 1540
  1.0 13.4 %copy-start.7 = (f32[16,8]{0,1:T(8,128)S(1)}, f32[16,8]{0,1:T(8,128)}, u32[]{:S(2)}) copy-start(f32[16,8]{0,1:T(8,128)} %param.23) | copy-start | bytes 1540
  6.0 18.4 %all-to-all-start = ((bf16[16,16,512]{2,1,0:T(8,128)(2,1)}), bf16[16,16,512]{2,1,0:T(8,128)(2,1)S(1)}, u32[]{:S(2)}, u32[]{:S(2)}) async-start(bf16[16,16,512]{2,1,0:T(8,128)(2,1)} %shard_map.118.after_ref), calls=%async_computation | async-start | bytes 524288 | tf_op jit(solution)/shard_map/all_to_all | solution.py:336
  27.2 14.9 %collective-permute-start.5 = (bf16[128,2048]{1,0:T(8,128)(2,1)S(1)}, bf16[128,2048]{1,0:T(8,128)(2,1)S(1)}, u32[]{:S(2)}, u32[]{:S(2)}) collective-permute-start(bf16[128,2048]{1,0:T(8,128)(2,1)S(1)} %get-tuple-element.27), channel_id=1, source_target_pairs={{0,4},{1,3},{2,6},{3,1},{4,0},{5,7},{6,2},{7,5},{8,12},{9,11},{10,... | collective-permute-start | bytes 1572872 | tf_op jit(solution)/shard_map/ppermute | solution.py:282
  29.6 13.5 %collective-permute-start.1 = (bf16[128,2048]{1,0:T(8,128)(2,1)S(1)}, bf16[128,2048]{1,0:T(8,128)(2,1)S(1)}, u32[]{:S(2)}, u32[]{:S(2)}) collective-permute-start(bf16[128,2048]{1,0:T(8,128)(2,1)S(1)} %get-tuple-element.25), channel_id=1, source_target_pairs={{0,2},{1,5},{2,0},{3,7},{4,6},{5,1},{6,4},{7,3},{8,10},{9,13},{10,... | collective-permute-start | bytes 1572872 | tf_op jit(solution)/shard_map/ppermute | solution.py:282
  42.2 8.0 %collective-permute-start.6 = (bf16[64,2048]{1,0:T(8,128)(2,1)S(1)}, bf16[64,2048]{1,0:T(8,128)(2,1)S(1)}, u32[]{:S(2)}, u32[]{:S(2)}) collective-permute-start(bf16[64,2048]{1,0:T(8,128)(2,1)S(1)} %slice.170), channel_id=1, source_target_pairs={{0,2},{1,5},{2,0},{3,7},{4,6},{5,1},{6,4},{7,3},{8,10},{9,13},{10,... | collective-permute-start | bytes 786440 | tf_op jit(solution)/shard_map/ppermute | solution.py:282
  43.2 21.7 %copy-start.4 = (bf16[16,4096]{1,0:T(8,128)(2,1)S(1)}, bf16[16,4096]{1,0:T(8,128)(2,1)}, u32[]{:S(2)}) copy-start(bf16[16,4096]{1,0:T(8,128)(2,1)} %param.12) | copy-start | bytes 393220
  43.2 7.2 %collective-permute-start.2 = (bf16[64,2048]{1,0:T(8,128)(2,1)S(1)}, bf16[64,2048]{1,0:T(8,128)(2,1)S(1)}, u32[]{:S(2)}, u32[]{:S(2)}) collective-permute-start(bf16[64,2048]{1,0:T(8,128)(2,1)S(1)} %slice.171), channel_id=1, source_target_pairs={{0,4},{1,3},{2,6},{3,1},{4,0},{5,7},{6,2},{7,5},{8,12},{9,11},{10,... | collective-permute-start | bytes 786440 | tf_op jit(solution)/shard_map/ppermute | solution.py:282
  50.3 5.0 %collective-permute-start.7 = (bf16[32,2048]{1,0:T(8,128)(2,1)S(1)}, bf16[32,2048]{1,0:T(8,128)(2,1)S(1)}, u32[]{:S(2)}, u32[]{:S(2)}) collective-permute-start(bf16[32,2048]{1,0:T(8,128)(2,1)S(1)} %slice.174), channel_id=1, source_target_pairs={{0,8},{1,9},{2,10},{3,11},{4,12},{5,13},{6,14},{7,15},{8,0},{9,1},... | collective-permute-start | bytes 393224 | tf_op jit(solution)/shard_map/ppermute | solution.py:282
  50.5 6.5 %collective-permute-start.3 = (bf16[32,2048]{1,0:T(8,128)(2,1)S(1)}, bf16[32,2048]{1,0:T(8,128)(2,1)S(1)}, u32[]{:S(2)}, u32[]{:S(2)}) collective-permute-start(bf16[32,2048]{1,0:T(8,128)(2,1)S(1)} %slice.175), channel_id=1, source_target_pairs={{0,8},{1,9},{2,10},{3,11},{4,12},{5,13},{6,14},{7,15},{8,0},{9,1},... | collective-permute-start | bytes 393224 | tf_op jit(solution)/shard_map/ppermute | solution.py:282
  55.4 5.7 %collective-permute-start.8 = (bf16[16,2048]{1,0:T(8,128)(2,1)S(1)}, bf16[16,2048]{1,0:T(8,128)(2,1)S(1)}, u32[]{:S(2)}, u32[]{:S(2)}) collective-permute-start(bf16[16,2048]{1,0:T(8,128)(2,1)S(1)} %slice.178), channel_id=1, source_target_pairs={{0,16},{1,17},{2,18},{3,19},{4,20},{5,21},{6,22},{7,23},{8,24},{9,... | collective-permute-start | bytes 196616 | tf_op jit(solution)/shard_map/ppermute | solution.py:282
  57.1 7.8 %collective-permute-start.4 = (bf16[16,2048]{1,0:T(8,128)(2,1)S(1)}, bf16[16,2048]{1,0:T(8,128)(2,1)S(1)}, u32[]{:S(2)}, u32[]{:S(2)}) collective-permute-start(bf16[16,2048]{1,0:T(8,128)(2,1)S(1)} %slice.179), channel_id=1, source_target_pairs={{0,16},{1,17},{2,18},{3,19},{4,20},{5,21},{6,22},{7,23},{8,24},{9,... | collective-permute-start | bytes 196616 | tf_op jit(solution)/shard_map/ppermute | solution.py:282
  65.2 5.9 %collective-permute-start.16 = (bf16[16,2048]{1,0:T(8,128)(2,1)S(1)}, bf16[16,2048]{1,0:T(8,128)(2,1)S(1)}, u32[]{:S(2)}, u32[]{:S(2)}) collective-permute-start(bf16[16,2048]{1,0:T(8,128)(2,1)S(1)} %get-tuple-element.29), channel_id=1, source_target_pairs={{0,16},{1,17},{2,18},{3,19},{4,20},{5,21},{6,22},{7,23},{8,24},{9,... | collective-permute-start | bytes 196616 | tf_op jit(solution)/shard_map/ppermute | solution.py:297
  65.3 6.6 %collective-permute-start.12 = (bf16[16,2176]{1,0:T(8,128)(2,1)S(1)}, bf16[16,2176]{1,0:T(8,128)(2,1)S(1)}, u32[]{:S(2)}, u32[]{:S(2)}) collective-permute-start(bf16[16,2176]{1,0:T(8,128)(2,1)S(1)} %pad_maximum_fusion.6), channel_id=1, source_target_pairs={{0,16},{1,17},{2,18},{3,19},{4,20},{5,21},{6,22},{7,23},{8,24},{9,... | collective-permute-start | bytes 208904 | tf_op jit(solution)/shard_map/ppermute | solution.py:297
  71.1 6.6 %collective-permute-start.17 = (bf16[32,2048]{1,0:T(8,128)(2,1)S(1)}, bf16[32,2048]{1,0:T(8,128)(2,1)S(1)}, u32[]{:S(2)}, u32[]{:S(2)}) collective-permute-start(bf16[32,2048]{1,0:T(8,128)(2,1)S(1)} %pad_maximum_fusion.4), channel_id=1, source_target_pairs={{0,8},{1,9},{2,10},{3,11},{4,12},{5,13},{6,14},{7,15},{8,0},{9,1},... | collective-permute-start | bytes 393224 | tf_op jit(solution)/shard_map/ppermute | solution.py:297
  71.9 5.8 %collective-permute-start.13 = (bf16[32,2176]{1,0:T(8,128)(2,1)S(1)}, bf16[32,2176]{1,0:T(8,128)(2,1)S(1)}, u32[]{:S(2)}, u32[]{:S(2)}) collective-permute-start(bf16[32,2176]{1,0:T(8,128)(2,1)S(1)} %pad_maximum_fusion.3), channel_id=1, source_target_pairs={{0,8},{1,9},{2,10},{3,11},{4,12},{5,13},{6,14},{7,15},{8,0},{9,1},... | collective-permute-start | bytes 417800 | tf_op jit(solution)/shard_map/ppermute | solution.py:297
  77.7 9.6 %collective-permute-start.14 = (bf16[64,2176]{1,0:T(8,128)(2,1)S(1)}, bf16[64,2176]{1,0:T(8,128)(2,1)S(1)}, u32[]{:S(2)}, u32[]{:S(2)}) collective-permute-start(bf16[64,2176]{1,0:T(8,128)(2,1)S(1)} %pad_maximum_fusion.1), channel_id=1, source_target_pairs={{0,4},{1,3},{2,6},{3,1},{4,0},{5,7},{6,2},{7,5},{8,12},{9,11},{10,... | collective-permute-start | bytes 835592 | tf_op jit(solution)/shard_map/ppermute | solution.py:297
  77.8 10.2 %collective-permute-start.18 = (bf16[64,2048]{1,0:T(8,128)(2,1)S(1)}, bf16[64,2048]{1,0:T(8,128)(2,1)S(1)}, u32[]{:S(2)}, u32[]{:S(2)}) collective-permute-start(bf16[64,2048]{1,0:T(8,128)(2,1)S(1)} %pad_maximum_fusion.2), channel_id=1, source_target_pairs={{0,2},{1,5},{2,0},{3,7},{4,6},{5,1},{6,4},{7,3},{8,10},{9,13},{10,... | collective-permute-start | bytes 786440 | tf_op jit(solution)/shard_map/ppermute | solution.py:297
  87.3 9.9 %collective-permute-start.15 = (bf16[128,2176]{1,0:T(8,128)(2,1)S(1)}, bf16[128,2176]{1,0:T(8,128)(2,1)S(1)}, u32[]{:S(2)}, u32[]{:S(2)}) collective-permute-start(bf16[128,2176]{1,0:T(8,128)(2,1)S(1)} %pad_maximum_fusion.refs_0_), channel_id=1, source_target_pairs={{0,2},{1,5},{2,0},{3,7},{4,6},{5,1},{6,4},{7,3},{8,10},{9,13},{10,... | collective-permute-start | bytes 1671176 | tf_op jit(solution)/shard_map/ppermute | solution.py:297
  88.0 9.2 %collective-permute-start.19 = (bf16[128,2048]{1,0:T(8,128)(2,1)S(1)}, bf16[128,2048]{1,0:T(8,128)(2,1)S(1)}, u32[]{:S(2)}, u32[]{:S(2)}) collective-permute-start(bf16[128,2048]{1,0:T(8,128)(2,1)S(1)} %constant_dynamic-update-slice_fusion.refs_2_.after_ref), channel_id=1, source_target_pairs={{0,4},{1,3},{2,6},{3,1},{4,0},{5,7},{6,2},{7,5},{8,12},{9,11},{10,... | collective-permute-start | bytes 1572872 | tf_op jit(solution)/shard_map/ppermute | solution.py:297
  108.5 9.6 %collective-permute-start.20 = (bf16[128,2048]{1,0:T(8,128)(2,1)S(1)}, bf16[128,2048]{1,0:T(8,128)(2,1)S(1)}, u32[]{:S(2)}, u32[]{:S(2)}) collective-permute-start(bf16[128,2048]{1,0:T(8,128)(2,1)S(1)} %get-tuple-element.40), channel_id=1, source_target_pairs={{0,2},{1,5},{2,0},{3,7},{4,6},{5,1},{6,4},{7,3},{8,10},{9,13},{10,... | collective-permute-start | bytes 1572872 | tf_op jit(solution)/shard_map/ppermute | solution.py:282
  110.9 9.8 %collective-permute-start.24 = (bf16[128,2048]{1,0:T(8,128)(2,1)S(1)}, bf16[128,2048]{1,0:T(8,128)(2,1)S(1)}, u32[]{:S(2)}, u32[]{:S(2)}) collective-permute-start(bf16[128,2048]{1,0:T(8,128)(2,1)S(1)} %get-tuple-element.42), channel_id=1, source_target_pairs={{0,4},{1,3},{2,6},{3,1},{4,0},{5,7},{6,2},{7,5},{8,12},{9,11},{10,... | collective-permute-start | bytes 1572872 | tf_op jit(solution)/shard_map/ppermute | solution.py:282
  118.2 6.4 %collective-permute-start.21 = (bf16[64,2048]{1,0:T(8,128)(2,1)S(1)}, bf16[64,2048]{1,0:T(8,128)(2,1)S(1)}, u32[]{:S(2)}, u32[]{:S(2)}) collective-permute-start(bf16[64,2048]{1,0:T(8,128)(2,1)S(1)} %slice.169), channel_id=1, source_target_pairs={{0,4},{1,3},{2,6},{3,1},{4,0},{5,7},{6,2},{7,5},{8,12},{9,11},{10,... | collective-permute-start | bytes 786440 | tf_op jit(solution)/shard_map/ppermute | solution.py:282
  120.9 6.4 %collective-permute-start.25 = (bf16[64,2048]{1,0:T(8,128)(2,1)S(1)}, bf16[64,2048]{1,0:T(8,128)(2,1)S(1)}, u32[]{:S(2)}, u32[]{:S(2)}) collective-permute-start(bf16[64,2048]{1,0:T(8,128)(2,1)S(1)} %slice.168), channel_id=1, source_target_pairs={{0,2},{1,5},{2,0},{3,7},{4,6},{5,1},{6,4},{7,3},{8,10},{9,13},{10,... | collective-permute-start | bytes 786440 | tf_op jit(solution)/shard_map/ppermute | solution.py:282
  124.7 5.0 %collective-permute-start.22 = (bf16[32,2048]{1,0:T(8,128)(2,1)S(1)}, bf16[32,2048]{1,0:T(8,128)(2,1)S(1)}, u32[]{:S(2)}, u32[]{:S(2)}) collective-permute-start(bf16[32,2048]{1,0:T(8,128)(2,1)S(1)} %slice.173), channel_id=1, source_target_pairs={{0,8},{1,9},{2,10},{3,11},{4,12},{5,13},{6,14},{7,15},{8,0},{9,1},... | collective-permute-start | bytes 393224 | tf_op jit(solution)/shard_map/ppermute | solution.py:282
  127.4 5.0 %collective-permute-start.26 = (bf16[32,2048]{1,0:T(8,128)(2,1)S(1)}, bf16[32,2048]{1,0:T(8,128)(2,1)S(1)}, u32[]{:S(2)}, u32[]{:S(2)}) collective-permute-start(bf16[32,2048]{1,0:T(8,128)(2,1)S(1)} %slice.172), channel_id=1, source_target_pairs={{0,8},{1,9},{2,10},{3,11},{4,12},{5,13},{6,14},{7,15},{8,0},{9,1},... | collective-permute-start | bytes 393224 | tf_op jit(solution)/shard_map/ppermute | solution.py:282
  129.8 5.9 %collective-permute-start.23 = (bf16[16,2048]{1,0:T(8,128)(2,1)S(1)}, bf16[16,2048]{1,0:T(8,128)(2,1)S(1)}, u32[]{:S(2)}, u32[]{:S(2)}) collective-permute-start(bf16[16,2048]{1,0:T(8,128)(2,1)S(1)} %slice.177), channel_id=1, source_target_pairs={{0,16},{1,17},{2,18},{3,19},{4,20},{5,21},{6,22},{7,23},{8,24},{9,... | collective-permute-start | bytes 196616 | tf_op jit(solution)/shard_map/ppermute | solution.py:282
  132.5 5.9 %collective-permute-start.27 = (bf16[16,2048]{1,0:T(8,128)(2,1)S(1)}, bf16[16,2048]{1,0:T(8,128)(2,1)S(1)}, u32[]{:S(2)}, u32[]{:S(2)}) collective-permute-start(bf16[16,2048]{1,0:T(8,128)(2,1)S(1)} %slice.176), channel_id=1, source_target_pairs={{0,16},{1,17},{2,18},{3,19},{4,20},{5,21},{6,22},{7,23},{8,24},{9,... | collective-permute-start | bytes 196616 | tf_op jit(solution)/shard_map/ppermute | solution.py:282
  (11 other events, 51.0 us)

commit v7 on v6

--- a/solution.py
+++ b/solution.py
@@ -16,7 +16,8 @@
 BF16 = jnp.bfloat16
 
 
-CHUNKS = 2
+REDUCE = ((4, (0, 1, 2)), (4, (1, 0, 2)))
+GATHER = ((3, (0, 1, 2)), (3, (1, 0, 2)), (2, (2, 0, 1)))
 
 
 GROUP = 8
@@ -110,15 +111,23 @@
 P_TILE = 512
 
 
-def quarters(chunk, half):
-    size = half // 2
-    order = (0, 2, 1, 3) if chunk % 2 else (0, 1, 2, 3)
-    for place, quarter in enumerate(order):
-        at = place % 2 * size
-        yield place // 2, slice(at, at + size), slice(quarter * size, (quarter + 1) * size)
-
-
-def project_kernel(chunk, index_ref, blocks_ref, own_ref, other_ref, keep_ref, send_ref, ordered):
+def spans(chunks, width):
+    at = 0
+    for eighths, order in chunks:
+        size = width * eighths // 8
+        yield at, size, order
+        at += size
+
+
+def octants(order, half):
+    size = half // 4
+    for place in range(8):
+        base = sum((place >> (2 - step) & 1) << (2 - order[step]) for step in range(3))
+        at = place % 4 * size
+        yield place // 4, slice(at, at + size), slice(base * size, (base + 1) * size)
+
+
+def project_kernel(order, after_ref, index_ref, blocks_ref, own_ref, other_ref, keep_ref, send_ref, ordered):
     chips, rows, features = blocks_ref.shape
     half = features // 2
     for k in range(chips):
@@ -127,7 +136,7 @@
         lanes = slice(at, at + P_TILE)
         total = jnp.dot(ordered[:, :half], own_ref[:, lanes], preferred_element_type=F32)
         total = total + jnp.dot(ordered[:, half:], other_ref[:, lanes], preferred_element_type=F32)
-        for to, here, where in quarters(chunk, keep_ref.shape[0]):
+        for to, here, where in octants(order, keep_ref.shape[0]):
             (keep_ref, send_ref)[to][here, lanes] = total[where].astype(BF16)
 
 
@@ -135,22 +144,28 @@
     return pl.BlockSpec(shape, lambda s: (0,) * len(shape))
 
 
-def project(chunk, index, blocks, own, other):
+def project(span, after, index, blocks, own, other):
     chips, rows, features = blocks.shape
-    depth, width = own.shape
-    size = width // CHUNKS
-    weights = pl.BlockSpec((depth, size), lambda s: (0, chunk))
+    depth = own.shape[0]
+    first, size, order = span
+    weights = pl.BlockSpec((depth, size), lambda s: (0, first // size))
     half = (chips * rows // 2, size)
     return pl.pallas_call(
-        functools.partial(project_kernel, chunk),
+        functools.partial(project_kernel, order),
         out_shape=[jax.ShapeDtypeStruct(half, BF16)] * 2,
         grid=(1,),
-        in_specs=[pl.BlockSpec(memory_space=pltpu.SMEM), whole(blocks.shape), weights, weights],
+        in_specs=[
+            pl.BlockSpec(memory_space=pl.ANY),
+            pl.BlockSpec(memory_space=pltpu.SMEM),
+            whole(blocks.shape),
+            weights,
+            weights,
+        ],
         out_specs=[whole(half)] * 2,
         scratch_shapes=[pltpu.VMEM((chips * rows, features), BF16)],
         compiler_params=pltpu.CompilerParams(vmem_limit_bytes=16 << 20),
         cost_estimate=pl.CostEstimate(flops=2 * blocks.size * size, bytes_accessed=4 * depth * size, transcendentals=0),
-    )(index, blocks, own, other)
+    )(after, index, blocks, own, other)
 
 
 def bring_kernel(after_ref, *refs):
@@ -189,12 +204,12 @@
 
 
 def first_kernel(chip_ref, *refs):
-    pieces, (gate_ref, up_ref, tokens_ref, active_ref, weights_ref) = refs[: 2 * CHUNKS], refs[2 * CHUNKS :]
+    pieces, (gate_ref, up_ref, tokens_ref, active_ref, weights_ref) = refs[:-5], refs[-5:]
     half = pieces[0].shape[0]
-    chunk = tokens_ref.shape[1] // CHUNKS
-    for c in range(CHUNKS):
-        for side, here, where in quarters(c, half):
-            tokens_ref[where, c * chunk : (c + 1) * chunk] = pieces[2 * c + side][here, :chunk]
+    for c, (at, size, order) in enumerate(spans(GATHER, tokens_ref.shape[1])):
+        for side, here, where in octants(order, half):
+            tokens_ref[where, at : at + size] = pieces[2 * c + side][here, :size]
+    chunk = GATHER[0][0] * tokens_ref.shape[1] // 8
     first, chips = chip_ref[0], chip_ref[1]
     lane = lax.broadcasted_iota(jnp.int32, (half, pieces[0].shape[1] - chunk), 1)
     mine = (lane == first) | (lane == first + chips) | (lane == first + 2 * chips)
@@ -205,13 +220,13 @@
     activate(tokens_ref, gate_ref, up_ref, active_ref)
 
 
-def down_kernel(chunk, active0, active1, weights_ref, down0, down1, keep_ref, send_ref):
+def down_kernel(order, after_ref, active0, active1, weights_ref, down0, down1, keep_ref, send_ref):
     for at in range(0, keep_ref.shape[1], N_TILE):
         lanes = slice(at, at + N_TILE)
         total = jnp.dot(active0[...], down0[:, lanes], preferred_element_type=F32)
         total = total + jnp.dot(active1[...], down1[:, lanes], preferred_element_type=F32)
         total = total * weights_ref[...]
-        for to, here, where in quarters(chunk, keep_ref.shape[0]):
+        for to, here, where in octants(order, keep_ref.shape[0]):
             (keep_ref, send_ref)[to][here, lanes] = total[where].astype(BF16)
 
 
@@ -219,7 +234,6 @@
     half = pieces[0].shape[0]
     rows = 2 * half
     width, hidden = gates[0].shape
-    size = width // CHUNKS
     params = pltpu.CompilerParams(vmem_limit_bytes=20 << 20)
     cost = pl.CostEstimate(flops=4 * rows * width * hidden, bytes_accessed=4 * width * hidden, transcendentals=rows * hidden)
     vmem = pl.BlockSpec(memory_space=pltpu.VMEM)
@@ -227,7 +241,7 @@
     tokens, active0, weights = pl.pallas_call(
         first_kernel,
         out_shape=[jax.ShapeDtypeStruct((rows, width), BF16), active, jax.ShapeDtypeStruct((rows, 1), F32)],
-        in_specs=[pl.BlockSpec(memory_space=pltpu.SMEM)] + [vmem] * (2 * CHUNKS + 2),
+        in_specs=[pl.BlockSpec(memory_space=pltpu.SMEM)] + [vmem] * (len(pieces) + 2),
         out_specs=[vmem] * 3,
         compiler_params=params,
         cost_estimate=cost,
@@ -241,17 +255,18 @@
         cost_estimate=cost,
     )(tokens, gates[1], ups[1])
     results = []
-    for c in range(CHUNKS):
-        block = pl.BlockSpec((hidden, size), lambda s: (0, c))
+    for first, size, order in spans(REDUCE, width):
+        block = pl.BlockSpec((hidden, size), functools.partial(lambda s, index: (0, index), index=first // size))
         results += pl.pallas_call(
-            functools.partial(down_kernel, c),
+            functools.partial(down_kernel, order),
             out_shape=[jax.ShapeDtypeStruct((half, size), BF16)] * 2,
             grid=(1,),
-            in_specs=[whole((rows, hidden)), whole((rows, hidden)), whole((rows, 1)), block, block],
+            in_specs=[pl.BlockSpec(memory_space=pl.ANY), whole((rows, hidden)), whole((rows, hidden)), whole((rows, 1))]
+            + [block, block],
             out_specs=[whole((half, size))] * 2,
             compiler_params=params,
             cost_estimate=pl.CostEstimate(flops=4 * rows * size * hidden, bytes_accessed=4 * size * hidden, transcendentals=0),
-        )(active0, active1, weights, *downs)
+        )(results[-1] if results else active1, active0, active1, weights, *downs)
     return results
 
 
@@ -259,27 +274,27 @@
     values = [part.astype(F32) for part in hidden_state]
     square = sum(jnp.sum(part * part, axis=-1, keepdims=True) for part in values)
     scale = lax.rsqrt(square / norm_gain.size + 1e-06)
-    gains = jnp.split(norm_gain, CHUNKS)
+    gains = [norm_gain[at : at + size] for at, size, _ in spans(REDUCE, norm_gain.size)]
     return [(part * scale * gain).astype(BF16) for part, gain in zip(values, gains)]
 
 
-def step_bits(devices):
-    bits = [1 << i for i in range(1, devices.bit_length() - 1)]
-    other = bits[1::-1] + bits[2:] if len(bits) > 1 else bits
-    return bits, other
-
-
-def swap_step(step, chunk, devices):
-    orders = step_bits(devices)
-    return [(i, i ^ orders[(i + chunk) & 1][step]) for i in range(devices)]
+def step_bits(devices, order=(0, 1, 2)):
+    even = [1 << i for i in range(1, devices.bit_length() - 1)]
+    odd = even[1::-1] + even[2:]
+    return [[bits[i] for i in order] + bits[3:] for bits in (even, odd)]
+
+
+def swap_step(step, order, devices):
+    orders = step_bits(devices, order)
+    return [(i, i ^ orders[i & 1][step]) for i in range(devices)]
 
 
 def reduce_slots(pieces, devices):
     steps = devices.bit_length() - 2
     kept, sent = list(pieces[::2]), list(pieces[1::2])
     for step in range(steps):
-        for c in range(CHUNKS):
-            came = lax.ppermute(sent[c], "dp", swap_step(step, c, devices))
+        for c, (_, order) in enumerate(REDUCE):
+            came = lax.ppermute(sent[c], "dp", swap_step(step, order, devices))
             kept[c] = kept[c].astype(F32) + came.astype(F32)
             half = kept[c].shape[0] // 2
             if step < steps - 1:
@@ -293,8 +308,8 @@
     steps = devices.bit_length() - 2
     pieces = []
     for step in reversed(range(steps)):
-        for c in range(CHUNKS):
-            came = lax.ppermute(own[c], "dp", swap_step(step, c, devices))
+        for c, (_, order) in enumerate(GATHER):
+            came = lax.ppermute(own[c], "dp", swap_step(step, order, devices))
             if step == 0:
                 pieces += [own[c], came]
             else:
@@ -316,7 +331,7 @@
     expert_ids,
     combine_weights,
 ):
-    rows = residual.shape[0]
+    rows, width = residual.shape
     devices = lax.axis_size("dp")
     chips = devices // 2
     me = lax.axis_index("dp")
@@ -332,7 +347,7 @@
     down_other = lax.ppermute(w_down[0], "dp", core_swap)
 
     attn_out = attend(core[None], queries, new_kv, cache_kv, lengths, chips)
-    (out_other,) = bring(attn_out, (out_other,))
+    out_own, out_other = bring(attn_out, (out_weight, out_other))
     blocks = lax.all_to_all(
         attn_out, "dp", split_axis=0, concat_axis=0, axis_index_groups=core_groups, tiled=True
     )
@@ -343,10 +358,13 @@
     for step in range(steps):
         here = jnp.where(core == 0, orders[0][step], orders[1][step]) // 2
         offset = offset + here * ((slot >> (steps - 1 - step)) & 1)
-    partial = [part for c in range(CHUNKS) for part in project(c, chip ^ offset, blocks, out_weight, out_other)]
+    cuts = list(spans(REDUCE, width))
+    partial = []
+    for span in cuts:
+        partial += project(span, partial[-1] if partial else blocks, chip ^ offset, blocks, out_own, out_other)
     projected = reduce_slots(partial, devices)
     hidden_state = [
-        (part.astype(F32) + add).astype(BF16) for part, add in zip(jnp.split(residual, CHUNKS, axis=1), projected)
+        (residual[:, at : at + size].astype(F32) + add).astype(BF16) for (at, size, _), add in zip(cuts, projected)
     ]
     normed = normalize(hidden_state, norm_gain)
 
@@ -358,9 +376,11 @@
     extra = jnp.concatenate([mix_hi, mix_mid, mix_low], axis=1)
     extra = jnp.pad(extra, ((0, 0), (0, -extra.shape[1] % 128)))
     normed, gate_other, up_other, down_other = lax.optimization_barrier((normed, gate_other, up_other, down_other))
-    normed = [jnp.concatenate([normed[0], extra], axis=1)] + list(normed[1:])
+    normed = jnp.concatenate(normed, axis=1)
+    normed = [normed[:, at : at + size] for at, size, _ in spans(GATHER, width)]
+    normed[0] = jnp.concatenate([normed[0], extra], axis=1)
     pieces = gather_slots(normed, devices)
-    gate_other, up_other, down_other = bring(pieces[2], (gate_other, up_other, down_other))
+    gate_other, up_other, down_other = bring(pieces[-2], (gate_other, up_other, down_other))
     place = jnp.stack([chip, jnp.int32(chips)])
     outs = experts(place, pieces, (w_gate[0], gate_other), (w_up[0], up_other), (w_down[0], down_other))
     mixture = reduce_slots(outs, devices)

time: 139 us -> 137 us (0.986)
  waiting for transfers between devices: 67.2 us -> 49.2 us
  starting transfers between devices: 36.1 us -> 47.6 us
  local copies, waits for them, and re-layouts: 7.92 us -> 11.3 us
    ppermute x24 -> x28, waiting for transfers between devices: 61.4 us -> 47.9 us  [the longest x16 37.9 us: reduce_slots(): came = lax.ppermute(sent[c], 'dp', swap_step(step, order, devices))]
    ppermute x24 -> x28, starting transfers between devices: 26.8 us -> 38.2 us  [the longest x16 22.9 us: reduce_slots(): came = lax.ppermute(sent[c], 'dp', swap_step(step, order, devices))]
    all_to_all x1, waiting for transfers between devices: 5.8 us -> 1.3 us  [per_device(): lax.all_to_all(attn_out, 'dp', split_axis=0, concat_axis=0, axis_index_gr...]
    unnamed x33 -> x30, local copies, waits for them, and re-layouts: 7.67 us -> 11.1 us
  transfers between devices with their start and end apart: 29 -> 33, of which waited for: 19 -> 16; matrix products, arithmetic and copies ran while one was open for 1% -> 2% of each run, Pallas kernels for 11% -> 12%
where the time goes in v7:
time: 137 us; the launch traced here: 136 us
  waiting for transfers between devices  49.2 us (36%)
  starting transfers between devices  47.6 us (35%)
  Pallas kernels  25.2 us (18%)
  local copies, waits for them, and re-layouts  11.3 us (8%)
  other arithmetic  2.26 us (2%)
    ppermute x16, waiting for transfers between devices, reduce_slots(): came = lax.ppermute(sent[c], 'dp', swap_step(step, order, devices))  37.9 us
    ppermute x16, starting transfers between devices, reduce_slots(): came = lax.ppermute(sent[c], 'dp', swap_step(step, order, devices))  22.9 us
    ppermute x12, starting transfers between devices, gather_slots(): came = lax.ppermute(own[c], 'dp', swap_step(step, order, devices))  15.3 us
    unnamed x30, local copies, waits for them, and re-layouts  11.1 us
    ppermute x12, waiting for transfers between devices, gather_slots(): came = lax.ppermute(own[c], 'dp', swap_step(step, order, devices))  9.99 us
    all_to_all x1, starting transfers between devices, per_device(): lax.all_to_all(attn_out, 'dp', split_axis=0, concat_axis=0, axis_index_gr...  8.32 us
    pallas_call x2, Pallas kernels, bring(): pl.pallas_call(bring_kernel, out_shape=[jax.ShapeDtypeStruct(a.shape, a.d...  6.86 us
    pallas_call x1, Pallas kernels, attend(): pl.pallas_call(attend_kernel, out_shape=jax.ShapeDtypeStruct((chips, rows...  4.89 us
  transfers between devices with their start and end apart: 33, of which 16 were waited for; matrix products, arithmetic and copies ran while one was open for 2% of the time, Pallas kernels for 12%

profile of v7, /device:TPU:0, one launch (start us, length us, event | category | flops | bytes accessed | tf_op | source)
XLA Modules:
  0.0 136.1 jit_solution(158883703432768227)
XLA Ops:
  1.0 4.9 %shard_map.118.after_ref = bf16[16,16,512]{2,1,0:T(8,128)(2,1)} custom-call(s32[1]{0:T(128)} %bitcast.core_ref, s32[16]{0:T(128)} %lengths_ref.1, bf16[16,8192]{1,0:T(8,128)(2,1)} %q_ref.1, bf16[2,16,512]{2,1,0:T(8,128)(2,1)} %new_ref.1, bf16[2,16,128,512]{3,2,1,0:T(8,128)(2,1)} %cache_ref.1), custom_call_target="tpu_custom_call" | custom-call | flops 67108864 | bytes 4194304 | tf_op jit(solution)/shard_map/pallas_call | solution.py:94
  5.9 8.3 %all-to-all-start = ((bf16[16,16,512]{2,1,0:T(8,128)(2,1)}), bf16[16,16,512]{2,1,0:T(8,128)(2,1)S(1)}, u32[]{:S(2)}, u32[]{:S(2)}) async-start(bf16[16,16,512]{2,1,0:T(8,128)(2,1)} %shard_map.118.after_ref), calls=%async_computation | async-start | bytes 524288 | tf_op jit(solution)/shard_map/all_to_all | solution.py:351
  15.8 1.4 copy-done.4
  18.1 1.6 %copy-done.3 = bf16[256,4096]{1,0:T(8,128)(2,1)S(1)} copy-done((bf16[256,4096]{1,0:T(8,128)(2,1)S(1)}, bf16[256,4096]{1,0:T(8,128)(2,1)}, u32[]{:S(2)}) %copy-start.3) | copy-done | bytes 2097176
  19.7 1.6 %copy-done.5 = bf16[256,4096]{1,0:T(8,128)(2,1)S(1)} copy-done((bf16[256,4096]{1,0:T(8,128)(2,1)S(1)}, bf16[256,4096]{1,0:T(8,128)(2,1)}, u32[]{:S(2)}) %copy-start.5) | copy-done | bytes 2097176
  24.3 1.6 %copy-done.1 = bf16[256,4096]{1,0:T(8,128)(2,1)S(1)} copy-done((bf16[256,4096]{1,0:T(8,128)(2,1)S(1)}, bf16[256,4096]{1,0:T(8,128)(2,1)}, u32[]{:S(2)}) %copy-start.1) | copy-done | bytes 2097176
  30.7 12.5 %collective-permute-done.5 = bf16[128,2048]{1,0:T(8,128)(2,1)S(1)} collective-permute-done((bf16[128,2048]{1,0:T(8,128)(2,1)S(1)}, bf16[128,2048]{1,0:T(8,128)(2,1)S(1)}, u32[]{:S(2)}, u32[]{:S(2)}) %collective-permute-start.5) | collective-permute-done | bytes 524320 | tf_op jit(solution)/shard_map/ppermute | solution.py:297
  44.8 5.1 %collective-permute-done.6 = bf16[64,2048]{1,0:T(8,128)(2,1)S(1)} collective-permute-done((bf16[64,2048]{1,0:T(8,128)(2,1)S(1)}, bf16[64,2048]{1,0:T(8,128)(2,1)S(1)}, u32[]{:S(2)}, u32[]{:S(2)}) %collective-permute-start.6) | collective-permute-done | bytes 262176 | tf_op jit(solution)/shard_map/ppermute | solution.py:297
  49.9 1.9 %collective-permute-start.7 = (bf16[32,2048]{1,0:T(8,128)(2,1)S(1)}, bf16[32,2048]{1,0:T(8,128)(2,1)S(1)}, u32[]{:S(2)}, u32[]{:S(2)}) collective-permute-start(bf16[32,2048]{1,0:T(8,128)(2,1)S(1)} %slice.204), channel_id=1, source_target_pairs={{0,8},{1,9},{2,10},{3,11},{4,12},{5,13},{6,14},{7,15},{8,0},{9,1},... | collective-permute-start | bytes 393224 | tf_op jit(solution)/shard_map/ppermute | solution.py:297
  52.2 3.5 %collective-permute-done.7 = bf16[32,2048]{1,0:T(8,128)(2,1)S(1)} collective-permute-done((bf16[32,2048]{1,0:T(8,128)(2,1)S(1)}, bf16[32,2048]{1,0:T(8,128)(2,1)S(1)}, u32[]{:S(2)}, u32[]{:S(2)}) %collective-permute-start.7) | collective-permute-done | bytes 131104 | tf_op jit(solution)/shard_map/ppermute | solution.py:297
  55.7 2.6 %collective-permute-start.8 = (bf16[16,2048]{1,0:T(8,128)(2,1)S(1)}, bf16[16,2048]{1,0:T(8,128)(2,1)S(1)}, u32[]{:S(2)}, u32[]{:S(2)}) collective-permute-start(bf16[16,2048]{1,0:T(8,128)(2,1)S(1)} %slice.208), channel_id=1, source_target_pairs={{0,16},{1,17},{2,18},{3,19},{4,20},{5,21},{6,22},{7,23},{8,24},{9,... | collective-permute-start | bytes 196616 | tf_op jit(solution)/shard_map/ppermute | solution.py:297
  58.4 2.2 %collective-permute-start.4 = (bf16[16,2048]{1,0:T(8,128)(2,1)S(1)}, bf16[16,2048]{1,0:T(8,128)(2,1)S(1)}, u32[]{:S(2)}, u32[]{:S(2)}) collective-permute-start(bf16[16,2048]{1,0:T(8,128)(2,1)S(1)} %slice.209), channel_id=1, source_target_pairs={{0,16},{1,17},{2,18},{3,19},{4,20},{5,21},{6,22},{7,23},{8,24},{9,... | collective-permute-start | bytes 196616 | tf_op jit(solution)/shard_map/ppermute | solution.py:297
  61.0 2.7 %collective-permute-done.4 = bf16[16,2048]{1,0:T(8,128)(2,1)S(1)} collective-permute-done((bf16[16,2048]{1,0:T(8,128)(2,1)S(1)}, bf16[16,2048]{1,0:T(8,128)(2,1)S(1)}, u32[]{:S(2)}, u32[]{:S(2)}) %collective-permute-start.4) | collective-permute-done | bytes 65568 | tf_op jit(solution)/shard_map/ppermute | solution.py:297
  64.0 2.4 %collective-permute-start.20 = (bf16[16,1024]{1,0:T(8,128)(2,1)S(1)}, bf16[16,1024]{1,0:T(8,128)(2,1)S(1)}, u32[]{:S(2)}, u32[]{:S(2)}) collective-permute-start(bf16[16,1024]{1,0:T(8,128)(2,1)S(1)} %slice.123), channel_id=1, source_target_pairs={{0,16},{1,17},{2,18},{3,19},{4,20},{5,21},{6,22},{7,23},{8,24},{9,... | collective-permute-start | bytes 98312 | tf_op jit(solution)/shard_map/ppermute | solution.py:312
  67.0 2.3 %collective-permute-start.12 = (bf16[16,1664]{1,0:T(8,128)(2,1)S(1)}, bf16[16,1664]{1,0:T(8,128)(2,1)S(1)}, u32[]{:S(2)}, u32[]{:S(2)}) collective-permute-start(bf16[16,1664]{1,0:T(8,128)(2,1)S(1)} %pad_maximum_fusion.10), channel_id=1, source_target_pairs={{0,16},{1,17},{2,18},{3,19},{4,20},{5,21},{6,22},{7,23},{8,24},{9,... | collective-permute-start | bytes 159752 | tf_op jit(solution)/shard_map/ppermute | solution.py:312
  69.4 2.4 %collective-permute-start.21 = (bf16[32,1024]{1,0:T(8,128)(2,1)S(1)}, bf16[32,1024]{1,0:T(8,128)(2,1)S(1)}, u32[]{:S(2)}, u32[]{:S(2)}) collective-permute-start(bf16[32,1024]{1,0:T(8,128)(2,1)S(1)} %pad_maximum_fusion.9), channel_id=1, source_target_pairs={{0,4},{1,3},{2,6},{3,1},{4,0},{5,7},{6,2},{7,5},{8,12},{9,11},{10,... | collective-permute-start | bytes 196616 | tf_op jit(solution)/shard_map/ppermute | solution.py:312
  71.8 2.8 %collective-permute-start.17 = (bf16[32,1536]{1,0:T(8,128)(2,1)S(1)}, bf16[32,1536]{1,0:T(8,128)(2,1)S(1)}, u32[]{:S(2)}, u32[]{:S(2)}) collective-permute-start(bf16[32,1536]{1,0:T(8,128)(2,1)S(1)} %pad_maximum_fusion.8), channel_id=1, source_target_pairs={{0,8},{1,9},{2,10},{3,11},{4,12},{5,13},{6,14},{7,15},{8,0},{9,1},... | collective-permute-start | bytes 294920 | tf_op jit(solution)/shard_map/ppermute | solution.py:312
  75.3 4.1 %collective-permute-done.13 = bf16[32,1664]{1,0:T(8,128)(2,1)S(1)} collective-permute-done((bf16[32,1664]{1,0:T(8,128)(2,1)S(1)}, bf16[32,1664]{1,0:T(8,128)(2,1)S(1)}, u32[]{:S(2)}, u32[]{:S(2)}) %collective-permute-start.13) | collective-permute-done | bytes 106528 | tf_op jit(solution)/shard_map/ppermute | solution.py:312
  80.5 4.8 %collective-permute-done.14 = bf16[64,1664]{1,0:T(8,128)(2,1)S(1)} collective-permute-done((bf16[64,1664]{1,0:T(8,128)(2,1)S(1)}, bf16[64,1664]{1,0:T(8,128)(2,1)S(1)}, u32[]{:S(2)}, u32[]{:S(2)}) %collective-permute-start.14) | collective-permute-done | bytes 213024 | tf_op jit(solution)/shard_map/ppermute | solution.py:312
  86.6 1.6 %collective-permute-start.19 = (bf16[128,1536]{1,0:T(8,128)(2,1)S(1)}, bf16[128,1536]{1,0:T(8,128)(2,1)S(1)}, u32[]{:S(2)}, u32[]{:S(2)}) collective-permute-start(bf16[128,1536]{1,0:T(8,128)(2,1)S(1)} %pad_maximum_fusion.1.refs_2_), channel_id=1, source_target_pairs={{0,4},{1,3},{2,6},{3,1},{4,0},{5,7},{6,2},{7,5},{8,12},{9,11},{10,... | collective-permute-start | bytes 1179656 | tf_op jit(solution)/shard_map/ppermute | solution.py:312
  89.6 6.6 %shard_map.123 = (bf16[4096,768]{1,0:T(8,128)(2,1)S(1)}, bf16[4096,768]{1,0:T(8,128)(2,1)S(1)}, bf16[768,4096]{1,0:T(8,128)(2,1)S(1)}) custom-call(bf16[128,1024]{1,0:T(8,128)(2,1)S(1)} %pad_maximum_fusion.2.refs_4_.after_ref, bf16[4096,768]{1,0:T(8,128)(2,1)} %collective-permute-done.9.refs_0_, bf16[4096,768]{1,0:T(8,128)(2,1)} %collective-permute-done.10.refs_1_, ...), custom_call_target="tpu_custom_call" | custom-call | bytes 18874368 | tf_op jit(solution)/shard_map/pallas_call | solution.py:183
  97.3 4.0 %shard_map.122 = (bf16[256,4096]{1,0:T(8,128)(2,1)S(1)}, bf16[256,768]{1,0:T(8,128)(2,1)S(1)}, f32[256,1]{1,0:T(8,128)S(1)}) custom-call(s32[2]{0:T(128)S(1)} %pad_add_fusion.chip_ref, bf16[128,1664]{1,0:T(8,128)(2,1)S(1)} %pad_maximum_fusion.refs_0_, bf16[128,1664]{1,0:T(8,128)(2,1)S(1)} %collective-permute-done.15.refs_1_, ...), custom_call_target="tpu_custom_call" | custom-call | flops 3221225472 | bytes 12582912 | tf_op jit(solution)/shard_map/pallas_call | solution.py:241
  101.3 3.4 %shard_map.124.after_ref.active1 = bf16[256,768]{1,0:T(8,128)(2,1)S(1)} custom-call(bf16[256,4096]{1,0:T(8,128)(2,1)S(1)} %get-tuple-element.34.tokens_ref, bf16[4096,768]{1,0:T(8,128)(2,1)S(1)} %get-tuple-element.38.gate_ref, bf16[4096,768]{1,0:T(8,128)(2,1)S(1)} %get-tuple-element.39.up_ref), custom_call_target="tpu_custom_call" | custom-call | flops 3221225472 | bytes 12582912 | tf_op jit(solution)/shard_map/pallas_call | solution.py:249
  104.7 1.8 %shard_map.125 = (bf16[128,2048]{1,0:T(8,128)(2,1)S(1)}, bf16[128,2048]{1,0:T(8,128)(2,1)S(1)}) custom-call(bf16[256,768]{1,0:T(8,128)(2,1)S(1)} %shard_map.124.after_ref.active1, bf16[256,768]{1,0:T(8,128)(2,1)S(1)} %get-tuple-element.40.active0, bf16[256,768]{1,0:T(8,128)(2,1)S(1)} %shard_map.124.after_ref.active1, ...), custom_call_target="tpu_custom_call" | custom-call | flops 1610612736 | bytes 6291456 | tf_op jit(solution)/shard_map/pallas_call | solution.py:260
  107.3 1.8 %shard_map.126 = (bf16[128,2048]{1,0:T(8,128)(2,1)S(1)}, bf16[128,2048]{1,0:T(8,128)(2,1)S(1)}) custom-call(bf16[128,2048]{1,0:T(8,128)(2,1)S(1)} %get-tuple-element.44.after_ref, bf16[256,768]{1,0:T(8,128)(2,1)S(1)} %get-tuple-element.40.active0, bf16[256,768]{1,0:T(8,128)(2,1)S(1)} %shard_map.124.after_ref.active1, ...), custom_call_target="tpu_custom_call" | custom-call | flops 1610612736 | bytes 6291456 | tf_op jit(solution)/shard_map/pallas_call | solution.py:260
  109.1 1.4 %collective-permute-start.28 = (bf16[128,2048]{1,0:T(8,128)(2,1)S(1)}, bf16[128,2048]{1,0:T(8,128)(2,1)S(1)}, u32[]{:S(2)}, u32[]{:S(2)}) collective-permute-start(bf16[128,2048]{1,0:T(8,128)(2,1)S(1)} %get-tuple-element.46), channel_id=1, source_target_pairs={{0,4},{1,3},{2,6},{3,1},{4,0},{5,7},{6,2},{7,5},{8,12},{9,11},{10,... | collective-permute-start | bytes 1572872 | tf_op jit(solution)/shard_map/ppermute | solution.py:297
  110.5 5.5 %collective-permute-done.24 = bf16[128,2048]{1,0:T(8,128)(2,1)S(1)} collective-permute-done((bf16[128,2048]{1,0:T(8,128)(2,1)S(1)}, bf16[128,2048]{1,0:T(8,128)(2,1)S(1)}, u32[]{:S(2)}, u32[]{:S(2)}) %collective-permute-start.24) | collective-permute-done | bytes 524320 | tf_op jit(solution)/shard_map/ppermute | solution.py:297
  119.9 2.7 %collective-permute-done.25 = bf16[64,2048]{1,0:T(8,128)(2,1)S(1)} collective-permute-done((bf16[64,2048]{1,0:T(8,128)(2,1)S(1)}, bf16[64,2048]{1,0:T(8,128)(2,1)S(1)}, u32[]{:S(2)}, u32[]{:S(2)}) %collective-permute-start.25) | collective-permute-done | bytes 262176 | tf_op jit(solution)/shard_map/ppermute | solution.py:297
  125.1 1.6 %collective-permute-start.30 = (bf16[32,2048]{1,0:T(8,128)(2,1)S(1)}, bf16[32,2048]{1,0:T(8,128)(2,1)S(1)}, u32[]{:S(2)}, u32[]{:S(2)}) collective-permute-start(bf16[32,2048]{1,0:T(8,128)(2,1)S(1)} %slice.202), channel_id=1, source_target_pairs={{0,8},{1,9},{2,10},{3,11},{4,12},{5,13},{6,14},{7,15},{8,0},{9,1},... | collective-permute-start | bytes 393224 | tf_op jit(solution)/shard_map/ppermute | solution.py:297
  127.8 2.3 %collective-permute-start.27 = (bf16[16,2048]{1,0:T(8,128)(2,1)S(1)}, bf16[16,2048]{1,0:T(8,128)(2,1)S(1)}, u32[]{:S(2)}, u32[]{:S(2)}) collective-permute-start(bf16[16,2048]{1,0:T(8,128)(2,1)S(1)} %slice.207), channel_id=1, source_target_pairs={{0,16},{1,17},{2,18},{3,19},{4,20},{5,21},{6,22},{7,23},{8,24},{9,... | collective-permute-start | bytes 196616 | tf_op jit(solution)/shard_map/ppermute | solution.py:297
  130.2 2.9 %collective-permute-start.31 = (bf16[16,2048]{1,0:T(8,128)(2,1)S(1)}, bf16[16,2048]{1,0:T(8,128)(2,1)S(1)}, u32[]{:S(2)}, u32[]{:S(2)}) collective-permute-start(bf16[16,2048]{1,0:T(8,128)(2,1)S(1)} %slice.206), channel_id=1, source_target_pairs={{0,16},{1,17},{2,18},{3,19},{4,20},{5,21},{6,22},{7,23},{8,24},{9,... | collective-permute-start | bytes 196616 | tf_op jit(solution)/shard_map/ppermute | solution.py:297
  133.1 2.3 %collective-permute-done.31 = bf16[16,2048]{1,0:T(8,128)(2,1)S(1)} collective-permute-done((bf16[16,2048]{1,0:T(8,128)(2,1)S(1)}, bf16[16,2048]{1,0:T(8,128)(2,1)S(1)}, u32[]{:S(2)}, u32[]{:S(2)}) %collective-permute-start.31) | collective-permute-done | bytes 65568 | tf_op jit(solution)/shard_map/ppermute | solution.py:297
  (124 shorter events, 29.1 us)
Async XLA Ops:
  0.0 15.8 %collective-permute-start = (bf16[256,4096]{1,0:T(8,128)(2,1)}, bf16[256,4096]{1,0:T(8,128)(2,1)S(1)}, u32[]{:S(2)}, u32[]{:S(2)}) collective-permute-start(bf16[256,4096]{1,0:T(8,128)(2,1)} %refs_0_.1), channel_id=1, source_target_pairs={{0,1},{1,0},{2,3},{3,2},{4,5},{5,4},{6,7},{7,6},{8,9},{9,8},{10,11... | collective-permute-start | bytes 6291464 | tf_op jit(solution)/shard_map/ppermute | solution.py:344
  0.5 63.5 %collective-permute-start.11 = (bf16[768,4096]{1,0:T(8,128)(2,1)}, bf16[768,4096]{1,0:T(8,128)(2,1)}, u32[]{:S(2)}, u32[]{:S(2)}) collective-permute-start(bf16[768,4096]{1,0:T(8,128)(2,1)} %bitcast.5), channel_id=1, source_target_pairs={{0,1},{1,0},{2,3},{3,2},{4,5},{5,4},{6,7},{7,6},{8,9},{9,8},{10,11... | collective-permute-start | bytes 18874376 | tf_op jit(solution)/shard_map/ppermute | solution.py:347
  0.5 63.4 %collective-permute-start.10 = (bf16[4096,768]{1,0:T(8,128)(2,1)}, bf16[4096,768]{1,0:T(8,128)(2,1)}, u32[]{:S(2)}, u32[]{:S(2)}) collective-permute-start(bf16[4096,768]{1,0:T(8,128)(2,1)} %bitcast.14), channel_id=1, source_target_pairs={{0,1},{1,0},{2,3},{3,2},{4,5},{5,4},{6,7},{7,6},{8,9},{9,8},{10,11... | collective-permute-start | bytes 18874376 | tf_op jit(solution)/shard_map/ppermute | solution.py:346
  1.0 63.0 %collective-permute-start.9 = (bf16[4096,768]{1,0:T(8,128)(2,1)}, bf16[4096,768]{1,0:T(8,128)(2,1)}, u32[]{:S(2)}, u32[]{:S(2)}) collective-permute-start(bf16[4096,768]{1,0:T(8,128)(2,1)} %bitcast.10), channel_id=1, source_target_pairs={{0,1},{1,0},{2,3},{3,2},{4,5},{5,4},{6,7},{7,6},{8,9},{9,8},{10,11... | collective-permute-start | bytes 18874376 | tf_op jit(solution)/shard_map/ppermute | solution.py:345
  5.9 18.4 %all-to-all-start = ((bf16[16,16,512]{2,1,0:T(8,128)(2,1)}), bf16[16,16,512]{2,1,0:T(8,128)(2,1)S(1)}, u32[]{:S(2)}, u32[]{:S(2)}) async-start(bf16[16,16,512]{2,1,0:T(8,128)(2,1)} %shard_map.118.after_ref), calls=%async_computation | async-start | bytes 524288 | tf_op jit(solution)/shard_map/all_to_all | solution.py:351
  28.4 14.9 %collective-permute-start.5 = (bf16[128,2048]{1,0:T(8,128)(2,1)S(1)}, bf16[128,2048]{1,0:T(8,128)(2,1)S(1)}, u32[]{:S(2)}, u32[]{:S(2)}) collective-permute-start(bf16[128,2048]{1,0:T(8,128)(2,1)S(1)} %get-tuple-element.31), channel_id=1, source_target_pairs={{0,4},{1,3},{2,6},{3,1},{4,0},{5,7},{6,2},{7,5},{8,12},{9,11},{10,... | collective-permute-start | bytes 1572872 | tf_op jit(solution)/shard_map/ppermute | solution.py:297
  29.5 14.0 %collective-permute-start.1 = (bf16[128,2048]{1,0:T(8,128)(2,1)S(1)}, bf16[128,2048]{1,0:T(8,128)(2,1)S(1)}, u32[]{:S(2)}, u32[]{:S(2)}) collective-permute-start(bf16[128,2048]{1,0:T(8,128)(2,1)S(1)} %get-tuple-element.29.after_ref), channel_id=1, source_target_pairs={{0,2},{1,5},{2,0},{3,7},{4,6},{5,1},{6,4},{7,3},{8,10},{9,13},{10,... | collective-permute-start | bytes 1572872 | tf_op jit(solution)/shard_map/ppermute | solution.py:297
  43.4 6.4 %collective-permute-start.6 = (bf16[64,2048]{1,0:T(8,128)(2,1)S(1)}, bf16[64,2048]{1,0:T(8,128)(2,1)S(1)}, u32[]{:S(2)}, u32[]{:S(2)}) collective-permute-start(bf16[64,2048]{1,0:T(8,128)(2,1)S(1)} %slice.200), channel_id=1, source_target_pairs={{0,2},{1,5},{2,0},{3,7},{4,6},{5,1},{6,4},{7,3},{8,10},{9,13},{10,... | collective-permute-start | bytes 786440 | tf_op jit(solution)/shard_map/ppermute | solution.py:297
  43.7 8.2 %collective-permute-start.2 = (bf16[64,2048]{1,0:T(8,128)(2,1)S(1)}, bf16[64,2048]{1,0:T(8,128)(2,1)S(1)}, u32[]{:S(2)}, u32[]{:S(2)}) collective-permute-start(bf16[64,2048]{1,0:T(8,128)(2,1)S(1)} %slice.201), channel_id=1, source_target_pairs={{0,4},{1,3},{2,6},{3,1},{4,0},{5,7},{6,2},{7,5},{8,12},{9,11},{10,... | collective-permute-start | bytes 786440 | tf_op jit(solution)/shard_map/ppermute | solution.py:297
  49.9 5.7 %collective-permute-start.7 = (bf16[32,2048]{1,0:T(8,128)(2,1)S(1)}, bf16[32,2048]{1,0:T(8,128)(2,1)S(1)}, u32[]{:S(2)}, u32[]{:S(2)}) collective-permute-start(bf16[32,2048]{1,0:T(8,128)(2,1)S(1)} %slice.204), channel_id=1, source_target_pairs={{0,8},{1,9},{2,10},{3,11},{4,12},{5,13},{6,14},{7,15},{8,0},{9,1},... | collective-permute-start | bytes 393224 | tf_op jit(solution)/shard_map/ppermute | solution.py:297
  51.9 6.4 %collective-permute-start.3 = (bf16[32,2048]{1,0:T(8,128)(2,1)S(1)}, bf16[32,2048]{1,0:T(8,128)(2,1)S(1)}, u32[]{:S(2)}, u32[]{:S(2)}) collective-permute-start(bf16[32,2048]{1,0:T(8,128)(2,1)S(1)} %slice.205), channel_id=1, source_target_pairs={{0,8},{1,9},{2,10},{3,11},{4,12},{5,13},{6,14},{7,15},{8,0},{9,1},... | collective-permute-start | bytes 393224 | tf_op jit(solution)/shard_map/ppermute | solution.py:297
  55.7 5.2 %collective-permute-start.8 = (bf16[16,2048]{1,0:T(8,128)(2,1)S(1)}, bf16[16,2048]{1,0:T(8,128)(2,1)S(1)}, u32[]{:S(2)}, u32[]{:S(2)}) collective-permute-start(bf16[16,2048]{1,0:T(8,128)(2,1)S(1)} %slice.208), channel_id=1, source_target_pairs={{0,16},{1,17},{2,18},{3,19},{4,20},{5,21},{6,22},{7,23},{8,24},{9,... | collective-permute-start | bytes 196616 | tf_op jit(solution)/shard_map/ppermute | solution.py:297
  58.4 5.2 %collective-permute-start.4 = (bf16[16,2048]{1,0:T(8,128)(2,1)S(1)}, bf16[16,2048]{1,0:T(8,128)(2,1)S(1)}, u32[]{:S(2)}, u32[]{:S(2)}) collective-permute-start(bf16[16,2048]{1,0:T(8,128)(2,1)S(1)} %slice.209), channel_id=1, source_target_pairs={{0,16},{1,17},{2,18},{3,19},{4,20},{5,21},{6,22},{7,23},{8,24},{9,... | collective-permute-start | bytes 196616 | tf_op jit(solution)/shard_map/ppermute | solution.py:297
  64.0 5.4 %collective-permute-start.20 = (bf16[16,1024]{1,0:T(8,128)(2,1)S(1)}, bf16[16,1024]{1,0:T(8,128)(2,1)S(1)}, u32[]{:S(2)}, u32[]{:S(2)}) collective-permute-start(bf16[16,1024]{1,0:T(8,128)(2,1)S(1)} %slice.123), channel_id=1, source_target_pairs={{0,16},{1,17},{2,18},{3,19},{4,20},{5,21},{6,22},{7,23},{8,24},{9,... | collective-permute-start | bytes 98312 | tf_op jit(solution)/shard_map/ppermute | solution.py:312
  66.4 5.4 %collective-permute-start.16 = (bf16[16,1536]{1,0:T(8,128)(2,1)S(1)}, bf16[16,1536]{1,0:T(8,128)(2,1)S(1)}, u32[]{:S(2)}, u32[]{:S(2)}) collective-permute-start(bf16[16,1536]{1,0:T(8,128)(2,1)S(1)} %get-tuple-element.53), channel_id=1, source_target_pairs={{0,16},{1,17},{2,18},{3,19},{4,20},{5,21},{6,22},{7,23},{8,24},{9,... | collective-permute-start | bytes 147464 | tf_op jit(solution)/shard_map/ppermute | solution.py:312
  67.0 7.6 %collective-permute-start.12 = (bf16[16,1664]{1,0:T(8,128)(2,1)S(1)}, bf16[16,1664]{1,0:T(8,128)(2,1)S(1)}, u32[]{:S(2)}, u32[]{:S(2)}) collective-permute-start(bf16[16,1664]{1,0:T(8,128)(2,1)S(1)} %pad_maximum_fusion.10), channel_id=1, source_target_pairs={{0,16},{1,17},{2,18},{3,19},{4,20},{5,21},{6,22},{7,23},{8,24},{9,... | collective-permute-start | bytes 159752 | tf_op jit(solution)/shard_map/ppermute | solution.py:312
  69.4 5.8 %collective-permute-start.21 = (bf16[32,1024]{1,0:T(8,128)(2,1)S(1)}, bf16[32,1024]{1,0:T(8,128)(2,1)S(1)}, u32[]{:S(2)}, u32[]{:S(2)}) collective-permute-start(bf16[32,1024]{1,0:T(8,128)(2,1)S(1)} %pad_maximum_fusion.9), channel_id=1, source_target_pairs={{0,4},{1,3},{2,6},{3,1},{4,0},{5,7},{6,2},{7,5},{8,12},{9,11},{10,... | collective-permute-start | bytes 196616 | tf_op jit(solution)/shard_map/ppermute | solution.py:312
  71.8 8.6 %collective-permute-start.17 = (bf16[32,1536]{1,0:T(8,128)(2,1)S(1)}, bf16[32,1536]{1,0:T(8,128)(2,1)S(1)}, u32[]{:S(2)}, u32[]{:S(2)}) collective-permute-start(bf16[32,1536]{1,0:T(8,128)(2,1)S(1)} %pad_maximum_fusion.8), channel_id=1, source_target_pairs={{0,8},{1,9},{2,10},{3,11},{4,12},{5,13},{6,14},{7,15},{8,0},{9,1},... | collective-permute-start | bytes 294920 | tf_op jit(solution)/shard_map/ppermute | solution.py:312
  75.2 13.0 %collective-permute-start.22 = (bf16[64,1024]{1,0:T(8,128)(2,1)S(1)}, bf16[64,1024]{1,0:T(8,128)(2,1)S(1)}, u32[]{:S(2)}, u32[]{:S(2)}) collective-permute-start(bf16[64,1024]{1,0:T(8,128)(2,1)S(1)} %pad_maximum_fusion.5), channel_id=1, source_target_pairs={{0,2},{1,5},{2,0},{3,7},{4,6},{5,1},{6,4},{7,3},{8,10},{9,13},{10,... | collective-permute-start | bytes 393224 | tf_op jit(solution)/shard_map/ppermute | solution.py:312
  79.4 5.9 %collective-permute-start.14 = (bf16[64,1664]{1,0:T(8,128)(2,1)S(1)}, bf16[64,1664]{1,0:T(8,128)(2,1)S(1)}, u32[]{:S(2)}, u32[]{:S(2)}) collective-permute-start(bf16[64,1664]{1,0:T(8,128)(2,1)S(1)} %pad_maximum_fusion.3), channel_id=1, source_target_pairs={{0,4},{1,3},{2,6},{3,1},{4,0},{5,7},{6,2},{7,5},{8,12},{9,11},{10,... | collective-permute-start | bytes 638984 | tf_op jit(solution)/shard_map/ppermute | solution.py:312
  80.4 6.1 %collective-permute-start.18 = (bf16[64,1536]{1,0:T(8,128)(2,1)S(1)}, bf16[64,1536]{1,0:T(8,128)(2,1)S(1)}, u32[]{:S(2)}, u32[]{:S(2)}) collective-permute-start(bf16[64,1536]{1,0:T(8,128)(2,1)S(1)} %pad_maximum_fusion.4), channel_id=1, source_target_pairs={{0,2},{1,5},{2,0},{3,7},{4,6},{5,1},{6,4},{7,3},{8,10},{9,13},{10,... | collective-permute-start | bytes 589832 | tf_op jit(solution)/shard_map/ppermute | solution.py:312
  85.4 10.8 %collective-permute-start.15 = (bf16[128,1664]{1,0:T(8,128)(2,1)S(1)}, bf16[128,1664]{1,0:T(8,128)(2,1)S(1)}, u32[]{:S(2)}, u32[]{:S(2)}) collective-permute-start(bf16[128,1664]{1,0:T(8,128)(2,1)S(1)} %pad_maximum_fusion.refs_0_), channel_id=1, source_target_pairs={{0,2},{1,5},{2,0},{3,7},{4,6},{5,1},{6,4},{7,3},{8,10},{9,13},{10,... | collective-permute-start | bytes 1277960 | tf_op jit(solution)/shard_map/ppermute | solution.py:312
  86.6 9.6 %collective-permute-start.19 = (bf16[128,1536]{1,0:T(8,128)(2,1)S(1)}, bf16[128,1536]{1,0:T(8,128)(2,1)S(1)}, u32[]{:S(2)}, u32[]{:S(2)}) collective-permute-start(bf16[128,1536]{1,0:T(8,128)(2,1)S(1)} %pad_maximum_fusion.1.refs_2_), channel_id=1, source_target_pairs={{0,4},{1,3},{2,6},{3,1},{4,0},{5,7},{6,2},{7,5},{8,12},{9,11},{10,... | collective-permute-start | bytes 1179656 | tf_op jit(solution)/shard_map/ppermute | solution.py:312
  88.2 8.0 %collective-permute-start.23 = (bf16[128,1024]{1,0:T(8,128)(2,1)S(1)}, bf16[128,1024]{1,0:T(8,128)(2,1)S(1)}, u32[]{:S(2)}, u32[]{:S(2)}) collective-permute-start(bf16[128,1024]{1,0:T(8,128)(2,1)S(1)} %pad_maximum_fusion.2.refs_4_.after_ref), channel_id=1, source_target_pairs={{0,8},{1,9},{2,10},{3,11},{4,12},{5,13},{6,14},{7,15},{8,0},{9,1},... | collective-permute-start | bytes 786440 | tf_op jit(solution)/shard_map/ppermute | solution.py:312
  106.5 9.5 %collective-permute-start.24 = (bf16[128,2048]{1,0:T(8,128)(2,1)S(1)}, bf16[128,2048]{1,0:T(8,128)(2,1)S(1)}, u32[]{:S(2)}, u32[]{:S(2)}) collective-permute-start(bf16[128,2048]{1,0:T(8,128)(2,1)S(1)} %get-tuple-element.44.after_ref), channel_id=1, source_target_pairs={{0,2},{1,5},{2,0},{3,7},{4,6},{5,1},{6,4},{7,3},{8,10},{9,13},{10,... | collective-permute-start | bytes 1572872 | tf_op jit(solution)/shard_map/ppermute | solution.py:297
  109.1 9.3 %collective-permute-start.28 = (bf16[128,2048]{1,0:T(8,128)(2,1)S(1)}, bf16[128,2048]{1,0:T(8,128)(2,1)S(1)}, u32[]{:S(2)}, u32[]{:S(2)}) collective-permute-start(bf16[128,2048]{1,0:T(8,128)(2,1)S(1)} %get-tuple-element.46), channel_id=1, source_target_pairs={{0,4},{1,3},{2,6},{3,1},{4,0},{5,7},{6,2},{7,5},{8,12},{9,11},{10,... | collective-permute-start | bytes 1572872 | tf_op jit(solution)/shard_map/ppermute | solution.py:297
  116.2 6.4 %collective-permute-start.25 = (bf16[64,2048]{1,0:T(8,128)(2,1)S(1)}, bf16[64,2048]{1,0:T(8,128)(2,1)S(1)}, u32[]{:S(2)}, u32[]{:S(2)}) collective-permute-start(bf16[64,2048]{1,0:T(8,128)(2,1)S(1)} %slice.199), channel_id=1, source_target_pairs={{0,4},{1,3},{2,6},{3,1},{4,0},{5,7},{6,2},{7,5},{8,12},{9,11},{10,... | collective-permute-start | bytes 786440 | tf_op jit(solution)/shard_map/ppermute | solution.py:297
  118.6 6.4 %collective-permute-start.29 = (bf16[64,2048]{1,0:T(8,128)(2,1)S(1)}, bf16[64,2048]{1,0:T(8,128)(2,1)S(1)}, u32[]{:S(2)}, u32[]{:S(2)}) collective-permute-start(bf16[64,2048]{1,0:T(8,128)(2,1)S(1)} %slice.198), channel_id=1, source_target_pairs={{0,2},{1,5},{2,0},{3,7},{4,6},{5,1},{6,4},{7,3},{8,10},{9,13},{10,... | collective-permute-start | bytes 786440 | tf_op jit(solution)/shard_map/ppermute | solution.py:297
  122.7 5.0 %collective-permute-start.26 = (bf16[32,2048]{1,0:T(8,128)(2,1)S(1)}, bf16[32,2048]{1,0:T(8,128)(2,1)S(1)}, u32[]{:S(2)}, u32[]{:S(2)}) collective-permute-start(bf16[32,2048]{1,0:T(8,128)(2,1)S(1)} %slice.203), channel_id=1, source_target_pairs={{0,8},{1,9},{2,10},{3,11},{4,12},{5,13},{6,14},{7,15},{8,0},{9,1},... | collective-permute-start | bytes 393224 | tf_op jit(solution)/shard_map/ppermute | solution.py:297
  125.1 5.0 %collective-permute-start.30 = (bf16[32,2048]{1,0:T(8,128)(2,1)S(1)}, bf16[32,2048]{1,0:T(8,128)(2,1)S(1)}, u32[]{:S(2)}, u32[]{:S(2)}) collective-permute-start(bf16[32,2048]{1,0:T(8,128)(2,1)S(1)} %slice.202), channel_id=1, source_target_pairs={{0,8},{1,9},{2,10},{3,11},{4,12},{5,13},{6,14},{7,15},{8,0},{9,1},... | collective-permute-start | bytes 393224 | tf_op jit(solution)/shard_map/ppermute | solution.py:297
  127.8 5.3 %collective-permute-start.27 = (bf16[16,2048]{1,0:T(8,128)(2,1)S(1)}, bf16[16,2048]{1,0:T(8,128)(2,1)S(1)}, u32[]{:S(2)}, u32[]{:S(2)}) collective-permute-start(bf16[16,2048]{1,0:T(8,128)(2,1)S(1)} %slice.207), channel_id=1, source_target_pairs={{0,16},{1,17},{2,18},{3,19},{4,20},{5,21},{6,22},{7,23},{8,24},{9,... | collective-permute-start | bytes 196616 | tf_op jit(solution)/shard_map/ppermute | solution.py:297
  130.2 5.2 %collective-permute-start.31 = (bf16[16,2048]{1,0:T(8,128)(2,1)S(1)}, bf16[16,2048]{1,0:T(8,128)(2,1)S(1)}, u32[]{:S(2)}, u32[]{:S(2)}) collective-permute-start(bf16[16,2048]{1,0:T(8,128)(2,1)S(1)} %slice.206), channel_id=1, source_target_pairs={{0,16},{1,17},{2,18},{3,19},{4,20},{5,21},{6,22},{7,23},{8,24},{9,... | collective-permute-start | bytes 196616 | tf_op jit(solution)/shard_map/ppermute | solution.py:297
  (15 other events, 102.9 us)

commit v8 on v7

--- a/solution.py
+++ b/solution.py
@@ -16,7 +16,7 @@
 BF16 = jnp.bfloat16
 
 
-REDUCE = ((4, (0, 1, 2)), (4, (1, 0, 2)))
+REDUCE = ((4, (0, 1, 2)), (4, (1, 2, 0)))
 GATHER = ((3, (0, 1, 2)), (3, (1, 0, 2)), (2, (2, 0, 1)))
 
 
@@ -127,7 +127,7 @@
         yield place // 4, slice(at, at + size), slice(base * size, (base + 1) * size)
 
 
-def project_kernel(order, after_ref, index_ref, blocks_ref, own_ref, other_ref, keep_ref, send_ref, ordered):
+def project_kernel(order, index_ref, blocks_ref, own_ref, other_ref, keep_ref, send_ref, ordered):
     chips, rows, features = blocks_ref.shape
     half = features // 2
     for k in range(chips):
@@ -144,7 +144,7 @@
     return pl.BlockSpec(shape, lambda s: (0,) * len(shape))
 
 
-def project(span, after, index, blocks, own, other):
+def project(span, index, blocks, own, other):
     chips, rows, features = blocks.shape
     depth = own.shape[0]
     first, size, order = span
@@ -155,7 +155,6 @@
         out_shape=[jax.ShapeDtypeStruct(half, BF16)] * 2,
         grid=(1,),
         in_specs=[
-            pl.BlockSpec(memory_space=pl.ANY),
             pl.BlockSpec(memory_space=pltpu.SMEM),
             whole(blocks.shape),
             weights,
@@ -165,7 +164,7 @@
         scratch_shapes=[pltpu.VMEM((chips * rows, features), BF16)],
         compiler_params=pltpu.CompilerParams(vmem_limit_bytes=16 << 20),
         cost_estimate=pl.CostEstimate(flops=2 * blocks.size * size, bytes_accessed=4 * depth * size, transcendentals=0),
-    )(after, index, blocks, own, other)
+    )(index, blocks, own, other)
 
 
 def bring_kernel(after_ref, *refs):
@@ -280,7 +279,7 @@
 
 def step_bits(devices, order=(0, 1, 2)):
     even = [1 << i for i in range(1, devices.bit_length() - 1)]
-    odd = even[1::-1] + even[2:]
+    odd = [even[i] for i in (2, 0, 1)] + even[3:]
     return [[bits[i] for i in order] + bits[3:] for bits in (even, odd)]
 
 
@@ -347,7 +346,6 @@
     down_other = lax.ppermute(w_down[0], "dp", core_swap)
 
     attn_out = attend(core[None], queries, new_kv, cache_kv, lengths, chips)
-    out_own, out_other = bring(attn_out, (out_weight, out_other))
     blocks = lax.all_to_all(
         attn_out, "dp", split_axis=0, concat_axis=0, axis_index_groups=core_groups, tiled=True
     )
@@ -361,7 +359,7 @@
     cuts = list(spans(REDUCE, width))
     partial = []
     for span in cuts:
-        partial += project(span, partial[-1] if partial else blocks, chip ^ offset, blocks, out_own, out_other)
+        partial += project(span, chip ^ offset, blocks, out_weight, out_other)
     projected = reduce_slots(partial, devices)
     hidden_state = [
         (residual[:, at : at + size].astype(F32) + add).astype(BF16) for (at, size, _), add in zip(cuts, projected)

time: 137 us -> 133 us (0.971)
  waiting for transfers between devices: 49.2 us -> 60.7 us
  starting transfers between devices: 47.6 us -> 39 us
  local copies, waits for them, and re-layouts: 11.3 us -> 3.46 us
  Pallas kernels: 25.2 us -> 27 us
    unnamed x30 -> x20, local copies, waits for them, and re-layouts: 11.1 us -> 3.22 us
    all_to_all x1, waiting for transfers between devices: 1.3 us -> 8.55 us  [per_device(): lax.all_to_all(attn_out, 'dp', split_axis=0, concat_axis=0, axis_index_gr...]
    ppermute x16, starting transfers between devices: 22.9 us -> 17.8 us  [reduce_slots(): came = lax.ppermute(sent[c], 'dp', swap_step(step, order, devices))]
    ppermute x12, starting transfers between devices: 15.3 us -> 11.9 us  [gather_slots(): came = lax.ppermute(own[c], 'dp', swap_step(step, order, devices))]
    ppermute x16, waiting for transfers between devices: 37.9 us -> 40.3 us  [reduce_slots(): came = lax.ppermute(sent[c], 'dp', swap_step(step, order, devices))]
    ppermute x12, waiting for transfers between devices: 9.99 us -> 11.9 us  [gather_slots(): came = lax.ppermute(own[c], 'dp', swap_step(step, order, devices))]
    pallas_call x2, Pallas kernels: 2.49 us -> 4 us  [project(): pl.pallas_call(functools.partial(project_kernel, order), out_shape=[jax.S...]
    pallas_call x2 -> x1, Pallas kernels: 6.86 us -> 7.07 us  [bring(): pl.pallas_call(bring_kernel, out_shape=[jax.ShapeDtypeStruct(a.shape, a.d...]
  transfers between devices with their start and end apart: 33 -> 33, of which waited for: 16 -> 22; matrix products, arithmetic and copies ran while one was open for 2% -> 2% of each run, Pallas kernels for 12% -> 13%
where the time goes in v8:
time: 133 us
  waiting for transfers between devices  60.7 us (46%)
  starting transfers between devices  39 us (29%)
  Pallas kernels  27 us (20%)
  local copies, waits for them, and re-layouts  3.46 us (3%)
  other arithmetic  2.27 us (2%)
    ppermute x16, waiting for transfers between devices, reduce_slots(): came = lax.ppermute(sent[c], 'dp', swap_step(step, order, devices))  40.3 us
    ppermute x16, starting transfers between devices, reduce_slots(): came = lax.ppermute(sent[c], 'dp', swap_step(step, order, devices))  17.8 us
    ppermute x12, waiting for transfers between devices, gather_slots(): came = lax.ppermute(own[c], 'dp', swap_step(step, order, devices))  11.9 us
    ppermute x12, starting transfers between devices, gather_slots(): came = lax.ppermute(own[c], 'dp', swap_step(step, order, devices))  11.9 us
    all_to_all x1, waiting for transfers between devices, per_device(): lax.all_to_all(attn_out, 'dp', split_axis=0, concat_axis=0, axis_index_gr...  8.55 us
    all_to_all x1, starting transfers between devices, per_device(): lax.all_to_all(attn_out, 'dp', split_axis=0, concat_axis=0, axis_index_gr...  8.31 us
    pallas_call x1, Pallas kernels, bring(): pl.pallas_call(bring_kernel, out_shape=[jax.ShapeDtypeStruct(a.shape, a.d...  7.07 us
    pallas_call x1, Pallas kernels, attend(): pl.pallas_call(attend_kernel, out_shape=jax.ShapeDtypeStruct((chips, rows...  4.91 us
  transfers between devices with their start and end apart: 33, of which 22 were waited for; matrix products, arithmetic and copies ran while one was open for 2% of the time, Pallas kernels for 13%

profile of v8, /device:TPU:0, one launch (start us, length us, event | category | flops | bytes accessed | tf_op | source)
XLA Modules:
  0.0 132.9 jit_solution(9905055070869555948)
XLA Ops:
  1.0 4.9 %shard_map.118 = bf16[16,16,512]{2,1,0:T(8,128)(2,1)} custom-call(s32[1]{0:T(128)} %bitcast.core_ref, s32[16]{0:T(128)} %lengths_ref.1, bf16[16,8192]{1,0:T(8,128)(2,1)} %q_ref.1, bf16[2,16,512]{2,1,0:T(8,128)(2,1)} %new_ref.1, bf16[2,16,128,512]{3,2,1,0:T(8,128)(2,1)} %cache_ref.1), custom_call_target="tpu_custom_call" | custom-call | flops 67108864 | bytes 4194304 | tf_op jit(solution)/shard_map/pallas_call | solution.py:94
  6.0 8.3 %all-to-all-start = ((bf16[16,16,512]{2,1,0:T(8,128)(2,1)}), bf16[16,16,512]{2,1,0:T(8,128)(2,1)S(1)}, u32[]{:S(2)}, u32[]{:S(2)}) async-start(bf16[16,16,512]{2,1,0:T(8,128)(2,1)} %shard_map.118), calls=%async_computation | async-start | bytes 524288 | tf_op jit(solution)/shard_map/all_to_all | solution.py:349
  15.8 8.5 %all-to-all-done.blocks_ref = bf16[16,16,512]{2,1,0:T(8,128)(2,1)S(1)} async-done(((bf16[16,16,512]{2,1,0:T(8,128)(2,1)}), bf16[16,16,512]{2,1,0:T(8,128)(2,1)S(1)}, u32[]{:S(2)}, u32[]{:S(2)}) %all-to-all-start) | async-done | bytes 262176 | tf_op jit(solution)/shard_map/all_to_all | solution.py:349
  24.4 2.0 %shard_map.120 = (bf16[128,2048]{1,0:T(8,128)(2,1)S(1)}, bf16[128,2048]{1,0:T(8,128)(2,1)S(1)}) custom-call(s32[16]{0:T(128)S(1)} %add_xor_fusion.index_ref, bf16[16,16,512]{2,1,0:T(8,128)(2,1)S(1)} %all-to-all-done.blocks_ref, bf16[256,4096]{1,0:T(8,128)(2,1)S(1)} %copy-done, bf16[256,4096]{1,0:T(8,128)(2,1)} %collective-permute-done.other_ref), custom_call_target="tpu_custom_call" | custom-call | flops 536870912 | bytes 2097152 | tf_op jit(solution)/shard_map/pallas_call | solution.py:153
  27.5 2.0 %shard_map.119 = (bf16[128,2048]{1,0:T(8,128)(2,1)S(1)}, bf16[128,2048]{1,0:T(8,128)(2,1)S(1)}) custom-call(s32[16]{0:T(128)S(1)} %add_xor_fusion.index_ref, bf16[16,16,512]{2,1,0:T(8,128)(2,1)S(1)} %all-to-all-done.blocks_ref, bf16[256,4096]{1,0:T(8,128)(2,1)S(1)} %copy-done, bf16[256,4096]{1,0:T(8,128)(2,1)} %collective-permute-done.other_ref), custom_call_target="tpu_custom_call" | custom-call | flops 536870912 | bytes 2097152 | tf_op jit(solution)/shard_map/pallas_call | solution.py:153
  30.2 5.5 %collective-permute-done.5 = bf16[128,2048]{1,0:T(8,128)(2,1)S(1)} collective-permute-done((bf16[128,2048]{1,0:T(8,128)(2,1)S(1)}, bf16[128,2048]{1,0:T(8,128)(2,1)S(1)}, u32[]{:S(2)}, u32[]{:S(2)}) %collective-permute-start.5) | collective-permute-done | bytes 524320 | tf_op jit(solution)/shard_map/ppermute | solution.py:296
  35.8 1.5 %collective-permute-start.6 = (bf16[64,2048]{1,0:T(8,128)(2,1)S(1)}, bf16[64,2048]{1,0:T(8,128)(2,1)S(1)}, u32[]{:S(2)}, u32[]{:S(2)}) collective-permute-start(bf16[64,2048]{1,0:T(8,128)(2,1)S(1)} %slice.200), channel_id=1, source_target_pairs={{0,8},{1,5},{2,10},{3,7},{4,12},{5,1},{6,14},{7,3},{8,0},{9,13},{1... | collective-permute-start | bytes 786440 | tf_op jit(solution)/shard_map/ppermute | solution.py:296
  37.4 1.4 %collective-permute-done.1 = bf16[128,2048]{1,0:T(8,128)(2,1)S(1)} collective-permute-done((bf16[128,2048]{1,0:T(8,128)(2,1)S(1)}, bf16[128,2048]{1,0:T(8,128)(2,1)S(1)}, u32[]{:S(2)}, u32[]{:S(2)}) %collective-permute-start.1) | collective-permute-done | bytes 524320 | tf_op jit(solution)/shard_map/ppermute | solution.py:296
  39.0 2.7 %collective-permute-start.2 = (bf16[64,2048]{1,0:T(8,128)(2,1)S(1)}, bf16[64,2048]{1,0:T(8,128)(2,1)S(1)}, u32[]{:S(2)}, u32[]{:S(2)}) collective-permute-start(bf16[64,2048]{1,0:T(8,128)(2,1)S(1)} %slice.201), channel_id=1, source_target_pairs={{0,4},{1,3},{2,6},{3,1},{4,0},{5,7},{6,2},{7,5},{8,12},{9,11},{10,... | collective-permute-start | bytes 786440 | tf_op jit(solution)/shard_map/ppermute | solution.py:296
  41.6 1.5 %collective-permute-done.6 = bf16[64,2048]{1,0:T(8,128)(2,1)S(1)} collective-permute-done((bf16[64,2048]{1,0:T(8,128)(2,1)S(1)}, bf16[64,2048]{1,0:T(8,128)(2,1)S(1)}, u32[]{:S(2)}, u32[]{:S(2)}) %collective-permute-start.6) | collective-permute-done | bytes 262176 | tf_op jit(solution)/shard_map/ppermute | solution.py:296
  43.3 3.7 %collective-permute-done.2 = bf16[64,2048]{1,0:T(8,128)(2,1)S(1)} collective-permute-done((bf16[64,2048]{1,0:T(8,128)(2,1)S(1)}, bf16[64,2048]{1,0:T(8,128)(2,1)S(1)}, u32[]{:S(2)}, u32[]{:S(2)}) %collective-permute-start.2) | collective-permute-done | bytes 262176 | tf_op jit(solution)/shard_map/ppermute | solution.py:296
  49.6 3.3 %collective-permute-done.3 = bf16[32,2048]{1,0:T(8,128)(2,1)S(1)} collective-permute-done((bf16[32,2048]{1,0:T(8,128)(2,1)S(1)}, bf16[32,2048]{1,0:T(8,128)(2,1)S(1)}, u32[]{:S(2)}, u32[]{:S(2)}) %collective-permute-start.3) | collective-permute-done | bytes 131104 | tf_op jit(solution)/shard_map/ppermute | solution.py:296
  53.6 6.6 %collective-permute-done.4 = bf16[16,2048]{1,0:T(8,128)(2,1)S(1)} collective-permute-done((bf16[16,2048]{1,0:T(8,128)(2,1)S(1)}, bf16[16,2048]{1,0:T(8,128)(2,1)S(1)}, u32[]{:S(2)}, u32[]{:S(2)}) %collective-permute-start.4) | collective-permute-done | bytes 65568 | tf_op jit(solution)/shard_map/ppermute | solution.py:296
  60.6 3.0 %collective-permute-start.16 = (bf16[16,1536]{1,0:T(8,128)(2,1)S(1)}, bf16[16,1536]{1,0:T(8,128)(2,1)S(1)}, u32[]{:S(2)}, u32[]{:S(2)}) collective-permute-start(bf16[16,1536]{1,0:T(8,128)(2,1)S(1)} %get-tuple-element.49), channel_id=1, source_target_pairs={{0,16},{1,17},{2,18},{3,19},{4,20},{5,21},{6,22},{7,23},{8,24},{9,... | collective-permute-start | bytes 147464 | tf_op jit(solution)/shard_map/ppermute | solution.py:311
  63.6 1.8 %collective-permute-done.20 = bf16[16,1024]{1,0:T(8,128)(2,1)S(1)} collective-permute-done((bf16[16,1024]{1,0:T(8,128)(2,1)S(1)}, bf16[16,1024]{1,0:T(8,128)(2,1)S(1)}, u32[]{:S(2)}, u32[]{:S(2)}) %collective-permute-start.20) | collective-permute-done | bytes 32800 | tf_op jit(solution)/shard_map/ppermute | solution.py:311
  66.7 1.7 %collective-permute-start.17 = (bf16[32,1536]{1,0:T(8,128)(2,1)S(1)}, bf16[32,1536]{1,0:T(8,128)(2,1)S(1)}, u32[]{:S(2)}, u32[]{:S(2)}) collective-permute-start(bf16[32,1536]{1,0:T(8,128)(2,1)S(1)} %pad_maximum_fusion.8), channel_id=1, source_target_pairs={{0,8},{1,5},{2,10},{3,7},{4,12},{5,1},{6,14},{7,3},{8,0},{9,13},{1... | collective-permute-start | bytes 294920 | tf_op jit(solution)/shard_map/ppermute | solution.py:311
  70.8 4.3 %collective-permute-done.13 = bf16[32,1664]{1,0:T(8,128)(2,1)S(1)} collective-permute-done((bf16[32,1664]{1,0:T(8,128)(2,1)S(1)}, bf16[32,1664]{1,0:T(8,128)(2,1)S(1)}, u32[]{:S(2)}, u32[]{:S(2)}) %collective-permute-start.13) | collective-permute-done | bytes 106528 | tf_op jit(solution)/shard_map/ppermute | solution.py:311
  76.7 4.3 %collective-permute-done.14 = bf16[64,1664]{1,0:T(8,128)(2,1)S(1)} collective-permute-done((bf16[64,1664]{1,0:T(8,128)(2,1)S(1)}, bf16[64,1664]{1,0:T(8,128)(2,1)S(1)}, u32[]{:S(2)}, u32[]{:S(2)}) %collective-permute-start.14) | collective-permute-done | bytes 213024 | tf_op jit(solution)/shard_map/ppermute | solution.py:311
  84.5 7.1 %shard_map.122 = (bf16[4096,768]{1,0:T(8,128)(2,1)S(1)}, bf16[4096,768]{1,0:T(8,128)(2,1)S(1)}, bf16[768,4096]{1,0:T(8,128)(2,1)S(1)}) custom-call(bf16[128,1024]{1,0:T(8,128)(2,1)S(1)} %pad_maximum_fusion.2.refs_4_.after_ref, bf16[4096,768]{1,0:T(8,128)(2,1)} %collective-permute-done.9.refs_0_, bf16[4096,768]{1,0:T(8,128)(2,1)} %collective-permute-done.10.refs_1_, ...), custom_call_target="tpu_custom_call" | custom-call | bytes 18874368 | tf_op jit(solution)/shard_map/pallas_call | solution.py:182
  93.3 4.0 %shard_map.121 = (bf16[256,4096]{1,0:T(8,128)(2,1)S(1)}, bf16[256,768]{1,0:T(8,128)(2,1)S(1)}, f32[256,1]{1,0:T(8,128)S(1)}) custom-call(s32[2]{0:T(128)S(1)} %pad_add_fusion.chip_ref, bf16[128,1664]{1,0:T(8,128)(2,1)S(1)} %pad_maximum_fusion.refs_0_, bf16[128,1664]{1,0:T(8,128)(2,1)S(1)} %collective-permute-done.15.refs_1_, ...), custom_call_target="tpu_custom_call" | custom-call | flops 3221225472 | bytes 12582912 | tf_op jit(solution)/shard_map/pallas_call | solution.py:240
  97.3 3.4 %shard_map.123.after_ref.active1 = bf16[256,768]{1,0:T(8,128)(2,1)S(1)} custom-call(bf16[256,4096]{1,0:T(8,128)(2,1)S(1)} %get-tuple-element.30.tokens_ref, bf16[4096,768]{1,0:T(8,128)(2,1)S(1)} %get-tuple-element.34.gate_ref, bf16[4096,768]{1,0:T(8,128)(2,1)S(1)} %get-tuple-element.35.up_ref), custom_call_target="tpu_custom_call" | custom-call | flops 3221225472 | bytes 12582912 | tf_op jit(solution)/shard_map/pallas_call | solution.py:248
  100.8 1.8 %shard_map.124 = (bf16[128,2048]{1,0:T(8,128)(2,1)S(1)}, bf16[128,2048]{1,0:T(8,128)(2,1)S(1)}) custom-call(bf16[256,768]{1,0:T(8,128)(2,1)S(1)} %shard_map.123.after_ref.active1, bf16[256,768]{1,0:T(8,128)(2,1)S(1)} %get-tuple-element.36.active0, bf16[256,768]{1,0:T(8,128)(2,1)S(1)} %shard_map.123.after_ref.active1, ...), custom_call_target="tpu_custom_call" | custom-call | flops 1610612736 | bytes 6291456 | tf_op jit(solution)/shard_map/pallas_call | solution.py:259
  102.6 1.5 %collective-permute-start.24 = (bf16[128,2048]{1,0:T(8,128)(2,1)S(1)}, bf16[128,2048]{1,0:T(8,128)(2,1)S(1)}, u32[]{:S(2)}, u32[]{:S(2)}) collective-permute-start(bf16[128,2048]{1,0:T(8,128)(2,1)S(1)} %get-tuple-element.40.after_ref), channel_id=1, source_target_pairs={{0,2},{1,9},{2,0},{3,11},{4,6},{5,13},{6,4},{7,15},{8,10},{9,1},{1... | collective-permute-start | bytes 1572872 | tf_op jit(solution)/shard_map/ppermute | solution.py:296
  104.1 1.8 %shard_map.125 = (bf16[128,2048]{1,0:T(8,128)(2,1)S(1)}, bf16[128,2048]{1,0:T(8,128)(2,1)S(1)}) custom-call(bf16[128,2048]{1,0:T(8,128)(2,1)S(1)} %get-tuple-element.40.after_ref, bf16[256,768]{1,0:T(8,128)(2,1)S(1)} %get-tuple-element.36.active0, bf16[256,768]{1,0:T(8,128)(2,1)S(1)} %shard_map.123.after_ref.active1, ...), custom_call_target="tpu_custom_call" | custom-call | flops 1610612736 | bytes 6291456 | tf_op jit(solution)/shard_map/pallas_call | solution.py:259
  106.7 5.1 %collective-permute-done.24 = bf16[128,2048]{1,0:T(8,128)(2,1)S(1)} collective-permute-done((bf16[128,2048]{1,0:T(8,128)(2,1)S(1)}, bf16[128,2048]{1,0:T(8,128)(2,1)S(1)}, u32[]{:S(2)}, u32[]{:S(2)}) %collective-permute-start.24) | collective-permute-done | bytes 524320 | tf_op jit(solution)/shard_map/ppermute | solution.py:296
  113.4 1.8 %collective-permute-done.28 = bf16[128,2048]{1,0:T(8,128)(2,1)S(1)} collective-permute-done((bf16[128,2048]{1,0:T(8,128)(2,1)S(1)}, bf16[128,2048]{1,0:T(8,128)(2,1)S(1)}, u32[]{:S(2)}, u32[]{:S(2)}) %collective-permute-start.28) | collective-permute-done | bytes 524320 | tf_op jit(solution)/shard_map/ppermute | solution.py:296
  116.7 1.8 %collective-permute-done.25 = bf16[64,2048]{1,0:T(8,128)(2,1)S(1)} collective-permute-done((bf16[64,2048]{1,0:T(8,128)(2,1)S(1)}, bf16[64,2048]{1,0:T(8,128)(2,1)S(1)}, u32[]{:S(2)}, u32[]{:S(2)}) %collective-permute-start.25) | collective-permute-done | bytes 262176 | tf_op jit(solution)/shard_map/ppermute | solution.py:296
  118.5 1.4 %collective-permute-start.26 = (bf16[32,2048]{1,0:T(8,128)(2,1)S(1)}, bf16[32,2048]{1,0:T(8,128)(2,1)S(1)}, u32[]{:S(2)}, u32[]{:S(2)}) collective-permute-start(bf16[32,2048]{1,0:T(8,128)(2,1)S(1)} %slice.203), channel_id=1, source_target_pairs={{0,8},{1,5},{2,10},{3,7},{4,12},{5,1},{6,14},{7,3},{8,0},{9,13},{1... | collective-permute-start | bytes 393224 | tf_op jit(solution)/shard_map/ppermute | solution.py:296
  119.9 1.9 %collective-permute-done.29 = bf16[64,2048]{1,0:T(8,128)(2,1)S(1)} collective-permute-done((bf16[64,2048]{1,0:T(8,128)(2,1)S(1)}, bf16[64,2048]{1,0:T(8,128)(2,1)S(1)}, u32[]{:S(2)}, u32[]{:S(2)}) %collective-permute-start.29) | collective-permute-done | bytes 262176 | tf_op jit(solution)/shard_map/ppermute | solution.py:296
  123.6 1.4 %collective-permute-start.27 = (bf16[16,2048]{1,0:T(8,128)(2,1)S(1)}, bf16[16,2048]{1,0:T(8,128)(2,1)S(1)}, u32[]{:S(2)}, u32[]{:S(2)}) collective-permute-start(bf16[16,2048]{1,0:T(8,128)(2,1)S(1)} %slice.207), channel_id=1, source_target_pairs={{0,16},{1,17},{2,18},{3,19},{4,20},{5,21},{6,22},{7,23},{8,24},{9,... | collective-permute-start | bytes 196616 | tf_op jit(solution)/shard_map/ppermute | solution.py:296
  125.0 1.9 %collective-permute-done.30 = bf16[32,2048]{1,0:T(8,128)(2,1)S(1)} collective-permute-done((bf16[32,2048]{1,0:T(8,128)(2,1)S(1)}, bf16[32,2048]{1,0:T(8,128)(2,1)S(1)}, u32[]{:S(2)}, u32[]{:S(2)}) %collective-permute-start.30) | collective-permute-done | bytes 131104 | tf_op jit(solution)/shard_map/ppermute | solution.py:296
  128.9 3.3 %collective-permute-done.31 = bf16[16,2048]{1,0:T(8,128)(2,1)S(1)} collective-permute-done((bf16[16,2048]{1,0:T(8,128)(2,1)S(1)}, bf16[16,2048]{1,0:T(8,128)(2,1)S(1)}, u32[]{:S(2)}, u32[]{:S(2)}) %collective-permute-start.31) | collective-permute-done | bytes 65568 | tf_op jit(solution)/shard_map/ppermute | solution.py:296
  (113 shorter events, 27.1 us)
Async XLA Ops:
  0.0 24.4 %collective-permute-start = (bf16[256,4096]{1,0:T(8,128)(2,1)}, bf16[256,4096]{1,0:T(8,128)(2,1)}, u32[]{:S(2)}, u32[]{:S(2)}) collective-permute-start(bf16[256,4096]{1,0:T(8,128)(2,1)} %own_ref.3), channel_id=1, source_target_pairs={{0,1},{1,0},{2,3},{3,2},{4,5},{5,4},{6,7},{7,6},{8,9},{9,8},{10,11... | collective-permute-start | bytes 6291464 | tf_op jit(solution)/shard_map/ppermute | solution.py:343
  0.5 60.0 %collective-permute-start.11 = (bf16[768,4096]{1,0:T(8,128)(2,1)}, bf16[768,4096]{1,0:T(8,128)(2,1)}, u32[]{:S(2)}, u32[]{:S(2)}) collective-permute-start(bf16[768,4096]{1,0:T(8,128)(2,1)} %bitcast.5), channel_id=1, source_target_pairs={{0,1},{1,0},{2,3},{3,2},{4,5},{5,4},{6,7},{7,6},{8,9},{9,8},{10,11... | collective-permute-start | bytes 18874376 | tf_op jit(solution)/shard_map/ppermute | solution.py:346
  0.5 59.9 %collective-permute-start.10 = (bf16[4096,768]{1,0:T(8,128)(2,1)}, bf16[4096,768]{1,0:T(8,128)(2,1)}, u32[]{:S(2)}, u32[]{:S(2)}) collective-permute-start(bf16[4096,768]{1,0:T(8,128)(2,1)} %bitcast.14), channel_id=1, source_target_pairs={{0,1},{1,0},{2,3},{3,2},{4,5},{5,4},{6,7},{7,6},{8,9},{9,8},{10,11... | collective-permute-start | bytes 18874376 | tf_op jit(solution)/shard_map/ppermute | solution.py:345
  1.0 59.5 %collective-permute-start.9 = (bf16[4096,768]{1,0:T(8,128)(2,1)}, bf16[4096,768]{1,0:T(8,128)(2,1)}, u32[]{:S(2)}, u32[]{:S(2)}) collective-permute-start(bf16[4096,768]{1,0:T(8,128)(2,1)} %bitcast.10), channel_id=1, source_target_pairs={{0,1},{1,0},{2,3},{3,2},{4,5},{5,4},{6,7},{7,6},{8,9},{9,8},{10,11... | collective-permute-start | bytes 18874376 | tf_op jit(solution)/shard_map/ppermute | solution.py:344
  6.0 18.4 %all-to-all-start = ((bf16[16,16,512]{2,1,0:T(8,128)(2,1)}), bf16[16,16,512]{2,1,0:T(8,128)(2,1)S(1)}, u32[]{:S(2)}, u32[]{:S(2)}) async-start(bf16[16,16,512]{2,1,0:T(8,128)(2,1)} %shard_map.118), calls=%async_computation | async-start | bytes 524288 | tf_op jit(solution)/shard_map/all_to_all | solution.py:349
  26.4 9.3 %collective-permute-start.5 = (bf16[128,2048]{1,0:T(8,128)(2,1)S(1)}, bf16[128,2048]{1,0:T(8,128)(2,1)S(1)}, u32[]{:S(2)}, u32[]{:S(2)}) collective-permute-start(bf16[128,2048]{1,0:T(8,128)(2,1)S(1)} %get-tuple-element.27), channel_id=1, source_target_pairs={{0,4},{1,3},{2,6},{3,1},{4,0},{5,7},{6,2},{7,5},{8,12},{9,11},{10,... | collective-permute-start | bytes 1572872 | tf_op jit(solution)/shard_map/ppermute | solution.py:296
  29.5 9.2 %collective-permute-start.1 = (bf16[128,2048]{1,0:T(8,128)(2,1)S(1)}, bf16[128,2048]{1,0:T(8,128)(2,1)S(1)}, u32[]{:S(2)}, u32[]{:S(2)}) collective-permute-start(bf16[128,2048]{1,0:T(8,128)(2,1)S(1)} %get-tuple-element.25), channel_id=1, source_target_pairs={{0,2},{1,9},{2,0},{3,11},{4,6},{5,13},{6,4},{7,15},{8,10},{9,1},{1... | collective-permute-start | bytes 1572872 | tf_op jit(solution)/shard_map/ppermute | solution.py:296
  35.8 7.3 %collective-permute-start.6 = (bf16[64,2048]{1,0:T(8,128)(2,1)S(1)}, bf16[64,2048]{1,0:T(8,128)(2,1)S(1)}, u32[]{:S(2)}, u32[]{:S(2)}) collective-permute-start(bf16[64,2048]{1,0:T(8,128)(2,1)S(1)} %slice.200), channel_id=1, source_target_pairs={{0,8},{1,5},{2,10},{3,7},{4,12},{5,1},{6,14},{7,3},{8,0},{9,13},{1... | collective-permute-start | bytes 786440 | tf_op jit(solution)/shard_map/ppermute | solution.py:296
  39.0 8.1 %collective-permute-start.2 = (bf16[64,2048]{1,0:T(8,128)(2,1)S(1)}, bf16[64,2048]{1,0:T(8,128)(2,1)S(1)}, u32[]{:S(2)}, u32[]{:S(2)}) collective-permute-start(bf16[64,2048]{1,0:T(8,128)(2,1)S(1)} %slice.201), channel_id=1, source_target_pairs={{0,4},{1,3},{2,6},{3,1},{4,0},{5,7},{6,2},{7,5},{8,12},{9,11},{10,... | collective-permute-start | bytes 786440 | tf_op jit(solution)/shard_map/ppermute | solution.py:296
  43.3 5.0 %collective-permute-start.7 = (bf16[32,2048]{1,0:T(8,128)(2,1)S(1)}, bf16[32,2048]{1,0:T(8,128)(2,1)S(1)}, u32[]{:S(2)}, u32[]{:S(2)}) collective-permute-start(bf16[32,2048]{1,0:T(8,128)(2,1)S(1)} %slice.204), channel_id=1, source_target_pairs={{0,2},{1,9},{2,0},{3,11},{4,6},{5,13},{6,4},{7,15},{8,10},{9,1},{1... | collective-permute-start | bytes 393224 | tf_op jit(solution)/shard_map/ppermute | solution.py:296
  47.1 5.7 %collective-permute-start.3 = (bf16[32,2048]{1,0:T(8,128)(2,1)S(1)}, bf16[32,2048]{1,0:T(8,128)(2,1)S(1)}, u32[]{:S(2)}, u32[]{:S(2)}) collective-permute-start(bf16[32,2048]{1,0:T(8,128)(2,1)S(1)} %slice.205), channel_id=1, source_target_pairs={{0,8},{1,5},{2,10},{3,7},{4,12},{5,1},{6,14},{7,3},{8,0},{9,13},{1... | collective-permute-start | bytes 393224 | tf_op jit(solution)/shard_map/ppermute | solution.py:296
  48.3 5.2 %collective-permute-start.8 = (bf16[16,2048]{1,0:T(8,128)(2,1)S(1)}, bf16[16,2048]{1,0:T(8,128)(2,1)S(1)}, u32[]{:S(2)}, u32[]{:S(2)}) collective-permute-start(bf16[16,2048]{1,0:T(8,128)(2,1)S(1)} %slice.208), channel_id=1, source_target_pairs={{0,16},{1,17},{2,18},{3,19},{4,20},{5,21},{6,22},{7,23},{8,24},{9,... | collective-permute-start | bytes 196616 | tf_op jit(solution)/shard_map/ppermute | solution.py:296
  52.9 7.2 %collective-permute-start.4 = (bf16[16,2048]{1,0:T(8,128)(2,1)S(1)}, bf16[16,2048]{1,0:T(8,128)(2,1)S(1)}, u32[]{:S(2)}, u32[]{:S(2)}) collective-permute-start(bf16[16,2048]{1,0:T(8,128)(2,1)S(1)} %slice.209), channel_id=1, source_target_pairs={{0,16},{1,17},{2,18},{3,19},{4,20},{5,21},{6,22},{7,23},{8,24},{9,... | collective-permute-start | bytes 196616 | tf_op jit(solution)/shard_map/ppermute | solution.py:296
  60.5 5.0 %collective-permute-start.20 = (bf16[16,1024]{1,0:T(8,128)(2,1)S(1)}, bf16[16,1024]{1,0:T(8,128)(2,1)S(1)}, u32[]{:S(2)}, u32[]{:S(2)}) collective-permute-start(bf16[16,1024]{1,0:T(8,128)(2,1)S(1)} %slice.123), channel_id=1, source_target_pairs={{0,16},{1,17},{2,18},{3,19},{4,20},{5,21},{6,22},{7,23},{8,24},{9,... | collective-permute-start | bytes 98312 | tf_op jit(solution)/shard_map/ppermute | solution.py:311
  60.6 6.1 %collective-permute-start.16 = (bf16[16,1536]{1,0:T(8,128)(2,1)S(1)}, bf16[16,1536]{1,0:T(8,128)(2,1)S(1)}, u32[]{:S(2)}, u32[]{:S(2)}) collective-permute-start(bf16[16,1536]{1,0:T(8,128)(2,1)S(1)} %get-tuple-element.49), channel_id=1, source_target_pairs={{0,16},{1,17},{2,18},{3,19},{4,20},{5,21},{6,22},{7,23},{8,24},{9,... | collective-permute-start | bytes 147464 | tf_op jit(solution)/shard_map/ppermute | solution.py:311
  63.5 5.6 %collective-permute-start.12 = (bf16[16,1664]{1,0:T(8,128)(2,1)S(1)}, bf16[16,1664]{1,0:T(8,128)(2,1)S(1)}, u32[]{:S(2)}, u32[]{:S(2)}) collective-permute-start(bf16[16,1664]{1,0:T(8,128)(2,1)S(1)} %pad_maximum_fusion.10), channel_id=1, source_target_pairs={{0,16},{1,17},{2,18},{3,19},{4,20},{5,21},{6,22},{7,23},{8,24},{9,... | collective-permute-start | bytes 159752 | tf_op jit(solution)/shard_map/ppermute | solution.py:311
  66.7 9.8 %collective-permute-start.17 = (bf16[32,1536]{1,0:T(8,128)(2,1)S(1)}, bf16[32,1536]{1,0:T(8,128)(2,1)S(1)}, u32[]{:S(2)}, u32[]{:S(2)}) collective-permute-start(bf16[32,1536]{1,0:T(8,128)(2,1)S(1)} %pad_maximum_fusion.8), channel_id=1, source_target_pairs={{0,8},{1,5},{2,10},{3,7},{4,12},{5,1},{6,14},{7,3},{8,0},{9,13},{1... | collective-permute-start | bytes 294920 | tf_op jit(solution)/shard_map/ppermute | solution.py:311
  69.2 5.9 %collective-permute-start.13 = (bf16[32,1664]{1,0:T(8,128)(2,1)S(1)}, bf16[32,1664]{1,0:T(8,128)(2,1)S(1)}, u32[]{:S(2)}, u32[]{:S(2)}) collective-permute-start(bf16[32,1664]{1,0:T(8,128)(2,1)S(1)} %pad_maximum_fusion.7), channel_id=1, source_target_pairs={{0,8},{1,5},{2,10},{3,7},{4,12},{5,1},{6,14},{7,3},{8,0},{9,13},{1... | collective-permute-start | bytes 319496 | tf_op jit(solution)/shard_map/ppermute | solution.py:311
  69.7 13.3 %collective-permute-start.22 = (bf16[64,1024]{1,0:T(8,128)(2,1)S(1)}, bf16[64,1024]{1,0:T(8,128)(2,1)S(1)}, u32[]{:S(2)}, u32[]{:S(2)}) collective-permute-start(bf16[64,1024]{1,0:T(8,128)(2,1)S(1)} %pad_maximum_fusion.5), channel_id=1, source_target_pairs={{0,2},{1,9},{2,0},{3,11},{4,6},{5,13},{6,4},{7,15},{8,10},{9,1},{1... | collective-permute-start | bytes 393224 | tf_op jit(solution)/shard_map/ppermute | solution.py:311
  75.1 5.9 %collective-permute-start.14 = (bf16[64,1664]{1,0:T(8,128)(2,1)S(1)}, bf16[64,1664]{1,0:T(8,128)(2,1)S(1)}, u32[]{:S(2)}, u32[]{:S(2)}) collective-permute-start(bf16[64,1664]{1,0:T(8,128)(2,1)S(1)} %pad_maximum_fusion.3), channel_id=1, source_target_pairs={{0,4},{1,3},{2,6},{3,1},{4,0},{5,7},{6,2},{7,5},{8,12},{9,11},{10,... | collective-permute-start | bytes 638984 | tf_op jit(solution)/shard_map/ppermute | solution.py:311
  76.5 5.7 %collective-permute-start.18 = (bf16[64,1536]{1,0:T(8,128)(2,1)S(1)}, bf16[64,1536]{1,0:T(8,128)(2,1)S(1)}, u32[]{:S(2)}, u32[]{:S(2)}) collective-permute-start(bf16[64,1536]{1,0:T(8,128)(2,1)S(1)} %pad_maximum_fusion.4), channel_id=1, source_target_pairs={{0,2},{1,9},{2,0},{3,11},{4,6},{5,13},{6,4},{7,15},{8,10},{9,1},{1... | collective-permute-start | bytes 589832 | tf_op jit(solution)/shard_map/ppermute | solution.py:311
  81.1 10.6 %collective-permute-start.15 = (bf16[128,1664]{1,0:T(8,128)(2,1)S(1)}, bf16[128,1664]{1,0:T(8,128)(2,1)S(1)}, u32[]{:S(2)}, u32[]{:S(2)}) collective-permute-start(bf16[128,1664]{1,0:T(8,128)(2,1)S(1)} %pad_maximum_fusion.refs_0_), channel_id=1, source_target_pairs={{0,2},{1,9},{2,0},{3,11},{4,6},{5,13},{6,4},{7,15},{8,10},{9,1},{1... | collective-permute-start | bytes 1277960 | tf_op jit(solution)/shard_map/ppermute | solution.py:311
  82.3 9.4 %collective-permute-start.19 = (bf16[128,1536]{1,0:T(8,128)(2,1)S(1)}, bf16[128,1536]{1,0:T(8,128)(2,1)S(1)}, u32[]{:S(2)}, u32[]{:S(2)}) collective-permute-start(bf16[128,1536]{1,0:T(8,128)(2,1)S(1)} %pad_maximum_fusion.1.refs_2_), channel_id=1, source_target_pairs={{0,4},{1,3},{2,6},{3,1},{4,0},{5,7},{6,2},{7,5},{8,12},{9,11},{10,... | collective-permute-start | bytes 1179656 | tf_op jit(solution)/shard_map/ppermute | solution.py:311
  83.1 8.5 %collective-permute-start.23 = (bf16[128,1024]{1,0:T(8,128)(2,1)S(1)}, bf16[128,1024]{1,0:T(8,128)(2,1)S(1)}, u32[]{:S(2)}, u32[]{:S(2)}) collective-permute-start(bf16[128,1024]{1,0:T(8,128)(2,1)S(1)} %pad_maximum_fusion.2.refs_4_.after_ref), channel_id=1, source_target_pairs={{0,8},{1,5},{2,10},{3,7},{4,12},{5,1},{6,14},{7,3},{8,0},{9,13},{1... | collective-permute-start | bytes 786440 | tf_op jit(solution)/shard_map/ppermute | solution.py:311
  102.6 9.2 %collective-permute-start.24 = (bf16[128,2048]{1,0:T(8,128)(2,1)S(1)}, bf16[128,2048]{1,0:T(8,128)(2,1)S(1)}, u32[]{:S(2)}, u32[]{:S(2)}) collective-permute-start(bf16[128,2048]{1,0:T(8,128)(2,1)S(1)} %get-tuple-element.40.after_ref), channel_id=1, source_target_pairs={{0,2},{1,9},{2,0},{3,11},{4,6},{5,13},{6,4},{7,15},{8,10},{9,1},{1... | collective-permute-start | bytes 1572872 | tf_op jit(solution)/shard_map/ppermute | solution.py:296
  105.9 9.2 %collective-permute-start.28 = (bf16[128,2048]{1,0:T(8,128)(2,1)S(1)}, bf16[128,2048]{1,0:T(8,128)(2,1)S(1)}, u32[]{:S(2)}, u32[]{:S(2)}) collective-permute-start(bf16[128,2048]{1,0:T(8,128)(2,1)S(1)} %get-tuple-element.42), channel_id=1, source_target_pairs={{0,4},{1,3},{2,6},{3,1},{4,0},{5,7},{6,2},{7,5},{8,12},{9,11},{10,... | collective-permute-start | bytes 1572872 | tf_op jit(solution)/shard_map/ppermute | solution.py:296
  112.0 6.4 %collective-permute-start.25 = (bf16[64,2048]{1,0:T(8,128)(2,1)S(1)}, bf16[64,2048]{1,0:T(8,128)(2,1)S(1)}, u32[]{:S(2)}, u32[]{:S(2)}) collective-permute-start(bf16[64,2048]{1,0:T(8,128)(2,1)S(1)} %slice.199), channel_id=1, source_target_pairs={{0,4},{1,3},{2,6},{3,1},{4,0},{5,7},{6,2},{7,5},{8,12},{9,11},{10,... | collective-permute-start | bytes 786440 | tf_op jit(solution)/shard_map/ppermute | solution.py:296
  115.3 6.4 %collective-permute-start.29 = (bf16[64,2048]{1,0:T(8,128)(2,1)S(1)}, bf16[64,2048]{1,0:T(8,128)(2,1)S(1)}, u32[]{:S(2)}, u32[]{:S(2)}) collective-permute-start(bf16[64,2048]{1,0:T(8,128)(2,1)S(1)} %slice.198), channel_id=1, source_target_pairs={{0,8},{1,5},{2,10},{3,7},{4,12},{5,1},{6,14},{7,3},{8,0},{9,13},{1... | collective-permute-start | bytes 786440 | tf_op jit(solution)/shard_map/ppermute | solution.py:296
  118.5 5.0 %collective-permute-start.26 = (bf16[32,2048]{1,0:T(8,128)(2,1)S(1)}, bf16[32,2048]{1,0:T(8,128)(2,1)S(1)}, u32[]{:S(2)}, u32[]{:S(2)}) collective-permute-start(bf16[32,2048]{1,0:T(8,128)(2,1)S(1)} %slice.203), channel_id=1, source_target_pairs={{0,8},{1,5},{2,10},{3,7},{4,12},{5,1},{6,14},{7,3},{8,0},{9,13},{1... | collective-permute-start | bytes 393224 | tf_op jit(solution)/shard_map/ppermute | solution.py:296
  121.9 5.0 %collective-permute-start.30 = (bf16[32,2048]{1,0:T(8,128)(2,1)S(1)}, bf16[32,2048]{1,0:T(8,128)(2,1)S(1)}, u32[]{:S(2)}, u32[]{:S(2)}) collective-permute-start(bf16[32,2048]{1,0:T(8,128)(2,1)S(1)} %slice.202), channel_id=1, source_target_pairs={{0,2},{1,9},{2,0},{3,11},{4,6},{5,13},{6,4},{7,15},{8,10},{9,1},{1... | collective-permute-start | bytes 393224 | tf_op jit(solution)/shard_map/ppermute | solution.py:296
  123.6 5.2 %collective-permute-start.27 = (bf16[16,2048]{1,0:T(8,128)(2,1)S(1)}, bf16[16,2048]{1,0:T(8,128)(2,1)S(1)}, u32[]{:S(2)}, u32[]{:S(2)}) collective-permute-start(bf16[16,2048]{1,0:T(8,128)(2,1)S(1)} %slice.207), channel_id=1, source_target_pairs={{0,16},{1,17},{2,18},{3,19},{4,20},{5,21},{6,22},{7,23},{8,24},{9,... | collective-permute-start | bytes 196616 | tf_op jit(solution)/shard_map/ppermute | solution.py:296
  127.0 5.2 %collective-permute-start.31 = (bf16[16,2048]{1,0:T(8,128)(2,1)S(1)}, bf16[16,2048]{1,0:T(8,128)(2,1)S(1)}, u32[]{:S(2)}, u32[]{:S(2)}) collective-permute-start(bf16[16,2048]{1,0:T(8,128)(2,1)S(1)} %slice.206), channel_id=1, source_target_pairs={{0,16},{1,17},{2,18},{3,19},{4,20},{5,21},{6,22},{7,23},{8,24},{9,... | collective-permute-start | bytes 196616 | tf_op jit(solution)/shard_map/ppermute | solution.py:296
  (10 other events, 134.1 us)

commit v9 on v8

--- a/solution.py
+++ b/solution.py
@@ -17,7 +17,7 @@
 
 
 REDUCE = ((4, (0, 1, 2)), (4, (1, 2, 0)))
-GATHER = ((3, (0, 1, 2)), (3, (1, 0, 2)), (2, (2, 0, 1)))
+GATHER = ((3, (0, 1, 2)), (3, (1, 2, 0)), (2, (2, 0, 1)))
 
 
 GROUP = 8

time: 133 us -> 133 us (level)
  starting transfers between devices: 39 us -> 35.9 us
  waiting for transfers between devices: 60.7 us -> 63.1 us
    ppermute x16, waiting for transfers between devices: 40.3 us -> 42.1 us  [reduce_slots(): came = lax.ppermute(sent[c], 'dp', swap_step(step, order, devices))]
    ppermute x16, starting transfers between devices: 17.8 us -> 16.1 us  [reduce_slots(): came = lax.ppermute(sent[c], 'dp', swap_step(step, order, devices))]
    ppermute x12, starting transfers between devices: 11.9 us -> 10.4 us  [gather_slots(): came = lax.ppermute(own[c], 'dp', swap_step(step, order, devices))]
  transfers between devices with their start and end apart: 33 -> 33, of which waited for: 22 -> 22; matrix products, arithmetic and copies ran while one was open for 2% -> 3% of each run, Pallas kernels for 13% -> 13%
where the time goes in v9:
time: 133 us
  waiting for transfers between devices  63.1 us (47%)
  starting transfers between devices  35.9 us (27%)
  Pallas kernels  26.8 us (20%)
  local copies, waits for them, and re-layouts  4.1 us (3%)
  other arithmetic  2.27 us (2%)
    ppermute x16, waiting for transfers between devices, reduce_slots(): came = lax.ppermute(sent[c], 'dp', swap_step(step, order, devices))  42.1 us
    ppermute x16, starting transfers between devices, reduce_slots(): came = lax.ppermute(sent[c], 'dp', swap_step(step, order, devices))  16.1 us
    ppermute x12, waiting for transfers between devices, gather_slots(): came = lax.ppermute(own[c], 'dp', swap_step(step, order, devices))  12.5 us
    ppermute x12, starting transfers between devices, gather_slots(): came = lax.ppermute(own[c], 'dp', swap_step(step, order, devices))  10.4 us
    all_to_all x1, waiting for transfers between devices, per_device(): lax.all_to_all(attn_out, 'dp', split_axis=0, concat_axis=0, axis_index_gr...  8.55 us
    all_to_all x1, starting transfers between devices, per_device(): lax.all_to_all(attn_out, 'dp', split_axis=0, concat_axis=0, axis_index_gr...  8.31 us
    pallas_call x1, Pallas kernels, bring(): pl.pallas_call(bring_kernel, out_shape=[jax.ShapeDtypeStruct(a.shape, a.d...  6.89 us
    pallas_call x1, Pallas kernels, attend(): pl.pallas_call(attend_kernel, out_shape=jax.ShapeDtypeStruct((chips, rows...  4.91 us
  transfers between devices with their start and end apart: 33, of which 22 were waited for; matrix products, arithmetic and copies ran while one was open for 3% of the time, Pallas kernels for 13%

profile of v9, /device:TPU:0, one launch (start us, length us, event | category | flops | bytes accessed | tf_op | source)
XLA Modules:
  0.0 132.6 jit_solution(17309249648596362236)
XLA Ops:
  1.0 4.9 %shard_map.118 = bf16[16,16,512]{2,1,0:T(8,128)(2,1)} custom-call(s32[1]{0:T(128)} %bitcast.core_ref, s32[16]{0:T(128)} %lengths_ref.1, bf16[16,8192]{1,0:T(8,128)(2,1)} %q_ref.1, bf16[2,16,512]{2,1,0:T(8,128)(2,1)} %new_ref.1, bf16[2,16,128,512]{3,2,1,0:T(8,128)(2,1)} %cache_ref.1), custom_call_target="tpu_custom_call" | custom-call | flops 67108864 | bytes 4194304 | tf_op jit(solution)/shard_map/pallas_call | solution.py:94
  6.0 8.3 %all-to-all-start = ((bf16[16,16,512]{2,1,0:T(8,128)(2,1)}), bf16[16,16,512]{2,1,0:T(8,128)(2,1)S(1)}, u32[]{:S(2)}, u32[]{:S(2)}) async-start(bf16[16,16,512]{2,1,0:T(8,128)(2,1)} %shard_map.118), calls=%async_computation | async-start | bytes 524288 | tf_op jit(solution)/shard_map/all_to_all | solution.py:349
  15.8 8.5 %all-to-all-done.blocks_ref = bf16[16,16,512]{2,1,0:T(8,128)(2,1)S(1)} async-done(((bf16[16,16,512]{2,1,0:T(8,128)(2,1)}), bf16[16,16,512]{2,1,0:T(8,128)(2,1)S(1)}, u32[]{:S(2)}, u32[]{:S(2)}) %all-to-all-start) | async-done | bytes 262176 | tf_op jit(solution)/shard_map/all_to_all | solution.py:349
  24.4 2.0 %shard_map.120 = (bf16[128,2048]{1,0:T(8,128)(2,1)S(1)}, bf16[128,2048]{1,0:T(8,128)(2,1)S(1)}) custom-call(s32[16]{0:T(128)S(1)} %add_xor_fusion.index_ref, bf16[16,16,512]{2,1,0:T(8,128)(2,1)S(1)} %all-to-all-done.blocks_ref, bf16[256,4096]{1,0:T(8,128)(2,1)S(1)} %copy-done, bf16[256,4096]{1,0:T(8,128)(2,1)} %collective-permute-done.other_ref), custom_call_target="tpu_custom_call" | custom-call | flops 536870912 | bytes 2097152 | tf_op jit(solution)/shard_map/pallas_call | solution.py:153
  27.5 2.0 %shard_map.119 = (bf16[128,2048]{1,0:T(8,128)(2,1)S(1)}, bf16[128,2048]{1,0:T(8,128)(2,1)S(1)}) custom-call(s32[16]{0:T(128)S(1)} %add_xor_fusion.index_ref, bf16[16,16,512]{2,1,0:T(8,128)(2,1)S(1)} %all-to-all-done.blocks_ref, bf16[256,4096]{1,0:T(8,128)(2,1)S(1)} %copy-done, bf16[256,4096]{1,0:T(8,128)(2,1)} %collective-permute-done.other_ref), custom_call_target="tpu_custom_call" | custom-call | flops 536870912 | bytes 2097152 | tf_op jit(solution)/shard_map/pallas_call | solution.py:153
  30.2 5.5 %collective-permute-done.5 = bf16[128,2048]{1,0:T(8,128)(2,1)S(1)} collective-permute-done((bf16[128,2048]{1,0:T(8,128)(2,1)S(1)}, bf16[128,2048]{1,0:T(8,128)(2,1)S(1)}, u32[]{:S(2)}, u32[]{:S(2)}) %collective-permute-start.5) | collective-permute-done | bytes 524320 | tf_op jit(solution)/shard_map/ppermute | solution.py:296
  35.8 1.5 %collective-permute-start.6 = (bf16[64,2048]{1,0:T(8,128)(2,1)S(1)}, bf16[64,2048]{1,0:T(8,128)(2,1)S(1)}, u32[]{:S(2)}, u32[]{:S(2)}) collective-permute-start(bf16[64,2048]{1,0:T(8,128)(2,1)S(1)} %slice.200), channel_id=1, source_target_pairs={{0,8},{1,5},{2,10},{3,7},{4,12},{5,1},{6,14},{7,3},{8,0},{9,13},{1... | collective-permute-start | bytes 786440 | tf_op jit(solution)/shard_map/ppermute | solution.py:296
  37.4 1.4 %collective-permute-done.1 = bf16[128,2048]{1,0:T(8,128)(2,1)S(1)} collective-permute-done((bf16[128,2048]{1,0:T(8,128)(2,1)S(1)}, bf16[128,2048]{1,0:T(8,128)(2,1)S(1)}, u32[]{:S(2)}, u32[]{:S(2)}) %collective-permute-start.1) | collective-permute-done | bytes 524320 | tf_op jit(solution)/shard_map/ppermute | solution.py:296
  39.0 2.7 %collective-permute-start.2 = (bf16[64,2048]{1,0:T(8,128)(2,1)S(1)}, bf16[64,2048]{1,0:T(8,128)(2,1)S(1)}, u32[]{:S(2)}, u32[]{:S(2)}) collective-permute-start(bf16[64,2048]{1,0:T(8,128)(2,1)S(1)} %slice.201), channel_id=1, source_target_pairs={{0,4},{1,3},{2,6},{3,1},{4,0},{5,7},{6,2},{7,5},{8,12},{9,11},{10,... | collective-permute-start | bytes 786440 | tf_op jit(solution)/shard_map/ppermute | solution.py:296
  41.6 1.5 %collective-permute-done.6 = bf16[64,2048]{1,0:T(8,128)(2,1)S(1)} collective-permute-done((bf16[64,2048]{1,0:T(8,128)(2,1)S(1)}, bf16[64,2048]{1,0:T(8,128)(2,1)S(1)}, u32[]{:S(2)}, u32[]{:S(2)}) %collective-permute-start.6) | collective-permute-done | bytes 262176 | tf_op jit(solution)/shard_map/ppermute | solution.py:296
  43.3 3.7 %collective-permute-done.2 = bf16[64,2048]{1,0:T(8,128)(2,1)S(1)} collective-permute-done((bf16[64,2048]{1,0:T(8,128)(2,1)S(1)}, bf16[64,2048]{1,0:T(8,128)(2,1)S(1)}, u32[]{:S(2)}, u32[]{:S(2)}) %collective-permute-start.2) | collective-permute-done | bytes 262176 | tf_op jit(solution)/shard_map/ppermute | solution.py:296
  49.6 3.3 %collective-permute-done.3 = bf16[32,2048]{1,0:T(8,128)(2,1)S(1)} collective-permute-done((bf16[32,2048]{1,0:T(8,128)(2,1)S(1)}, bf16[32,2048]{1,0:T(8,128)(2,1)S(1)}, u32[]{:S(2)}, u32[]{:S(2)}) %collective-permute-start.3) | collective-permute-done | bytes 131104 | tf_op jit(solution)/shard_map/ppermute | solution.py:296
  53.6 6.6 %collective-permute-done.4 = bf16[16,2048]{1,0:T(8,128)(2,1)S(1)} collective-permute-done((bf16[16,2048]{1,0:T(8,128)(2,1)S(1)}, bf16[16,2048]{1,0:T(8,128)(2,1)S(1)}, u32[]{:S(2)}, u32[]{:S(2)}) %collective-permute-start.4) | collective-permute-done | bytes 65568 | tf_op jit(solution)/shard_map/ppermute | solution.py:296
  60.6 3.0 %collective-permute-start.16 = (bf16[16,1536]{1,0:T(8,128)(2,1)S(1)}, bf16[16,1536]{1,0:T(8,128)(2,1)S(1)}, u32[]{:S(2)}, u32[]{:S(2)}) collective-permute-start(bf16[16,1536]{1,0:T(8,128)(2,1)S(1)} %get-tuple-element.49), channel_id=1, source_target_pairs={{0,16},{1,17},{2,18},{3,19},{4,20},{5,21},{6,22},{7,23},{8,24},{9,... | collective-permute-start | bytes 147464 | tf_op jit(solution)/shard_map/ppermute | solution.py:311
  63.6 1.8 %collective-permute-done.20 = bf16[16,1024]{1,0:T(8,128)(2,1)S(1)} collective-permute-done((bf16[16,1024]{1,0:T(8,128)(2,1)S(1)}, bf16[16,1024]{1,0:T(8,128)(2,1)S(1)}, u32[]{:S(2)}, u32[]{:S(2)}) %collective-permute-start.20) | collective-permute-done | bytes 32800 | tf_op jit(solution)/shard_map/ppermute | solution.py:311
  68.8 1.3 %collective-permute-done.21 = bf16[32,1024]{1,0:T(8,128)(2,1)S(1)} collective-permute-done((bf16[32,1024]{1,0:T(8,128)(2,1)S(1)}, bf16[32,1024]{1,0:T(8,128)(2,1)S(1)}, u32[]{:S(2)}, u32[]{:S(2)}) %collective-permute-start.21) | collective-permute-done | bytes 65568 | tf_op jit(solution)/shard_map/ppermute | solution.py:311
  71.2 3.5 %collective-permute-done.13 = bf16[32,1664]{1,0:T(8,128)(2,1)S(1)} collective-permute-done((bf16[32,1664]{1,0:T(8,128)(2,1)S(1)}, bf16[32,1664]{1,0:T(8,128)(2,1)S(1)}, u32[]{:S(2)}, u32[]{:S(2)}) %collective-permute-start.13) | collective-permute-done | bytes 106528 | tf_op jit(solution)/shard_map/ppermute | solution.py:311
  76.1 4.4 %collective-permute-done.14 = bf16[64,1664]{1,0:T(8,128)(2,1)S(1)} collective-permute-done((bf16[64,1664]{1,0:T(8,128)(2,1)S(1)}, bf16[64,1664]{1,0:T(8,128)(2,1)S(1)}, u32[]{:S(2)}, u32[]{:S(2)}) %collective-permute-start.14) | collective-permute-done | bytes 213024 | tf_op jit(solution)/shard_map/ppermute | solution.py:311
  83.7 6.9 %shard_map.122 = (bf16[4096,768]{1,0:T(8,128)(2,1)S(1)}, bf16[4096,768]{1,0:T(8,128)(2,1)S(1)}, bf16[768,4096]{1,0:T(8,128)(2,1)S(1)}) custom-call(bf16[128,1024]{1,0:T(8,128)(2,1)S(1)} %pad_maximum_fusion.2.refs_4_.after_ref, bf16[4096,768]{1,0:T(8,128)(2,1)} %collective-permute-done.9.refs_0_, bf16[4096,768]{1,0:T(8,128)(2,1)} %collective-permute-done.10.refs_1_, ...), custom_call_target="tpu_custom_call" | custom-call | bytes 18874368 | tf_op jit(solution)/shard_map/pallas_call | solution.py:182
  92.9 4.0 %shard_map.121 = (bf16[256,4096]{1,0:T(8,128)(2,1)S(1)}, bf16[256,768]{1,0:T(8,128)(2,1)S(1)}, f32[256,1]{1,0:T(8,128)S(1)}) custom-call(s32[2]{0:T(128)S(1)} %pad_add_fusion.chip_ref, bf16[128,1664]{1,0:T(8,128)(2,1)S(1)} %pad_maximum_fusion.refs_0_, bf16[128,1664]{1,0:T(8,128)(2,1)S(1)} %collective-permute-done.15.refs_1_, ...), custom_call_target="tpu_custom_call" | custom-call | flops 3221225472 | bytes 12582912 | tf_op jit(solution)/shard_map/pallas_call | solution.py:240
  96.9 3.4 %shard_map.123.after_ref.active1 = bf16[256,768]{1,0:T(8,128)(2,1)S(1)} custom-call(bf16[256,4096]{1,0:T(8,128)(2,1)S(1)} %get-tuple-element.30.tokens_ref, bf16[4096,768]{1,0:T(8,128)(2,1)S(1)} %get-tuple-element.34.gate_ref, bf16[4096,768]{1,0:T(8,128)(2,1)S(1)} %get-tuple-element.35.up_ref), custom_call_target="tpu_custom_call" | custom-call | flops 3221225472 | bytes 12582912 | tf_op jit(solution)/shard_map/pallas_call | solution.py:248
  100.4 1.8 %shard_map.124 = (bf16[128,2048]{1,0:T(8,128)(2,1)S(1)}, bf16[128,2048]{1,0:T(8,128)(2,1)S(1)}) custom-call(bf16[256,768]{1,0:T(8,128)(2,1)S(1)} %shard_map.123.after_ref.active1, bf16[256,768]{1,0:T(8,128)(2,1)S(1)} %get-tuple-element.36.active0, bf16[256,768]{1,0:T(8,128)(2,1)S(1)} %shard_map.123.after_ref.active1, ...), custom_call_target="tpu_custom_call" | custom-call | flops 1610612736 | bytes 6291456 | tf_op jit(solution)/shard_map/pallas_call | solution.py:259
  102.2 1.3 collective-permute-start.24
  103.5 1.8 %shard_map.125 = (bf16[128,2048]{1,0:T(8,128)(2,1)S(1)}, bf16[128,2048]{1,0:T(8,128)(2,1)S(1)}) custom-call(bf16[128,2048]{1,0:T(8,128)(2,1)S(1)} %get-tuple-element.40.after_ref, bf16[256,768]{1,0:T(8,128)(2,1)S(1)} %get-tuple-element.36.active0, bf16[256,768]{1,0:T(8,128)(2,1)S(1)} %shard_map.123.after_ref.active1, ...), custom_call_target="tpu_custom_call" | custom-call | flops 1610612736 | bytes 6291456 | tf_op jit(solution)/shard_map/pallas_call | solution.py:259
  106.2 5.2 %collective-permute-done.24 = bf16[128,2048]{1,0:T(8,128)(2,1)S(1)} collective-permute-done((bf16[128,2048]{1,0:T(8,128)(2,1)S(1)}, bf16[128,2048]{1,0:T(8,128)(2,1)S(1)}, u32[]{:S(2)}, u32[]{:S(2)}) %collective-permute-start.24) | collective-permute-done | bytes 524320 | tf_op jit(solution)/shard_map/ppermute | solution.py:296
  112.8 1.7 %collective-permute-done.28 = bf16[128,2048]{1,0:T(8,128)(2,1)S(1)} collective-permute-done((bf16[128,2048]{1,0:T(8,128)(2,1)S(1)}, bf16[128,2048]{1,0:T(8,128)(2,1)S(1)}, u32[]{:S(2)}, u32[]{:S(2)}) %collective-permute-start.28) | collective-permute-done | bytes 524320 | tf_op jit(solution)/shard_map/ppermute | solution.py:296
  115.0 3.0 %collective-permute-done.25 = bf16[64,2048]{1,0:T(8,128)(2,1)S(1)} collective-permute-done((bf16[64,2048]{1,0:T(8,128)(2,1)S(1)}, bf16[64,2048]{1,0:T(8,128)(2,1)S(1)}, u32[]{:S(2)}, u32[]{:S(2)}) %collective-permute-start.25) | collective-permute-done | bytes 262176 | tf_op jit(solution)/shard_map/ppermute | solution.py:296
  119.0 2.1 %collective-permute-done.29 = bf16[64,2048]{1,0:T(8,128)(2,1)S(1)} collective-permute-done((bf16[64,2048]{1,0:T(8,128)(2,1)S(1)}, bf16[64,2048]{1,0:T(8,128)(2,1)S(1)}, u32[]{:S(2)}, u32[]{:S(2)}) %collective-permute-start.29) | collective-permute-done | bytes 262176 | tf_op jit(solution)/shard_map/ppermute | solution.py:296
  123.2 1.4 %collective-permute-start.27 = (bf16[16,2048]{1,0:T(8,128)(2,1)S(1)}, bf16[16,2048]{1,0:T(8,128)(2,1)S(1)}, u32[]{:S(2)}, u32[]{:S(2)}) collective-permute-start(bf16[16,2048]{1,0:T(8,128)(2,1)S(1)} %slice.207), channel_id=1, source_target_pairs={{0,16},{1,17},{2,18},{3,19},{4,20},{5,21},{6,22},{7,23},{8,24},{9,... | collective-permute-start | bytes 196616 | tf_op jit(solution)/shard_map/ppermute | solution.py:296
  124.6 1.7 %collective-permute-done.30 = bf16[32,2048]{1,0:T(8,128)(2,1)S(1)} collective-permute-done((bf16[32,2048]{1,0:T(8,128)(2,1)S(1)}, bf16[32,2048]{1,0:T(8,128)(2,1)S(1)}, u32[]{:S(2)}, u32[]{:S(2)}) %collective-permute-start.30) | collective-permute-done | bytes 131104 | tf_op jit(solution)/shard_map/ppermute | solution.py:296
  127.3 1.8 %collective-permute-done.27 = bf16[16,2048]{1,0:T(8,128)(2,1)S(1)} collective-permute-done((bf16[16,2048]{1,0:T(8,128)(2,1)S(1)}, bf16[16,2048]{1,0:T(8,128)(2,1)S(1)}, u32[]{:S(2)}, u32[]{:S(2)}) %collective-permute-start.27) | collective-permute-done | bytes 65568 | tf_op jit(solution)/shard_map/ppermute | solution.py:296
  129.2 2.8 %collective-permute-done.31 = bf16[16,2048]{1,0:T(8,128)(2,1)S(1)} collective-permute-done((bf16[16,2048]{1,0:T(8,128)(2,1)S(1)}, bf16[16,2048]{1,0:T(8,128)(2,1)S(1)}, u32[]{:S(2)}, u32[]{:S(2)}) %collective-permute-start.31) | collective-permute-done | bytes 65568 | tf_op jit(solution)/shard_map/ppermute | solution.py:296
  (113 shorter events, 27.2 us)
Async XLA Ops:
  0.0 24.4 %collective-permute-start = (bf16[256,4096]{1,0:T(8,128)(2,1)}, bf16[256,4096]{1,0:T(8,128)(2,1)}, u32[]{:S(2)}, u32[]{:S(2)}) collective-permute-start(bf16[256,4096]{1,0:T(8,128)(2,1)} %own_ref.3), channel_id=1, source_target_pairs={{0,1},{1,0},{2,3},{3,2},{4,5},{5,4},{6,7},{7,6},{8,9},{9,8},{10,11... | collective-permute-start | bytes 6291464 | tf_op jit(solution)/shard_map/ppermute | solution.py:343
  0.5 60.0 %collective-permute-start.11 = (bf16[768,4096]{1,0:T(8,128)(2,1)}, bf16[768,4096]{1,0:T(8,128)(2,1)}, u32[]{:S(2)}, u32[]{:S(2)}) collective-permute-start(bf16[768,4096]{1,0:T(8,128)(2,1)} %bitcast.5), channel_id=1, source_target_pairs={{0,1},{1,0},{2,3},{3,2},{4,5},{5,4},{6,7},{7,6},{8,9},{9,8},{10,11... | collective-permute-start | bytes 18874376 | tf_op jit(solution)/shard_map/ppermute | solution.py:346
  0.5 59.9 %collective-permute-start.10 = (bf16[4096,768]{1,0:T(8,128)(2,1)}, bf16[4096,768]{1,0:T(8,128)(2,1)}, u32[]{:S(2)}, u32[]{:S(2)}) collective-permute-start(bf16[4096,768]{1,0:T(8,128)(2,1)} %bitcast.14), channel_id=1, source_target_pairs={{0,1},{1,0},{2,3},{3,2},{4,5},{5,4},{6,7},{7,6},{8,9},{9,8},{10,11... | collective-permute-start | bytes 18874376 | tf_op jit(solution)/shard_map/ppermute | solution.py:345
  1.0 59.5 %collective-permute-start.9 = (bf16[4096,768]{1,0:T(8,128)(2,1)}, bf16[4096,768]{1,0:T(8,128)(2,1)}, u32[]{:S(2)}, u32[]{:S(2)}) collective-permute-start(bf16[4096,768]{1,0:T(8,128)(2,1)} %bitcast.10), channel_id=1, source_target_pairs={{0,1},{1,0},{2,3},{3,2},{4,5},{5,4},{6,7},{7,6},{8,9},{9,8},{10,11... | collective-permute-start | bytes 18874376 | tf_op jit(solution)/shard_map/ppermute | solution.py:344
  6.0 18.4 %all-to-all-start = ((bf16[16,16,512]{2,1,0:T(8,128)(2,1)}), bf16[16,16,512]{2,1,0:T(8,128)(2,1)S(1)}, u32[]{:S(2)}, u32[]{:S(2)}) async-start(bf16[16,16,512]{2,1,0:T(8,128)(2,1)} %shard_map.118), calls=%async_computation | async-start | bytes 524288 | tf_op jit(solution)/shard_map/all_to_all | solution.py:349
  26.4 9.3 %collective-permute-start.5 = (bf16[128,2048]{1,0:T(8,128)(2,1)S(1)}, bf16[128,2048]{1,0:T(8,128)(2,1)S(1)}, u32[]{:S(2)}, u32[]{:S(2)}) collective-permute-start(bf16[128,2048]{1,0:T(8,128)(2,1)S(1)} %get-tuple-element.27), channel_id=1, source_target_pairs={{0,4},{1,3},{2,6},{3,1},{4,0},{5,7},{6,2},{7,5},{8,12},{9,11},{10,... | collective-permute-start | bytes 1572872 | tf_op jit(solution)/shard_map/ppermute | solution.py:296
  29.5 9.2 %collective-permute-start.1 = (bf16[128,2048]{1,0:T(8,128)(2,1)S(1)}, bf16[128,2048]{1,0:T(8,128)(2,1)S(1)}, u32[]{:S(2)}, u32[]{:S(2)}) collective-permute-start(bf16[128,2048]{1,0:T(8,128)(2,1)S(1)} %get-tuple-element.25), channel_id=1, source_target_pairs={{0,2},{1,9},{2,0},{3,11},{4,6},{5,13},{6,4},{7,15},{8,10},{9,1},{1... | collective-permute-start | bytes 1572872 | tf_op jit(solution)/shard_map/ppermute | solution.py:296
  35.8 7.3 %collective-permute-start.6 = (bf16[64,2048]{1,0:T(8,128)(2,1)S(1)}, bf16[64,2048]{1,0:T(8,128)(2,1)S(1)}, u32[]{:S(2)}, u32[]{:S(2)}) collective-permute-start(bf16[64,2048]{1,0:T(8,128)(2,1)S(1)} %slice.200), channel_id=1, source_target_pairs={{0,8},{1,5},{2,10},{3,7},{4,12},{5,1},{6,14},{7,3},{8,0},{9,13},{1... | collective-permute-start | bytes 786440 | tf_op jit(solution)/shard_map/ppermute | solution.py:296
  39.0 8.1 %collective-permute-start.2 = (bf16[64,2048]{1,0:T(8,128)(2,1)S(1)}, bf16[64,2048]{1,0:T(8,128)(2,1)S(1)}, u32[]{:S(2)}, u32[]{:S(2)}) collective-permute-start(bf16[64,2048]{1,0:T(8,128)(2,1)S(1)} %slice.201), channel_id=1, source_target_pairs={{0,4},{1,3},{2,6},{3,1},{4,0},{5,7},{6,2},{7,5},{8,12},{9,11},{10,... | collective-permute-start | bytes 786440 | tf_op jit(solution)/shard_map/ppermute | solution.py:296
  43.3 5.0 %collective-permute-start.7 = (bf16[32,2048]{1,0:T(8,128)(2,1)S(1)}, bf16[32,2048]{1,0:T(8,128)(2,1)S(1)}, u32[]{:S(2)}, u32[]{:S(2)}) collective-permute-start(bf16[32,2048]{1,0:T(8,128)(2,1)S(1)} %slice.204), channel_id=1, source_target_pairs={{0,2},{1,9},{2,0},{3,11},{4,6},{5,13},{6,4},{7,15},{8,10},{9,1},{1... | collective-permute-start | bytes 393224 | tf_op jit(solution)/shard_map/ppermute | solution.py:296
  47.1 5.7 %collective-permute-start.3 = (bf16[32,2048]{1,0:T(8,128)(2,1)S(1)}, bf16[32,2048]{1,0:T(8,128)(2,1)S(1)}, u32[]{:S(2)}, u32[]{:S(2)}) collective-permute-start(bf16[32,2048]{1,0:T(8,128)(2,1)S(1)} %slice.205), channel_id=1, source_target_pairs={{0,8},{1,5},{2,10},{3,7},{4,12},{5,1},{6,14},{7,3},{8,0},{9,13},{1... | collective-permute-start | bytes 393224 | tf_op jit(solution)/shard_map/ppermute | solution.py:296
  48.3 5.2 %collective-permute-start.8 = (bf16[16,2048]{1,0:T(8,128)(2,1)S(1)}, bf16[16,2048]{1,0:T(8,128)(2,1)S(1)}, u32[]{:S(2)}, u32[]{:S(2)}) collective-permute-start(bf16[16,2048]{1,0:T(8,128)(2,1)S(1)} %slice.208), channel_id=1, source_target_pairs={{0,16},{1,17},{2,18},{3,19},{4,20},{5,21},{6,22},{7,23},{8,24},{9,... | collective-permute-start | bytes 196616 | tf_op jit(solution)/shard_map/ppermute | solution.py:296
  52.9 7.2 %collective-permute-start.4 = (bf16[16,2048]{1,0:T(8,128)(2,1)S(1)}, bf16[16,2048]{1,0:T(8,128)(2,1)S(1)}, u32[]{:S(2)}, u32[]{:S(2)}) collective-permute-start(bf16[16,2048]{1,0:T(8,128)(2,1)S(1)} %slice.209), channel_id=1, source_target_pairs={{0,16},{1,17},{2,18},{3,19},{4,20},{5,21},{6,22},{7,23},{8,24},{9,... | collective-permute-start | bytes 196616 | tf_op jit(solution)/shard_map/ppermute | solution.py:296
  60.5 5.0 %collective-permute-start.20 = (bf16[16,1024]{1,0:T(8,128)(2,1)S(1)}, bf16[16,1024]{1,0:T(8,128)(2,1)S(1)}, u32[]{:S(2)}, u32[]{:S(2)}) collective-permute-start(bf16[16,1024]{1,0:T(8,128)(2,1)S(1)} %slice.123), channel_id=1, source_target_pairs={{0,16},{1,17},{2,18},{3,19},{4,20},{5,21},{6,22},{7,23},{8,24},{9,... | collective-permute-start | bytes 98312 | tf_op jit(solution)/shard_map/ppermute | solution.py:311
  60.6 6.2 %collective-permute-start.16 = (bf16[16,1536]{1,0:T(8,128)(2,1)S(1)}, bf16[16,1536]{1,0:T(8,128)(2,1)S(1)}, u32[]{:S(2)}, u32[]{:S(2)}) collective-permute-start(bf16[16,1536]{1,0:T(8,128)(2,1)S(1)} %get-tuple-element.49), channel_id=1, source_target_pairs={{0,16},{1,17},{2,18},{3,19},{4,20},{5,21},{6,22},{7,23},{8,24},{9,... | collective-permute-start | bytes 147464 | tf_op jit(solution)/shard_map/ppermute | solution.py:311
  63.5 5.2 %collective-permute-start.12 = (bf16[16,1664]{1,0:T(8,128)(2,1)S(1)}, bf16[16,1664]{1,0:T(8,128)(2,1)S(1)}, u32[]{:S(2)}, u32[]{:S(2)}) collective-permute-start(bf16[16,1664]{1,0:T(8,128)(2,1)S(1)} %pad_maximum_fusion.10), channel_id=1, source_target_pairs={{0,16},{1,17},{2,18},{3,19},{4,20},{5,21},{6,22},{7,23},{8,24},{9,... | collective-permute-start | bytes 159752 | tf_op jit(solution)/shard_map/ppermute | solution.py:311
  66.8 9.2 %collective-permute-start.17 = (bf16[32,1536]{1,0:T(8,128)(2,1)S(1)}, bf16[32,1536]{1,0:T(8,128)(2,1)S(1)}, u32[]{:S(2)}, u32[]{:S(2)}) collective-permute-start(bf16[32,1536]{1,0:T(8,128)(2,1)S(1)} %pad_maximum_fusion.8), channel_id=1, source_target_pairs={{0,2},{1,9},{2,0},{3,11},{4,6},{5,13},{6,4},{7,15},{8,10},{9,1},{1... | collective-permute-start | bytes 294920 | tf_op jit(solution)/shard_map/ppermute | solution.py:311
  68.8 5.9 %collective-permute-start.13 = (bf16[32,1664]{1,0:T(8,128)(2,1)S(1)}, bf16[32,1664]{1,0:T(8,128)(2,1)S(1)}, u32[]{:S(2)}, u32[]{:S(2)}) collective-permute-start(bf16[32,1664]{1,0:T(8,128)(2,1)S(1)} %pad_maximum_fusion.7), channel_id=1, source_target_pairs={{0,8},{1,5},{2,10},{3,7},{4,12},{5,1},{6,14},{7,3},{8,0},{9,13},{1... | collective-permute-start | bytes 319496 | tf_op jit(solution)/shard_map/ppermute | solution.py:311
  70.2 12.4 %collective-permute-start.22 = (bf16[64,1024]{1,0:T(8,128)(2,1)S(1)}, bf16[64,1024]{1,0:T(8,128)(2,1)S(1)}, u32[]{:S(2)}, u32[]{:S(2)}) collective-permute-start(bf16[64,1024]{1,0:T(8,128)(2,1)S(1)} %pad_maximum_fusion.5), channel_id=1, source_target_pairs={{0,2},{1,9},{2,0},{3,11},{4,6},{5,13},{6,4},{7,15},{8,10},{9,1},{1... | collective-permute-start | bytes 393224 | tf_op jit(solution)/shard_map/ppermute | solution.py:311
  74.7 5.9 %collective-permute-start.14 = (bf16[64,1664]{1,0:T(8,128)(2,1)S(1)}, bf16[64,1664]{1,0:T(8,128)(2,1)S(1)}, u32[]{:S(2)}, u32[]{:S(2)}) collective-permute-start(bf16[64,1664]{1,0:T(8,128)(2,1)S(1)} %pad_maximum_fusion.3), channel_id=1, source_target_pairs={{0,4},{1,3},{2,6},{3,1},{4,0},{5,7},{6,2},{7,5},{8,12},{9,11},{10,... | collective-permute-start | bytes 638984 | tf_op jit(solution)/shard_map/ppermute | solution.py:311
  76.0 5.7 %collective-permute-start.18 = (bf16[64,1536]{1,0:T(8,128)(2,1)S(1)}, bf16[64,1536]{1,0:T(8,128)(2,1)S(1)}, u32[]{:S(2)}, u32[]{:S(2)}) collective-permute-start(bf16[64,1536]{1,0:T(8,128)(2,1)S(1)} %pad_maximum_fusion.4), channel_id=1, source_target_pairs={{0,8},{1,5},{2,10},{3,7},{4,12},{5,1},{6,14},{7,3},{8,0},{9,13},{1... | collective-permute-start | bytes 589832 | tf_op jit(solution)/shard_map/ppermute | solution.py:311
  80.6 10.0 %collective-permute-start.15 = (bf16[128,1664]{1,0:T(8,128)(2,1)S(1)}, bf16[128,1664]{1,0:T(8,128)(2,1)S(1)}, u32[]{:S(2)}, u32[]{:S(2)}) collective-permute-start(bf16[128,1664]{1,0:T(8,128)(2,1)S(1)} %pad_maximum_fusion.refs_0_), channel_id=1, source_target_pairs={{0,2},{1,9},{2,0},{3,11},{4,6},{5,13},{6,4},{7,15},{8,10},{9,1},{1... | collective-permute-start | bytes 1277960 | tf_op jit(solution)/shard_map/ppermute | solution.py:311
  81.7 8.8 %collective-permute-start.19 = (bf16[128,1536]{1,0:T(8,128)(2,1)S(1)}, bf16[128,1536]{1,0:T(8,128)(2,1)S(1)}, u32[]{:S(2)}, u32[]{:S(2)}) collective-permute-start(bf16[128,1536]{1,0:T(8,128)(2,1)S(1)} %pad_maximum_fusion.1.refs_2_), channel_id=1, source_target_pairs={{0,4},{1,3},{2,6},{3,1},{4,0},{5,7},{6,2},{7,5},{8,12},{9,11},{10,... | collective-permute-start | bytes 1179656 | tf_op jit(solution)/shard_map/ppermute | solution.py:311
  82.7 7.9 %collective-permute-start.23 = (bf16[128,1024]{1,0:T(8,128)(2,1)S(1)}, bf16[128,1024]{1,0:T(8,128)(2,1)S(1)}, u32[]{:S(2)}, u32[]{:S(2)}) collective-permute-start(bf16[128,1024]{1,0:T(8,128)(2,1)S(1)} %pad_maximum_fusion.2.refs_4_.after_ref), channel_id=1, source_target_pairs={{0,8},{1,5},{2,10},{3,7},{4,12},{5,1},{6,14},{7,3},{8,0},{9,13},{1... | collective-permute-start | bytes 786440 | tf_op jit(solution)/shard_map/ppermute | solution.py:311
  102.2 9.2 %collective-permute-start.24 = (bf16[128,2048]{1,0:T(8,128)(2,1)S(1)}, bf16[128,2048]{1,0:T(8,128)(2,1)S(1)}, u32[]{:S(2)}, u32[]{:S(2)}) collective-permute-start(bf16[128,2048]{1,0:T(8,128)(2,1)S(1)} %get-tuple-element.40.after_ref), channel_id=1, source_target_pairs={{0,2},{1,9},{2,0},{3,11},{4,6},{5,13},{6,4},{7,15},{8,10},{9,1},{1... | collective-permute-start | bytes 1572872 | tf_op jit(solution)/shard_map/ppermute | solution.py:296
  105.3 9.2 %collective-permute-start.28 = (bf16[128,2048]{1,0:T(8,128)(2,1)S(1)}, bf16[128,2048]{1,0:T(8,128)(2,1)S(1)}, u32[]{:S(2)}, u32[]{:S(2)}) collective-permute-start(bf16[128,2048]{1,0:T(8,128)(2,1)S(1)} %get-tuple-element.42), channel_id=1, source_target_pairs={{0,4},{1,3},{2,6},{3,1},{4,0},{5,7},{6,2},{7,5},{8,12},{9,11},{10,... | collective-permute-start | bytes 1572872 | tf_op jit(solution)/shard_map/ppermute | solution.py:296
  111.6 6.4 %collective-permute-start.25 = (bf16[64,2048]{1,0:T(8,128)(2,1)S(1)}, bf16[64,2048]{1,0:T(8,128)(2,1)S(1)}, u32[]{:S(2)}, u32[]{:S(2)}) collective-permute-start(bf16[64,2048]{1,0:T(8,128)(2,1)S(1)} %slice.199), channel_id=1, source_target_pairs={{0,4},{1,3},{2,6},{3,1},{4,0},{5,7},{6,2},{7,5},{8,12},{9,11},{10,... | collective-permute-start | bytes 786440 | tf_op jit(solution)/shard_map/ppermute | solution.py:296
  114.7 6.4 %collective-permute-start.29 = (bf16[64,2048]{1,0:T(8,128)(2,1)S(1)}, bf16[64,2048]{1,0:T(8,128)(2,1)S(1)}, u32[]{:S(2)}, u32[]{:S(2)}) collective-permute-start(bf16[64,2048]{1,0:T(8,128)(2,1)S(1)} %slice.198), channel_id=1, source_target_pairs={{0,8},{1,5},{2,10},{3,7},{4,12},{5,1},{6,14},{7,3},{8,0},{9,13},{1... | collective-permute-start | bytes 786440 | tf_op jit(solution)/shard_map/ppermute | solution.py:296
  118.1 5.0 %collective-permute-start.26 = (bf16[32,2048]{1,0:T(8,128)(2,1)S(1)}, bf16[32,2048]{1,0:T(8,128)(2,1)S(1)}, u32[]{:S(2)}, u32[]{:S(2)}) collective-permute-start(bf16[32,2048]{1,0:T(8,128)(2,1)S(1)} %slice.203), channel_id=1, source_target_pairs={{0,8},{1,5},{2,10},{3,7},{4,12},{5,1},{6,14},{7,3},{8,0},{9,13},{1... | collective-permute-start | bytes 393224 | tf_op jit(solution)/shard_map/ppermute | solution.py:296
  121.2 5.0 %collective-permute-start.30 = (bf16[32,2048]{1,0:T(8,128)(2,1)S(1)}, bf16[32,2048]{1,0:T(8,128)(2,1)S(1)}, u32[]{:S(2)}, u32[]{:S(2)}) collective-permute-start(bf16[32,2048]{1,0:T(8,128)(2,1)S(1)} %slice.202), channel_id=1, source_target_pairs={{0,2},{1,9},{2,0},{3,11},{4,6},{5,13},{6,4},{7,15},{8,10},{9,1},{1... | collective-permute-start | bytes 393224 | tf_op jit(solution)/shard_map/ppermute | solution.py:296
  123.2 5.9 %collective-permute-start.27 = (bf16[16,2048]{1,0:T(8,128)(2,1)S(1)}, bf16[16,2048]{1,0:T(8,128)(2,1)S(1)}, u32[]{:S(2)}, u32[]{:S(2)}) collective-permute-start(bf16[16,2048]{1,0:T(8,128)(2,1)S(1)} %slice.207), channel_id=1, source_target_pairs={{0,16},{1,17},{2,18},{3,19},{4,20},{5,21},{6,22},{7,23},{8,24},{9,... | collective-permute-start | bytes 196616 | tf_op jit(solution)/shard_map/ppermute | solution.py:296
  126.3 5.7 %collective-permute-start.31 = (bf16[16,2048]{1,0:T(8,128)(2,1)S(1)}, bf16[16,2048]{1,0:T(8,128)(2,1)S(1)}, u32[]{:S(2)}, u32[]{:S(2)}) collective-permute-start(bf16[16,2048]{1,0:T(8,128)(2,1)S(1)} %slice.206), channel_id=1, source_target_pairs={{0,16},{1,17},{2,18},{3,19},{4,20},{5,21},{6,22},{7,23},{8,24},{9,... | collective-permute-start | bytes 196616 | tf_op jit(solution)/shard_map/ppermute | solution.py:296
  (10 other events, 134.9 us)

commit v10 on v8

--- a/solution.py
+++ b/solution.py
@@ -108,7 +108,7 @@
     )(core, lengths, queries, new_kv, cache_kv)
 
 
-P_TILE = 512
+P_TILE = 1024
 
 
 def spans(chunks, width):

time: 133 us -> 133 us (level)
  no operation moved by 1% of the time
where the time goes in v10:
time: 133 us
  waiting for transfers between devices  60.8 us (46%)
  starting transfers between devices  38.9 us (29%)
  Pallas kernels  27 us (20%)
  local copies, waits for them, and re-layouts  3.47 us (3%)
  other arithmetic  2.27 us (2%)
    ppermute x16, waiting for transfers between devices, reduce_slots(): came = lax.ppermute(sent[c], 'dp', swap_step(step, order, devices))  40.3 us
    ppermute x16, starting transfers between devices, reduce_slots(): came = lax.ppermute(sent[c], 'dp', swap_step(step, order, devices))  17.7 us
    ppermute x12, waiting for transfers between devices, gather_slots(): came = lax.ppermute(own[c], 'dp', swap_step(step, order, devices))  11.9 us
    ppermute x12, starting transfers between devices, gather_slots(): came = lax.ppermute(own[c], 'dp', swap_step(step, order, devices))  11.9 us
    all_to_all x1, waiting for transfers between devices, per_device(): lax.all_to_all(attn_out, 'dp', split_axis=0, concat_axis=0, axis_index_gr...  8.55 us
    all_to_all x1, starting transfers between devices, per_device(): lax.all_to_all(attn_out, 'dp', split_axis=0, concat_axis=0, axis_index_gr...  8.31 us
    pallas_call x1, Pallas kernels, bring(): pl.pallas_call(bring_kernel, out_shape=[jax.ShapeDtypeStruct(a.shape, a.d...  7.07 us
    pallas_call x1, Pallas kernels, attend(): pl.pallas_call(attend_kernel, out_shape=jax.ShapeDtypeStruct((chips, rows...  4.91 us
  transfers between devices with their start and end apart: 33, of which 22 were waited for; matrix products, arithmetic and copies ran while one was open for 2% of the time, Pallas kernels for 13%

profile of v10, /device:TPU:0, one launch (start us, length us, event | category | flops | bytes accessed | tf_op | source)
XLA Modules:
  0.0 132.9 jit_solution(6911918560217701380)
XLA Ops:
  1.0 4.9 %shard_map.118 = bf16[16,16,512]{2,1,0:T(8,128)(2,1)} custom-call(s32[1]{0:T(128)} %bitcast.core_ref, s32[16]{0:T(128)} %lengths_ref.1, bf16[16,8192]{1,0:T(8,128)(2,1)} %q_ref.1, bf16[2,16,512]{2,1,0:T(8,128)(2,1)} %new_ref.1, bf16[2,16,128,512]{3,2,1,0:T(8,128)(2,1)} %cache_ref.1), custom_call_target="tpu_custom_call" | custom-call | flops 67108864 | bytes 4194304 | tf_op jit(solution)/shard_map/pallas_call | solution.py:94
  6.0 8.3 %all-to-all-start = ((bf16[16,16,512]{2,1,0:T(8,128)(2,1)}), bf16[16,16,512]{2,1,0:T(8,128)(2,1)S(1)}, u32[]{:S(2)}, u32[]{:S(2)}) async-start(bf16[16,16,512]{2,1,0:T(8,128)(2,1)} %shard_map.118), calls=%async_computation | async-start | bytes 524288 | tf_op jit(solution)/shard_map/all_to_all | solution.py:349
  15.8 8.5 %all-to-all-done.blocks_ref = bf16[16,16,512]{2,1,0:T(8,128)(2,1)S(1)} async-done(((bf16[16,16,512]{2,1,0:T(8,128)(2,1)}), bf16[16,16,512]{2,1,0:T(8,128)(2,1)S(1)}, u32[]{:S(2)}, u32[]{:S(2)}) %all-to-all-start) | async-done | bytes 262176 | tf_op jit(solution)/shard_map/all_to_all | solution.py:349
  24.4 2.0 %shard_map.120 = (bf16[128,2048]{1,0:T(8,128)(2,1)S(1)}, bf16[128,2048]{1,0:T(8,128)(2,1)S(1)}) custom-call(s32[16]{0:T(128)S(1)} %add_xor_fusion.index_ref, bf16[16,16,512]{2,1,0:T(8,128)(2,1)S(1)} %all-to-all-done.blocks_ref, bf16[256,4096]{1,0:T(8,128)(2,1)S(1)} %copy-done, bf16[256,4096]{1,0:T(8,128)(2,1)} %collective-permute-done.other_ref), custom_call_target="tpu_custom_call" | custom-call | flops 536870912 | bytes 2097152 | tf_op jit(solution)/shard_map/pallas_call | solution.py:153
  27.5 2.0 %shard_map.119 = (bf16[128,2048]{1,0:T(8,128)(2,1)S(1)}, bf16[128,2048]{1,0:T(8,128)(2,1)S(1)}) custom-call(s32[16]{0:T(128)S(1)} %add_xor_fusion.index_ref, bf16[16,16,512]{2,1,0:T(8,128)(2,1)S(1)} %all-to-all-done.blocks_ref, bf16[256,4096]{1,0:T(8,128)(2,1)S(1)} %copy-done, bf16[256,4096]{1,0:T(8,128)(2,1)} %collective-permute-done.other_ref), custom_call_target="tpu_custom_call" | custom-call | flops 536870912 | bytes 2097152 | tf_op jit(solution)/shard_map/pallas_call | solution.py:153
  30.2 5.5 %collective-permute-done.5 = bf16[128,2048]{1,0:T(8,128)(2,1)S(1)} collective-permute-done((bf16[128,2048]{1,0:T(8,128)(2,1)S(1)}, bf16[128,2048]{1,0:T(8,128)(2,1)S(1)}, u32[]{:S(2)}, u32[]{:S(2)}) %collective-permute-start.5) | collective-permute-done | bytes 524320 | tf_op jit(solution)/shard_map/ppermute | solution.py:296
  35.8 1.5 %collective-permute-start.6 = (bf16[64,2048]{1,0:T(8,128)(2,1)S(1)}, bf16[64,2048]{1,0:T(8,128)(2,1)S(1)}, u32[]{:S(2)}, u32[]{:S(2)}) collective-permute-start(bf16[64,2048]{1,0:T(8,128)(2,1)S(1)} %slice.200), channel_id=1, source_target_pairs={{0,8},{1,5},{2,10},{3,7},{4,12},{5,1},{6,14},{7,3},{8,0},{9,13},{1... | collective-permute-start | bytes 786440 | tf_op jit(solution)/shard_map/ppermute | solution.py:296
  37.4 1.4 %collective-permute-done.1 = bf16[128,2048]{1,0:T(8,128)(2,1)S(1)} collective-permute-done((bf16[128,2048]{1,0:T(8,128)(2,1)S(1)}, bf16[128,2048]{1,0:T(8,128)(2,1)S(1)}, u32[]{:S(2)}, u32[]{:S(2)}) %collective-permute-start.1) | collective-permute-done | bytes 524320 | tf_op jit(solution)/shard_map/ppermute | solution.py:296
  39.0 2.7 %collective-permute-start.2 = (bf16[64,2048]{1,0:T(8,128)(2,1)S(1)}, bf16[64,2048]{1,0:T(8,128)(2,1)S(1)}, u32[]{:S(2)}, u32[]{:S(2)}) collective-permute-start(bf16[64,2048]{1,0:T(8,128)(2,1)S(1)} %slice.201), channel_id=1, source_target_pairs={{0,4},{1,3},{2,6},{3,1},{4,0},{5,7},{6,2},{7,5},{8,12},{9,11},{10,... | collective-permute-start | bytes 786440 | tf_op jit(solution)/shard_map/ppermute | solution.py:296
  41.7 1.5 %collective-permute-done.6 = bf16[64,2048]{1,0:T(8,128)(2,1)S(1)} collective-permute-done((bf16[64,2048]{1,0:T(8,128)(2,1)S(1)}, bf16[64,2048]{1,0:T(8,128)(2,1)S(1)}, u32[]{:S(2)}, u32[]{:S(2)}) %collective-permute-start.6) | collective-permute-done | bytes 262176 | tf_op jit(solution)/shard_map/ppermute | solution.py:296
  43.4 3.7 %collective-permute-done.2 = bf16[64,2048]{1,0:T(8,128)(2,1)S(1)} collective-permute-done((bf16[64,2048]{1,0:T(8,128)(2,1)S(1)}, bf16[64,2048]{1,0:T(8,128)(2,1)S(1)}, u32[]{:S(2)}, u32[]{:S(2)}) %collective-permute-start.2) | collective-permute-done | bytes 262176 | tf_op jit(solution)/shard_map/ppermute | solution.py:296
  49.6 3.3 %collective-permute-done.3 = bf16[32,2048]{1,0:T(8,128)(2,1)S(1)} collective-permute-done((bf16[32,2048]{1,0:T(8,128)(2,1)S(1)}, bf16[32,2048]{1,0:T(8,128)(2,1)S(1)}, u32[]{:S(2)}, u32[]{:S(2)}) %collective-permute-start.3) | collective-permute-done | bytes 131104 | tf_op jit(solution)/shard_map/ppermute | solution.py:296
  53.6 6.6 %collective-permute-done.4 = bf16[16,2048]{1,0:T(8,128)(2,1)S(1)} collective-permute-done((bf16[16,2048]{1,0:T(8,128)(2,1)S(1)}, bf16[16,2048]{1,0:T(8,128)(2,1)S(1)}, u32[]{:S(2)}, u32[]{:S(2)}) %collective-permute-start.4) | collective-permute-done | bytes 65568 | tf_op jit(solution)/shard_map/ppermute | solution.py:296
  60.6 3.0 %collective-permute-start.16 = (bf16[16,1536]{1,0:T(8,128)(2,1)S(1)}, bf16[16,1536]{1,0:T(8,128)(2,1)S(1)}, u32[]{:S(2)}, u32[]{:S(2)}) collective-permute-start(bf16[16,1536]{1,0:T(8,128)(2,1)S(1)} %get-tuple-element.49), channel_id=1, source_target_pairs={{0,16},{1,17},{2,18},{3,19},{4,20},{5,21},{6,22},{7,23},{8,24},{9,... | collective-permute-start | bytes 147464 | tf_op jit(solution)/shard_map/ppermute | solution.py:311
  63.6 1.8 %collective-permute-done.20 = bf16[16,1024]{1,0:T(8,128)(2,1)S(1)} collective-permute-done((bf16[16,1024]{1,0:T(8,128)(2,1)S(1)}, bf16[16,1024]{1,0:T(8,128)(2,1)S(1)}, u32[]{:S(2)}, u32[]{:S(2)}) %collective-permute-start.20) | collective-permute-done | bytes 32800 | tf_op jit(solution)/shard_map/ppermute | solution.py:311
  66.7 1.7 %collective-permute-start.17 = (bf16[32,1536]{1,0:T(8,128)(2,1)S(1)}, bf16[32,1536]{1,0:T(8,128)(2,1)S(1)}, u32[]{:S(2)}, u32[]{:S(2)}) collective-permute-start(bf16[32,1536]{1,0:T(8,128)(2,1)S(1)} %pad_maximum_fusion.8), channel_id=1, source_target_pairs={{0,8},{1,5},{2,10},{3,7},{4,12},{5,1},{6,14},{7,3},{8,0},{9,13},{1... | collective-permute-start | bytes 294920 | tf_op jit(solution)/shard_map/ppermute | solution.py:311
  70.8 4.3 %collective-permute-done.13 = bf16[32,1664]{1,0:T(8,128)(2,1)S(1)} collective-permute-done((bf16[32,1664]{1,0:T(8,128)(2,1)S(1)}, bf16[32,1664]{1,0:T(8,128)(2,1)S(1)}, u32[]{:S(2)}, u32[]{:S(2)}) %collective-permute-start.13) | collective-permute-done | bytes 106528 | tf_op jit(solution)/shard_map/ppermute | solution.py:311
  76.7 4.3 %collective-permute-done.14 = bf16[64,1664]{1,0:T(8,128)(2,1)S(1)} collective-permute-done((bf16[64,1664]{1,0:T(8,128)(2,1)S(1)}, bf16[64,1664]{1,0:T(8,128)(2,1)S(1)}, u32[]{:S(2)}, u32[]{:S(2)}) %collective-permute-start.14) | collective-permute-done | bytes 213024 | tf_op jit(solution)/shard_map/ppermute | solution.py:311
  84.5 7.1 %shard_map.122 = (bf16[4096,768]{1,0:T(8,128)(2,1)S(1)}, bf16[4096,768]{1,0:T(8,128)(2,1)S(1)}, bf16[768,4096]{1,0:T(8,128)(2,1)S(1)}) custom-call(bf16[128,1024]{1,0:T(8,128)(2,1)S(1)} %pad_maximum_fusion.2.refs_4_.after_ref, bf16[4096,768]{1,0:T(8,128)(2,1)} %collective-permute-done.9.refs_0_, bf16[4096,768]{1,0:T(8,128)(2,1)} %collective-permute-done.10.refs_1_, ...), custom_call_target="tpu_custom_call" | custom-call | bytes 18874368 | tf_op jit(solution)/shard_map/pallas_call | solution.py:182
  93.4 4.0 %shard_map.121 = (bf16[256,4096]{1,0:T(8,128)(2,1)S(1)}, bf16[256,768]{1,0:T(8,128)(2,1)S(1)}, f32[256,1]{1,0:T(8,128)S(1)}) custom-call(s32[2]{0:T(128)S(1)} %pad_add_fusion.chip_ref, bf16[128,1664]{1,0:T(8,128)(2,1)S(1)} %pad_maximum_fusion.refs_0_, bf16[128,1664]{1,0:T(8,128)(2,1)S(1)} %collective-permute-done.15.refs_1_, ...), custom_call_target="tpu_custom_call" | custom-call | flops 3221225472 | bytes 12582912 | tf_op jit(solution)/shard_map/pallas_call | solution.py:240
  97.3 3.4 %shard_map.123.after_ref.active1 = bf16[256,768]{1,0:T(8,128)(2,1)S(1)} custom-call(bf16[256,4096]{1,0:T(8,128)(2,1)S(1)} %get-tuple-element.30.tokens_ref, bf16[4096,768]{1,0:T(8,128)(2,1)S(1)} %get-tuple-element.34.gate_ref, bf16[4096,768]{1,0:T(8,128)(2,1)S(1)} %get-tuple-element.35.up_ref), custom_call_target="tpu_custom_call" | custom-call | flops 3221225472 | bytes 12582912 | tf_op jit(solution)/shard_map/pallas_call | solution.py:248
  100.8 1.8 %shard_map.124 = (bf16[128,2048]{1,0:T(8,128)(2,1)S(1)}, bf16[128,2048]{1,0:T(8,128)(2,1)S(1)}) custom-call(bf16[256,768]{1,0:T(8,128)(2,1)S(1)} %shard_map.123.after_ref.active1, bf16[256,768]{1,0:T(8,128)(2,1)S(1)} %get-tuple-element.36.active0, bf16[256,768]{1,0:T(8,128)(2,1)S(1)} %shard_map.123.after_ref.active1, ...), custom_call_target="tpu_custom_call" | custom-call | flops 1610612736 | bytes 6291456 | tf_op jit(solution)/shard_map/pallas_call | solution.py:259
  102.6 1.5 %collective-permute-start.24 = (bf16[128,2048]{1,0:T(8,128)(2,1)S(1)}, bf16[128,2048]{1,0:T(8,128)(2,1)S(1)}, u32[]{:S(2)}, u32[]{:S(2)}) collective-permute-start(bf16[128,2048]{1,0:T(8,128)(2,1)S(1)} %get-tuple-element.40.after_ref), channel_id=1, source_target_pairs={{0,2},{1,9},{2,0},{3,11},{4,6},{5,13},{6,4},{7,15},{8,10},{9,1},{1... | collective-permute-start | bytes 1572872 | tf_op jit(solution)/shard_map/ppermute | solution.py:296
  104.1 1.8 %shard_map.125 = (bf16[128,2048]{1,0:T(8,128)(2,1)S(1)}, bf16[128,2048]{1,0:T(8,128)(2,1)S(1)}) custom-call(bf16[128,2048]{1,0:T(8,128)(2,1)S(1)} %get-tuple-element.40.after_ref, bf16[256,768]{1,0:T(8,128)(2,1)S(1)} %get-tuple-element.36.active0, bf16[256,768]{1,0:T(8,128)(2,1)S(1)} %shard_map.123.after_ref.active1, ...), custom_call_target="tpu_custom_call" | custom-call | flops 1610612736 | bytes 6291456 | tf_op jit(solution)/shard_map/pallas_call | solution.py:259
  106.8 5.1 %collective-permute-done.24 = bf16[128,2048]{1,0:T(8,128)(2,1)S(1)} collective-permute-done((bf16[128,2048]{1,0:T(8,128)(2,1)S(1)}, bf16[128,2048]{1,0:T(8,128)(2,1)S(1)}, u32[]{:S(2)}, u32[]{:S(2)}) %collective-permute-start.24) | collective-permute-done | bytes 524320 | tf_op jit(solution)/shard_map/ppermute | solution.py:296
  113.4 1.8 %collective-permute-done.28 = bf16[128,2048]{1,0:T(8,128)(2,1)S(1)} collective-permute-done((bf16[128,2048]{1,0:T(8,128)(2,1)S(1)}, bf16[128,2048]{1,0:T(8,128)(2,1)S(1)}, u32[]{:S(2)}, u32[]{:S(2)}) %collective-permute-start.28) | collective-permute-done | bytes 524320 | tf_op jit(solution)/shard_map/ppermute | solution.py:296
  116.7 1.8 %collective-permute-done.25 = bf16[64,2048]{1,0:T(8,128)(2,1)S(1)} collective-permute-done((bf16[64,2048]{1,0:T(8,128)(2,1)S(1)}, bf16[64,2048]{1,0:T(8,128)(2,1)S(1)}, u32[]{:S(2)}, u32[]{:S(2)}) %collective-permute-start.25) | collective-permute-done | bytes 262176 | tf_op jit(solution)/shard_map/ppermute | solution.py:296
  118.5 1.4 %collective-permute-start.26 = (bf16[32,2048]{1,0:T(8,128)(2,1)S(1)}, bf16[32,2048]{1,0:T(8,128)(2,1)S(1)}, u32[]{:S(2)}, u32[]{:S(2)}) collective-permute-start(bf16[32,2048]{1,0:T(8,128)(2,1)S(1)} %slice.203), channel_id=1, source_target_pairs={{0,8},{1,5},{2,10},{3,7},{4,12},{5,1},{6,14},{7,3},{8,0},{9,13},{1... | collective-permute-start | bytes 393224 | tf_op jit(solution)/shard_map/ppermute | solution.py:296
  119.9 1.9 %collective-permute-done.29 = bf16[64,2048]{1,0:T(8,128)(2,1)S(1)} collective-permute-done((bf16[64,2048]{1,0:T(8,128)(2,1)S(1)}, bf16[64,2048]{1,0:T(8,128)(2,1)S(1)}, u32[]{:S(2)}, u32[]{:S(2)}) %collective-permute-start.29) | collective-permute-done | bytes 262176 | tf_op jit(solution)/shard_map/ppermute | solution.py:296
  123.6 1.4 %collective-permute-start.27 = (bf16[16,2048]{1,0:T(8,128)(2,1)S(1)}, bf16[16,2048]{1,0:T(8,128)(2,1)S(1)}, u32[]{:S(2)}, u32[]{:S(2)}) collective-permute-start(bf16[16,2048]{1,0:T(8,128)(2,1)S(1)} %slice.207), channel_id=1, source_target_pairs={{0,16},{1,17},{2,18},{3,19},{4,20},{5,21},{6,22},{7,23},{8,24},{9,... | collective-permute-start | bytes 196616 | tf_op jit(solution)/shard_map/ppermute | solution.py:296
  125.0 1.9 %collective-permute-done.30 = bf16[32,2048]{1,0:T(8,128)(2,1)S(1)} collective-permute-done((bf16[32,2048]{1,0:T(8,128)(2,1)S(1)}, bf16[32,2048]{1,0:T(8,128)(2,1)S(1)}, u32[]{:S(2)}, u32[]{:S(2)}) %collective-permute-start.30) | collective-permute-done | bytes 131104 | tf_op jit(solution)/shard_map/ppermute | solution.py:296
  128.9 3.3 %collective-permute-done.31 = bf16[16,2048]{1,0:T(8,128)(2,1)S(1)} collective-permute-done((bf16[16,2048]{1,0:T(8,128)(2,1)S(1)}, bf16[16,2048]{1,0:T(8,128)(2,1)S(1)}, u32[]{:S(2)}, u32[]{:S(2)}) %collective-permute-start.31) | collective-permute-done | bytes 65568 | tf_op jit(solution)/shard_map/ppermute | solution.py:296
  (113 shorter events, 27.1 us)
Async XLA Ops:
  0.0 24.4 %collective-permute-start = (bf16[256,4096]{1,0:T(8,128)(2,1)}, bf16[256,4096]{1,0:T(8,128)(2,1)}, u32[]{:S(2)}, u32[]{:S(2)}) collective-permute-start(bf16[256,4096]{1,0:T(8,128)(2,1)} %own_ref.3), channel_id=1, source_target_pairs={{0,1},{1,0},{2,3},{3,2},{4,5},{5,4},{6,7},{7,6},{8,9},{9,8},{10,11... | collective-permute-start | bytes 6291464 | tf_op jit(solution)/shard_map/ppermute | solution.py:343
  0.5 60.0 %collective-permute-start.11 = (bf16[768,4096]{1,0:T(8,128)(2,1)}, bf16[768,4096]{1,0:T(8,128)(2,1)}, u32[]{:S(2)}, u32[]{:S(2)}) collective-permute-start(bf16[768,4096]{1,0:T(8,128)(2,1)} %bitcast.5), channel_id=1, source_target_pairs={{0,1},{1,0},{2,3},{3,2},{4,5},{5,4},{6,7},{7,6},{8,9},{9,8},{10,11... | collective-permute-start | bytes 18874376 | tf_op jit(solution)/shard_map/ppermute | solution.py:346
  0.5 59.9 %collective-permute-start.10 = (bf16[4096,768]{1,0:T(8,128)(2,1)}, bf16[4096,768]{1,0:T(8,128)(2,1)}, u32[]{:S(2)}, u32[]{:S(2)}) collective-permute-start(bf16[4096,768]{1,0:T(8,128)(2,1)} %bitcast.14), channel_id=1, source_target_pairs={{0,1},{1,0},{2,3},{3,2},{4,5},{5,4},{6,7},{7,6},{8,9},{9,8},{10,11... | collective-permute-start | bytes 18874376 | tf_op jit(solution)/shard_map/ppermute | solution.py:345
  1.0 59.5 %collective-permute-start.9 = (bf16[4096,768]{1,0:T(8,128)(2,1)}, bf16[4096,768]{1,0:T(8,128)(2,1)}, u32[]{:S(2)}, u32[]{:S(2)}) collective-permute-start(bf16[4096,768]{1,0:T(8,128)(2,1)} %bitcast.10), channel_id=1, source_target_pairs={{0,1},{1,0},{2,3},{3,2},{4,5},{5,4},{6,7},{7,6},{8,9},{9,8},{10,11... | collective-permute-start | bytes 18874376 | tf_op jit(solution)/shard_map/ppermute | solution.py:344
  6.0 18.4 %all-to-all-start = ((bf16[16,16,512]{2,1,0:T(8,128)(2,1)}), bf16[16,16,512]{2,1,0:T(8,128)(2,1)S(1)}, u32[]{:S(2)}, u32[]{:S(2)}) async-start(bf16[16,16,512]{2,1,0:T(8,128)(2,1)} %shard_map.118), calls=%async_computation | async-start | bytes 524288 | tf_op jit(solution)/shard_map/all_to_all | solution.py:349
  26.4 9.3 %collective-permute-start.5 = (bf16[128,2048]{1,0:T(8,128)(2,1)S(1)}, bf16[128,2048]{1,0:T(8,128)(2,1)S(1)}, u32[]{:S(2)}, u32[]{:S(2)}) collective-permute-start(bf16[128,2048]{1,0:T(8,128)(2,1)S(1)} %get-tuple-element.27), channel_id=1, source_target_pairs={{0,4},{1,3},{2,6},{3,1},{4,0},{5,7},{6,2},{7,5},{8,12},{9,11},{10,... | collective-permute-start | bytes 1572872 | tf_op jit(solution)/shard_map/ppermute | solution.py:296
  29.5 9.2 %collective-permute-start.1 = (bf16[128,2048]{1,0:T(8,128)(2,1)S(1)}, bf16[128,2048]{1,0:T(8,128)(2,1)S(1)}, u32[]{:S(2)}, u32[]{:S(2)}) collective-permute-start(bf16[128,2048]{1,0:T(8,128)(2,1)S(1)} %get-tuple-element.25), channel_id=1, source_target_pairs={{0,2},{1,9},{2,0},{3,11},{4,6},{5,13},{6,4},{7,15},{8,10},{9,1},{1... | collective-permute-start | bytes 1572872 | tf_op jit(solution)/shard_map/ppermute | solution.py:296
  35.8 7.3 %collective-permute-start.6 = (bf16[64,2048]{1,0:T(8,128)(2,1)S(1)}, bf16[64,2048]{1,0:T(8,128)(2,1)S(1)}, u32[]{:S(2)}, u32[]{:S(2)}) collective-permute-start(bf16[64,2048]{1,0:T(8,128)(2,1)S(1)} %slice.200), channel_id=1, source_target_pairs={{0,8},{1,5},{2,10},{3,7},{4,12},{5,1},{6,14},{7,3},{8,0},{9,13},{1... | collective-permute-start | bytes 786440 | tf_op jit(solution)/shard_map/ppermute | solution.py:296
  39.0 8.1 %collective-permute-start.2 = (bf16[64,2048]{1,0:T(8,128)(2,1)S(1)}, bf16[64,2048]{1,0:T(8,128)(2,1)S(1)}, u32[]{:S(2)}, u32[]{:S(2)}) collective-permute-start(bf16[64,2048]{1,0:T(8,128)(2,1)S(1)} %slice.201), channel_id=1, source_target_pairs={{0,4},{1,3},{2,6},{3,1},{4,0},{5,7},{6,2},{7,5},{8,12},{9,11},{10,... | collective-permute-start | bytes 786440 | tf_op jit(solution)/shard_map/ppermute | solution.py:296
  43.3 5.0 %collective-permute-start.7 = (bf16[32,2048]{1,0:T(8,128)(2,1)S(1)}, bf16[32,2048]{1,0:T(8,128)(2,1)S(1)}, u32[]{:S(2)}, u32[]{:S(2)}) collective-permute-start(bf16[32,2048]{1,0:T(8,128)(2,1)S(1)} %slice.204), channel_id=1, source_target_pairs={{0,2},{1,9},{2,0},{3,11},{4,6},{5,13},{6,4},{7,15},{8,10},{9,1},{1... | collective-permute-start | bytes 393224 | tf_op jit(solution)/shard_map/ppermute | solution.py:296
  47.1 5.7 %collective-permute-start.3 = (bf16[32,2048]{1,0:T(8,128)(2,1)S(1)}, bf16[32,2048]{1,0:T(8,128)(2,1)S(1)}, u32[]{:S(2)}, u32[]{:S(2)}) collective-permute-start(bf16[32,2048]{1,0:T(8,128)(2,1)S(1)} %slice.205), channel_id=1, source_target_pairs={{0,8},{1,5},{2,10},{3,7},{4,12},{5,1},{6,14},{7,3},{8,0},{9,13},{1... | collective-permute-start | bytes 393224 | tf_op jit(solution)/shard_map/ppermute | solution.py:296
  48.4 5.2 %collective-permute-start.8 = (bf16[16,2048]{1,0:T(8,128)(2,1)S(1)}, bf16[16,2048]{1,0:T(8,128)(2,1)S(1)}, u32[]{:S(2)}, u32[]{:S(2)}) collective-permute-start(bf16[16,2048]{1,0:T(8,128)(2,1)S(1)} %slice.208), channel_id=1, source_target_pairs={{0,16},{1,17},{2,18},{3,19},{4,20},{5,21},{6,22},{7,23},{8,24},{9,... | collective-permute-start | bytes 196616 | tf_op jit(solution)/shard_map/ppermute | solution.py:296
  52.9 7.2 %collective-permute-start.4 = (bf16[16,2048]{1,0:T(8,128)(2,1)S(1)}, bf16[16,2048]{1,0:T(8,128)(2,1)S(1)}, u32[]{:S(2)}, u32[]{:S(2)}) collective-permute-start(bf16[16,2048]{1,0:T(8,128)(2,1)S(1)} %slice.209), channel_id=1, source_target_pairs={{0,16},{1,17},{2,18},{3,19},{4,20},{5,21},{6,22},{7,23},{8,24},{9,... | collective-permute-start | bytes 196616 | tf_op jit(solution)/shard_map/ppermute | solution.py:296
  60.5 5.0 %collective-permute-start.20 = (bf16[16,1024]{1,0:T(8,128)(2,1)S(1)}, bf16[16,1024]{1,0:T(8,128)(2,1)S(1)}, u32[]{:S(2)}, u32[]{:S(2)}) collective-permute-start(bf16[16,1024]{1,0:T(8,128)(2,1)S(1)} %slice.123), channel_id=1, source_target_pairs={{0,16},{1,17},{2,18},{3,19},{4,20},{5,21},{6,22},{7,23},{8,24},{9,... | collective-permute-start | bytes 98312 | tf_op jit(solution)/shard_map/ppermute | solution.py:311
  60.6 6.1 %collective-permute-start.16 = (bf16[16,1536]{1,0:T(8,128)(2,1)S(1)}, bf16[16,1536]{1,0:T(8,128)(2,1)S(1)}, u32[]{:S(2)}, u32[]{:S(2)}) collective-permute-start(bf16[16,1536]{1,0:T(8,128)(2,1)S(1)} %get-tuple-element.49), channel_id=1, source_target_pairs={{0,16},{1,17},{2,18},{3,19},{4,20},{5,21},{6,22},{7,23},{8,24},{9,... | collective-permute-start | bytes 147464 | tf_op jit(solution)/shard_map/ppermute | solution.py:311
  63.5 5.6 %collective-permute-start.12 = (bf16[16,1664]{1,0:T(8,128)(2,1)S(1)}, bf16[16,1664]{1,0:T(8,128)(2,1)S(1)}, u32[]{:S(2)}, u32[]{:S(2)}) collective-permute-start(bf16[16,1664]{1,0:T(8,128)(2,1)S(1)} %pad_maximum_fusion.10), channel_id=1, source_target_pairs={{0,16},{1,17},{2,18},{3,19},{4,20},{5,21},{6,22},{7,23},{8,24},{9,... | collective-permute-start | bytes 159752 | tf_op jit(solution)/shard_map/ppermute | solution.py:311
  66.7 9.8 %collective-permute-start.17 = (bf16[32,1536]{1,0:T(8,128)(2,1)S(1)}, bf16[32,1536]{1,0:T(8,128)(2,1)S(1)}, u32[]{:S(2)}, u32[]{:S(2)}) collective-permute-start(bf16[32,1536]{1,0:T(8,128)(2,1)S(1)} %pad_maximum_fusion.8), channel_id=1, source_target_pairs={{0,8},{1,5},{2,10},{3,7},{4,12},{5,1},{6,14},{7,3},{8,0},{9,13},{1... | collective-permute-start | bytes 294920 | tf_op jit(solution)/shard_map/ppermute | solution.py:311
  69.2 5.9 %collective-permute-start.13 = (bf16[32,1664]{1,0:T(8,128)(2,1)S(1)}, bf16[32,1664]{1,0:T(8,128)(2,1)S(1)}, u32[]{:S(2)}, u32[]{:S(2)}) collective-permute-start(bf16[32,1664]{1,0:T(8,128)(2,1)S(1)} %pad_maximum_fusion.7), channel_id=1, source_target_pairs={{0,8},{1,5},{2,10},{3,7},{4,12},{5,1},{6,14},{7,3},{8,0},{9,13},{1... | collective-permute-start | bytes 319496 | tf_op jit(solution)/shard_map/ppermute | solution.py:311
  69.7 13.3 %collective-permute-start.22 = (bf16[64,1024]{1,0:T(8,128)(2,1)S(1)}, bf16[64,1024]{1,0:T(8,128)(2,1)S(1)}, u32[]{:S(2)}, u32[]{:S(2)}) collective-permute-start(bf16[64,1024]{1,0:T(8,128)(2,1)S(1)} %pad_maximum_fusion.5), channel_id=1, source_target_pairs={{0,2},{1,9},{2,0},{3,11},{4,6},{5,13},{6,4},{7,15},{8,10},{9,1},{1... | collective-permute-start | bytes 393224 | tf_op jit(solution)/shard_map/ppermute | solution.py:311
  75.1 5.9 %collective-permute-start.14 = (bf16[64,1664]{1,0:T(8,128)(2,1)S(1)}, bf16[64,1664]{1,0:T(8,128)(2,1)S(1)}, u32[]{:S(2)}, u32[]{:S(2)}) collective-permute-start(bf16[64,1664]{1,0:T(8,128)(2,1)S(1)} %pad_maximum_fusion.3), channel_id=1, source_target_pairs={{0,4},{1,3},{2,6},{3,1},{4,0},{5,7},{6,2},{7,5},{8,12},{9,11},{10,... | collective-permute-start | bytes 638984 | tf_op jit(solution)/shard_map/ppermute | solution.py:311
  76.5 5.7 %collective-permute-start.18 = (bf16[64,1536]{1,0:T(8,128)(2,1)S(1)}, bf16[64,1536]{1,0:T(8,128)(2,1)S(1)}, u32[]{:S(2)}, u32[]{:S(2)}) collective-permute-start(bf16[64,1536]{1,0:T(8,128)(2,1)S(1)} %pad_maximum_fusion.4), channel_id=1, source_target_pairs={{0,2},{1,9},{2,0},{3,11},{4,6},{5,13},{6,4},{7,15},{8,10},{9,1},{1... | collective-permute-start | bytes 589832 | tf_op jit(solution)/shard_map/ppermute | solution.py:311
  81.1 10.6 %collective-permute-start.15 = (bf16[128,1664]{1,0:T(8,128)(2,1)S(1)}, bf16[128,1664]{1,0:T(8,128)(2,1)S(1)}, u32[]{:S(2)}, u32[]{:S(2)}) collective-permute-start(bf16[128,1664]{1,0:T(8,128)(2,1)S(1)} %pad_maximum_fusion.refs_0_), channel_id=1, source_target_pairs={{0,2},{1,9},{2,0},{3,11},{4,6},{5,13},{6,4},{7,15},{8,10},{9,1},{1... | collective-permute-start | bytes 1277960 | tf_op jit(solution)/shard_map/ppermute | solution.py:311
  82.3 9.4 %collective-permute-start.19 = (bf16[128,1536]{1,0:T(8,128)(2,1)S(1)}, bf16[128,1536]{1,0:T(8,128)(2,1)S(1)}, u32[]{:S(2)}, u32[]{:S(2)}) collective-permute-start(bf16[128,1536]{1,0:T(8,128)(2,1)S(1)} %pad_maximum_fusion.1.refs_2_), channel_id=1, source_target_pairs={{0,4},{1,3},{2,6},{3,1},{4,0},{5,7},{6,2},{7,5},{8,12},{9,11},{10,... | collective-permute-start | bytes 1179656 | tf_op jit(solution)/shard_map/ppermute | solution.py:311
  83.1 8.5 %collective-permute-start.23 = (bf16[128,1024]{1,0:T(8,128)(2,1)S(1)}, bf16[128,1024]{1,0:T(8,128)(2,1)S(1)}, u32[]{:S(2)}, u32[]{:S(2)}) collective-permute-start(bf16[128,1024]{1,0:T(8,128)(2,1)S(1)} %pad_maximum_fusion.2.refs_4_.after_ref), channel_id=1, source_target_pairs={{0,8},{1,5},{2,10},{3,7},{4,12},{5,1},{6,14},{7,3},{8,0},{9,13},{1... | collective-permute-start | bytes 786440 | tf_op jit(solution)/shard_map/ppermute | solution.py:311
  102.6 9.2 %collective-permute-start.24 = (bf16[128,2048]{1,0:T(8,128)(2,1)S(1)}, bf16[128,2048]{1,0:T(8,128)(2,1)S(1)}, u32[]{:S(2)}, u32[]{:S(2)}) collective-permute-start(bf16[128,2048]{1,0:T(8,128)(2,1)S(1)} %get-tuple-element.40.after_ref), channel_id=1, source_target_pairs={{0,2},{1,9},{2,0},{3,11},{4,6},{5,13},{6,4},{7,15},{8,10},{9,1},{1... | collective-permute-start | bytes 1572872 | tf_op jit(solution)/shard_map/ppermute | solution.py:296
  105.9 9.2 %collective-permute-start.28 = (bf16[128,2048]{1,0:T(8,128)(2,1)S(1)}, bf16[128,2048]{1,0:T(8,128)(2,1)S(1)}, u32[]{:S(2)}, u32[]{:S(2)}) collective-permute-start(bf16[128,2048]{1,0:T(8,128)(2,1)S(1)} %get-tuple-element.42), channel_id=1, source_target_pairs={{0,4},{1,3},{2,6},{3,1},{4,0},{5,7},{6,2},{7,5},{8,12},{9,11},{10,... | collective-permute-start | bytes 1572872 | tf_op jit(solution)/shard_map/ppermute | solution.py:296
  112.0 6.4 %collective-permute-start.25 = (bf16[64,2048]{1,0:T(8,128)(2,1)S(1)}, bf16[64,2048]{1,0:T(8,128)(2,1)S(1)}, u32[]{:S(2)}, u32[]{:S(2)}) collective-permute-start(bf16[64,2048]{1,0:T(8,128)(2,1)S(1)} %slice.199), channel_id=1, source_target_pairs={{0,4},{1,3},{2,6},{3,1},{4,0},{5,7},{6,2},{7,5},{8,12},{9,11},{10,... | collective-permute-start | bytes 786440 | tf_op jit(solution)/shard_map/ppermute | solution.py:296
  115.4 6.4 %collective-permute-start.29 = (bf16[64,2048]{1,0:T(8,128)(2,1)S(1)}, bf16[64,2048]{1,0:T(8,128)(2,1)S(1)}, u32[]{:S(2)}, u32[]{:S(2)}) collective-permute-start(bf16[64,2048]{1,0:T(8,128)(2,1)S(1)} %slice.198), channel_id=1, source_target_pairs={{0,8},{1,5},{2,10},{3,7},{4,12},{5,1},{6,14},{7,3},{8,0},{9,13},{1... | collective-permute-start | bytes 786440 | tf_op jit(solution)/shard_map/ppermute | solution.py:296
  118.5 5.0 %collective-permute-start.26 = (bf16[32,2048]{1,0:T(8,128)(2,1)S(1)}, bf16[32,2048]{1,0:T(8,128)(2,1)S(1)}, u32[]{:S(2)}, u32[]{:S(2)}) collective-permute-start(bf16[32,2048]{1,0:T(8,128)(2,1)S(1)} %slice.203), channel_id=1, source_target_pairs={{0,8},{1,5},{2,10},{3,7},{4,12},{5,1},{6,14},{7,3},{8,0},{9,13},{1... | collective-permute-start | bytes 393224 | tf_op jit(solution)/shard_map/ppermute | solution.py:296
  121.9 5.0 %collective-permute-start.30 = (bf16[32,2048]{1,0:T(8,128)(2,1)S(1)}, bf16[32,2048]{1,0:T(8,128)(2,1)S(1)}, u32[]{:S(2)}, u32[]{:S(2)}) collective-permute-start(bf16[32,2048]{1,0:T(8,128)(2,1)S(1)} %slice.202), channel_id=1, source_target_pairs={{0,2},{1,9},{2,0},{3,11},{4,6},{5,13},{6,4},{7,15},{8,10},{9,1},{1... | collective-permute-start | bytes 393224 | tf_op jit(solution)/shard_map/ppermute | solution.py:296
  123.6 5.2 %collective-permute-start.27 = (bf16[16,2048]{1,0:T(8,128)(2,1)S(1)}, bf16[16,2048]{1,0:T(8,128)(2,1)S(1)}, u32[]{:S(2)}, u32[]{:S(2)}) collective-permute-start(bf16[16,2048]{1,0:T(8,128)(2,1)S(1)} %slice.207), channel_id=1, source_target_pairs={{0,16},{1,17},{2,18},{3,19},{4,20},{5,21},{6,22},{7,23},{8,24},{9,... | collective-permute-start | bytes 196616 | tf_op jit(solution)/shard_map/ppermute | solution.py:296
  127.0 5.2 %collective-permute-start.31 = (bf16[16,2048]{1,0:T(8,128)(2,1)S(1)}, bf16[16,2048]{1,0:T(8,128)(2,1)S(1)}, u32[]{:S(2)}, u32[]{:S(2)}) collective-permute-start(bf16[16,2048]{1,0:T(8,128)(2,1)S(1)} %slice.206), channel_id=1, source_target_pairs={{0,16},{1,17},{2,18},{3,19},{4,20},{5,21},{6,22},{7,23},{8,24},{9,... | collective-permute-start | bytes 196616 | tf_op jit(solution)/shard_map/ppermute | solution.py:296
  (10 other events, 134.1 us)
